TPU v7x, 32 devices: a whole 2x2x4 slice. The times are simulated.
32 devices in a mesh: replica: 2 (over y), fsdp: 4 (over x, core), context: 4 (over z).
Axes of the slice: x: 2, y: 2, z: 4, core: 2. Of those that a mesh axis runs over, the one named last changes fastest.
Arguments:
- tokens: bfloat16 [8, 1024, 2048], P(('replica', 'fsdp'), 'context'), may hold values from -6 to 6
- places: int32 [8, 1024], P(('replica', 'fsdp')), may hold values from 0 to 1023, as said below
- cotangent: bfloat16 [8, 1024, 2048], P(('replica', 'fsdp'), 'context'), may hold values from -6 to 6
- gain_attn: bfloat16 [2048], P(('fsdp', 'context')), may hold values from 0.5 to 1.5
- gain_mlp: bfloat16 [2048], P(('fsdp', 'context')), may hold values from 0.5 to 1.5
- w_query: bfloat16 [2048, 2048], P(('fsdp', 'context')), may hold values from -0.125 to 0.125
- key_projection: bfloat16 [2048, 512], P(('fsdp', 'context')), may hold values from -0.125 to 0.125
- value_projection: bfloat16 [2048, 512], P(('fsdp', 'context')), may hold values from -0.125 to 0.125
- w_out: bfloat16 [2048, 2048], P(('fsdp', 'context')), may hold values from -0.5 to 0.5
- w_gate: bfloat16 [2048, 8192], P(None, ('fsdp', 'context')), may hold values from -0.125 to 0.125
- w_up: bfloat16 [2048, 8192], P(None, ('fsdp', 'context')), may hold values from -0.125 to 0.125
- w_down: bfloat16 [8192, 2048], P(('fsdp', 'context')), may hold values from -0.0625 to 0.0625
Outputs:
- out: bfloat16 [8, 1024, 2048], P(('replica', 'fsdp'), 'context')
- grad_tokens: bfloat16 [8, 1024, 2048], P(('replica', 'fsdp'), 'context')
- grad_w_query: float32 [2048, 2048], P(('fsdp', 'context'))
- grad_w_key: float32 [2048, 512], P(('fsdp', 'context'))
- grad_w_value: float32 [2048, 512], P(('fsdp', 'context'))
- grad_w_out: float32 [2048, 2048], P(('fsdp', 'context'))
- grad_w_gate: float32 [2048, 8192], P(None, ('fsdp', 'context'))
- grad_w_up: float32 [2048, 8192], P(None, ('fsdp', 'context'))
- grad_w_down: float32 [8192, 2048], P(('fsdp', 'context'))
- grad_gain_attn: float32 [2048], P(('fsdp', 'context'))
- grad_gain_mlp: float32 [2048], P(('fsdp', 'context'))
Inputs may be any that keep to these rules, and one draw needn't show every extreme that they name: `places`: each row lists every position of its sequence once, in 8 runs of 128 consecutive ascending positions; the order of the runs varies from sequence to sequence.
All inputs are finite; a program needn't handle non-finite values.
Results may differ from a plain program's by a relative error of at most 0.018.
Values may be sent and summed in bfloat16 or wider, within the bound.
A program may use at most 512 MiB of HBM per device.

v0:
```python
import jax
import jax.numpy as jnp
from jax import lax
from jax.sharding import PartitionSpec as P

QUERY_HEADS = 32
KEY_VALUE_HEADS = 8
HEAD_SIZE = 64


norm_eps = 1e-05
rope_base = 500000.0


def frequencies(half):
    return rope_base ** (-2.0 * jnp.arange(half, dtype=jnp.float32) / (2.0 * half))


def apply_rotary(angle_table, rotary_angles):
    half = angle_table.shape[-1] // 2
    first_half = angle_table[..., :half]
    second_half = angle_table[..., half:]
    cosine = jnp.cos(rotary_angles)[..., None, :]
    sine = jnp.sin(rotary_angles)[..., None, :]
    return jnp.concatenate(
        [first_half * cosine - second_half * sine, second_half * cosine + first_half * sine],
        axis=-1,
    )


def inverse_rotary(angle_table, rotary_angles):
    half = angle_table.shape[-1] // 2
    first_half = angle_table[..., :half]
    second_half = angle_table[..., half:]
    cosine = jnp.cos(rotary_angles)[..., None, :]
    sine = jnp.sin(rotary_angles)[..., None, :]
    return jnp.concatenate(
        [first_half * cosine + second_half * sine, second_half * cosine - first_half * sine],
        axis=-1,
    )


def times_t(left, right):
    return lax.dot_general(
        left, right, (((0,), (0,)), ((), ())), preferred_element_type=jnp.float32
    )


def times_nt(left, right):
    return lax.dot_general(
        left, right, (((1,), (1,)), ((), ())), preferred_element_type=jnp.float32
    )


def query_head_rows(angle_table, sequence_total, segment_length):
    reshaped_heads = angle_table.reshape(
        sequence_total, segment_length, KEY_VALUE_HEADS, QUERY_HEADS // KEY_VALUE_HEADS, HEAD_SIZE
    )
    return jnp.transpose(reshaped_heads, (0, 2, 1, 3, 4)).reshape(
        sequence_total * KEY_VALUE_HEADS, segment_length, QUERY_HEADS // KEY_VALUE_HEADS, HEAD_SIZE
    )


def key_heads(angle_table, sequence_total, total_length):
    reshaped_heads = angle_table.reshape(sequence_total, total_length, KEY_VALUE_HEADS, HEAD_SIZE)
    return jnp.transpose(reshaped_heads, (0, 2, 1, 3)).reshape(
        sequence_total * KEY_VALUE_HEADS, total_length, HEAD_SIZE
    )


def merge_queries(angle_table, sequence_total, segment_length):
    reshaped_heads = angle_table.reshape(
        sequence_total, KEY_VALUE_HEADS, segment_length, QUERY_HEADS // KEY_VALUE_HEADS, HEAD_SIZE
    )
    return jnp.transpose(reshaped_heads, (0, 2, 1, 3, 4)).reshape(
        sequence_total * segment_length, QUERY_HEADS * HEAD_SIZE
    )


def merge_keys(angle_table, sequence_total, total_length):
    reshaped_heads = angle_table.reshape(sequence_total, KEY_VALUE_HEADS, total_length, HEAD_SIZE)
    return jnp.transpose(reshaped_heads, (0, 2, 1, 3)).reshape(
        sequence_total, total_length, KEY_VALUE_HEADS * HEAD_SIZE
    )


def softmax_weights(part_query, part_key, place_query, place_key):
    allowed = place_key[None, :] <= place_query[:, None]
    scores = jnp.einsum(
        "qrd,kd->rqk", part_query, part_key, preferred_element_type=jnp.float32
    ) * HEAD_SIZE ** (-0.5)
    scores = jnp.where(allowed[None], scores, -1e30)
    return jax.nn.softmax(scores, axis=-1)


def forward_head(packed):
    part_query, part_key, part_value, place_query, place_key = packed
    probs = softmax_weights(part_query, part_key, place_query, place_key)
    return jnp.einsum(
        "rqk,kd->qrd", probs.astype(jnp.bfloat16), part_value, preferred_element_type=jnp.float32
    )


def backward_head(packed):
    part_query, part_key, part_value, part_grad, place_query, place_key = packed
    probs = softmax_weights(part_query, part_key, place_query, place_key)
    grad_probs = jnp.einsum(
        "qrd,kd->rqk", part_grad, part_value, preferred_element_type=jnp.float32
    )
    row_delta = jnp.sum(probs * grad_probs, axis=-1, keepdims=True)
    grad_scores = (probs * (grad_probs - row_delta)).astype(jnp.bfloat16)
    grad_query = jnp.einsum(
        "rqk,kd->qrd", grad_scores, part_key, preferred_element_type=jnp.float32
    ) * HEAD_SIZE ** (-0.5)
    grad_key = jnp.einsum(
        "rqk,qrd->kd", grad_scores, part_query, preferred_element_type=jnp.float32
    ) * HEAD_SIZE ** (-0.5)
    value_gradient = jnp.einsum(
        "rqk,qrd->kd", probs.astype(jnp.bfloat16), part_grad, preferred_element_type=jnp.float32
    )
    return (grad_query, grad_key, value_gradient)


def feed_forward(normed_rows, gate_w, up_w, down_w):
    gate_pre = jnp.dot(normed_rows, gate_w, preferred_element_type=jnp.float32)
    up_proj = jnp.dot(normed_rows, up_w, preferred_element_type=jnp.float32)
    sigmoid_gate = jax.nn.sigmoid(gate_pre)
    hidden = (gate_pre * sigmoid_gate * up_proj).astype(jnp.bfloat16)
    return (
        jnp.dot(hidden, down_w, preferred_element_type=jnp.float32),
        (gate_pre, up_proj, sigmoid_gate, hidden),
    )


def feed_back(normed_rows, grad_rows, gate_w, up_w, down_w, kept_values):
    gate_pre, up_proj, sigmoid_gate, hidden = kept_values
    grad_hidden = times_nt(grad_rows, down_w)
    term_down = times_t(hidden, grad_rows)
    grad_gate = (
        grad_hidden * up_proj * (sigmoid_gate * (1.0 + gate_pre * (1.0 - sigmoid_gate)))
    ).astype(jnp.bfloat16)
    grad_up = (grad_hidden * (gate_pre * sigmoid_gate)).astype(jnp.bfloat16)
    grad_normed = times_nt(grad_gate, gate_w) + times_nt(grad_up, up_w)
    return (grad_normed, times_t(normed_rows, grad_gate), times_t(normed_rows, grad_up), term_down)


def body(
    tokens,
    places,
    cotangent,
    gain_attn,
    gain_mlp,
    w_query,
    key_projection,
    value_projection,
    w_out,
    w_gate,
    w_up,
    w_down,
):
    sequence_total, segment_length, width = tokens.shape
    total_length = places.shape[1]
    total_rows = sequence_total * segment_length
    position = lax.axis_index("context")
    local_positions = lax.dynamic_slice_in_dim(places, position * segment_length, segment_length, 1)
    rotary_angles = local_positions.reshape(total_rows).astype(jnp.float32)[:, None] * frequencies(
        HEAD_SIZE // 2
    )
    gain_one, gain_two, query_w, key_weight_local, value_w, out_w = (
        lax.all_gather(gain_attn, ("fsdp", "context"), axis=0, tiled=True),
        lax.all_gather(gain_mlp, ("fsdp", "context"), axis=0, tiled=True),
        lax.all_gather(w_query, ("fsdp", "context"), axis=0, tiled=True),
        lax.all_gather(key_projection, ("fsdp", "context"), axis=0, tiled=True),
        lax.all_gather(value_projection, ("fsdp", "context"), axis=0, tiled=True),
        lax.all_gather(w_out, ("fsdp", "context"), axis=0, tiled=True),
    )
    gain_first = gain_one.astype(jnp.float32)
    gain_second = gain_two.astype(jnp.float32)
    inputs_f = tokens.astype(jnp.float32).reshape(total_rows, width)
    factor_one = lax.rsqrt(jnp.mean(inputs_f * inputs_f, axis=-1, keepdims=True) + norm_eps)
    unit_one = inputs_f * factor_one
    normed_tokens = (unit_one * gain_first).astype(jnp.bfloat16)
    query_pre = jnp.dot(normed_tokens, query_w, preferred_element_type=jnp.float32).reshape(
        total_rows, QUERY_HEADS, HEAD_SIZE
    )
    key_unrotated = jnp.dot(
        normed_tokens, key_weight_local, preferred_element_type=jnp.float32
    ).reshape(total_rows, KEY_VALUE_HEADS, HEAD_SIZE)
    value_matrix_rows = jnp.dot(normed_tokens, value_w, preferred_element_type=jnp.float32).astype(
        jnp.bfloat16
    )
    query_rows = apply_rotary(query_pre, rotary_angles).astype(jnp.bfloat16)
    key_matrix_rows = (
        apply_rotary(key_unrotated, rotary_angles)
        .astype(jnp.bfloat16)
        .reshape(sequence_total, segment_length, KEY_VALUE_HEADS * HEAD_SIZE)
    )
    key_all, value_all = (
        lax.all_gather(key_matrix_rows, "context", axis=1, tiled=True),
        lax.all_gather(
            value_matrix_rows.reshape(sequence_total, segment_length, KEY_VALUE_HEADS * HEAD_SIZE),
            "context",
            axis=1,
            tiled=True,
        ),
    )
    head_query = query_head_rows(query_rows, sequence_total, segment_length)
    head_key = key_heads(key_all, sequence_total, total_length)
    head_value = key_heads(value_all, sequence_total, total_length)
    query_positions = jnp.repeat(local_positions, KEY_VALUE_HEADS, axis=0)
    key_positions = jnp.repeat(places, KEY_VALUE_HEADS, axis=0)
    attended = lax.map(
        forward_head, (head_query, head_key, head_value, query_positions, key_positions)
    )
    attended = merge_queries(attended, sequence_total, segment_length).astype(jnp.bfloat16)
    middle = inputs_f + jnp.dot(attended, out_w, preferred_element_type=jnp.float32)
    factor_two = lax.rsqrt(jnp.mean(middle * middle, axis=-1, keepdims=True) + norm_eps)
    unit_two = middle * factor_two
    normed_mlp = (unit_two * gain_second).astype(jnp.bfloat16)
    tangent = cotangent.reshape(total_rows, width)
    tangent_f = tangent.astype(jnp.float32)
    local_cols = w_gate.shape[1]
    half_cols = local_cols // 2
    branch = jnp.zeros((total_rows, width), jnp.float32)
    grad_normed = jnp.zeros((total_rows, width), jnp.float32)
    gate_shares = []
    up_shares = []
    down_shares = []
    for half_index in range(2):
        first_col = half_index * half_cols
        gate_w, up_w, down_w = (
            lax.all_gather(
                w_gate[:, first_col : first_col + half_cols],
                ("fsdp", "context"),
                axis=1,
                tiled=True,
            ),
            lax.all_gather(
                w_up[:, first_col : first_col + half_cols], ("fsdp", "context"), axis=1, tiled=True
            ),
            lax.all_gather(
                w_down[first_col : first_col + half_cols, :],
                ("fsdp", "context"),
                axis=0,
                tiled=True,
            ),
        )
        branch_half, kept_values = feed_forward(normed_mlp, gate_w, up_w, down_w)
        branch = branch + branch_half
        grad_half, term_gate, term_up, term_down = feed_back(
            normed_mlp, tangent, gate_w, up_w, down_w, kept_values
        )
        grad_normed = grad_normed + grad_half
        down_shares.append(
            lax.psum_scatter(term_down, ("fsdp", "context"), scatter_dimension=0, tiled=True)
        )
        share_gate, share_up = (
            lax.psum_scatter(term_gate, ("fsdp", "context"), scatter_dimension=1, tiled=True),
            lax.psum_scatter(term_up, ("fsdp", "context"), scatter_dimension=1, tiled=True),
        )
        gate_shares.append(share_gate)
        up_shares.append(share_up)
    outcome = middle + branch
    grad_w_gate = jnp.concatenate(gate_shares, axis=1)
    grad_w_up = jnp.concatenate(up_shares, axis=1)
    grad_w_down = jnp.concatenate(down_shares, axis=0)
    scaled_two = grad_normed * gain_second
    term_gain_two = jnp.sum(grad_normed * unit_two, axis=0)
    grad_middle = tangent_f + factor_two * (
        scaled_two - unit_two * jnp.mean(scaled_two * unit_two, axis=-1, keepdims=True)
    )
    grad_branch = grad_middle.astype(jnp.bfloat16)
    term_out = times_t(attended, grad_branch)
    grad_attended = times_nt(grad_branch, out_w).astype(jnp.bfloat16)
    head_grad = query_head_rows(grad_attended, sequence_total, segment_length)
    grad_q, grad_k, grad_v = lax.map(
        backward_head, (head_query, head_key, head_value, head_grad, query_positions, key_positions)
    )
    local_key_gradient, local_value_gradient = (
        lax.psum_scatter(
            merge_keys(grad_k, sequence_total, total_length).astype(jnp.bfloat16),
            "context",
            scatter_dimension=1,
            tiled=True,
        ).astype(jnp.float32),
        lax.psum_scatter(
            merge_keys(grad_v, sequence_total, total_length).astype(jnp.bfloat16),
            "context",
            scatter_dimension=1,
            tiled=True,
        ).astype(jnp.float32),
    )
    grad_query = (
        inverse_rotary(
            merge_queries(grad_q, sequence_total, segment_length).reshape(
                total_rows, QUERY_HEADS, HEAD_SIZE
            ),
            rotary_angles,
        )
        .reshape(total_rows, QUERY_HEADS * HEAD_SIZE)
        .astype(jnp.bfloat16)
    )
    grad_key = (
        inverse_rotary(
            local_key_gradient.reshape(total_rows, KEY_VALUE_HEADS, HEAD_SIZE), rotary_angles
        )
        .reshape(total_rows, KEY_VALUE_HEADS * HEAD_SIZE)
        .astype(jnp.bfloat16)
    )
    value_gradient = local_value_gradient.reshape(total_rows, KEY_VALUE_HEADS * HEAD_SIZE).astype(
        jnp.bfloat16
    )
    grad_normed_one = (
        times_nt(grad_query, query_w)
        + times_nt(grad_key, key_weight_local)
        + times_nt(value_gradient, value_w)
    )
    term_query = times_t(normed_tokens, grad_query)
    term_key = times_t(normed_tokens, grad_key)
    term_value = times_t(normed_tokens, value_gradient)
    scaled_one = grad_normed_one * gain_first
    term_gain_one = jnp.sum(grad_normed_one * unit_one, axis=0)
    grad_inputs = grad_middle + factor_one * (
        scaled_one - unit_one * jnp.mean(scaled_one * unit_one, axis=-1, keepdims=True)
    )
    share_query, share_key, share_value, share_out, share_gain_one, share_gain_two = (
        lax.psum_scatter(term_query, ("fsdp", "context"), scatter_dimension=0, tiled=True),
        lax.psum_scatter(term_key, ("fsdp", "context"), scatter_dimension=0, tiled=True),
        lax.psum_scatter(term_value, ("fsdp", "context"), scatter_dimension=0, tiled=True),
        lax.psum_scatter(term_out, ("fsdp", "context"), scatter_dimension=0, tiled=True),
        lax.psum_scatter(term_gain_one, ("fsdp", "context"), scatter_dimension=0, tiled=True),
        lax.psum_scatter(term_gain_two, ("fsdp", "context"), scatter_dimension=0, tiled=True),
    )
    summed = (
        lax.psum(share_query.astype(jnp.bfloat16), "replica").astype(jnp.float32),
        lax.psum(share_key.astype(jnp.bfloat16), "replica").astype(jnp.float32),
        lax.psum(share_value.astype(jnp.bfloat16), "replica").astype(jnp.float32),
        lax.psum(share_out.astype(jnp.bfloat16), "replica").astype(jnp.float32),
        lax.psum(grad_w_gate.astype(jnp.bfloat16), "replica").astype(jnp.float32),
        lax.psum(grad_w_up.astype(jnp.bfloat16), "replica").astype(jnp.float32),
        lax.psum(grad_w_down.astype(jnp.bfloat16), "replica").astype(jnp.float32),
        lax.psum(share_gain_one.astype(jnp.bfloat16), "replica").astype(jnp.float32),
        lax.psum(share_gain_two.astype(jnp.bfloat16), "replica").astype(jnp.float32),
    )
    out = outcome.astype(jnp.bfloat16).reshape(sequence_total, segment_length, width)
    grad_tokens = grad_inputs.astype(jnp.bfloat16).reshape(sequence_total, segment_length, width)
    return (
        out,
        grad_tokens,
        summed[0],
        summed[1],
        summed[2],
        summed[3],
        summed[4],
        summed[5],
        summed[6],
        summed[7],
        summed[8],
    )


def solution(mesh):
    placed = (
        P(("replica", "fsdp"), "context", None),
        P(("replica", "fsdp"), None),
        P(("replica", "fsdp"), "context", None),
        P(("fsdp", "context")),
        P(("fsdp", "context")),
        P(("fsdp", "context"), None),
        P(("fsdp", "context"), None),
        P(("fsdp", "context"), None),
        P(("fsdp", "context"), None),
        P(None, ("fsdp", "context")),
        P(None, ("fsdp", "context")),
        P(("fsdp", "context"), None),
    )
    return jax.shard_map(
        body,
        mesh=mesh,
        in_specs=placed,
        out_specs=(
            P(("replica", "fsdp"), "context", None),
            P(("replica", "fsdp"), "context", None),
            P(("fsdp", "context"), None),
            P(("fsdp", "context"), None),
            P(("fsdp", "context"), None),
            P(("fsdp", "context"), None),
            P(None, ("fsdp", "context")),
            P(None, ("fsdp", "context")),
            P(("fsdp", "context"), None),
            P(("fsdp", "context")),
            P(("fsdp", "context")),
        ),
        check_vma=False,
    )
```

profile of v0, /device:TPU:0, one launch (start us, length us, event | category | flops | bytes accessed | tf_op | source)
XLA Modules:
  0.0 4063.2 jit_solution(17377958322553168627)
XLA Ops:
  8.7 33.9 all-gather.1
  44.2 10.1 all-gather.16.cloned.1.call-done
  58.6 38.0 all-gather.18.cloned.1.call-done
  110.5 30.7 all-gather.2
  143.7 58.4 %all-gather.22.cloned.1.call-done = bf16[2048,2048]{1,0:T(8,128)(2,1)} async-done(((bf16[128,2048]{1,0:T(8,128)(2,1)}), bf16[2048,2048]{1,0:T(8,128)(2,1)}) %all-gather.22.cloned.1.call-update) | async-done | bytes 8388624 | tf_op jit(solution)/shard_map/all_gather | solution.py:172
  202.1 12.3 copy.45
  214.4 5.8 fusion.134
  220.8 11.8 all-gather.20.cloned.1.call-done
  232.6 59.9 %while.26 = (s32[]{:T(128)}, bf16[8,256,4,64]{1,3,2,0:T(8,128)(2,1)S(1)}, bf16[8,1024,64]{1,2,0:T(8,128)(2,1)}, s32[8,1024]{1,0:T(8,128)S(1)}, s32[8,256]{1,0:T(...) while((s32[]{:T(128)}, bf16[8,256,4,64]{1,3,2,0:T(8,128)(2,1)S(1)}, ...), condition=%wide.region_4.5_spmd.clone, body=%wide.region_1.4_spmd.sunk.clone | while | flops 274990080 | bytes 9593949 | solution.py:212
  232.8 4.4 fusion.278
  240.2 4.4 fusion.278
  292.5 15.4 all-gather.24.cloned.1.call-done
  307.9 6.2 multiply_reduce_fusion.2
  314.3 124.8 %all-gather.26.cloned.1.call-done = bf16[2048,4096]{1,0:T(8,128)(2,1)} async-done(((bf16[2048,256]{1,0:T(8,128)(2,1)}), bf16[2048,4096]{1,0:T(8,128)(2,1)}) %all-gather.26.cloned.1.call-update) | async-done | bytes 16777232 | tf_op jit(solution)/shard_map/all_gather | solution.py:232
  439.1 10.1 fusion.177
  449.3 121.0 %all-gather.28.cloned.1.call-done = bf16[2048,4096]{1,0:T(8,128)(2,1)} async-done(((bf16[2048,256]{1,0:T(8,128)(2,1)}), bf16[2048,4096]{1,0:T(8,128)(2,1)}) %all-gather.28.cloned.1.call-update) | async-done | bytes 16777232 | tf_op jit(solution)/shard_map/all_gather | solution.py:238
  570.3 10.1 fusion.178
  580.5 121.1 %all-gather.32.cloned.1.call-done = bf16[2048,4096]{1,0:T(8,128)(2,1)} async-done(((bf16[2048,256]{1,0:T(8,128)(2,1)}), bf16[2048,4096]{1,0:T(8,128)(2,1)}) %all-gather.32.cloned.1.call-update) | async-done | bytes 16777232 | tf_op jit(solution)/shard_map/all_gather | solution.py:232
  701.5 10.5 fusion.180
  712.1 119.9 %all-gather.34.cloned.1.call-done = bf16[2048,4096]{1,0:T(8,128)(2,1)} async-done(((bf16[2048,256]{1,0:T(8,128)(2,1)}), bf16[2048,4096]{1,0:T(8,128)(2,1)}) %all-gather.34.cloned.1.call-update) | async-done | bytes 16777232 | tf_op jit(solution)/shard_map/all_gather | solution.py:238
  832.0 10.2 fusion.181
  842.2 117.1 %all-gather.36.cloned.1.call-done = bf16[4096,2048]{1,0:T(8,128)(2,1)} async-done(((bf16[256,2048]{1,0:T(8,128)(2,1)}), bf16[4096,2048]{1,0:T(8,128)(2,1)}) %all-gather.36.cloned.1.call-update) | async-done | bytes 16777232 | tf_op jit(solution)/shard_map/all_gather | solution.py:241
  959.3 13.8 multiply_convert_fusion
  973.1 12.4 fusion.183
  985.5 101.0 %all-gather.30.cloned.1.call-done = bf16[4096,2048]{1,0:T(8,128)(2,1)} async-done(((bf16[256,2048]{1,0:T(8,128)(2,1)}), bf16[4096,2048]{1,0:T(8,128)(2,1)}) %all-gather.30.cloned.1.call-update) | async-done | bytes 16777232 | tf_op jit(solution)/shard_map/all_gather | solution.py:241
  1086.5 13.1 multiply_convert_fusion.2
  1099.6 12.2 fusion.182
  1111.8 12.8 convolution_add_fusion.2
  1124.6 14.6 multiply_reduce_fusion
  1142.3 7.5 convolution_convert_fusion
  1151.3 118.0 %while.27 = (s32[]{:T(128)}, f32[8,256,4,64]{1,3,2,0:T(8,128)}, bf16[8,1024,64]{1,2,0:T(8,128)(2,1)}, bf16[8,1024,64]{1,2,0:T(8,128)(2,1)}, bf16[8,1024,64]{1,2,...) while((s32[]{:T(128)}, f32[8,256,4,64]{1,3,2,0:T(8,128)}, ...), condition=%wide.region_11.12_spmd.clone, body=%wide.region_7.11_spmd.sunk.clone | while | flops 685113344 | bytes 50507920 | solution.py:276
  1151.6 4.5 fusion.288
  1166.3 4.5 fusion.288
  1181.1 4.5 fusion.288
  1195.8 4.5 fusion.288
  1210.6 4.5 fusion.288
  1225.3 4.5 fusion.288
  1240.1 4.5 fusion.288
  1254.8 4.5 fusion.288
  1270.0 24.9 reduce-scatter.13.cloned.1.call-done
  1299.6 23.3 reduce-scatter.15.cloned.1.call-done
  1330.2 9.0 fusion.138
  1340.5 8.3 fusion.146
  1350.7 13.6 fusion.186
  1365.9 13.4 fusion.185
  1380.9 13.3 fusion.188
  1395.9 13.4 fusion.187
  1411.4 14.3 fusion.126
  1427.2 13.6 fusion.128
  1442.7 32.3 reduce-scatter.21.cloned.1.call-done
  1476.6 180.0 %reduce-scatter.17.cloned.1.call-done = f32[128,2048]{1,0:T(8,128)} async-done(((f32[2048,2048]{1,0:T(8,128)}), f32[128,2048]{1,0:T(8,128)}) %reduce-scatter.17.cloned.1.call-update) | async-done | bytes 1048592 | tf_op jit(solution)/shard_map/reduce_scatter | solution.py:327
  1658.8 179.5 %reduce-scatter.23.cloned.1.call-done = f32[128,2048]{1,0:T(8,128)} async-done(((f32[2048,2048]{1,0:T(8,128)}), f32[128,2048]{1,0:T(8,128)}) %reduce-scatter.23.cloned.1.call-update) | async-done | bytes 1048592 | tf_op jit(solution)/shard_map/reduce_scatter | solution.py:330
  1840.3 333.9 %reduce-scatter.27.cloned.1.call-done = f32[2048,256]{1,0:T(8,128)} async-done(((f32[2048,4096]{1,0:T(8,128)}), f32[2048,256]{1,0:T(8,128)}) %reduce-scatter.27.cloned.1.call-update) | async-done | bytes 2097168 | tf_op jit(solution)/shard_map/reduce_scatter | solution.py:258
  2175.9 334.3 %reduce-scatter.25.cloned.1.call-done = f32[2048,256]{1,0:T(8,128)} async-done(((f32[2048,4096]{1,0:T(8,128)}), f32[2048,256]{1,0:T(8,128)}) %reduce-scatter.25.cloned.1.call-update) | async-done | bytes 2097168 | tf_op jit(solution)/shard_map/reduce_scatter | solution.py:258
  2511.9 334.3 %reduce-scatter.31.cloned.1.call-done = f32[2048,256]{1,0:T(8,128)} async-done(((f32[2048,4096]{1,0:T(8,128)}), f32[2048,256]{1,0:T(8,128)}) %reduce-scatter.31.cloned.1.call-update) | async-done | bytes 2097168 | tf_op jit(solution)/shard_map/reduce_scatter | solution.py:259
  2847.9 334.5 %reduce-scatter.29.cloned.1.call-done = f32[2048,256]{1,0:T(8,128)} async-done(((f32[2048,4096]{1,0:T(8,128)}), f32[2048,256]{1,0:T(8,128)}) %reduce-scatter.29.cloned.1.call-update) | async-done | bytes 2097168 | tf_op jit(solution)/shard_map/reduce_scatter | solution.py:259
  3185.1 333.5 %reduce-scatter.35.cloned.1.call-done = f32[256,2048]{1,0:T(8,128)} async-done(((f32[4096,2048]{1,0:T(8,128)}), f32[256,2048]{1,0:T(8,128)}) %reduce-scatter.35.cloned.1.call-update) | async-done | bytes 2097168 | tf_op jit(solution)/shard_map/reduce_scatter | solution.py:255
  3524.3 330.2 %reduce-scatter.33.cloned.1.call-done = f32[256,2048]{1,0:T(8,128)} async-done(((f32[4096,2048]{1,0:T(8,128)}), f32[256,2048]{1,0:T(8,128)}) %reduce-scatter.33.cloned.1.call-update) | async-done | bytes 2097168 | tf_op jit(solution)/shard_map/reduce_scatter | solution.py:255
  3859.7 6.4 fusion.184
  3866.2 9.7 fusion.179
  3876.4 7.0 fusion.113
  3887.8 59.7 %all-reduce.2 = (bf16[2048]{0:T(1024)(128)(2,1)S(1)}, bf16[2048]{0:T(1024)(128)(2,1)S(1)}) all-reduce(f32[2048]{0:T(1024)S(1)} %get-tuple-element.108, f32[2048]{0:T(1024)S(1)} %copy-done.47), channel_id=15, replica_groups=mesh['replica'=2,'fsdp'=4,'context'=4] {'fsdp','context'}, use_global_device_ids=true, to_apply=%region_33.34.clone | all-reduce | flops 4096 | bytes 24576
  3947.7 4.9 all-reduce.3
  3956.9 84.1 %all-reduce.7.cloned.1.call-done = (bf16[128,2048]{1,0:T(8,128)(2,1)}, bf16[128,512]{1,0:T(8,128)(2,1)}, bf16[128,512]{1,0:T(8,128)(2,1)}, bf16[128,2048]{1,0:T(...) async-done(((bf16[128,2048]{1,0:T(8,128)(2,1)}, bf16[128,512]{1,0:T(8,128)(2,1)}, bf16[128,512]{1,0:T(8,128)(2,1)}, ...) | async-done | bytes 7602192 | tf_op jit(solution)/shard_map/psum | solution.py:335
  (345 shorter events, 236.0 us)
Async XLA Ops:
  7.2 47.1 %all-gather.16.cloned.1.call-start = ((), (), s32[]{:S(2)}) async-start(), calls=%async_computation.12 | async-start | bytes 2228224 | tf_op jit(solution)/shard_map/all_gather | solution.py:174
  7.9 88.7 %all-gather.18.cloned.1.call-start = ((), (), s32[]{:S(2)}) async-start(), calls=%async_computation.13 | async-start | bytes 2228224 | tf_op jit(solution)/shard_map/all_gather | solution.py:173
  8.7 132.7 %all-gather.38.cloned.1.call-start = ((), (), s32[]{:S(2)}) async-start(), calls=%async_computation.35 | async-start | bytes 1310720 | tf_op jit(solution)/shard_map/all_gather | solution.py:200
  42.6 171.8 %copy-start.37 = (f32[16,1,128]{2,1,0:T(1,128)}, f32[16,1,128]{2,1,0:T(1,128)S(1)}, u32[]{:S(2)}) copy-start(f32[16,1,128]{2,1,0:T(1,128)S(1)} %convert_element_type.281) | copy-start | bytes 24580
  44.2 170.3 %copy-start.44 = (f32[256]{0:T(256)}, f32[256]{0:T(256)S(1)}, u32[]{:S(2)}) copy-start(f32[256]{0:T(256)S(1)} %add_rsqrt_fusion.1) | copy-start | bytes 3076
  54.3 4.1 copy-start.48
  57.7 144.4 %all-gather.22.cloned.1.call-start = ((), (), s32[]{:S(2)}) async-start(), calls=%async_computation.15 | async-start | bytes 8912896 | tf_op jit(solution)/shard_map/all_gather | solution.py:172
  58.3 174.3 %all-gather.20.cloned.1.call-start = ((), (), s32[]{:S(2)}) async-start(), calls=%async_computation.14 | async-start | bytes 1310720 | tf_op jit(solution)/shard_map/all_gather | solution.py:199
  58.6 161.7 %copy-start.40 = (f32[256,32]{0,1:T(8,128)}, f32[256,32]{0,1:T(8,128)S(1)}, u32[]{:S(2)}) copy-start(f32[256,32]{0,1:T(8,128)S(1)} %get-tuple-element.181) | copy-start | bytes 98308
  58.6 161.7 %copy-start.42 = (f32[256,32]{0,1:T(8,128)}, f32[256,32]{0,1:T(8,128)S(1)}, u32[]{:S(2)}) copy-start(f32[256,32]{0,1:T(8,128)S(1)} %get-tuple-element.182) | copy-start | bytes 98308
  96.6 3.0 copy-start.1
  101.3 206.5 %all-gather.24.cloned.1.call-start = ((), (), s32[]{:S(2)}) async-start(), calls=%async_computation.16 | async-start | bytes 8912896 | tf_op jit(solution)/shard_map/all_gather | solution.py:175
  101.9 337.2 %all-gather.26.cloned.1.call-start = ((), (), s32[]{:S(2)}) async-start(), calls=%async_computation.17 | async-start | bytes 17825792 | tf_op jit(solution)/shard_map/all_gather | solution.py:232
  103.7 466.7 %all-gather.28.cloned.1.call-start = ((), (), s32[]{:S(2)}) async-start(), calls=%async_computation.18 | async-start | bytes 17825792 | tf_op jit(solution)/shard_map/all_gather | solution.py:238
  106.8 594.7 %all-gather.32.cloned.1.call-start = ((), (), s32[]{:S(2)}) async-start(), calls=%async_computation.20 | async-start | bytes 17825792 | tf_op jit(solution)/shard_map/all_gather | solution.py:232
  107.6 724.5 %all-gather.34.cloned.1.call-start = ((), (), s32[]{:S(2)}) async-start(), calls=%async_computation.21 | async-start | bytes 17825792 | tf_op jit(solution)/shard_map/all_gather | solution.py:238
  108.1 851.2 %all-gather.36.cloned.1.call-start = ((), (), s32[]{:S(2)}) async-start(), calls=%async_computation.22 | async-start | bytes 17825792 | tf_op jit(solution)/shard_map/all_gather | solution.py:241
  109.9 976.6 %all-gather.30.cloned.1.call-start = ((), (), s32[]{:S(2)}) async-start(), calls=%async_computation.19 | async-start | bytes 17825792 | tf_op jit(solution)/shard_map/all_gather | solution.py:241
  110.5 1184.4 %reduce-scatter.13.cloned.1.call-start = ((), (), s32[]{:S(2)}) async-start(), calls=%async_computation.23 | async-start | bytes 1310720 | tf_op jit(solution)/shard_map/reduce_scatter | solution.py:280
  292.4 15.4 copy-start.10
  292.5 15.4 copy-start.23
  314.0 810.6 %copy-start.8 = (f32[256,2048]{1,0:T(8,128)}, f32[256,2048]{1,0:T(8,128)S(1)}, u32[]{:S(2)}) copy-start(f32[256,2048]{1,0:T(8,128)S(1)} %get-tuple-element.184) | copy-start | bytes 6291460
  314.3 517.7 %copy-start.4 = (bf16[256,2048]{1,0:T(8,128)(2,1)}, bf16[256,2048]{1,0:T(8,128)(2,1)S(1)}, u32[]{:S(2)}) copy-start(bf16[256,2048]{1,0:T(8,128)(2,1)S(1)} %multiply_convert_fusion.6) | copy-start | bytes 3145732
  973.1 113.4 %copy-start.12 = (bf16[1,256,2048]{2,1,0:T(8,128)(2,1)S(1)}, bf16[1,256,2048]{2,1,0:T(8,128)(2,1)}, u32[]{:S(2)}) copy-start(bf16[1,256,2048]{2,1,0:T(8,128)(2,1)} %param.18) | copy-start | bytes 3145732
  1142.3 196.9 %copy-start.6 = (f32[256,2048]{1,0:T(8,128)}, f32[256,2048]{1,0:T(8,128)S(1)}, u32[]{:S(2)}) copy-start(f32[256,2048]{1,0:T(8,128)S(1)} %multiply_add_fusion) | copy-start | bytes 6291460
  1156.0 3.5 copy-start
  1170.8 3.5 copy-start
  1185.5 3.5 copy-start
  1200.3 3.5 copy-start
  1215.0 3.5 copy-start
  1229.8 3.5 copy-start
  1244.6 3.5 copy-start
  1259.3 3.5 copy-start
  1269.3 26.5 copy-start.41
  1269.3 26.5 copy-start.43
  1269.3 27.3 copy-start.2
  1269.3 27.3 copy-start.38
  1269.4 27.3 copy-start.45
  1269.4 53.6 %reduce-scatter.15.cloned.1.call-start = ((), (), s32[]{:S(2)}) async-start(), calls=%async_computation.24 | async-start | bytes 1310720 | tf_op jit(solution)/shard_map/reduce_scatter | solution.py:286
  1270.0 171.1 %reduce-scatter.19.cloned.1.call-start = ((), (), s32[]{:S(2)}) async-start(), calls=%async_computation.26 | async-start | bytes 4456448 | tf_op jit(solution)/shard_map/reduce_scatter | solution.py:328
  1299.6 175.4 %reduce-scatter.21.cloned.1.call-start = ((), (), s32[]{:S(2)}) async-start(), calls=%async_computation.27 | async-start | bytes 4456448 | tf_op jit(solution)/shard_map/reduce_scatter | solution.py:329
  1326.8 329.9 %reduce-scatter.17.cloned.1.call-start = ((), (), s32[]{:S(2)}) async-start(), calls=%async_computation.25 | async-start | bytes 17825792 | tf_op jit(solution)/shard_map/reduce_scatter | solution.py:327
  1339.2 499.0 %reduce-scatter.23.cloned.1.call-start = ((), (), s32[]{:S(2)}) async-start(), calls=%async_computation.28 | async-start | bytes 17825792 | tf_op jit(solution)/shard_map/reduce_scatter | solution.py:330
  1348.9 825.4 %reduce-scatter.27.cloned.1.call-start = ((), (), s32[]{:S(2)}) async-start(), calls=%async_computation.30 | async-start | bytes 35651584 | tf_op jit(solution)/shard_map/reduce_scatter | solution.py:258
  1364.3 1145.9 %reduce-scatter.25.cloned.1.call-start = ((), (), s32[]{:S(2)}) async-start(), calls=%async_computation.29 | async-start | bytes 35651584 | tf_op jit(solution)/shard_map/reduce_scatter | solution.py:258
  1379.3 1466.9 %reduce-scatter.31.cloned.1.call-start = ((), (), s32[]{:S(2)}) async-start(), calls=%async_computation.32 | async-start | bytes 35651584 | tf_op jit(solution)/shard_map/reduce_scatter | solution.py:259
  1394.3 1788.2 %reduce-scatter.29.cloned.1.call-start = ((), (), s32[]{:S(2)}) async-start(), calls=%async_computation.31 | async-start | bytes 35651584 | tf_op jit(solution)/shard_map/reduce_scatter | solution.py:259
  1409.3 2109.2 %reduce-scatter.35.cloned.1.call-start = ((), (), s32[]{:S(2)}) async-start(), calls=%async_computation.34 | async-start | bytes 35651584 | tf_op jit(solution)/shard_map/reduce_scatter | solution.py:255
  1425.7 2428.9 %reduce-scatter.33.cloned.1.call-start = ((), (), s32[]{:S(2)}) async-start(), calls=%async_computation.33 | async-start | bytes 35651584 | tf_op jit(solution)/shard_map/reduce_scatter | solution.py:255
  1440.8 2600.2 %all-reduce.7.cloned.1.call-start = ((), (), s32[]{:S(2)}) async-start(), calls=%async_computation.36 | async-start | bytes 15204352 | tf_op jit(solution)/shard_map/psum | solution.py:335
  3524.3 331.9 %copy-start.17 = (bf16[256,2048]{1,0:T(8,128)(2,1)S(1)}, bf16[256,2048]{1,0:T(8,128)(2,1)}, u32[]{:S(2)}) copy-start(bf16[256,2048]{1,0:T(8,128)(2,1)} %convert.42) | copy-start | bytes 3145732
  3859.7 6.5 copy-start.22
  3859.7 16.2 slice-start
  3859.7 16.2 slice-start.1
  3866.2 9.7 copy-start.9
  3866.2 9.7 copy-start.20
  3866.2 9.7 slice-start.2
  3866.2 10.2 slice-start.3
  3876.4 7.0 copy-start.14
  3876.4 7.0 copy-start.25
  3885.3 68.3 %copy-start.7 = (f32[256,2048]{1,0:T(8,128)S(1)}, f32[256,2048]{1,0:T(8,128)}, u32[]{:S(2)}) copy-start(f32[256,2048]{1,0:T(8,128)} %copy-done.6) | copy-start | bytes 6291460
  4041.0 7.7 copy-start.32
  4048.6 2.6 copy-start.31
  4051.2 2.6 copy-start.30
  (23 other events, 35.3 us)
Sparse Core Ops, SparseCore 0:
  10.2 44.0 all-gather.15
  56.5 40.0 all-gather.17
  98.8 26.7 all-gather.37
  127.7 74.3 all-gather.21
  204.1 28.4 all-gather.19
  234.6 73.1 all-gather.23
  310.5 128.5 all-gather.25
  441.8 128.5 all-gather.27
  573.0 128.5 all-gather.31
  703.5 128.5 all-gather.33
  834.2 125.0 all-gather.35
  961.4 125.0 all-gather.29
  1269.5 25.3 reduce-scatter.12
  1297.1 25.7 reduce-scatter.14
  1327.2 71.2 reduce-scatter.18
  1403.3 71.7 reduce-scatter.20
  1479.0 177.6 reduce-scatter.16
  1660.6 177.5 reduce-scatter.22
  1842.5 331.6 reduce-scatter.26
  2178.3 331.8 reduce-scatter.24
  2514.5 331.7 reduce-scatter.30
  2850.5 331.9 reduce-scatter.28
  3186.7 331.8 reduce-scatter.34
  3522.7 331.8 reduce-scatter.32
  3858.2 182.7 all-reduce.6
where the time goes:
time: 4070 us; the launch traced here: 4060 us
  waiting for transfers between devices  3370 us (83%)
  matrix products  441 us (11%)
  blocking collectives  129 us (3%)
  other arithmetic  62.3 us (2%)
  local copies, waits for them, and re-layouts  44.5 us (1%)
    reduce_scatter x2, waiting for transfers between devices, body(): lax.psum_scatter(term_up, ('fsdp', 'context'), scatter_dimension=1, tiled...  669 us
    reduce_scatter x2, waiting for transfers between devices, body(): lax.psum_scatter(term_gate, ('fsdp', 'context'), scatter_dimension=1, til...  668 us
    reduce_scatter x2, waiting for transfers between devices, body(): lax.psum_scatter(term_down, ('fsdp', 'context'), scatter_dimension=0, til...  664 us
    all_gather x2, waiting for transfers between devices, body(): lax.all_gather(w_gate[:, first_col:first_col + half_cols], ('fsdp', 'cont...  246 us
    all_gather x2, waiting for transfers between devices, body(): lax.all_gather(w_up[:, first_col:first_col + half_cols], ('fsdp', 'contex...  241 us
    all_gather x2, waiting for transfers between devices, body(): lax.all_gather(w_down[first_col:first_col + half_cols, :], ('fsdp', 'cont...  218 us
    reduce_scatter x1, waiting for transfers between devices, body(): lax.psum_scatter(term_query, ('fsdp', 'context'), scatter_dimension=0, ti...  180 us
    reduce_scatter x1, waiting for transfers between devices, body(): lax.psum_scatter(term_out, ('fsdp', 'context'), scatter_dimension=0, tile...  179 us
  transfers between devices with their start and end apart: 25, of which 23 were waited for; matrix products, arithmetic and copies ran while one was open for 8% of the time, Pallas kernels for 0%

commit v1 on v0

--- a/solution.py
+++ b/solution.py
@@ -219,51 +219,20 @@
     normed_mlp = (unit_two * gain_second).astype(jnp.bfloat16)
     tangent = cotangent.reshape(total_rows, width)
     tangent_f = tangent.astype(jnp.float32)
-    local_cols = w_gate.shape[1]
-    half_cols = local_cols // 2
-    branch = jnp.zeros((total_rows, width), jnp.float32)
-    grad_normed = jnp.zeros((total_rows, width), jnp.float32)
-    gate_shares = []
-    up_shares = []
-    down_shares = []
-    for half_index in range(2):
-        first_col = half_index * half_cols
-        gate_w, up_w, down_w = (
-            lax.all_gather(
-                w_gate[:, first_col : first_col + half_cols],
-                ("fsdp", "context"),
-                axis=1,
-                tiled=True,
-            ),
-            lax.all_gather(
-                w_up[:, first_col : first_col + half_cols], ("fsdp", "context"), axis=1, tiled=True
-            ),
-            lax.all_gather(
-                w_down[first_col : first_col + half_cols, :],
-                ("fsdp", "context"),
-                axis=0,
-                tiled=True,
-            ),
-        )
-        branch_half, kept_values = feed_forward(normed_mlp, gate_w, up_w, down_w)
-        branch = branch + branch_half
-        grad_half, term_gate, term_up, term_down = feed_back(
-            normed_mlp, tangent, gate_w, up_w, down_w, kept_values
-        )
-        grad_normed = grad_normed + grad_half
-        down_shares.append(
-            lax.psum_scatter(term_down, ("fsdp", "context"), scatter_dimension=0, tiled=True)
-        )
-        share_gate, share_up = (
-            lax.psum_scatter(term_gate, ("fsdp", "context"), scatter_dimension=1, tiled=True),
-            lax.psum_scatter(term_up, ("fsdp", "context"), scatter_dimension=1, tiled=True),
-        )
-        gate_shares.append(share_gate)
-        up_shares.append(share_up)
+    group = ("fsdp", "context")
+    normed_all = lax.all_gather(normed_mlp, group, axis=0, tiled=True)
+    tangent_all = lax.all_gather(tangent, group, axis=0, tiled=True)
+    branch_part, kept_values = feed_forward(normed_all, w_gate, w_up, w_down)
+    grad_part, grad_w_gate, grad_w_up, grad_w_down = feed_back(
+        normed_all, tangent_all, w_gate, w_up, w_down, kept_values
+    )
+    grad_normed = lax.psum_scatter(
+        grad_part.astype(jnp.bfloat16), group, scatter_dimension=0, tiled=True
+    ).astype(jnp.float32)
+    branch = lax.psum_scatter(
+        branch_part.astype(jnp.bfloat16), group, scatter_dimension=0, tiled=True
+    ).astype(jnp.float32)
     outcome = middle + branch
-    grad_w_gate = jnp.concatenate(gate_shares, axis=1)
-    grad_w_up = jnp.concatenate(up_shares, axis=1)
-    grad_w_down = jnp.concatenate(down_shares, axis=0)
     scaled_two = grad_normed * gain_second
     term_gain_two = jnp.sum(grad_normed * unit_two, axis=0)
     grad_middle = tangent_f + factor_two * (
@@ -324,10 +293,10 @@
         scaled_one - unit_one * jnp.mean(scaled_one * unit_one, axis=-1, keepdims=True)
     )
     share_query, share_key, share_value, share_out, share_gain_one, share_gain_two = (
-        lax.psum_scatter(term_query, ("fsdp", "context"), scatter_dimension=0, tiled=True),
-        lax.psum_scatter(term_key, ("fsdp", "context"), scatter_dimension=0, tiled=True),
-        lax.psum_scatter(term_value, ("fsdp", "context"), scatter_dimension=0, tiled=True),
-        lax.psum_scatter(term_out, ("fsdp", "context"), scatter_dimension=0, tiled=True),
+        lax.psum_scatter(term_query.astype(jnp.bfloat16), ("fsdp", "context"), scatter_dimension=0, tiled=True),
+        lax.psum_scatter(term_key.astype(jnp.bfloat16), ("fsdp", "context"), scatter_dimension=0, tiled=True),
+        lax.psum_scatter(term_value.astype(jnp.bfloat16), ("fsdp", "context"), scatter_dimension=0, tiled=True),
+        lax.psum_scatter(term_out.astype(jnp.bfloat16), ("fsdp", "context"), scatter_dimension=0, tiled=True),
         lax.psum_scatter(term_gain_one, ("fsdp", "context"), scatter_dimension=0, tiled=True),
         lax.psum_scatter(term_gain_two, ("fsdp", "context"), scatter_dimension=0, tiled=True),
     )

time: 4070 us -> 1740 us (0.43)
  waiting for transfers between devices: 3370 us -> 1140 us
  matrix products: 441 us -> 375 us
    reduce_scatter x10 -> x6, waiting for transfers between devices: 2390 us -> 627 us  [the longest x1 180 us: body(): lax.psum_scatter(branch_part.astype(jnp.bfloat16), group, scatter_dimensi...]
    all_gather x6 -> x2, waiting for transfers between devices: 705 us -> 224 us  [the longest x1 124 us: body(): normed_all = lax.all_gather(normed_mlp, group, axis=0, tiled=True)]
    dot_general x10 -> x7, matrix products: 106 us -> 57.7 us  [times_t(): lax.dot_general(left, right, (((0,), (0,)), ((), ())), preferred_element_...]
    dot_general x10 -> x7, matrix products: 96.1 us -> 79.6 us  [times_nt(): lax.dot_general(left, right, (((1,), (1,)), ((), ())), preferred_element_...]
  transfers between devices with their start and end apart: 25 -> 17, of which waited for: 23 -> 16; matrix products, arithmetic and copies ran while one was open for 8% -> 13% of each run, Pallas kernels for 0% -> 0%
where the time goes in v1:
time: 1740 us; the launch traced here: 1730 us
  waiting for transfers between devices  1140 us (66%)
  matrix products  375 us (22%)
  blocking collectives  129 us (7%)
  other arithmetic  44.1 us (3%)
  local copies, waits for them, and re-layouts  25.3 us (1%)
    reduce_scatter x1, waiting for transfers between devices, body(): lax.psum_scatter(branch_part.astype(jnp.bfloat16), group, scatter_dimensi...  180 us
    reduce_scatter x1, waiting for transfers between devices, body(): lax.psum_scatter(grad_part.astype(jnp.bfloat16), group, scatter_dimension...  161 us
    all_gather x1, waiting for transfers between devices, body(): normed_all = lax.all_gather(normed_mlp, group, axis=0, tiled=True)  124 us
    reduce_scatter x1, waiting for transfers between devices, body(): lax.psum_scatter(term_query.astype(jnp.bfloat16), ('fsdp', 'context'), sc...  108 us
    reduce_scatter x1, waiting for transfers between devices, body(): lax.psum_scatter(term_out.astype(jnp.bfloat16), ('fsdp', 'context'), scat...  108 us
    psum x1, waiting for transfers between devices, body(): lax.psum(share_query.astype(jnp.bfloat16), 'replica').astype(jnp.float32)  104 us
    all_gather x1, waiting for transfers between devices, body(): tangent_all = lax.all_gather(tangent, group, axis=0, tiled=True)  99.9 us
    dot_general x7, matrix products, times_nt(): lax.dot_general(left, right, (((1,), (1,)), ((), ())), preferred_element_...  79.6 us
  transfers between devices with their start and end apart: 17, of which 16 were waited for; matrix products, arithmetic and copies ran while one was open for 13% of the time, Pallas kernels for 0%

profile of v1, /device:TPU:0, one launch (start us, length us, event | category | flops | bytes accessed | tf_op | source)
XLA Modules:
  0.0 1733.2 jit_solution(10847040161546984432)
XLA Ops:
  8.7 33.9 %all-gather.2 = bf16[16,1,128]{2,1,0:T(2,128)(2,1)S(1)} all-gather(bf16[1,1,128]{2,1,0:T(2,128)(2,1)} %bitcast.405), channel_id=1, replica_groups=mesh['replica'=2,'fsdp'=4,'context'=4] {'fsdp','context'}, dimensions={0}, use_global_device_ids=true | all-gather | bytes 4352 | tf_op jit(solution)/shard_map/all_gather | solution.py:170
  44.2 10.1 all-gather.13.cloned.1.call-done
  58.6 38.0 %all-gather.15.cloned.1.call-done = bf16[2048,512]{1,0:T(8,128)(2,1)} async-done(((bf16[128,512]{1,0:T(8,128)(2,1)}), bf16[2048,512]{1,0:T(8,128)(2,1)}) %all-gather.15.cloned.1.call-update) | async-done | bytes 2097168 | tf_op jit(solution)/shard_map/all_gather | solution.py:173
  96.7 4.0 copy.44
  104.6 30.5 %all-gather.3 = bf16[16,1,128]{2,1,0:T(2,128)(2,1)S(1)} all-gather(bf16[1,1,128]{2,1,0:T(2,128)(2,1)S(1)} %bitcast.406), channel_id=1, replica_groups=mesh['replica'=2,'fsdp'=4,'context'=4] {'fsdp','context'}, dimensions={0}, use_global_device_ids=true | all-gather | bytes 4352 | tf_op jit(solution)/shard_map/all_gather | solution.py:171
  138.4 63.7 %all-gather.19.cloned.1.call-done = bf16[2048,2048]{1,0:T(8,128)(2,1)} async-done(((bf16[128,2048]{1,0:T(8,128)(2,1)}), bf16[2048,2048]{1,0:T(8,128)(2,1)}) %all-gather.19.cloned.1.call-update) | async-done | bytes 8388624 | tf_op jit(solution)/shard_map/all_gather | solution.py:172
  202.1 12.3 copy.45
  214.5 5.8 fusion.135
  221.8 10.8 all-gather.17.cloned.1.call-done
  232.6 65.0 %while.26 = (s32[]{:T(128)}, bf16[8,256,4,64]{1,3,2,0:T(8,128)(2,1)}, bf16[8,1024,64]{1,2,0:T(8,128)(2,1)}, s32[8,1024]{1,0:T(8,128)S(1)}, s32[8,256]{1,0:T(8,12...) while((s32[]{:T(128)}, bf16[8,256,4,64]{1,3,2,0:T(8,128)(2,1)}, ...), condition=%wide.region_4.5_spmd.clone, body=%wide.region_1.4_spmd.sunk.clone | while | flops 274990080 | bytes 9593949 | solution.py:212
  232.9 4.5 fusion.248
  241.0 4.5 fusion.248
  249.1 4.5 fusion.248
  257.2 4.5 fusion.248
  265.3 4.5 fusion.248
  273.4 4.5 fusion.248
  281.6 4.5 fusion.248
  289.7 4.5 fusion.248
  297.6 10.3 all-gather.21.cloned.1.call-done
  307.9 6.2 multiply_reduce_fusion
  317.8 124.2 %all-gather.23.cloned.1.call-done = bf16[4096,2048]{1,0:T(8,128)(2,1)} async-done(((bf16[256,2048]{1,0:T(8,128)(2,1)}), bf16[4096,2048]{1,0:T(8,128)(2,1)}) %all-gather.23.cloned.1.call-update) | async-done | bytes 16777232 | tf_op jit(solution)/shard_map/all_gather | solution.py:223
  442.0 16.3 fusion.172
  458.3 11.0 fusion.171
  469.4 99.9 %all-gather.27.cloned.1.call-done = bf16[1,4096,2048]{2,1,0:T(8,128)(2,1)} async-done(((bf16[1,256,2048]{2,1,0:T(8,128)(2,1)}), bf16[1,4096,2048]{2,1,0:T(8,128)(2,1)}) %all-gather.27.cloned.1.call-update) | async-done | bytes 16777232 | tf_op jit(solution)/shard_map/all_gather | solution.py:224
  569.3 24.0 %multiply_convert_fusion = (bf16[4096,512]{1,0:T(8,128)(2,1)}, bf16[4096,512]{1,0:T(8,128)(2,1)}, bf16[4096,512]{1,0:T(8,128)(2,1)}) fusion(f32[4096,512]{1,0:T(8,128)} %fusion.171, f32[4096,512]{1,0:T(8,128)} %fusion.172, bf16[512,2048]{1,0:T(8,128)(2,1)S(1)} %copy-done, bf16[1,4096,2048]{2,1,0:T(8,128)(2,1)} %all-gather.27.cloned.1.call-done), kind=kOutput, calls=%fused_computation.93 | convolution fusion | flops 8621391872 | bytes 48234496 | tf_op jit(solution)/shard_map/dot_general | solution.py:50
  593.3 17.8 %fusion.173 = f32[4096,2048]{1,0:T(8,128)} fusion(bf16[4096,512]{1,0:T(8,128)(2,1)} %get-tuple-element.162, bf16[2048,512]{1,0:T(8,128)(2,1)} %param.25), kind=kOutput, calls=%fused_computation.181 | convolution fusion | flops 8589934592 | bytes 39845888 | tf_op jit(solution)/shard_map/dot_general | solution.py:50
  611.1 22.8 %add_convert_fusion = bf16[4096,2048]{1,0:T(8,128)(2,1)} fusion(f32[4096,2048]{1,0:T(8,128)} %fusion.173, bf16[4096,512]{1,0:T(8,128)(2,1)} %get-tuple-element.161, bf16[2048,512]{1,0:T(8,128)(2,1)} %param.26), kind=kOutput, calls=%fused_computation.87 | convolution fusion | flops 8606711808 | bytes 56623104 | tf_op jit(solution)/shard_map/dot_general | solution.py:50
  634.0 15.9 convolution_convert_fusion
  650.0 160.9 %reduce-scatter.11.cloned.1.call-done = bf16[256,2048]{1,0:T(8,128)(2,1)} async-done(((bf16[4096,2048]{1,0:T(8,128)(2,1)}), bf16[256,2048]{1,0:T(8,128)(2,1)}) %reduce-scatter.11.cloned.1.call-update) | async-done | bytes 1048592 | tf_op jit(solution)/shard_map/reduce_scatter | solution.py:229
  812.9 179.5 %reduce-scatter.9.cloned.1.call-done = bf16[256,2048]{1,0:T(8,128)(2,1)} async-done(((bf16[4096,2048]{1,0:T(8,128)(2,1)}), bf16[256,2048]{1,0:T(8,128)(2,1)}) %reduce-scatter.9.cloned.1.call-update) | async-done | bytes 1048592 | tf_op jit(solution)/shard_map/reduce_scatter | solution.py:232
  997.2 5.7 convolution_convert_fusion.7
  1003.7 121.5 %while.27 = (s32[]{:T(128)}, f32[8,256,4,64]{1,3,2,0:T(8,128)}, bf16[8,1024,64]{1,2,0:T(8,128)(2,1)}, bf16[8,1024,64]{1,2,0:T(8,128)(2,1)}, bf16[8,1024,64]{1,2,...) while((s32[]{:T(128)}, f32[8,256,4,64]{1,3,2,0:T(8,128)}, ...), condition=%wide.region_13.14_spmd.clone, body=%wide.region_9.13_spmd.sunk.clone | while | flops 685113344 | bytes 50507920 | solution.py:245
  1003.9 4.4 fusion.258
  1008.4 3.7 fusion.263
  1019.1 4.4 fusion.258
  1023.5 3.8 fusion.263
  1034.3 4.4 fusion.258
  1038.7 3.8 fusion.263
  1049.5 4.4 fusion.258
  1053.9 3.7 fusion.263
  1064.7 4.4 fusion.258
  1069.1 3.7 fusion.263
  1079.9 4.4 fusion.258
  1084.3 3.7 fusion.263
  1095.1 4.4 fusion.258
  1099.5 3.8 fusion.263
  1110.2 4.4 fusion.258
  1114.7 3.7 fusion.263
  1125.8 25.7 %reduce-scatter.15.cloned.1.call-done = bf16[1,256,512]{1,2,0:T(8,128)(2,1)} async-done(((bf16[1,1024,512]{1,2,0:T(8,128)(2,1)}), bf16[1,256,512]{1,2,0:T(8,128)(2,1)}) %reduce-scatter.15.cloned.1.call-update) | async-done | bytes 262160 | tf_op jit(solution)/shard_map/reduce_scatter | solution.py:255
  1154.8 24.8 %reduce-scatter.13.cloned.1.call-done = bf16[1,256,512]{1,2,0:T(8,128)(2,1)} async-done(((bf16[1,1024,512]{1,2,0:T(8,128)(2,1)}), bf16[1,256,512]{1,2,0:T(8,128)(2,1)}) %reduce-scatter.13.cloned.1.call-update) | async-done | bytes 262160 | tf_op jit(solution)/shard_map/reduce_scatter | solution.py:249
  1183.0 7.2 convolution_convert_fusion.1
  1192.3 5.8 convolution_convert_fusion.2
  1198.3 15.4 fusion.106
  1213.7 13.7 convolution_convert_fusion.5
  1227.4 10.2 convolution_convert_fusion.6
  1237.6 6.0 reduce-scatter.21.cloned.1.call-done
  1243.5 64.6 %reduce-scatter.19.cloned.1.call-done = bf16[128,512]{1,0:T(8,128)(2,1)} async-done(((bf16[2048,512]{1,0:T(8,128)(2,1)}), bf16[128,512]{1,0:T(8,128)(2,1)}) %reduce-scatter.19.cloned.1.call-update) | async-done | bytes 131088 | tf_op jit(solution)/shard_map/reduce_scatter | solution.py:297
  1308.2 107.5 %reduce-scatter.23.cloned.1.call-done = bf16[128,2048]{1,0:T(8,128)(2,1)} async-done(((bf16[2048,2048]{1,0:T(8,128)(2,1)}), bf16[128,2048]{1,0:T(8,128)(2,1)}) %reduce-scatter.23.cloned.1.call-update) | async-done | bytes 524304 | tf_op jit(solution)/shard_map/reduce_scatter | solution.py:299
  1415.7 108.3 %reduce-scatter.17.cloned.1.call-done = bf16[128,2048]{1,0:T(8,128)(2,1)} async-done(((bf16[2048,2048]{1,0:T(8,128)(2,1)}), bf16[128,2048]{1,0:T(8,128)(2,1)}) %reduce-scatter.17.cloned.1.call-update) | async-done | bytes 524304 | tf_op jit(solution)/shard_map/reduce_scatter | solution.py:296
  1525.9 5.9 fusion.174
  1536.6 60.0 %all-reduce.2 = (bf16[2048]{0:T(1024)(128)(2,1)S(1)}, bf16[2048]{0:T(1024)(128)(2,1)S(1)}) all-reduce(f32[2048]{0:T(1024)S(1)} %get-tuple-element.108, f32[2048]{0:T(1024)S(1)} %get-tuple-element.106), channel_id=12, replica_groups=mesh['replica'=2,'fsdp'=4,'context'=4] {'fsdp','context'}, use_global_device_ids=true, to_apply=%region_29.30.clone | all-reduce | flops 4096 | bytes 24576
  1596.7 5.0 all-reduce.3
  1602.7 3.8 fusion.133
  1606.5 104.5 %all-reduce.7.cloned.1.call-done = (bf16[128,2048]{1,0:T(8,128)(2,1)}, bf16[128,512]{1,0:T(8,128)(2,1)}, bf16[128,512]{1,0:T(8,128)(2,1)}, bf16[128,2048]{1,0:T(...) async-done(((bf16[128,2048]{1,0:T(8,128)(2,1)}, bf16[128,512]{1,0:T(8,128)(2,1)}, bf16[128,512]{1,0:T(8,128)(2,1)}, ...) | async-done | bytes 7602192 | tf_op jit(solution)/shard_map/psum | solution.py:304
  (257 shorter events, 144.3 us)
Async XLA Ops:
  7.2 562.1 %copy-start = (bf16[512,2048]{1,0:T(8,128)(2,1)S(1)}, bf16[512,2048]{1,0:T(8,128)(2,1)}, u32[]{:S(2)}) copy-start(bf16[512,2048]{1,0:T(8,128)(2,1)} %param.27) | copy-start | bytes 6291460
  7.2 47.1 %all-gather.13.cloned.1.call-start = ((), (), s32[]{:S(2)}) async-start(), calls=%async_computation.8 | async-start | bytes 2228224 | tf_op jit(solution)/shard_map/all_gather | solution.py:174
  7.9 88.7 %all-gather.15.cloned.1.call-start = ((), (), s32[]{:S(2)}) async-start(), calls=%async_computation.9 | async-start | bytes 2228224 | tf_op jit(solution)/shard_map/all_gather | solution.py:173
  8.7 127.5 %all-gather.25.cloned.1.call-start = ((), (), s32[]{:S(2)}) async-start(), calls=%async_computation.22 | async-start | bytes 1310720 | tf_op jit(solution)/shard_map/all_gather | solution.py:200
  42.6 171.8 %copy-start.20 = (f32[16,1,128]{2,1,0:T(1,128)}, f32[16,1,128]{2,1,0:T(1,128)S(1)}, u32[]{:S(2)}) copy-start(f32[16,1,128]{2,1,0:T(1,128)S(1)} %convert_element_type.295) | copy-start | bytes 24580
  44.2 170.3 %copy-start.22 = (f32[256]{0:T(256)}, f32[256]{0:T(256)S(1)}, u32[]{:S(2)}) copy-start(f32[256]{0:T(256)S(1)} %add_rsqrt_fusion.1) | copy-start | bytes 3076
  54.3 4.0 copy-start.24
  57.7 144.4 %all-gather.19.cloned.1.call-start = ((), (), s32[]{:S(2)}) async-start(), calls=%async_computation.11 | async-start | bytes 8912896 | tf_op jit(solution)/shard_map/all_gather | solution.py:172
  58.3 174.3 %all-gather.17.cloned.1.call-start = ((), (), s32[]{:S(2)}) async-start(), calls=%async_computation.10 | async-start | bytes 1310720 | tf_op jit(solution)/shard_map/all_gather | solution.py:199
  58.6 161.7 %copy-start.16 = (f32[256,32]{0,1:T(8,128)}, f32[256,32]{0,1:T(8,128)S(1)}, u32[]{:S(2)}) copy-start(f32[256,32]{0,1:T(8,128)S(1)} %get-tuple-element.174) | copy-start | bytes 98308
  58.6 161.7 %copy-start.18 = (f32[256,32]{0,1:T(8,128)}, f32[256,32]{0,1:T(8,128)S(1)}, u32[]{:S(2)}) copy-start(f32[256,32]{0,1:T(8,128)S(1)} %get-tuple-element.175) | copy-start | bytes 98308
  96.7 4.0 copy-start.3
  103.1 1.5 copy-start.25
  103.9 204.0 %all-gather.21.cloned.1.call-start = ((), (), s32[]{:S(2)}) async-start(), calls=%async_computation.12 | async-start | bytes 8912896 | tf_op jit(solution)/shard_map/all_gather | solution.py:175
  104.5 337.5 %all-gather.23.cloned.1.call-start = ((), (), s32[]{:S(2)}) async-start(), calls=%async_computation.13 | async-start | bytes 17825792 | tf_op jit(solution)/shard_map/all_gather | solution.py:223
  314.1 1.3 copy-start.5
  316.7 252.6 %all-gather.27.cloned.1.call-start = ((), (), s32[]{:S(2)}) async-start(), calls=%async_computation.23 | async-start | bytes 17825792 | tf_op jit(solution)/shard_map/all_gather | solution.py:224
  317.4 493.4 %reduce-scatter.11.cloned.1.call-start = ((), (), s32[]{:S(2)}) async-start(), calls=%async_computation.15 | async-start | bytes 17825792 | tf_op jit(solution)/shard_map/reduce_scatter | solution.py:229
  442.0 16.3 copy-start.26
  442.0 16.3 copy-start.27
  633.9 358.5 %reduce-scatter.9.cloned.1.call-start = ((), (), s32[]{:S(2)}) async-start(), calls=%async_computation.14 | async-start | bytes 17825792 | tf_op jit(solution)/shard_map/reduce_scatter | solution.py:232
  649.9 161.0 %copy-start.6 = (f32[256,2048]{1,0:T(8,128)S(1)}, f32[256,2048]{1,0:T(8,128)}, u32[]{:S(2)}) copy-start(f32[256,2048]{1,0:T(8,128)} %copy-done.5) | copy-start | bytes 6291460
  649.9 342.5 %copy-start.10 = (bf16[1,256,2048]{2,1,0:T(8,128)(2,1)S(1)}, bf16[1,256,2048]{2,1,0:T(8,128)(2,1)}, u32[]{:S(2)}) copy-start(bf16[1,256,2048]{2,1,0:T(8,128)(2,1)} %param.18) | copy-start | bytes 3145732
  649.9 501.6 %reduce-scatter.15.cloned.1.call-start = ((), (), s32[]{:S(2)}) async-start(), calls=%async_computation.17 | async-start | bytes 1310720 | tf_op jit(solution)/shard_map/reduce_scatter | solution.py:255
  995.8 1.4 copy-start.7
  1008.4 3.8 copy-start.2
  1023.5 3.8 copy-start.2
  1038.7 3.8 copy-start.2
  1053.9 3.7 copy-start.2
  1069.1 3.7 copy-start.2
  1084.3 3.8 copy-start.2
  1099.5 3.8 copy-start.2
  1114.7 3.7 copy-start.2
  1125.2 26.3 %copy-start.4 = (bf16[1,256,2048]{2,1,0:T(8,128)(2,1)S(1)}, bf16[1,256,2048]{2,1,0:T(8,128)(2,1)}, u32[]{:S(2)}) copy-start(bf16[1,256,2048]{2,1,0:T(8,128)(2,1)} %param.16) | copy-start | bytes 3145732
  1125.2 26.3 %copy-start.21 = (f32[16,1,128]{2,1,0:T(1,128)S(1)}, f32[16,1,128]{2,1,0:T(1,128)}, u32[]{:S(2)}) copy-start(f32[16,1,128]{2,1,0:T(1,128)} %copy-done.20) | copy-start | bytes 24580
  1125.2 26.3 %copy-start.23 = (f32[256]{0:T(256)S(1)}, f32[256]{0:T(256)}, u32[]{:S(2)}) copy-start(f32[256]{0:T(256)} %copy-done.22) | copy-start | bytes 3076
  1125.2 54.4 %reduce-scatter.13.cloned.1.call-start = ((), (), s32[]{:S(2)}) async-start(), calls=%async_computation.16 | async-start | bytes 1310720 | tf_op jit(solution)/shard_map/reduce_scatter | solution.py:249
  1125.8 117.8 %reduce-scatter.21.cloned.1.call-start = ((), (), s32[]{:S(2)}) async-start(), calls=%async_computation.20 | async-start | bytes 2228224 | tf_op jit(solution)/shard_map/reduce_scatter | solution.py:298
  1154.7 25.8 %copy-start.17 = (f32[256,32]{0,1:T(8,128)S(1)}, f32[256,32]{0,1:T(8,128)}, u32[]{:S(2)}) copy-start(f32[256,32]{0,1:T(8,128)} %copy-done.16) | copy-start | bytes 98308
  1154.7 25.8 %copy-start.19 = (f32[256,32]{0,1:T(8,128)S(1)}, f32[256,32]{0,1:T(8,128)}, u32[]{:S(2)}) copy-start(f32[256,32]{0,1:T(8,128)} %copy-done.18) | copy-start | bytes 98308
  1154.8 153.4 %reduce-scatter.19.cloned.1.call-start = ((), (), s32[]{:S(2)}) async-start(), calls=%async_computation.19 | async-start | bytes 2228224 | tf_op jit(solution)/shard_map/reduce_scatter | solution.py:297
  1180.7 2.3 copy-start.8
  1182.9 232.7 %reduce-scatter.23.cloned.1.call-start = ((), (), s32[]{:S(2)}) async-start(), calls=%async_computation.21 | async-start | bytes 8912896 | tf_op jit(solution)/shard_map/reduce_scatter | solution.py:299
  1190.2 333.7 %reduce-scatter.17.cloned.1.call-start = ((), (), s32[]{:S(2)}) async-start(), calls=%async_computation.18 | async-start | bytes 8912896 | tf_op jit(solution)/shard_map/reduce_scatter | solution.py:296
  1198.2 512.8 %all-reduce.7.cloned.1.call-start = ((), (), s32[]{:S(2)}) async-start(), calls=%async_computation.24 | async-start | bytes 15204352 | tf_op jit(solution)/shard_map/psum | solution.py:304
  1198.2 15.4 copy-start.29
  1198.2 29.1 %slice-start = ((s8[16777216]{0:T(1024)(128)(4,1)}), s8[4194304]{0:T(1024)(128)(4,1)S(1)}, s32[]{:S(2)}) async-start(s8[16777216]{0:T(1024)(128)(4,1)} %bitcast.407), calls=%async_computation.25 | async-start | bytes 8388608
  1198.2 29.1 %slice-start.1 = ((s8[16777216]{0:T(1024)(128)(4,1)}), s8[4194304]{0:T(1024)(128)(4,1)S(1)}, s32[]{:S(2)}) async-start(s8[16777216]{0:T(1024)(128)(4,1)} %bitcast.407), calls=%async_computation.26 | async-start | bytes 8388608
  1213.7 13.7 slice-start.2
  1213.7 13.7 slice-start.3
  1213.7 13.7 copy-start.30
  1524.0 0.7 copy-start.28
  1525.9 5.9 copy-start.9
  1531.8 2.2 copy-start.14
  1531.8 2.3 copy-start.15
  1711.0 7.7 copy-start.13
  1718.7 2.6 copy-start.12
  1721.3 2.6 copy-start.11
  1723.9 2.5 copy-start.1
Sparse Core Ops, SparseCore 0:
  10.2 44.0 all-gather.12
  56.5 40.0 all-gather.14
  98.8 26.7 all-gather.24
  127.7 74.3 all-gather.18
  204.1 28.4 all-gather.16
  234.7 73.2 all-gather.20
  316.8 125.1 all-gather.22
  444.2 125.0 all-gather.26
  634.1 176.7 reduce-scatter.10
  814.8 177.5 reduce-scatter.8
  1125.3 26.1 reduce-scatter.14
  1153.7 25.7 reduce-scatter.12
  1183.3 60.1 reduce-scatter.20
  1247.6 60.5 reduce-scatter.18
  1312.1 103.5 reduce-scatter.22
  1419.6 104.3 reduce-scatter.16
  1527.5 183.4 all-reduce.6

commit v2 on v1

--- a/solution.py
+++ b/solution.py
@@ -1,6 +1,10 @@
+import functools
+
 import jax
 import jax.numpy as jnp
 from jax import lax
+from jax.experimental import pallas as pl
+from jax.experimental.pallas import tpu as pltpu
 from jax.sharding import PartitionSpec as P
 
 QUERY_HEADS = 32
@@ -142,6 +146,533 @@
     grad_up = (grad_hidden * (gate_pre * sigmoid_gate)).astype(jnp.bfloat16)
     grad_normed = times_nt(grad_gate, gate_w) + times_nt(grad_up, up_w)
     return (grad_normed, times_t(normed_rows, grad_gate), times_t(normed_rows, grad_up), term_down)
+
+
+MESH = pl.DeviceIdType.MESH
+ANY = pl.BlockSpec(memory_space=pl.ANY)
+BF = jnp.bfloat16
+F32 = jnp.float32
+NN = (((1,), (0,)), ((), ()))
+NT = (((1,), (1,)), ((), ()))
+TN = (((0,), (0,)), ((), ()))
+
+
+def dot(left, right, dims):
+    return lax.dot_general(left, right, dims, preferred_element_type=F32)
+
+
+class Grid:
+    def __init__(self, chips, line):
+        self.chips, self.line = chips, line
+        self.replica = lax.axis_index("replica")
+        flat = lax.axis_index("fsdp")
+        self.x, self.core = flat // 2, flat % 2
+        self.z = lax.axis_index("context")
+        self.has_left, self.has_right = self.z > 0, self.z + 1 < line
+        self.left = (self.replica, flat, self.z - 1)
+        self.right = (self.replica, flat, self.z + 1)
+        self.across = (self.replica, (1 - self.x) * 2 + self.core, self.z)
+        self.twin = (self.replica, self.x * 2 + 1 - self.core, self.z)
+
+    def order(self, k):
+        z, n = self.z, self.line
+        near = 2 * jnp.minimum(z, n - 1 - z)
+        alternate = jnp.where(k % 2 == 1, z - (k + 1) // 2, z + k // 2)
+        return jnp.where(k <= near, alternate, jnp.where(2 * z < n, k, n - 1 - k))
+
+    def slot(self, x, z):
+        return x * self.line + z
+
+    def greet(self, twin):
+        barrier = pltpu.get_barrier_semaphore()
+
+        def tell(device):
+            pl.semaphore_signal(barrier, inc=1, device_id=device, device_id_type=MESH)
+
+        pl.when(self.has_left)(lambda: tell(self.left))
+        pl.when(self.has_right)(lambda: tell(self.right))
+        tell(self.across)
+        if twin:
+            tell(self.twin)
+        count = 1 + int(twin) + self.has_left.astype(jnp.int32) + self.has_right.astype(jnp.int32)
+        pl.semaphore_wait(barrier, count)
+
+
+def remote(src, dst, send, recv, device):
+    return pltpu.make_async_remote_copy(
+        src_ref=src, dst_ref=dst, send_sem=send, recv_sem=recv, device_id=device, device_id_type=MESH
+    )
+
+
+class Gather:
+    def __init__(self, grid, everything, send, recv, parts):
+        self.grid, self.everything, self.send, self.recv = grid, everything, send, recv
+        self.parts = parts
+        self.rows = everything.shape[1] // parts
+
+    def piece(self, x, z, part):
+        return self.everything.at[self.grid.slot(x, z), pl.ds(part * self.rows, self.rows)]
+
+    def copy(self, z, part, link):
+        grid = self.grid
+        device = (grid.right, grid.left, grid.across)[link]
+        here = self.piece(grid.x, z, part)
+        return remote(
+            here, here, self.send.at[z, part, link], self.recv.at[grid.slot(grid.x, z), part], device
+        )
+
+    def links(self, z, action):
+        grid = self.grid
+        for part in range(self.parts):
+            for link, go in (
+                (0, jnp.logical_and(z <= grid.z, grid.has_right)),
+                (1, jnp.logical_and(z >= grid.z, grid.has_left)),
+            ):
+                pl.when(go)(lambda part=part, link=link: action(self.copy(z, part, link)))
+            action(self.copy(z, part, 2))
+
+    def send_own(self):
+        self.links(self.grid.z, lambda c: c.start())
+
+    def forward(self, z):
+        grid = self.grid
+        for part in range(self.parts):
+            self.copy(z, part, 2).wait_recv()
+            for link, go in (
+                (0, jnp.logical_and(z < grid.z, grid.has_right)),
+                (1, jnp.logical_and(z > grid.z, grid.has_left)),
+            ):
+                pl.when(go)(lambda part=part, link=link: self.copy(z, part, link).start())
+            self.copy(z, part, 2).start()
+
+    def wait_across(self, z):
+        grid = self.grid
+        for part in range(self.parts):
+            here = self.piece(1 - grid.x, z, part)
+            sem = self.recv.at[grid.slot(1 - grid.x, z), part]
+            remote(here, here, self.send.at[z, part, 2], sem, grid.across).wait_recv()
+
+    def finish(self):
+        def step(z, carry):
+            self.links(z, lambda c: c.wait_send())
+            return carry
+
+        lax.fori_loop(0, self.grid.line, step, 0)
+
+
+class Scatter:
+    def __init__(self, grid, partial, from_across, from_line, total, sems, parts):
+        self.grid, self.partial, self.from_across = grid, partial, from_across
+        self.from_line, self.total = from_line, total
+        self.across_send, self.across_recv, self.line_send, self.line_recv = sems
+        self.parts = parts
+        self.rows = partial.shape[1] // parts
+
+    def run(self, part):
+        return pl.ds(part * self.rows, self.rows)
+
+    def across(self, z, part):
+        grid = self.grid
+        return remote(
+            self.partial.at[grid.slot(1 - grid.x, z), self.run(part)],
+            self.from_across.at[z, self.run(part)],
+            self.across_send.at[z, part],
+            self.across_recv.at[z, part],
+            grid.across,
+        )
+
+    def along(self, z, part, leftward):
+        grid = self.grid
+        place = z if leftward else z - 1 + grid.line - 1
+        return remote(
+            self.partial.at[grid.slot(grid.x, z), self.run(part)],
+            self.from_line.at[place, self.run(part)],
+            self.line_send.at[z, part],
+            self.line_recv.at[place, part],
+            grid.left if leftward else grid.right,
+        )
+
+    def send_across(self, z):
+        for part in range(self.parts):
+            self.across(z, part).start()
+
+    def add_line(self, z, part, leftward):
+        self.along(z, part, leftward).wait_recv()
+        place = z if leftward else z - 1 + self.grid.line - 1
+        self.total[...] += self.from_line[place, self.run(part)].astype(F32)
+
+    def gather_sum(self, z, part):
+        grid = self.grid
+        self.across(z, part).wait_recv()
+        self.total[...] = (
+            self.partial[grid.slot(grid.x, z), self.run(part)].astype(F32)
+            + self.from_across[z, self.run(part)].astype(F32)
+        )
+        pl.when(jnp.logical_and(z <= grid.z, grid.has_right))(lambda: self.add_line(z, part, True))
+        pl.when(jnp.logical_and(z >= grid.z, grid.has_left))(lambda: self.add_line(z, part, False))
+
+    def pass_on(self, z):
+        grid = self.grid
+        for part in range(self.parts):
+            self.gather_sum(z, part)
+            self.partial[grid.slot(grid.x, z), self.run(part)] = self.total[...].astype(BF)
+            pl.when(z < grid.z)(lambda part=part: self.along(z, part, True).start())
+            pl.when(z > grid.z)(lambda part=part: self.along(z, part, False).start())
+
+    def own(self, result):
+        for part in range(self.parts):
+            self.gather_sum(self.grid.z, part)
+            result[self.run(part)] = self.total[...]
+
+    def finish(self):
+        grid = self.grid
+
+        def step(z, carry):
+            for part in range(self.parts):
+                self.across(z, part).wait_send()
+                pl.when(z < grid.z)(lambda part=part: self.along(z, part, True).wait_send())
+                pl.when(z > grid.z)(lambda part=part: self.along(z, part, False).wait_send())
+            return carry
+
+        lax.fori_loop(0, grid.line, step, 0)
+
+
+def scatter_scratch(line, rows, width, parts):
+    return [
+        pltpu.VMEM((2 * line, rows, width), BF),
+        pltpu.VMEM((line, rows, width), BF),
+        pltpu.VMEM((2 * line - 2, rows, width), BF),
+        pltpu.VMEM((rows // parts, width), F32),
+        pltpu.SemaphoreType.DMA((line, parts)),
+        pltpu.SemaphoreType.DMA((line, parts)),
+        pltpu.SemaphoreType.DMA((line, parts)),
+        pltpu.SemaphoreType.DMA((2 * line - 2, parts)),
+    ]
+
+
+def load_pairs(pairs, sems):
+    copies = [pltpu.make_async_copy(src, dst, sems.at[i]) for i, (src, dst) in enumerate(pairs)]
+    for copy in copies:
+        copy.start()
+    for copy in copies:
+        copy.wait()
+
+
+def feed_kernel(
+    line, parts, tile,
+    normed, tangent, gate_own, gate_twin, up_own, up_twin, down_own, down_twin,
+    grad_sum, normed_all, tangent_all, hidden_all, grad_gate, grad_up, grad_down,
+    part_gate, part_up, part_down,
+    gate_w, up_w, down_w, hidden, dgate, dup, rows_n, rows_t,
+    partial, from_across, from_line, total, across_send, across_recv, line_send, line_recv,
+    gather_send, gather_recv, load_sem, wide, tile_sem, stage_a, stage_b, stage_sem, stage_recv, piece_a, piece_b, piece_sem, hidden_sem,
+):
+    grid = Grid(2, line)
+    rows, width = normed.shape
+    cols = gate_own.shape[1]
+    blocks = 2 * line
+    me = grid.slot(grid.x, grid.z)
+    grid.greet(True)
+    load_pairs([(normed, normed_all.at[me]), (tangent, tangent_all.at[me])], load_sem)
+    gathers = [
+        Gather(grid, normed_all, gather_send.at[0], gather_recv.at[0], parts),
+        Gather(grid, tangent_all, gather_send.at[1], gather_recv.at[1], parts),
+    ]
+    scatter = Scatter(
+        grid, partial, from_across, from_line, total,
+        (across_send, across_recv, line_send, line_recv), parts,
+    )
+    for gather in gathers:
+        gather.send_own()
+    load_pairs(
+        [
+            (gate_own, gate_w.at[:, pl.ds(0, cols)]),
+            (gate_twin, gate_w.at[:, pl.ds(cols, cols)]),
+            (up_own, up_w.at[:, pl.ds(0, cols)]),
+            (up_twin, up_w.at[:, pl.ds(cols, cols)]),
+            (down_own, down_w.at[pl.ds(0, cols)]),
+            (down_twin, down_w.at[pl.ds(cols, cols)]),
+        ],
+        load_sem,
+    )
+
+    def work(slot):
+        load_pairs([(normed_all.at[slot], rows_n), (tangent_all.at[slot], rows_t)], load_sem)
+        spot = pl.ds(pl.multiple_of(slot * rows, rows), rows)
+
+        def hidden_tile(j, carry):
+            c = pl.ds(pl.multiple_of(j * cols, cols), cols)
+            gate = dot(rows_n[...], gate_w[:, c], NN)
+            up = dot(rows_n[...], up_w[:, c], NN)
+            grad = dot(rows_t[...], down_w[c, :], NT)
+            sig = jax.nn.sigmoid(gate)
+            silu = gate * sig
+            hidden[spot, c] = (silu * up).astype(BF)
+            dgate[spot, c] = (grad * up * (sig * (1.0 + gate * (1.0 - sig)))).astype(BF)
+            dup[spot, c] = (grad * silu).astype(BF)
+            return carry
+
+        lax.fori_loop(0, 2, hidden_tile, 0)
+
+        def back_tile(j, carry):
+            c = pl.ds(pl.multiple_of(j * cols, cols), cols)
+            sums = dot(dgate[spot, :], gate_w[c, :], NT) + dot(dup[spot, :], up_w[c, :], NT)
+            partial[slot, :, c] = sums.astype(BF)
+            return carry
+
+        lax.fori_loop(0, width // cols, back_tile, 0)
+
+    def stage(k, carry):
+        @pl.when(k + 1 < line)
+        def _():
+            for gather in gathers:
+                gather.forward(grid.order(k + 1))
+
+        z = grid.order(k)
+
+        def side(j, inner):
+            @pl.when(j == 1)
+            def _():
+                for gather in gathers:
+                    gather.wait_across(z)
+
+            work(grid.slot(jnp.where(j == 0, grid.x, 1 - grid.x), z))
+            return inner
+
+        lax.fori_loop(0, 2, side, 0)
+        return carry
+
+    lax.fori_loop(0, line, stage, 0)
+    hidden_copy = pltpu.make_async_copy(hidden, hidden_all, hidden_sem)
+    hidden_copy.start()
+    for k in range(line - 1, -1, -1):
+        scatter.send_across(grid.order(k))
+
+    tiles = width // tile
+
+    def wide_loads(t, start):
+        j, buf = t % tiles, t % 2
+        c = pl.ds(pl.multiple_of(j * tile, tile), tile)
+        for i, source in enumerate((normed_all, tangent_all)):
+            copy = pltpu.make_async_copy(source.at[:, :, c], wide.at[buf, i], tile_sem.at[buf, i])
+            copy.start() if start else copy.wait()
+
+    def stages(t):
+        j, buf = t % tiles, t % 2
+        c = pl.ds(pl.multiple_of(j * tile, tile), tile)
+        return [
+            remote(src, dst, stage_sem.at[buf, i], stage_recv.at[j, i], grid.twin)
+            for i, (src, dst) in enumerate(
+                (
+                    (stage_a.at[buf, 0], part_gate.at[c, :]),
+                    (stage_a.at[buf, 1], part_up.at[c, :]),
+                    (stage_b.at[buf], part_down.at[:, c]),
+                )
+            )
+        ]
+
+    def results(t):
+        j, buf = t % tiles, t % 2
+        c = pl.ds(pl.multiple_of(j * tile, tile), tile)
+        return [
+            pltpu.make_async_copy(src, dst, stage_sem.at[buf, i])
+            for i, (src, dst) in enumerate(
+                (
+                    (stage_a.at[buf, 0], grad_gate.at[c, :]),
+                    (stage_a.at[buf, 1], grad_up.at[c, :]),
+                    (stage_b.at[buf], grad_down.at[:, c]),
+                )
+            )
+        ]
+
+    def pieces(t):
+        c = pl.ds(pl.multiple_of((t % tiles) * tile, tile), tile)
+        return [
+            (part_gate.at[c, :], piece_a.at[0]),
+            (part_up.at[c, :], piece_a.at[1]),
+            (part_down.at[:, c], piece_b),
+        ]
+
+    wide_loads(0, True)
+
+    def weights(t, carry):
+        buf = t % 2
+        pl.when(t + 1 < 2 * tiles)(lambda: wide_loads(t + 1, True))
+        wide_loads(t, False)
+        tall = blocks * rows
+        tokens = wide[buf, 0].reshape(tall, tile)
+        tangents = wide[buf, 1].reshape(tall, tile)
+
+        @pl.when(t < tiles)
+        def _():
+            theirs = slice(cols, 2 * cols)
+
+            @pl.when(t >= 2)
+            def _():
+                for copy in stages(t - 2):
+                    copy.wait_send()
+
+            stage_a[buf, 0] = dot(tokens, dgate[:, theirs], TN).astype(BF)
+            stage_a[buf, 1] = dot(tokens, dup[:, theirs], TN).astype(BF)
+            stage_b[buf] = dot(hidden[:, theirs], tangents, TN).astype(BF)
+            for copy in stages(t):
+                copy.start()
+
+        @pl.when(t >= tiles)
+        def _():
+            for copy in stages(t):
+                copy.wait_recv()
+            loads = [
+                pltpu.make_async_copy(src, dst, piece_sem.at[i])
+                for i, (src, dst) in enumerate(pieces(t))
+            ]
+            for copy in loads:
+                copy.start()
+
+            @pl.when(t < tiles + 2)
+            def _():
+                for copy in stages(t - 2):
+                    copy.wait_send()
+
+            @pl.when(t >= tiles + 2)
+            def _():
+                for copy in results(t - 2):
+                    copy.wait()
+
+            mine = slice(0, cols)
+            own_gate = dot(tokens, dgate[:, mine], TN)
+            own_up = dot(tokens, dup[:, mine], TN)
+            own_down = dot(hidden[:, mine], tangents, TN)
+            for copy in loads:
+                copy.wait()
+            stage_a[buf, 0] = (own_gate + piece_a[0].astype(F32)).astype(BF)
+            stage_a[buf, 1] = (own_up + piece_a[1].astype(F32)).astype(BF)
+            stage_b[buf] = (own_down + piece_b[...].astype(F32)).astype(BF)
+            for copy in results(t):
+                copy.start()
+
+        for k in range(line - 1, 0, -1):
+            when = 2 * tiles - 1 - (k - 1) * (tiles // (line - 1))
+            pl.when(t == when)(lambda k=k: scatter.pass_on(grid.order(k)))
+        return carry
+
+    lax.fori_loop(0, 2 * tiles, weights, 0)
+    scatter.own(grad_sum)
+    for t in (2 * tiles - 2, 2 * tiles - 1):
+        for copy in results(t):
+            copy.wait()
+    for gather in gathers:
+        gather.finish()
+    scatter.finish()
+    hidden_copy.wait()
+
+
+def feed_call(normed, tangent, gates, ups, downs, line):
+    rows, width = normed.shape
+    cols = gates[0].shape[1]
+    blocks, parts, tile = 2 * line, 2, 256
+    tiles = width // tile
+    tall = blocks * rows
+    shapes = jax.ShapeDtypeStruct
+    hbm = lambda *s: shapes(s, BF)
+    return pl.pallas_call(
+        functools.partial(feed_kernel, line, parts, tile),
+        out_shape=(
+            shapes((rows, width), F32),
+            hbm(blocks, rows, width), hbm(blocks, rows, width), hbm(tall, 2 * cols),
+            hbm(width, cols), hbm(width, cols), hbm(cols, width),
+            hbm(width, cols), hbm(width, cols), hbm(cols, width),
+        ),
+        in_specs=[ANY] * 8,
+        out_specs=(pl.BlockSpec(memory_space=pltpu.VMEM),) + (ANY,) * 9,
+        scratch_shapes=[
+            pltpu.VMEM((width, 2 * cols), BF), pltpu.VMEM((width, 2 * cols), BF), pltpu.VMEM((2 * cols, width), BF),
+            pltpu.VMEM((tall, 2 * cols), BF), pltpu.VMEM((tall, 2 * cols), BF), pltpu.VMEM((tall, 2 * cols), BF),
+            pltpu.VMEM((rows, width), BF), pltpu.VMEM((rows, width), BF),
+            *scatter_scratch(line, rows, width, parts),
+            pltpu.SemaphoreType.DMA((2, line, parts, 3)), pltpu.SemaphoreType.DMA((2, blocks, parts)),
+            pltpu.SemaphoreType.DMA((6,)),
+            pltpu.VMEM((2, 2, blocks, rows, tile), BF), pltpu.SemaphoreType.DMA((2, 2)),
+            pltpu.VMEM((2, 2, tile, cols), BF), pltpu.VMEM((2, cols, tile), BF),
+            pltpu.SemaphoreType.DMA((2, 3)), pltpu.SemaphoreType.DMA((tiles, 3)),
+            pltpu.VMEM((2, tile, cols), BF), pltpu.VMEM((cols, tile), BF), pltpu.SemaphoreType.DMA((3,)),
+            pltpu.SemaphoreType.DMA,
+        ],
+        compiler_params=pltpu.CompilerParams(
+            collective_id=1, has_side_effects=True, vmem_limit_bytes=63 * 2**20
+        ),
+        name="feed",
+    )(normed, tangent, gates[0], gates[1], ups[0], ups[1], downs[0], downs[1])
+
+
+def branch_kernel(
+    line, parts,
+    hidden_all, down_own, down_twin,
+    result,
+    down_w, hidden, load_sem,
+    partial, from_across, from_line, total, across_send, across_recv, line_send, line_recv,
+):
+    grid = Grid(2, line)
+    cols, width = down_own.shape
+    rows = partial.shape[1]
+    grid.greet(False)
+    load_pairs(
+        [
+            (down_own, down_w.at[pl.ds(0, cols)]),
+            (down_twin, down_w.at[pl.ds(cols, cols)]),
+            (hidden_all, hidden),
+        ],
+        load_sem,
+    )
+    scatter = Scatter(
+        grid, partial, from_across, from_line, total,
+        (across_send, across_recv, line_send, line_recv), parts,
+    )
+
+    def work(i, carry):
+        z = grid.order(line - 1 - i // 2)
+        slot = grid.slot(jnp.where(i % 2 == 0, 1 - grid.x, grid.x), z)
+        spot = pl.ds(pl.multiple_of(slot * rows, rows), rows)
+
+        def tile(j, inner):
+            c = pl.ds(pl.multiple_of(j * cols, cols), cols)
+            partial[slot, :, c] = dot(hidden[spot, :], down_w[:, c], NN).astype(BF)
+            return inner
+
+        lax.fori_loop(0, width // cols, tile, 0)
+        pl.when(i % 2 == 0)(lambda: scatter.send_across(z))
+        return carry
+
+    lax.fori_loop(0, 2 * line, work, 0)
+
+    def along(i, carry):
+        scatter.pass_on(grid.order(line - 1 - i))
+        return carry
+
+    lax.fori_loop(0, line - 1, along, 0)
+    scatter.own(result)
+    scatter.finish()
+
+
+def branch_call(hidden_all, downs, line, rows):
+    cols, width = downs[0].shape
+    parts = 2
+    return pl.pallas_call(
+        functools.partial(branch_kernel, line, parts),
+        out_shape=jax.ShapeDtypeStruct((rows, width), F32),
+        in_specs=[ANY] * 3,
+        out_specs=pl.BlockSpec(memory_space=pltpu.VMEM),
+        scratch_shapes=[
+            pltpu.VMEM((2 * cols, width), BF),
+            pltpu.VMEM(hidden_all.shape, BF),
+            pltpu.SemaphoreType.DMA((3,)),
+            *scatter_scratch(line, rows, width, parts),
+        ],
+        compiler_params=pltpu.CompilerParams(
+            collective_id=2, has_side_effects=True, vmem_limit_bytes=60 * 2**20
+        ),
+        name="branch",
+    )(hidden_all, downs[0], downs[1])
 
 
 def body(
@@ -157,6 +688,7 @@
     w_gate,
     w_up,
     w_down,
+    kernels,
 ):
     sequence_total, segment_length, width = tokens.shape
     total_length = places.shape[1]
@@ -219,19 +751,39 @@
     normed_mlp = (unit_two * gain_second).astype(jnp.bfloat16)
     tangent = cotangent.reshape(total_rows, width)
     tangent_f = tangent.astype(jnp.float32)
-    group = ("fsdp", "context")
-    normed_all = lax.all_gather(normed_mlp, group, axis=0, tiled=True)
-    tangent_all = lax.all_gather(tangent, group, axis=0, tiled=True)
-    branch_part, kept_values = feed_forward(normed_all, w_gate, w_up, w_down)
-    grad_part, grad_w_gate, grad_w_up, grad_w_down = feed_back(
-        normed_all, tangent_all, w_gate, w_up, w_down, kept_values
-    )
-    grad_normed = lax.psum_scatter(
-        grad_part.astype(jnp.bfloat16), group, scatter_dimension=0, tiled=True
-    ).astype(jnp.float32)
-    branch = lax.psum_scatter(
-        branch_part.astype(jnp.bfloat16), group, scatter_dimension=0, tiled=True
-    ).astype(jnp.float32)
+    if kernels:
+        line = lax.axis_size("context")
+        swap = [(i, i ^ 1) for i in range(lax.axis_size("fsdp"))]
+        gates, ups, downs = (
+            (w, lax.ppermute(w, "fsdp", swap)) for w in (w_gate, w_up, w_down)
+        )
+        grad_normed, _, _, hidden_all, *sums = feed_call(
+            normed_mlp, tangent, gates, ups, downs, line
+        )[:7]
+        branch = branch_call(hidden_all, downs, line, total_rows)
+        flip = [(i, 1 - i) for i in range(2)]
+        grad_w_gate, grad_w_up, grad_w_down = (
+            g.astype(jnp.float32) + lax.ppermute(g, "replica", flip).astype(jnp.float32)
+            for g in sums
+        )
+    else:
+        group = ("fsdp", "context")
+        normed_all = lax.all_gather(normed_mlp, group, axis=0, tiled=True)
+        tangent_all = lax.all_gather(tangent, group, axis=0, tiled=True)
+        branch_part, kept_values = feed_forward(normed_all, w_gate, w_up, w_down)
+        grad_part, grad_w_gate, grad_w_up, grad_w_down = feed_back(
+            normed_all, tangent_all, w_gate, w_up, w_down, kept_values
+        )
+        grad_normed = lax.psum_scatter(
+            grad_part.astype(jnp.bfloat16), group, scatter_dimension=0, tiled=True
+        ).astype(jnp.float32)
+        branch = lax.psum_scatter(
+            branch_part.astype(jnp.bfloat16), group, scatter_dimension=0, tiled=True
+        ).astype(jnp.float32)
+        grad_w_gate, grad_w_up, grad_w_down = (
+            lax.psum(g.astype(jnp.bfloat16), "replica").astype(jnp.float32)
+            for g in (grad_w_gate, grad_w_up, grad_w_down)
+        )
     outcome = middle + branch
     scaled_two = grad_normed * gain_second
     term_gain_two = jnp.sum(grad_normed * unit_two, axis=0)
@@ -305,9 +857,9 @@
         lax.psum(share_key.astype(jnp.bfloat16), "replica").astype(jnp.float32),
         lax.psum(share_value.astype(jnp.bfloat16), "replica").astype(jnp.float32),
         lax.psum(share_out.astype(jnp.bfloat16), "replica").astype(jnp.float32),
-        lax.psum(grad_w_gate.astype(jnp.bfloat16), "replica").astype(jnp.float32),
-        lax.psum(grad_w_up.astype(jnp.bfloat16), "replica").astype(jnp.float32),
-        lax.psum(grad_w_down.astype(jnp.bfloat16), "replica").astype(jnp.float32),
+        grad_w_gate,
+        grad_w_up,
+        grad_w_down,
         lax.psum(share_gain_one.astype(jnp.bfloat16), "replica").astype(jnp.float32),
         lax.psum(share_gain_two.astype(jnp.bfloat16), "replica").astype(jnp.float32),
     )
@@ -343,8 +895,9 @@
         P(None, ("fsdp", "context")),
         P(("fsdp", "context"), None),
     )
+    kernels = (mesh.shape["replica"], mesh.shape["fsdp"], mesh.shape["context"]) == (2, 4, 4)
     return jax.shard_map(
-        body,
+        functools.partial(body, kernels=kernels),
         mesh=mesh,
         in_specs=placed,
         out_specs=(

time: 1740 us -> 1380 us (0.79)
  waiting for transfers between devices: 1140 us -> 412 us
  Pallas kernels: 0 us -> 467 us
  matrix products: 375 us -> 209 us
  blocking collectives: 129 us -> 188 us
    pallas_call x0 -> x2, Pallas kernels: none -> 467 us  [the longest x1 370 us: feed_call(): pl.pallas_call(functools.partial(feed_kernel, line, parts, tile), out_sha...]
    reduce_scatter x2 -> x0, waiting for transfers between devices: 340 us -> none  [the longest x1 180 us: body(): lax.psum_scatter(branch_part.astype(jnp.bfloat16), group, scatter_dimensi...]
    all_gather x2 -> x0, waiting for transfers between devices: 224 us -> none  [the longest x1 124 us: body(): normed_all = lax.all_gather(normed_mlp, group, axis=0, tiled=True)]
    reduce_scatter x1, waiting for transfers between devices: 64.6 us -> 0.01 us  [body(): lax.psum_scatter(term_key.astype(jnp.bfloat16), ('fsdp', 'context'), scat...]
    psum x1, waiting for transfers between devices: 104 us -> 39.9 us  [body(): lax.psum(share_query.astype(jnp.bfloat16), 'replica').astype(jnp.float32)]
    dot_general x7 -> x4, matrix products: 79.6 us -> 16.1 us  [times_nt(): lax.dot_general(left, right, (((1,), (1,)), ((), ())), preferred_element_...]
    psum x1, blocking collectives: 4.98 us -> 65.4 us  [body(): lax.psum(share_gain_one.astype(jnp.bfloat16), 'replica').astype(jnp.float32)]
    dot_general x3 -> x0, matrix products: 43.2 us -> none  [the longest x1 16.3 us: feed_forward(): up_proj = jnp.dot(normed_rows, up_w, preferred_element_type=jnp.float32)]
  transfers between devices with their start and end apart: 17 -> 19, of which waited for: 16 -> 10; matrix products, arithmetic and copies ran while one was open for 13% -> 11% of each run, Pallas kernels for 0% -> 0%
where the time goes in v2:
time: 1380 us; the launch traced here: 1370 us
  Pallas kernels  467 us (34%)
  waiting for transfers between devices  412 us (30%)
  matrix products  209 us (15%)
  blocking collectives  188 us (14%)
  other arithmetic  46.9 us (3%)
  local copies, waits for them, and re-layouts  29.9 us (2%)
  between operations  15.4 us (1%)
    pallas_call x1, Pallas kernels, feed_call(): pl.pallas_call(functools.partial(feed_kernel, line, parts, tile), out_sha...  370 us
    reduce_scatter x1, waiting for transfers between devices, body(): lax.psum_scatter(term_query.astype(jnp.bfloat16), ('fsdp', 'context'), sc...  108 us
    pallas_call x1, Pallas kernels, branch_call(): pl.pallas_call(functools.partial(branch_kernel, line, parts), out_shape=j...  96.9 us
    sub x16, matrix products, softmax_weights(): return jax.nn.softmax(scores, axis=-1)  70.9 us
    reduce_scatter x1, waiting for transfers between devices, body(): lax.psum_scatter(term_out.astype(jnp.bfloat16), ('fsdp', 'context'), scat...  68.9 us
    all_gather x1, waiting for transfers between devices, body(): lax.all_gather(w_query, ('fsdp', 'context'), axis=0, tiled=True)  66.5 us
    psum x1, blocking collectives, body(): lax.psum(share_gain_one.astype(jnp.bfloat16), 'replica').astype(jnp.float32)  65.4 us
    unnamed x1, blocking collectives  58.1 us
  transfers between devices with their start and end apart: 19, of which 10 were waited for; matrix products, arithmetic and copies ran while one was open for 11% of the time, Pallas kernels for 0%

profile of v2, /device:TPU:0, one launch (start us, length us, event | category | flops | bytes accessed | tf_op | source)
XLA Modules:
  0.0 1374.1 jit_solution(11939980678621909808)
XLA Ops:
  8.7 33.9 %all-gather.1 = bf16[16,1,128]{2,1,0:T(2,128)(2,1)S(1)} all-gather(bf16[1,1,128]{2,1,0:T(2,128)(2,1)} %bitcast.382), channel_id=1, replica_groups=mesh['replica'=2,'fsdp'=4,'context'=4] {'fsdp','context'}, dimensions={0}, use_global_device_ids=true | all-gather | bytes 4352 | tf_op jit(solution)/shard_map/all_gather | solution.py:702
  44.2 10.1 all-gather.10.cloned.1.call-done
  54.3 3.4 convolution_convert_fusion.5
  58.6 38.0 %all-gather.12.cloned.1.call-done = bf16[2048,512]{1,0:T(8,128)(2,1)} async-done(((bf16[128,512]{1,0:T(8,128)(2,1)}), bf16[2048,512]{1,0:T(8,128)(2,1)}) %all-gather.12.cloned.1.call-update) | async-done | bytes 2097168 | tf_op jit(solution)/shard_map/all_gather | solution.py:705
  96.6 3.0 copy.44
  102.8 30.3 %all-gather.2 = bf16[16,1,128]{2,1,0:T(2,128)(2,1)S(1)} all-gather(bf16[1,1,128]{2,1,0:T(2,128)(2,1)S(1)} %bitcast.383), channel_id=1, replica_groups=mesh['replica'=2,'fsdp'=4,'context'=4] {'fsdp','context'}, dimensions={0}, use_global_device_ids=true | all-gather | bytes 4352 | tf_op jit(solution)/shard_map/all_gather | solution.py:703
  135.6 66.5 %all-gather.16.cloned.1.call-done = bf16[2048,2048]{1,0:T(8,128)(2,1)} async-done(((bf16[128,2048]{1,0:T(8,128)(2,1)}), bf16[2048,2048]{1,0:T(8,128)(2,1)}) %all-gather.16.cloned.1.call-update) | async-done | bytes 8388624 | tf_op jit(solution)/shard_map/all_gather | solution.py:704
  202.1 12.4 copy.45
  214.5 5.8 fusion.121
  220.8 11.8 all-gather.14.cloned.1.call-done
  232.6 59.9 %while.26 = (s32[]{:T(128)}, bf16[8,256,4,64]{1,3,2,0:T(8,128)(2,1)S(1)}, bf16[8,1024,64]{1,2,0:T(8,128)(2,1)}, s32[8,1024]{1,0:T(8,128)S(1)}, s32[8,256]{1,0:T(...) while((s32[]{:T(128)}, bf16[8,256,4,64]{1,3,2,0:T(8,128)(2,1)S(1)}, ...), condition=%wide.region_4.5_spmd.clone, body=%wide.region_1.4_spmd.sunk.clone | while | flops 274990080 | bytes 9593941 | solution.py:744
  232.8 4.4 fusion.215
  240.3 4.4 fusion.215
  244.7 2.8 fusion.216
  247.7 4.4 fusion.215
  252.1 2.8 fusion.216
  255.2 4.4 fusion.215
  262.6 4.4 fusion.215
  267.0 3.2 fusion.216
  270.4 4.4 fusion.215
  274.8 2.8 fusion.216
  277.9 4.4 fusion.215
  282.3 2.7 fusion.216
  285.3 4.4 fusion.215
  289.7 2.7 fusion.216
  292.5 15.4 %all-gather.18.cloned.1.call-done = bf16[2048,2048]{1,0:T(8,128)(2,1)} async-done(((bf16[128,2048]{1,0:T(8,128)(2,1)}), bf16[2048,2048]{1,0:T(8,128)(2,1)}) %all-gather.18.cloned.1.call-update) | async-done | bytes 8388624 | tf_op jit(solution)/shard_map/all_gather | solution.py:707
  307.9 5.8 multiply_reduce_fusion.2
  316.3 370.0 %feed.1 = (f32[256,2048]{1,0:T(8,128)}, bf16[8,256,2048]{2,1,0:T(8,128)(2,1)}, bf16[8,256,2048]{2,1,0:T(8,128)(2,1)}, bf16[2048,1024]{1,0:T(8,128)(2,1)}, bf16[2...) custom-call(bf16[256,2048]{1,0:T(8,128)(2,1)} %multiply_convert_fusi, ...), custom_call_target="tpu_custom_call" | custom-call | tf_op jit(solution)/shard_map/feed/pallas_call | solution.py:578
  686.3 2.8 multiply_reduce_fusion
  689.1 96.9 %branch.1 = f32[256,2048]{1,0:T(8,128)} custom-call(bf16[2048,1024]{1,0:T(8,128)(2,1)} %get-tuple-element.108.hidden_all, bf16[512,2048]{1,0:T(8,128)(2,1)} %down_own.3, bf16[512,2048]{1,0:T(8,128)(2,1)} %collective-permute-done.2.down_twin), custom_call_target="tpu_custom_call" | custom-call | tf_op jit(solution)/shard_map/branch/pallas_call | solution.py:660
  786.0 3.9 multiply_add_fusion
  791.2 6.7 convolution_convert_fusion.4
  799.9 112.5 %while.27 = (s32[]{:T(128)}, f32[8,256,4,64]{1,3,2,0:T(8,128)S(1)}, bf16[8,1024,64]{1,2,0:T(8,128)(2,1)}, bf16[8,1024,64]{1,2,0:T(8,128)(2,1)}, bf16[8,1024,64]{...) while((s32[]{:T(128)}, f32[8,256,4,64]{1,3,2,0:T(8,128)S(1)}, ...), condition=%wide.region_11.12_spmd.clone, body=%wide.region_7.11_spmd.sunk.clone | while | flops 685113344 | bytes 50507912 | solution.py:797
  800.1 4.5 fusion.225
  804.6 3.1 fusion.226
  814.2 4.5 fusion.225
  818.6 3.1 fusion.226
  828.3 4.5 fusion.225
  832.7 3.1 fusion.226
  842.3 4.5 fusion.225
  846.8 3.1 fusion.226
  856.4 4.5 fusion.225
  860.8 3.1 fusion.226
  870.4 4.5 fusion.225
  874.9 3.1 fusion.226
  884.5 4.5 fusion.225
  889.0 3.1 fusion.226
  898.6 4.5 fusion.225
  903.0 3.1 fusion.226
  914.5 24.7 %reduce-scatter.7.cloned.1.call-done = bf16[1,256,512]{1,2,0:T(8,128)(2,1)} async-done(((bf16[1,1024,512]{1,2,0:T(8,128)(2,1)}), bf16[1,256,512]{1,2,0:T(8,128)(2,1)}) %reduce-scatter.7.cloned.1.call-update) | async-done | bytes 262160 | tf_op jit(solution)/shard_map/reduce_scatter | solution.py:801
  942.6 24.9 %reduce-scatter.9.cloned.1.call-done = bf16[1,256,512]{1,2,0:T(8,128)(2,1)} async-done(((bf16[1,1024,512]{1,2,0:T(8,128)(2,1)}), bf16[1,256,512]{1,2,0:T(8,128)(2,1)}) %reduce-scatter.9.cloned.1.call-update) | async-done | bytes 262160 | tf_op jit(solution)/shard_map/reduce_scatter | solution.py:807
  967.5 3.2 convolution_convert_fusion.2
  970.7 6.8 convolution_convert_fusion
  980.8 5.8 convolution_convert_fusion.1
  992.1 6.1 fusion.157
  1002.3 58.1 %all-reduce.2 = (bf16[2048]{0:T(1024)(128)(2,1)S(1)}, bf16[2048]{0:T(1024)(128)(2,1)S(1)}) all-reduce(f32[2048]{0:T(1024)S(1)} %get-tuple-element.118, f32[2048]{0:T(1024)S(1)} %get-tuple-element.116), channel_id=9, replica_groups=mesh['replica'=2,'fsdp'=4,'context'=4] {'fsdp','context'}, use_global_device_ids=true, to_apply=%region_24.25.clone | all-reduce | flops 4096 | bytes 24576
  1060.6 65.4 %all-reduce.3 = (bf16[128]{0:T(256)(128)(2,1)S(1)}, bf16[128]{0:T(256)(128)(2,1)S(1)}) all-reduce(bf16[128]{0:T(256)(128)(2,1)S(1)} %dynamic-slice.7, bf16[128]{0:T(256)(128)(2,1)S(1)} %dynamic-slice.6), channel_id=1, replica_groups=mesh['replica'=2,'fsdp'=4,'context'=4] {'replica'}, use_global_device_ids=true, to_apply=%region_25.26 | all-reduce | flops 256 | bytes 1024 | tf_op jit(solution)/shard_map/psum | solution.py:863
  1127.1 3.3 fusion.119
  1130.4 5.1 convert_add_fusion
  1135.5 68.9 %reduce-scatter.17.cloned.1.call-done = bf16[128,2048]{1,0:T(8,128)(2,1)} async-done(((bf16[2048,2048]{1,0:T(8,128)(2,1)}), bf16[128,2048]{1,0:T(8,128)(2,1)}) %reduce-scatter.17.cloned.1.call-update) | async-done | bytes 524304 | tf_op jit(solution)/shard_map/reduce_scatter | solution.py:851
  1204.4 108.4 %reduce-scatter.11.cloned.1.call-done = bf16[128,2048]{1,0:T(8,128)(2,1)} async-done(((bf16[2048,2048]{1,0:T(8,128)(2,1)}), bf16[128,2048]{1,0:T(8,128)(2,1)}) %reduce-scatter.11.cloned.1.call-update) | async-done | bytes 524304 | tf_op jit(solution)/shard_map/reduce_scatter | solution.py:848
  1312.9 4.4 convert_add_fusion.1
  1317.2 4.2 convert_add_fusion.2
  1321.4 39.9 %all-reduce.7.cloned.1.call-done = (bf16[128,2048]{1,0:T(8,128)(2,1)}, bf16[128,512]{1,0:T(8,128)(2,1)}, bf16[128,512]{1,0:T(8,128)(2,1)}, bf16[128,2048]{1,0:T(8,128)(2,1)}) async-done(((bf16[128,2048]{1,0:T(8,128)(2,1)}, bf16[128,512]{1,0:T(8,128)(2,1)}, bf16[128,512]{1,0:T(8,128)(2,1)}, bf16[128,2048]{1,0:T(8,128)(2,1)}), (bf16[128,2048]{1,0:T(8,128)(2,1)}, bf16[128,512]{1,0:T(8,128)(2,1)}, ...) | async-done | bytes 1310736 | tf_op jit(solution)/shard_map/psum | solution.py:856
  (227 shorter events, 98.9 us)
Async XLA Ops:
  7.2 47.1 %all-gather.10.cloned.1.call-start = ((), (), s32[]{:S(2)}) async-start(), calls=%async_computation.6 | async-start | bytes 2228224 | tf_op jit(solution)/shard_map/all_gather | solution.py:706
  7.9 88.7 %all-gather.12.cloned.1.call-start = ((), (), s32[]{:S(2)}) async-start(), calls=%async_computation.7 | async-start | bytes 2228224 | tf_op jit(solution)/shard_map/all_gather | solution.py:705
  8.7 124.6 %all-gather.20.cloned.1.call-start = ((), (), s32[]{:S(2)}) async-start(), calls=%async_computation.17 | async-start | bytes 1310720 | tf_op jit(solution)/shard_map/all_gather | solution.py:732
  54.3 4.1 copy-start.21
  57.7 144.4 %all-gather.16.cloned.1.call-start = ((), (), s32[]{:S(2)}) async-start(), calls=%async_computation.9 | async-start | bytes 8912896 | tf_op jit(solution)/shard_map/all_gather | solution.py:704
  58.3 174.3 %all-gather.14.cloned.1.call-start = ((), (), s32[]{:S(2)}) async-start(), calls=%async_computation.8 | async-start | bytes 1310720 | tf_op jit(solution)/shard_map/all_gather | solution.py:731
  96.6 3.0 copy-start.1
  100.5 2.3 copy-start.22
  101.3 206.6 %all-gather.18.cloned.1.call-start = ((), (), s32[]{:S(2)}) async-start(), calls=%async_computation.10 | async-start | bytes 8912896 | tf_op jit(solution)/shard_map/all_gather | solution.py:707
  101.9 837.3 %reduce-scatter.7.cloned.1.call-start = ((), (), s32[]{:S(2)}) async-start(), calls=%async_computation.11 | async-start | bytes 1310720 | tf_op jit(solution)/shard_map/reduce_scatter | solution.py:801
  102.0 214.3 %collective-permute-start.2 = (bf16[512,2048]{1,0:T(8,128)(2,1)}, bf16[512,2048]{1,0:T(8,128)(2,1)}, u32[]{:S(2)}, u32[]{:S(2)}) collective-permute-start(bf16[512,2048]{1,0:T(8,128)(2,1)} %down_own.3), channel_id=1, source_target_pairs={{0,4},{4,0},{8,12},{12,8},{1,5},{5,1},{9,13},{13,9},{2,6},{6,2},{1... | collective-permute-start | bytes 6291464 | tf_op jit(solution)/shard_map/ppermute | solution.py:758
  102.3 214.0 %collective-permute-start = (bf16[2048,512]{1,0:T(8,128)(2,1)}, bf16[2048,512]{1,0:T(8,128)(2,1)}, u32[]{:S(2)}, u32[]{:S(2)}) collective-permute-start(bf16[2048,512]{1,0:T(8,128)(2,1)} %gate_own.1), channel_id=1, source_target_pairs={{0,4},{4,0},{8,12},{12,8},{1,5},{5,1},{9,13},{13,9},{2,6},{6,2},{1... | collective-permute-start | bytes 6291464 | tf_op jit(solution)/shard_map/ppermute | solution.py:758
  102.5 213.7 %collective-permute-start.1 = (bf16[2048,512]{1,0:T(8,128)(2,1)}, bf16[2048,512]{1,0:T(8,128)(2,1)}, u32[]{:S(2)}, u32[]{:S(2)}) collective-permute-start(bf16[2048,512]{1,0:T(8,128)(2,1)} %up_own.1), channel_id=1, source_target_pairs={{0,4},{4,0},{8,12},{12,8},{1,5},{5,1},{9,13},{13,9},{2,6},{6,2},{1... | collective-permute-start | bytes 6291464 | tf_op jit(solution)/shard_map/ppermute | solution.py:758
  292.5 21.2 %copy-start.7 = (bf16[8,256,4,64]{1,3,2,0:T(8,128)(2,1)}, bf16[8,256,4,64]{1,3,2,0:T(8,128)(2,1)S(1)}, u32[]{:S(2)}) copy-start(bf16[8,256,4,64]{1,3,2,0:T(8,128)(2,1)S(1)} %get-tuple-element.107) | copy-start | bytes 3145732
  292.5 21.2 %copy-start.11 = (bf16[8,256,4,64]{1,3,2,0:T(8,128)(2,1)}, bf16[8,256,4,64]{1,3,2,0:T(8,128)(2,1)S(1)}, u32[]{:S(2)}) copy-start(bf16[8,256,4,64]{1,3,2,0:T(8,128)(2,1)S(1)} %get-tuple-element.425) | copy-start | bytes 3145732
  313.7 1.3 copy-start.3
  689.1 96.9 %copy-start.4 = (f32[256,2048]{1,0:T(8,128)S(1)}, f32[256,2048]{1,0:T(8,128)}, u32[]{:S(2)}) copy-start(f32[256,2048]{1,0:T(8,128)} %copy-done.3) | copy-start | bytes 6291460
  689.1 96.9 %copy-start.9 = (bf16[1,256,2048]{2,1,0:T(8,128)(2,1)S(1)}, bf16[1,256,2048]{2,1,0:T(8,128)(2,1)}, u32[]{:S(2)}) copy-start(bf16[1,256,2048]{2,1,0:T(8,128)(2,1)} %param.18) | copy-start | bytes 3145732
  789.9 1.3 copy-start.5
  797.9 1.9 copy-start.12
  804.6 3.5 copy-start
  818.6 3.5 copy-start
  832.7 3.5 copy-start
  846.8 3.5 copy-start
  860.8 3.5 copy-start
  874.9 3.5 copy-start
  889.0 3.5 copy-start
  903.0 3.5 copy-start
  912.4 1.3 copy-start.13
  913.7 26.6 %copy-start.2 = (bf16[1,256,2048]{2,1,0:T(8,128)(2,1)S(1)}, bf16[1,256,2048]{2,1,0:T(8,128)(2,1)}, u32[]{:S(2)}) copy-start(bf16[1,256,2048]{2,1,0:T(8,128)(2,1)} %param.16) | copy-start | bytes 3145732
  913.7 53.8 %reduce-scatter.9.cloned.1.call-start = ((), (), s32[]{:S(2)}) async-start(), calls=%async_computation.12 | async-start | bytes 1310720 | tf_op jit(solution)/shard_map/reduce_scatter | solution.py:807
  914.5 221.0 %reduce-scatter.13.cloned.1.call-start = ((), (), s32[]{:S(2)}) async-start(), calls=%async_computation.14 | async-start | bytes 2228224 | tf_op jit(solution)/shard_map/reduce_scatter | solution.py:849
  942.6 28.2 %copy-start.6 = (f32[256,2048]{1,0:T(8,128)S(1)}, f32[256,2048]{1,0:T(8,128)}, u32[]{:S(2)}) copy-start(f32[256,2048]{1,0:T(8,128)} %copy-done.5) | copy-start | bytes 6291460
  942.6 192.9 %reduce-scatter.15.cloned.1.call-start = ((), (), s32[]{:S(2)}) async-start(), calls=%async_computation.15 | async-start | bytes 2228224 | tf_op jit(solution)/shard_map/reduce_scatter | solution.py:850
  970.7 233.8 %reduce-scatter.17.cloned.1.call-start = ((), (), s32[]{:S(2)}) async-start(), calls=%async_computation.16 | async-start | bytes 8912896 | tf_op jit(solution)/shard_map/reduce_scatter | solution.py:851
  977.6 335.2 %reduce-scatter.11.cloned.1.call-start = ((), (), s32[]{:S(2)}) async-start(), calls=%async_computation.13 | async-start | bytes 8912896 | tf_op jit(solution)/shard_map/reduce_scatter | solution.py:848
  979.9 1.0 copy-start.10
  986.6 0.7 copy-start.23
  986.7 374.7 %all-reduce.7.cloned.1.call-start = ((), (), s32[]{:S(2)}) async-start(), calls=%async_computation.18 | async-start | bytes 2621440 | tf_op jit(solution)/shard_map/psum | solution.py:856
  988.5 141.9 %collective-permute-start.5 = (bf16[512,2048]{1,0:T(8,128)(2,1)}, bf16[512,2048]{1,0:T(8,128)(2,1)}, u32[]{:S(2)}, u32[]{:S(2)}) collective-permute-start(bf16[512,2048]{1,0:T(8,128)(2,1)} %get-tuple-element.115), channel_id=1, source_target_pairs={{0,16},{16,0},{1,17},{17,1},{2,18},{18,2},{3,19},{19,3},{4,20},{20... | collective-permute-start | bytes 6291464 | tf_op jit(solution)/shard_map/ppermute | solution.py:766
  990.0 322.8 %collective-permute-start.4 = (bf16[2048,512]{1,0:T(8,128)(2,1)}, bf16[2048,512]{1,0:T(8,128)(2,1)}, u32[]{:S(2)}, u32[]{:S(2)}) collective-permute-start(bf16[2048,512]{1,0:T(8,128)(2,1)} %get-tuple-element.114), channel_id=1, source_target_pairs={{0,16},{16,0},{1,17},{17,1},{2,18},{18,2},{3,19},{19,3},{4,20},{20... | collective-permute-start | bytes 6291464 | tf_op jit(solution)/shard_map/ppermute | solution.py:766
  990.6 7.6 copy-start.8
  990.6 326.6 %collective-permute-start.3 = (bf16[2048,512]{1,0:T(8,128)(2,1)}, bf16[2048,512]{1,0:T(8,128)(2,1)}, u32[]{:S(2)}, u32[]{:S(2)}) collective-permute-start(bf16[2048,512]{1,0:T(8,128)(2,1)} %get-tuple-element.113), channel_id=1, source_target_pairs={{0,16},{16,0},{1,17},{17,1},{2,18},{18,2},{3,19},{19,3},{4,20},{20... | collective-permute-start | bytes 6291464 | tf_op jit(solution)/shard_map/ppermute | solution.py:766
  998.2 1.6 copy-start.14
  998.2 1.6 copy-start.18
  1127.1 3.3 copy-start.17
  1130.4 182.5 %copy-start.16 = (bf16[2048,512]{1,0:T(8,128)(2,1)S(1)}, bf16[2048,512]{1,0:T(8,128)(2,1)}, u32[]{:S(2)}) copy-start(bf16[2048,512]{1,0:T(8,128)(2,1)} %get-tuple-element.114) | copy-start | bytes 6291460
  1312.8 4.4 copy-start.15
  1361.4 4.3 copy-start.20
  1361.4 5.0 copy-start.19
Sparse Core Ops, SparseCore 0:
  10.2 44.0 all-gather.9
  56.5 40.0 all-gather.11
  98.8 26.8 all-gather.19
  127.7 74.3 all-gather.15
  204.1 28.4 all-gather.13
  234.7 73.1 all-gather.17
  913.9 25.3 reduce-scatter.6
  941.6 25.8 reduce-scatter.8
  971.8 60.2 reduce-scatter.12
  1036.1 60.5 reduce-scatter.14
  1100.8 103.5 reduce-scatter.16
  1208.3 104.3 reduce-scatter.10
  1315.2 46.0 all-reduce.6

commit v3 on v2

--- a/solution.py
+++ b/solution.py
@@ -173,6 +173,7 @@
         self.right = (self.replica, flat, self.z + 1)
         self.across = (self.replica, (1 - self.x) * 2 + self.core, self.z)
         self.twin = (self.replica, self.x * 2 + 1 - self.core, self.z)
+        self.mirror = (1 - self.replica, flat, self.z)
 
     def order(self, k):
         z, n = self.z, self.line
@@ -183,7 +184,7 @@
     def slot(self, x, z):
         return x * self.line + z
 
-    def greet(self, twin):
+    def greet(self, twin, mirror=False):
         barrier = pltpu.get_barrier_semaphore()
 
         def tell(device):
@@ -194,7 +195,9 @@
         tell(self.across)
         if twin:
             tell(self.twin)
-        count = 1 + int(twin) + self.has_left.astype(jnp.int32) + self.has_right.astype(jnp.int32)
+        if mirror:
+            tell(self.mirror)
+        count = 1 + int(twin) + int(mirror) + self.has_left.astype(jnp.int32) + self.has_right.astype(jnp.int32)
         pl.semaphore_wait(barrier, count)
 
 
@@ -205,45 +208,49 @@
 
 
 class Gather:
-    def __init__(self, grid, everything, send, recv, parts):
+    def __init__(self, grid, block, everything, send, recv, parts):
         self.grid, self.everything, self.send, self.recv = grid, everything, send, recv
+        self.block = block
         self.parts = parts
         self.rows = everything.shape[1] // parts
 
     def piece(self, x, z, part):
         return self.everything.at[self.grid.slot(x, z), pl.ds(part * self.rows, self.rows)]
 
-    def copy(self, z, part, link):
+    def copy(self, z, part, link, first=False):
         grid = self.grid
         device = (grid.right, grid.left, grid.across)[link]
-        here = self.piece(grid.x, z, part)
+        there = self.piece(grid.x, z, part)
+        here = self.block.at[pl.ds(part * self.rows, self.rows)] if first else there
         return remote(
-            here, here, self.send.at[z, part, link], self.recv.at[grid.slot(grid.x, z), part], device
-        )
-
-    def links(self, z, action):
+            here, there, self.send.at[z, part, link], self.recv.at[grid.slot(grid.x, z), part], device
+        )
+
+    def links(self, z, action, first=False):
         grid = self.grid
         for part in range(self.parts):
             for link, go in (
                 (0, jnp.logical_and(z <= grid.z, grid.has_right)),
                 (1, jnp.logical_and(z >= grid.z, grid.has_left)),
             ):
-                pl.when(go)(lambda part=part, link=link: action(self.copy(z, part, link)))
-            action(self.copy(z, part, 2))
+                pl.when(go)(lambda part=part, link=link: action(self.copy(z, part, link, first)))
+            action(self.copy(z, part, 2, first))
 
     def send_own(self):
-        self.links(self.grid.z, lambda c: c.start())
-
-    def forward(self, z):
+        self.links(self.grid.z, lambda c: c.start(), True)
+
+    def forward(self, distance, part):
         grid = self.grid
-        for part in range(self.parts):
-            self.copy(z, part, 2).wait_recv()
-            for link, go in (
-                (0, jnp.logical_and(z < grid.z, grid.has_right)),
-                (1, jnp.logical_and(z > grid.z, grid.has_left)),
-            ):
-                pl.when(go)(lambda part=part, link=link: self.copy(z, part, link).start())
-            self.copy(z, part, 2).start()
+        for z, there, link, go in (
+            (grid.z - distance, grid.z >= distance, 0, grid.has_right),
+            (grid.z + distance, grid.z + distance < grid.line, 1, grid.has_left),
+        ):
+
+            @pl.when(there)
+            def _(z=z, link=link, go=go):
+                self.copy(z, part, 2).wait_recv()
+                pl.when(go)(lambda: self.copy(z, part, link).start())
+                self.copy(z, part, 2).start()
 
     def wait_across(self, z):
         grid = self.grid
@@ -319,10 +326,12 @@
             pl.when(z < grid.z)(lambda part=part: self.along(z, part, True).start())
             pl.when(z > grid.z)(lambda part=part: self.along(z, part, False).start())
 
-    def own(self, result):
+    def own(self, result, after=None):
         for part in range(self.parts):
             self.gather_sum(self.grid.z, part)
-            result[self.run(part)] = self.total[...]
+            result[self.run(part)] = self.total[...].astype(result.dtype)
+            if after is not None:
+                after(part)
 
     def finish(self):
         grid = self.grid
@@ -373,10 +382,9 @@
     blocks = 2 * line
     me = grid.slot(grid.x, grid.z)
     grid.greet(True)
-    load_pairs([(normed, normed_all.at[me]), (tangent, tangent_all.at[me])], load_sem)
     gathers = [
-        Gather(grid, normed_all, gather_send.at[0], gather_recv.at[0], parts),
-        Gather(grid, tangent_all, gather_send.at[1], gather_recv.at[1], parts),
+        Gather(grid, normed, normed_all, gather_send.at[0], gather_recv.at[0], parts),
+        Gather(grid, tangent, tangent_all, gather_send.at[1], gather_recv.at[1], parts),
     ]
     scatter = Scatter(
         grid, partial, from_across, from_line, total,
@@ -392,9 +400,12 @@
             (up_twin, up_w.at[:, pl.ds(cols, cols)]),
             (down_own, down_w.at[pl.ds(0, cols)]),
             (down_twin, down_w.at[pl.ds(cols, cols)]),
+            (normed, rows_n),
+            (tangent, rows_t),
         ],
         load_sem,
     )
+    load_pairs([(rows_n, normed_all.at[me]), (rows_t, tangent_all.at[me])], load_sem)
 
     def work(slot):
         load_pairs([(normed_all.at[slot], rows_n), (tangent_all.at[slot], rows_t)], load_sem)
@@ -422,24 +433,29 @@
 
         lax.fori_loop(0, width // cols, back_tile, 0)
 
-    def stage(k, carry):
-        @pl.when(k + 1 < line)
+    def stage(distance, carry):
+        @pl.when(distance + 1 < line)
         def _():
             for gather in gathers:
-                gather.forward(grid.order(k + 1))
-
-        z = grid.order(k)
-
-        def side(j, inner):
-            @pl.when(j == 1)
+                for part in range(parts):
+                    gather.forward(distance + 1, part)
+
+        def visit(i, inner):
+            z = grid.z + jnp.where(i % 2 == 0, -distance, distance)
+            inside = jnp.logical_and(z >= 0, z < line)
+
+            @pl.when(jnp.logical_and(inside, jnp.logical_or(distance > 0, i % 2 == 0)))
             def _():
-                for gather in gathers:
-                    gather.wait_across(z)
-
-            work(grid.slot(jnp.where(j == 0, grid.x, 1 - grid.x), z))
+                @pl.when(i >= 2)
+                def _():
+                    for gather in gathers:
+                        gather.wait_across(z)
+
+                work(grid.slot(jnp.where(i < 2, grid.x, 1 - grid.x), z))
+
             return inner
 
-        lax.fori_loop(0, 2, side, 0)
+        lax.fori_loop(0, 4, visit, 0)
         return carry
 
     lax.fori_loop(0, line, stage, 0)
@@ -591,7 +607,7 @@
             pltpu.VMEM((rows, width), BF), pltpu.VMEM((rows, width), BF),
             *scatter_scratch(line, rows, width, parts),
             pltpu.SemaphoreType.DMA((2, line, parts, 3)), pltpu.SemaphoreType.DMA((2, blocks, parts)),
-            pltpu.SemaphoreType.DMA((6,)),
+            pltpu.SemaphoreType.DMA((8,)),
             pltpu.VMEM((2, 2, blocks, rows, tile), BF), pltpu.SemaphoreType.DMA((2, 2)),
             pltpu.VMEM((2, 2, tile, cols), BF), pltpu.VMEM((2, cols, tile), BF),
             pltpu.SemaphoreType.DMA((2, 3)), pltpu.SemaphoreType.DMA((tiles, 3)),
@@ -673,6 +689,117 @@
         ),
         name="branch",
     )(hidden_all, downs[0], downs[1])
+
+
+def sums_kernel(
+    line, parts,
+    normed, attended, grad_qkv, grad_out, gains,
+    result,
+    both_normed, both_attended, both_qkv, both_out, both_gains, load_sem, twin_send, twin_recv,
+    partial, from_across, from_line, total, across_send, across_recv, line_send, line_recv,
+    mine, theirs, mirror_send, mirror_recv,
+):
+    grid = Grid(2, line)
+    rows, width = normed.shape
+    run = partial.shape[1]
+    narrow = grad_qkv.shape[1]
+    grid.greet(True, True)
+    scatter = Scatter(
+        grid, partial, from_across, from_line, total,
+        (across_send, across_recv, line_send, line_recv), parts,
+    )
+    own, twin = pl.ds(0, rows), pl.ds(rows, rows)
+    pairs = [
+        (normed, both_normed.at[own], both_normed.at[twin]),
+        (grad_qkv, both_qkv.at[own], both_qkv.at[twin]),
+        (attended, both_attended.at[own], both_attended.at[twin]),
+        (grad_out, both_out.at[own], both_out.at[twin]),
+        (gains, both_gains.at[0], both_gains.at[1]),
+    ]
+    swaps = [
+        remote(src, there, twin_send.at[i], twin_recv.at[i], grid.twin)
+        for i, (src, _, there) in enumerate(pairs)
+    ]
+    for copy in swaps:
+        copy.start()
+    load_pairs([(src, here) for src, here, _ in pairs], load_sem)
+    for copy in swaps:
+        copy.wait()
+    tall = line * run
+    tile = 512
+
+    def column(j, carry):
+        x = jnp.where(j == 0, 1 - grid.x, grid.x)
+        features = pl.ds(pl.multiple_of((x * 2 + grid.core) * tall, tall), tall)
+        blocks = pl.ds(x * line, line)
+
+        def wide(left, right, first):
+            def step(i, inner):
+                c = pl.ds(pl.multiple_of(i * tile, tile), tile)
+                to = pl.ds(pl.multiple_of(first + i * tile, 128), tile)
+                value = dot(left[:, features], right[:, c], TN).astype(BF)
+                partial[blocks, :, to] = value.reshape(line, run, tile)
+                return inner
+
+            lax.fori_loop(0, right.shape[1] // tile, step, 0)
+
+        wide(both_normed, both_qkv, 0)
+        wide(both_attended, both_out, narrow)
+        pair = both_gains[0, features].astype(F32) + both_gains[1, features].astype(F32)
+        partial[blocks, :, narrow + width :] = pair.astype(BF).reshape(line, run, gains.shape[1])
+
+        @pl.when(j == 0)
+        def _():
+            for k in range(line - 1, -1, -1):
+                scatter.send_across(grid.order(k))
+
+        return carry
+
+    lax.fori_loop(0, 2, column, 0)
+
+    def along(i, carry):
+        scatter.pass_on(grid.order(line - 1 - i))
+        return carry
+
+    lax.fori_loop(0, line - 1, along, 0)
+
+    def swap(part):
+        here = scatter.run(part)
+        return remote(
+            mine.at[here], theirs.at[here], mirror_send.at[part], mirror_recv.at[part], grid.mirror
+        )
+
+    scatter.own(mine, lambda part: swap(part).start())
+    for part in range(parts):
+        swap(part).wait()
+        here = scatter.run(part)
+        result[here] = mine[here].astype(F32) + theirs[here].astype(F32)
+    scatter.finish()
+
+
+def sums_call(normed, attended, grad_qkv, grad_out, gains, line, run):
+    rows, width = normed.shape
+    narrow, few = grad_qkv.shape[1], gains.shape[1]
+    whole, parts = narrow + width + few, 4
+    return pl.pallas_call(
+        functools.partial(sums_kernel, line, parts),
+        out_shape=jax.ShapeDtypeStruct((run, whole), F32),
+        in_specs=[ANY] * 5,
+        out_specs=pl.BlockSpec(memory_space=pltpu.VMEM),
+        scratch_shapes=[
+            pltpu.VMEM((2 * rows, width), BF), pltpu.VMEM((2 * rows, width), BF),
+            pltpu.VMEM((2 * rows, narrow), BF), pltpu.VMEM((2 * rows, width), BF),
+            pltpu.VMEM((2, width, few), BF),
+            pltpu.SemaphoreType.DMA((5,)), pltpu.SemaphoreType.DMA((5,)), pltpu.SemaphoreType.DMA((5,)),
+            *scatter_scratch(line, run, whole, parts),
+            pltpu.VMEM((run, whole), BF), pltpu.VMEM((run, whole), BF),
+            pltpu.SemaphoreType.DMA((parts,)), pltpu.SemaphoreType.DMA((parts,)),
+        ],
+        compiler_params=pltpu.CompilerParams(
+            collective_id=3, has_side_effects=True, vmem_limit_bytes=60 * 2**20
+        ),
+        name="sums",
+    )(normed, attended, grad_qkv, grad_out, gains)
 
 
 def body(
@@ -791,7 +918,6 @@
         scaled_two - unit_two * jnp.mean(scaled_two * unit_two, axis=-1, keepdims=True)
     )
     grad_branch = grad_middle.astype(jnp.bfloat16)
-    term_out = times_t(attended, grad_branch)
     grad_attended = times_nt(grad_branch, out_w).astype(jnp.bfloat16)
     head_grad = query_head_rows(grad_attended, sequence_total, segment_length)
     grad_q, grad_k, grad_v = lax.map(
@@ -836,33 +962,47 @@
         + times_nt(grad_key, key_weight_local)
         + times_nt(value_gradient, value_w)
     )
-    term_query = times_t(normed_tokens, grad_query)
-    term_key = times_t(normed_tokens, grad_key)
-    term_value = times_t(normed_tokens, value_gradient)
     scaled_one = grad_normed_one * gain_first
     term_gain_one = jnp.sum(grad_normed_one * unit_one, axis=0)
     grad_inputs = grad_middle + factor_one * (
         scaled_one - unit_one * jnp.mean(scaled_one * unit_one, axis=-1, keepdims=True)
     )
-    share_query, share_key, share_value, share_out, share_gain_one, share_gain_two = (
-        lax.psum_scatter(term_query.astype(jnp.bfloat16), ("fsdp", "context"), scatter_dimension=0, tiled=True),
-        lax.psum_scatter(term_key.astype(jnp.bfloat16), ("fsdp", "context"), scatter_dimension=0, tiled=True),
-        lax.psum_scatter(term_value.astype(jnp.bfloat16), ("fsdp", "context"), scatter_dimension=0, tiled=True),
-        lax.psum_scatter(term_out.astype(jnp.bfloat16), ("fsdp", "context"), scatter_dimension=0, tiled=True),
-        lax.psum_scatter(term_gain_one, ("fsdp", "context"), scatter_dimension=0, tiled=True),
-        lax.psum_scatter(term_gain_two, ("fsdp", "context"), scatter_dimension=0, tiled=True),
-    )
-    summed = (
-        lax.psum(share_query.astype(jnp.bfloat16), "replica").astype(jnp.float32),
-        lax.psum(share_key.astype(jnp.bfloat16), "replica").astype(jnp.float32),
-        lax.psum(share_value.astype(jnp.bfloat16), "replica").astype(jnp.float32),
-        lax.psum(share_out.astype(jnp.bfloat16), "replica").astype(jnp.float32),
-        grad_w_gate,
-        grad_w_up,
-        grad_w_down,
-        lax.psum(share_gain_one.astype(jnp.bfloat16), "replica").astype(jnp.float32),
-        lax.psum(share_gain_two.astype(jnp.bfloat16), "replica").astype(jnp.float32),
-    )
+    if kernels:
+        gains = jnp.stack([term_gain_one, term_gain_two], axis=1).astype(jnp.bfloat16)
+        gains = jnp.pad(gains, ((0, 0), (0, 126)))
+        grad_qkv = jnp.concatenate([grad_query, grad_key, value_gradient], axis=1)
+        packed = sums_call(
+            normed_tokens, attended, grad_qkv, grad_branch, gains, line, w_query.shape[0]
+        )
+        ends, start = [], 0
+        for size in (width, grad_key.shape[1], grad_key.shape[1], width, 1, 1):
+            ends.append(packed[:, start : start + size])
+            start += size
+        summed = (*ends[:4], grad_w_gate, grad_w_up, grad_w_down, ends[4][:, 0], ends[5][:, 0])
+    else:
+        term_out = times_t(attended, grad_branch)
+        term_query = times_t(normed_tokens, grad_query)
+        term_key = times_t(normed_tokens, grad_key)
+        term_value = times_t(normed_tokens, value_gradient)
+        share_query, share_key, share_value, share_out, share_gain_one, share_gain_two = (
+            lax.psum_scatter(term_query.astype(jnp.bfloat16), ("fsdp", "context"), scatter_dimension=0, tiled=True),
+            lax.psum_scatter(term_key.astype(jnp.bfloat16), ("fsdp", "context"), scatter_dimension=0, tiled=True),
+            lax.psum_scatter(term_value.astype(jnp.bfloat16), ("fsdp", "context"), scatter_dimension=0, tiled=True),
+            lax.psum_scatter(term_out.astype(jnp.bfloat16), ("fsdp", "context"), scatter_dimension=0, tiled=True),
+            lax.psum_scatter(term_gain_one, ("fsdp", "context"), scatter_dimension=0, tiled=True),
+            lax.psum_scatter(term_gain_two, ("fsdp", "context"), scatter_dimension=0, tiled=True),
+        )
+        summed = (
+            lax.psum(share_query.astype(jnp.bfloat16), "replica").astype(jnp.float32),
+            lax.psum(share_key.astype(jnp.bfloat16), "replica").astype(jnp.float32),
+            lax.psum(share_value.astype(jnp.bfloat16), "replica").astype(jnp.float32),
+            lax.psum(share_out.astype(jnp.bfloat16), "replica").astype(jnp.float32),
+            grad_w_gate,
+            grad_w_up,
+            grad_w_down,
+            lax.psum(share_gain_one.astype(jnp.bfloat16), "replica").astype(jnp.float32),
+            lax.psum(share_gain_two.astype(jnp.bfloat16), "replica").astype(jnp.float32),
+        )
     out = outcome.astype(jnp.bfloat16).reshape(sequence_total, segment_length, width)
     grad_tokens = grad_inputs.astype(jnp.bfloat16).reshape(sequence_total, segment_length, width)
     return (

time: 1380 us -> 1080 us (0.78)
  waiting for transfers between devices: 412 us -> 143 us
  blocking collectives: 188 us -> 64.2 us
  Pallas kernels: 467 us -> 552 us
    reduce_scatter x4 -> x0, waiting for transfers between devices: 177 us -> none  [the longest x1 108 us: body(): lax.psum_scatter(term_query.astype(jnp.bfloat16), ('fsdp', 'context'), sc...]
    pallas_call x0 -> x1, Pallas kernels: none -> 144 us  [sums_call(): pl.pallas_call(functools.partial(sums_kernel, line, parts), out_shape=jax...]
    psum x1 -> x0, blocking collectives: 65.4 us -> none  [body(): lax.psum(share_gain_one.astype(jnp.bfloat16), 'replica').astype(jnp.float32)]
    pallas_call x1, Pallas kernels: 370 us -> 306 us  [feed_call(): pl.pallas_call(functools.partial(feed_kernel, line, parts, tile), out_sha...]
    unnamed x1 -> x0, blocking collectives: 58.1 us -> none
    psum x1 -> x0, waiting for transfers between devices: 39.9 us -> none  [body(): lax.psum(share_query.astype(jnp.bfloat16), 'replica').astype(jnp.float32)]
    reduce_scatter x1, waiting for transfers between devices: 24.9 us -> 0.01 us  [body(): lax.psum_scatter(merge_keys(grad_v, sequence_total, total_length).astype(...]
    reduce_scatter x1, waiting for transfers between devices: 24.7 us -> 0.01 us  [body(): lax.psum_scatter(merge_keys(grad_k, sequence_total, total_length).astype(...]
  transfers between devices with their start and end apart: 19 -> 14, of which waited for: 10 -> 5; matrix products, arithmetic and copies ran while one was open for 11% -> 14% of each run, Pallas kernels for 0% -> 23%
where the time goes in v3:
time: 1080 us; the launch traced here: 1070 us
  Pallas kernels  552 us (51%)
  matrix products  203 us (19%)
  waiting for transfers between devices  143 us (13%)
  blocking collectives  64.2 us (6%)
  local copies, waits for them, and re-layouts  41.3 us (4%)
  other arithmetic  41.2 us (4%)
  between operations  15 us (1%)
    pallas_call x1, Pallas kernels, feed_call(): pl.pallas_call(functools.partial(feed_kernel, line, parts, tile), out_sha...  306 us
    pallas_call x1, Pallas kernels, sums_call(): pl.pallas_call(functools.partial(sums_kernel, line, parts), out_shape=jax...  144 us
    pallas_call x1, Pallas kernels, branch_call(): pl.pallas_call(functools.partial(branch_kernel, line, parts), out_shape=j...  102 us
    sub x16, matrix products, softmax_weights(): return jax.nn.softmax(scores, axis=-1)  70.9 us
    all_gather x1, waiting for transfers between devices, body(): lax.all_gather(w_query, ('fsdp', 'context'), axis=0, tiled=True)  66.5 us
    all_gather x1, waiting for transfers between devices, body(): lax.all_gather(key_projection, ('fsdp', 'context'), axis=0, tiled=True)  38.4 us
    all_gather x1, blocking collectives, body(): lax.all_gather(gain_attn, ('fsdp', 'context'), axis=0, tiled=True)  33.9 us
    all_gather x1, blocking collectives, body(): lax.all_gather(gain_mlp, ('fsdp', 'context'), axis=0, tiled=True)  30.3 us
  transfers between devices with their start and end apart: 14, of which 5 were waited for; matrix products, arithmetic and copies ran while one was open for 14% of the time, Pallas kernels for 23%

profile of v3, /device:TPU:0, one launch (start us, length us, event | category | flops | bytes accessed | tf_op | source)
XLA Modules:
  0.0 1065.2 jit_solution(15249411423304816956)
XLA Ops:
  8.7 33.9 %all-gather.1 = bf16[16,1,128]{2,1,0:T(2,128)(2,1)S(1)} all-gather(bf16[1,1,128]{2,1,0:T(2,128)(2,1)} %bitcast.373), channel_id=1, replica_groups=mesh['replica'=2,'fsdp'=4,'context'=4] {'fsdp','context'}, dimensions={0}, use_global_device_ids=true | all-gather | bytes 4352 | tf_op jit(solution)/shard_map/all_gather | solution.py:829
  45.7 8.6 all-gather.10.cloned.1.call-done
  54.3 3.0 convolution_convert_fusion.1
  58.2 38.4 %all-gather.12.cloned.1.call-done = bf16[2048,512]{1,0:T(8,128)(2,1)} async-done(((bf16[128,512]{1,0:T(8,128)(2,1)}), bf16[2048,512]{1,0:T(8,128)(2,1)}) %all-gather.12.cloned.1.call-update) | async-done | bytes 2097168 | tf_op jit(solution)/shard_map/all_gather | solution.py:832
  96.6 3.0 copy.54
  102.8 30.3 %all-gather.2 = bf16[16,1,128]{2,1,0:T(2,128)(2,1)S(1)} all-gather(bf16[1,1,128]{2,1,0:T(2,128)(2,1)S(1)} %bitcast.374), channel_id=1, replica_groups=mesh['replica'=2,'fsdp'=4,'context'=4] {'fsdp','context'}, dimensions={0}, use_global_device_ids=true | all-gather | bytes 4352 | tf_op jit(solution)/shard_map/all_gather | solution.py:830
  135.6 66.5 %all-gather.16.cloned.1.call-done = bf16[2048,2048]{1,0:T(8,128)(2,1)} async-done(((bf16[128,2048]{1,0:T(8,128)(2,1)}), bf16[2048,2048]{1,0:T(8,128)(2,1)}) %all-gather.16.cloned.1.call-update) | async-done | bytes 8388624 | tf_op jit(solution)/shard_map/all_gather | solution.py:831
  202.1 12.4 %copy.55 = bf16[2048,2048]{1,0:T(8,128)(2,1)} copy(bf16[2048,2048]{0,1:T(8,128)(2,1)} %bitcast.339) | data formatting | bytes 16777216 | tf_op jit(solution)/shard_map/dot_general | solution.py:842
  214.5 5.8 fusion.121
  220.8 11.8 %all-gather.14.cloned.1.call-done = bf16[1,1024,512]{1,2,0:T(8,128)(2,1)} async-done(((bf16[1,256,512]{1,2,0:T(8,128)(2,1)}), bf16[1,1024,512]{1,2,0:T(8,128)(2,1)}) %all-gather.14.cloned.1.call-update) | async-done | bytes 1048592 | tf_op jit(solution)/shard_map/all_gather | solution.py:858
  232.6 59.9 %while.26 = (s32[]{:T(128)}, bf16[8,256,4,64]{1,3,2,0:T(8,128)(2,1)S(1)}, bf16[8,1024,64]{1,2,0:T(8,128)(2,1)}, s32[8,1024]{1,0:T(8,128)S(1)}, s32[8,256]{1,0:T(...) while((s32[]{:T(128)}, bf16[8,256,4,64]{1,3,2,0:T(8,128)(2,1)S(1)}, ...), condition=%wide.region_4.5_spmd.clone, body=%wide.region_1.4_spmd.sunk.clone | while | flops 274990080 | bytes 9593941 | solution.py:871
  232.8 4.4 fusion.204
  237.2 2.7 fusion.205
  240.3 4.4 fusion.204
  244.7 2.8 fusion.205
  247.7 4.4 fusion.204
  252.1 2.8 fusion.205
  255.2 4.4 fusion.204
  259.6 2.7 fusion.205
  262.6 4.4 fusion.204
  267.0 3.2 fusion.205
  270.4 4.4 fusion.204
  274.8 2.8 fusion.205
  277.9 4.4 fusion.204
  282.3 2.7 fusion.205
  285.3 4.4 fusion.204
  289.7 2.7 fusion.205
  292.5 15.4 %all-gather.18.cloned.1.call-done = bf16[2048,2048]{1,0:T(8,128)(2,1)} async-done(((bf16[128,2048]{1,0:T(8,128)(2,1)}), bf16[2048,2048]{1,0:T(8,128)(2,1)}) %all-gather.18.cloned.1.call-update) | async-done | bytes 8388624 | tf_op jit(solution)/shard_map/all_gather | solution.py:834
  307.9 5.8 multiply_reduce_fusion.2
  316.3 305.5 %feed.1 = (f32[256,2048]{1,0:T(8,128)}, bf16[8,256,2048]{2,1,0:T(8,128)(2,1)}, bf16[8,256,2048]{2,1,0:T(8,128)(2,1)}, bf16[2048,1024]{1,0:T(8,128)(2,1)}, bf16[2...) custom-call(bf16[256,2048]{1,0:T(8,128)(2,1)} %multiply_convert_fusi, ...), custom_call_target="tpu_custom_call" | custom-call | tf_op jit(solution)/shard_map/feed/pallas_call | solution.py:594
  621.9 2.9 multiply_reduce_fusion
  628.2 6.7 convolution_convert_fusion
  636.4 118.1 %while.27 = (s32[]{:T(128)}, f32[8,256,4,64]{1,3,2,0:T(8,128)}, bf16[8,1024,64]{1,2,0:T(8,128)(2,1)}, bf16[8,1024,64]{1,2,0:T(8,128)(2,1)}, bf16[8,1024,64]{1,2,...) while((s32[]{:T(128)}, f32[8,256,4,64]{1,3,2,0:T(8,128)}, ...), condition=%wide.region_11.12_spmd.clone, body=%wide.region_7.11_spmd.sunk.clone | while | flops 685113344 | bytes 50507912 | solution.py:923
  636.7 4.5 fusion.214
  641.1 3.1 fusion.215
  647.5 2.3 fusion.218
  651.4 4.5 fusion.214
  655.9 3.1 fusion.215
  662.2 2.3 fusion.218
  666.2 4.5 fusion.214
  670.6 3.1 fusion.215
  680.9 4.5 fusion.214
  685.4 3.1 fusion.215
  695.7 4.5 fusion.214
  700.1 3.1 fusion.215
  706.5 2.3 fusion.218
  710.4 4.5 fusion.214
  714.9 3.1 fusion.215
  725.2 4.5 fusion.214
  729.6 3.1 fusion.215
  739.9 4.5 fusion.214
  744.4 3.1 fusion.215
  754.5 2.4 copy.57
  765.3 101.8 %branch.1 = f32[256,2048]{1,0:T(8,128)} custom-call(bf16[2048,1024]{1,0:T(8,128)(2,1)} %get-tuple-element.108.hidden_all, bf16[512,2048]{1,0:T(8,128)(2,1)} %down_own.3, bf16[512,2048]{1,0:T(8,128)(2,1)} %collective-permute-done.2.down_twin), custom_call_target="tpu_custom_call" | custom-call | tf_op jit(solution)/shard_map/branch/pallas_call | solution.py:676
  867.0 7.1 fusion.147
  876.1 4.4 convolution_add_fusion.1
  880.5 4.5 fusion.114
  888.0 2.6 pad_maximum_fusion.grad_qkv
  890.6 144.4 %sums.1 = f32[128,5248]{1,0:T(8,128)} custom-call(bf16[256,2048]{1,0:T(8,128)(2,1)} %copy-done.12, bf16[256,2048]{1,0:T(8,128)(2,1)} %copy.61.attended, bf16[256,3072]{1,0:T(8,128)(2,1)} %pad_maximum_fusion.grad_qkv, bf16[256,2048]{1,0:T(8,128)(2,1)} %copy-done.13, bf16[2048,128]{1,0:T(8,128)(2,1)} %pad.4.gains), custom_call_target="tpu_custom_call" | custom-call | tf_op jit(solution)/shard_map/sums/pallas_call | solution.py:784
  1036.9 3.2 fusion.145
  1041.7 4.5 convert_add_fusion
  1046.3 4.4 convert_add_fusion.1
  1051.0 2.6 fusion.120
  1053.6 4.3 convert_add_fusion.2
  (206 shorter events, 87.8 us)
Async XLA Ops:
  7.2 47.1 %all-gather.10.cloned.1.call-start = ((), (), s32[]{:S(2)}) async-start(), calls=%async_computation.2 | async-start | bytes 2228224 | tf_op jit(solution)/shard_map/all_gather | solution.py:833
  7.9 88.7 %all-gather.12.cloned.1.call-start = ((), (), s32[]{:S(2)}) async-start(), calls=%async_computation.3 | async-start | bytes 2228224 | tf_op jit(solution)/shard_map/all_gather | solution.py:832
  8.7 124.6 %all-gather.20.cloned.1.call-start = ((), (), s32[]{:S(2)}) async-start(), calls=%async_computation.9 | async-start | bytes 1310720 | tf_op jit(solution)/shard_map/all_gather | solution.py:859
  45.7 12.2 %copy-start.12 = (bf16[256,2048]{1,0:T(8,128)(2,1)}, bf16[256,2048]{1,0:T(8,128)(2,1)S(1)}, u32[]{:S(2)}) copy-start(bf16[256,2048]{1,0:T(8,128)(2,1)S(1)} %fusion.108.normed) | copy-start | bytes 3145732
  45.7 12.3 %copy-start.19 = (s32[1,1024]{1,0:T(1,128)S(1)}, s32[1,1024]{1,0:T(1,128)}, u32[]{:S(2)}) copy-start(s32[1,1024]{1,0:T(1,128)} %param.17) | copy-start | bytes 12292
  57.3 144.8 %all-gather.16.cloned.1.call-start = ((), (), s32[]{:S(2)}) async-start(), calls=%async_computation.5 | async-start | bytes 8912896 | tf_op jit(solution)/shard_map/all_gather | solution.py:831
  57.9 174.7 %all-gather.14.cloned.1.call-start = ((), (), s32[]{:S(2)}) async-start(), calls=%async_computation.4 | async-start | bytes 1310720 | tf_op jit(solution)/shard_map/all_gather | solution.py:858
  96.6 3.0 copy-start.3
  100.5 2.3 copy-start.20
  101.3 206.5 %all-gather.18.cloned.1.call-start = ((), (), s32[]{:S(2)}) async-start(), calls=%async_computation.6 | async-start | bytes 8912896 | tf_op jit(solution)/shard_map/all_gather | solution.py:834
  101.9 772.2 %reduce-scatter.3.cloned.1.call-start = ((), (), s32[]{:S(2)}) async-start(), calls=%async_computation.7 | async-start | bytes 1310720 | tf_op jit(solution)/shard_map/reduce_scatter | solution.py:927
  102.0 214.3 %collective-permute-start.2 = (bf16[512,2048]{1,0:T(8,128)(2,1)}, bf16[512,2048]{1,0:T(8,128)(2,1)}, u32[]{:S(2)}, u32[]{:S(2)}) collective-permute-start(bf16[512,2048]{1,0:T(8,128)(2,1)} %down_own.3), channel_id=1, source_target_pairs={{0,4},{4,0},{8,12},{12,8},{1,5},{5,1},{9,13},{13,9},{2,6},{6,2},{1... | collective-permute-start | bytes 6291464 | tf_op jit(solution)/shard_map/ppermute | solution.py:885
  102.3 214.0 %collective-permute-start = (bf16[2048,512]{1,0:T(8,128)(2,1)}, bf16[2048,512]{1,0:T(8,128)(2,1)}, u32[]{:S(2)}, u32[]{:S(2)}) collective-permute-start(bf16[2048,512]{1,0:T(8,128)(2,1)} %gate_own.1), channel_id=1, source_target_pairs={{0,4},{4,0},{8,12},{12,8},{1,5},{5,1},{9,13},{13,9},{2,6},{6,2},{1... | collective-permute-start | bytes 6291464 | tf_op jit(solution)/shard_map/ppermute | solution.py:885
  102.5 213.7 %collective-permute-start.1 = (bf16[2048,512]{1,0:T(8,128)(2,1)}, bf16[2048,512]{1,0:T(8,128)(2,1)}, u32[]{:S(2)}, u32[]{:S(2)}) collective-permute-start(bf16[2048,512]{1,0:T(8,128)(2,1)} %up_own.1), channel_id=1, source_target_pairs={{0,4},{4,0},{8,12},{12,8},{1,5},{5,1},{9,13},{13,9},{2,6},{6,2},{1... | collective-permute-start | bytes 6291464 | tf_op jit(solution)/shard_map/ppermute | solution.py:885
  292.5 21.2 %copy-start.7 = (bf16[8,256,4,64]{1,3,2,0:T(8,128)(2,1)}, bf16[8,256,4,64]{1,3,2,0:T(8,128)(2,1)S(1)}, u32[]{:S(2)}) copy-start(bf16[8,256,4,64]{1,3,2,0:T(8,128)(2,1)S(1)} %get-tuple-element.107) | copy-start | bytes 3145732
  292.5 21.2 %copy-start.14 = (bf16[8,256,4,64]{1,3,2,0:T(8,128)(2,1)}, bf16[8,256,4,64]{1,3,2,0:T(8,128)(2,1)S(1)}, u32[]{:S(2)}) copy-start(bf16[8,256,4,64]{1,3,2,0:T(8,128)(2,1)S(1)} %get-tuple-element.405) | copy-start | bytes 3145732
  313.7 1.3 copy-start.1
  621.8 3.0 copy-start.2
  621.9 3.5 copy-start.5
  627.2 1.0 copy-start.13
  641.1 3.5 copy-start
  655.9 3.5 copy-start
  670.6 3.5 copy-start
  685.4 3.5 copy-start
  700.1 3.5 copy-start
  714.9 3.5 copy-start
  729.6 3.5 copy-start
  744.4 3.5 copy-start
  754.5 2.5 copy-start.8
  754.5 126.0 %reduce-scatter.5.cloned.1.call-start = ((), (), s32[]{:S(2)}) async-start(), calls=%async_computation.8 | async-start | bytes 1310720 | tf_op jit(solution)/shard_map/reduce_scatter | solution.py:933
  758.3 283.4 %collective-permute-start.5 = (bf16[512,2048]{1,0:T(8,128)(2,1)}, bf16[512,2048]{1,0:T(8,128)(2,1)}, u32[]{:S(2)}, u32[]{:S(2)}) collective-permute-start(bf16[512,2048]{1,0:T(8,128)(2,1)} %get-tuple-element.115), channel_id=1, source_target_pairs={{0,16},{16,0},{1,17},{17,1},{2,18},{18,2},{3,19},{19,3},{4,20},{20... | collective-permute-start | bytes 6291464 | tf_op jit(solution)/shard_map/ppermute | solution.py:893
  759.8 286.4 %collective-permute-start.4 = (bf16[2048,512]{1,0:T(8,128)(2,1)}, bf16[2048,512]{1,0:T(8,128)(2,1)}, u32[]{:S(2)}, u32[]{:S(2)}) collective-permute-start(bf16[2048,512]{1,0:T(8,128)(2,1)} %get-tuple-element.114), channel_id=1, source_target_pairs={{0,16},{16,0},{1,17},{17,1},{2,18},{18,2},{3,19},{19,3},{4,20},{20... | collective-permute-start | bytes 6291464 | tf_op jit(solution)/shard_map/ppermute | solution.py:893
  760.4 293.3 %collective-permute-start.3 = (bf16[2048,512]{1,0:T(8,128)(2,1)}, bf16[2048,512]{1,0:T(8,128)(2,1)}, u32[]{:S(2)}, u32[]{:S(2)}) collective-permute-start(bf16[2048,512]{1,0:T(8,128)(2,1)} %get-tuple-element.113), channel_id=1, source_target_pairs={{0,16},{16,0},{1,17},{17,1},{2,18},{18,2},{3,19},{19,3},{4,20},{20... | collective-permute-start | bytes 6291464 | tf_op jit(solution)/shard_map/ppermute | solution.py:893
  876.1 4.4 copy-start.4
  880.5 7.5 copy-start.18
  1036.9 4.9 copy-start.17
  1041.7 4.5 copy-start.16
  1046.2 4.4 copy-start.6
  1046.2 4.4 copy-start.9
  1046.2 4.4 copy-start.10
  1046.2 4.8 copy-start.11
  1051.0 2.6 copy-start.15
Sparse Core Ops, SparseCore 0:
  10.2 44.0 all-gather.9
  56.5 40.0 all-gather.11
  98.8 26.8 all-gather.19
  127.7 74.3 all-gather.15
  204.1 28.4 all-gather.13
  234.7 73.1 all-gather.17
  754.6 25.1 reduce-scatter.2
  782.8 42.9 reduce-scatter.4

commit v4 on v3

--- a/solution.py
+++ b/solution.py
@@ -215,7 +215,8 @@
         self.rows = everything.shape[1] // parts
 
     def piece(self, x, z, part):
-        return self.everything.at[self.grid.slot(x, z), pl.ds(part * self.rows, self.rows)]
+        start = pl.multiple_of(part * self.rows, self.rows)
+        return self.everything.at[self.grid.slot(x, z), pl.ds(start, self.rows)]
 
     def copy(self, z, part, link, first=False):
         grid = self.grid
@@ -278,6 +279,9 @@
     def run(self, part):
         return pl.ds(part * self.rows, self.rows)
 
+    def place(self, z):
+        return z if self.from_across is None else self.grid.slot(self.grid.x, z)
+
     def across(self, z, part):
         grid = self.grid
         return remote(
@@ -292,7 +296,7 @@
         grid = self.grid
         place = z if leftward else z - 1 + grid.line - 1
         return remote(
-            self.partial.at[grid.slot(grid.x, z), self.run(part)],
+            self.partial.at[self.place(z), self.run(part)],
             self.from_line.at[place, self.run(part)],
             self.line_send.at[z, part],
             self.line_recv.at[place, part],
@@ -310,11 +314,11 @@
 
     def gather_sum(self, z, part):
         grid = self.grid
-        self.across(z, part).wait_recv()
-        self.total[...] = (
-            self.partial[grid.slot(grid.x, z), self.run(part)].astype(F32)
-            + self.from_across[z, self.run(part)].astype(F32)
-        )
+        value = self.partial[self.place(z), self.run(part)].astype(F32)
+        if self.from_across is not None:
+            self.across(z, part).wait_recv()
+            value = value + self.from_across[z, self.run(part)].astype(F32)
+        self.total[...] = value
         pl.when(jnp.logical_and(z <= grid.z, grid.has_right))(lambda: self.add_line(z, part, True))
         pl.when(jnp.logical_and(z >= grid.z, grid.has_left))(lambda: self.add_line(z, part, False))
 
@@ -322,7 +326,7 @@
         grid = self.grid
         for part in range(self.parts):
             self.gather_sum(z, part)
-            self.partial[grid.slot(grid.x, z), self.run(part)] = self.total[...].astype(BF)
+            self.partial[self.place(z), self.run(part)] = self.total[...].astype(BF)
             pl.when(z < grid.z)(lambda part=part: self.along(z, part, True).start())
             pl.when(z > grid.z)(lambda part=part: self.along(z, part, False).start())
 
@@ -338,7 +342,8 @@
 
         def step(z, carry):
             for part in range(self.parts):
-                self.across(z, part).wait_send()
+                if self.from_across is not None:
+                    self.across(z, part).wait_send()
                 pl.when(z < grid.z)(lambda part=part: self.along(z, part, True).wait_send())
                 pl.when(z > grid.z)(lambda part=part: self.along(z, part, False).wait_send())
             return carry
@@ -369,8 +374,8 @@
 
 def feed_kernel(
     line, parts, tile,
-    normed, tangent, gate_own, gate_twin, up_own, up_twin, down_own, down_twin,
-    grad_sum, normed_all, tangent_all, hidden_all, grad_gate, grad_up, grad_down,
+    normed, tangent_all, gate_own, gate_twin, up_own, up_twin, down_own, down_twin,
+    grad_sum, normed_all, hidden_all, grad_gate, grad_up, grad_down,
     part_gate, part_up, part_down,
     gate_w, up_w, down_w, hidden, dgate, dup, rows_n, rows_t,
     partial, from_across, from_line, total, across_send, across_recv, line_send, line_recv,
@@ -384,7 +389,6 @@
     grid.greet(True)
     gathers = [
         Gather(grid, normed, normed_all, gather_send.at[0], gather_recv.at[0], parts),
-        Gather(grid, tangent, tangent_all, gather_send.at[1], gather_recv.at[1], parts),
     ]
     scatter = Scatter(
         grid, partial, from_across, from_line, total,
@@ -401,11 +405,10 @@
             (down_own, down_w.at[pl.ds(0, cols)]),
             (down_twin, down_w.at[pl.ds(cols, cols)]),
             (normed, rows_n),
-            (tangent, rows_t),
         ],
         load_sem,
     )
-    load_pairs([(rows_n, normed_all.at[me]), (rows_t, tangent_all.at[me])], load_sem)
+    load_pairs([(rows_n, normed_all.at[me])], load_sem)
 
     def work(slot):
         load_pairs([(normed_all.at[slot], rows_n), (tangent_all.at[slot], rows_t)], load_sem)
@@ -583,7 +586,7 @@
     hidden_copy.wait()
 
 
-def feed_call(normed, tangent, gates, ups, downs, line):
+def feed_call(normed, tangent_all, gates, ups, downs, line):
     rows, width = normed.shape
     cols = gates[0].shape[1]
     blocks, parts, tile = 2 * line, 2, 256
@@ -595,18 +598,18 @@
         functools.partial(feed_kernel, line, parts, tile),
         out_shape=(
             shapes((rows, width), F32),
-            hbm(blocks, rows, width), hbm(blocks, rows, width), hbm(tall, 2 * cols),
+            hbm(blocks, rows, width), hbm(tall, 2 * cols),
             hbm(width, cols), hbm(width, cols), hbm(cols, width),
             hbm(width, cols), hbm(width, cols), hbm(cols, width),
         ),
         in_specs=[ANY] * 8,
-        out_specs=(pl.BlockSpec(memory_space=pltpu.VMEM),) + (ANY,) * 9,
+        out_specs=(pl.BlockSpec(memory_space=pltpu.VMEM),) + (ANY,) * 8,
         scratch_shapes=[
             pltpu.VMEM((width, 2 * cols), BF), pltpu.VMEM((width, 2 * cols), BF), pltpu.VMEM((2 * cols, width), BF),
             pltpu.VMEM((tall, 2 * cols), BF), pltpu.VMEM((tall, 2 * cols), BF), pltpu.VMEM((tall, 2 * cols), BF),
             pltpu.VMEM((rows, width), BF), pltpu.VMEM((rows, width), BF),
             *scatter_scratch(line, rows, width, parts),
-            pltpu.SemaphoreType.DMA((2, line, parts, 3)), pltpu.SemaphoreType.DMA((2, blocks, parts)),
+            pltpu.SemaphoreType.DMA((1, line, parts, 3)), pltpu.SemaphoreType.DMA((1, blocks, parts)),
             pltpu.SemaphoreType.DMA((8,)),
             pltpu.VMEM((2, 2, blocks, rows, tile), BF), pltpu.SemaphoreType.DMA((2, 2)),
             pltpu.VMEM((2, 2, tile, cols), BF), pltpu.VMEM((2, cols, tile), BF),
@@ -618,77 +621,7 @@
             collective_id=1, has_side_effects=True, vmem_limit_bytes=63 * 2**20
         ),
         name="feed",
-    )(normed, tangent, gates[0], gates[1], ups[0], ups[1], downs[0], downs[1])
-
-
-def branch_kernel(
-    line, parts,
-    hidden_all, down_own, down_twin,
-    result,
-    down_w, hidden, load_sem,
-    partial, from_across, from_line, total, across_send, across_recv, line_send, line_recv,
-):
-    grid = Grid(2, line)
-    cols, width = down_own.shape
-    rows = partial.shape[1]
-    grid.greet(False)
-    load_pairs(
-        [
-            (down_own, down_w.at[pl.ds(0, cols)]),
-            (down_twin, down_w.at[pl.ds(cols, cols)]),
-            (hidden_all, hidden),
-        ],
-        load_sem,
-    )
-    scatter = Scatter(
-        grid, partial, from_across, from_line, total,
-        (across_send, across_recv, line_send, line_recv), parts,
-    )
-
-    def work(i, carry):
-        z = grid.order(line - 1 - i // 2)
-        slot = grid.slot(jnp.where(i % 2 == 0, 1 - grid.x, grid.x), z)
-        spot = pl.ds(pl.multiple_of(slot * rows, rows), rows)
-
-        def tile(j, inner):
-            c = pl.ds(pl.multiple_of(j * cols, cols), cols)
-            partial[slot, :, c] = dot(hidden[spot, :], down_w[:, c], NN).astype(BF)
-            return inner
-
-        lax.fori_loop(0, width // cols, tile, 0)
-        pl.when(i % 2 == 0)(lambda: scatter.send_across(z))
-        return carry
-
-    lax.fori_loop(0, 2 * line, work, 0)
-
-    def along(i, carry):
-        scatter.pass_on(grid.order(line - 1 - i))
-        return carry
-
-    lax.fori_loop(0, line - 1, along, 0)
-    scatter.own(result)
-    scatter.finish()
-
-
-def branch_call(hidden_all, downs, line, rows):
-    cols, width = downs[0].shape
-    parts = 2
-    return pl.pallas_call(
-        functools.partial(branch_kernel, line, parts),
-        out_shape=jax.ShapeDtypeStruct((rows, width), F32),
-        in_specs=[ANY] * 3,
-        out_specs=pl.BlockSpec(memory_space=pltpu.VMEM),
-        scratch_shapes=[
-            pltpu.VMEM((2 * cols, width), BF),
-            pltpu.VMEM(hidden_all.shape, BF),
-            pltpu.SemaphoreType.DMA((3,)),
-            *scatter_scratch(line, rows, width, parts),
-        ],
-        compiler_params=pltpu.CompilerParams(
-            collective_id=2, has_side_effects=True, vmem_limit_bytes=60 * 2**20
-        ),
-        name="branch",
-    )(hidden_all, downs[0], downs[1])
+    )(normed, tangent_all, gates[0], gates[1], ups[0], ups[1], downs[0], downs[1])
 
 
 def sums_kernel(
@@ -802,6 +735,511 @@
     )(normed, attended, grad_qkv, grad_out, gains)
 
 
+def weights_kernel(line, block, everything, send, recv, twin_send, twin_recv, staged, load_sem):
+    grid = Grid(2, line)
+    rows = block.shape[0] // 4
+    grid.greet(True, True)
+    near = grid.x * line + grid.z
+    carry_a, carry_b = grid.replica * 2, grid.replica * 2 + 1
+    other_a, other_b = (1 - grid.replica) * 2, (1 - grid.replica) * 2 + 1
+    right, left, across, mirror = range(4)
+    devices = (grid.right, grid.left, grid.across, grid.mirror)
+
+    def run(quarter):
+        return pl.ds(pl.multiple_of(quarter * rows, rows), rows)
+
+    def place(x, core, z, quarter):
+        return everything.at[(x * 2 + core) * line + z, run(quarter)]
+
+    def copy(x, z, quarter, link, first=False):
+        there = place(x, grid.core, z, quarter)
+        here = block.at[run(quarter)] if first else there
+        unit = x * line + z
+        return remote(
+            here, there, send.at[quarter, unit, link], recv.at[quarter, unit], devices[link]
+        )
+
+    def share(x, z, quarter, first=False):
+        there = place(x, grid.core, z, quarter)
+        here = block.at[run(quarter)] if first else there
+        unit = x * line + z
+        return remote(
+            here, there, twin_send.at[quarter, unit], twin_recv.at[quarter, unit], grid.twin
+        )
+
+    def arrived(x, z, quarter):
+        copy(x, z, quarter, across).wait_recv()
+        share(x, z, quarter).start()
+
+    copy(grid.x, grid.z, carry_b, across, True).start()
+    copy(grid.x, grid.z, carry_a, across, True).start()
+    copy(grid.x, grid.z, other_a, across, True).start()
+    for link, go in ((right, grid.has_right), (left, grid.has_left)):
+
+        @pl.when(go)
+        def _(link=link):
+            copy(grid.x, grid.z, carry_a, link, True).start()
+            copy(grid.x, grid.z, carry_b, link, True).start()
+
+    for quarter in range(4):
+        share(grid.x, grid.z, quarter, True).start()
+    load_pairs([(block, staged)], load_sem)
+    load_pairs([(staged, everything.at[(grid.x * 2 + grid.core) * line + grid.z])], load_sem)
+
+    arrived(1 - grid.x, grid.z, carry_b)
+    copy(1 - grid.x, grid.z, carry_b, mirror).start()
+    for link, go in ((right, grid.has_right), (left, grid.has_left)):
+        pl.when(go)(lambda link=link: copy(1 - grid.x, grid.z, carry_b, link).start())
+
+    def sides(distance):
+        return (
+            (grid.z - distance, grid.z >= distance, right, grid.has_right),
+            (grid.z + distance, grid.z + distance < line, left, grid.has_left),
+        )
+
+    def step(distance, carry):
+        for z, there, link, go in sides(distance):
+
+            @pl.when(there)
+            def _(z=z, link=link, go=go):
+                for x, quarter in (
+                    (grid.x, carry_a),
+                    (grid.x, carry_b),
+                    (1 - grid.x, carry_b),
+                ):
+                    arrived(x, z, quarter)
+                    copy(x, z, quarter, mirror).start()
+                    pl.when(go)(lambda x=x, quarter=quarter: copy(x, z, quarter, link).start())
+                copy(grid.x, z, carry_a, across).start()
+
+        for z, there, _, _ in sides(distance - 1):
+
+            @pl.when(jnp.logical_and(there, distance > 1))
+            def _(z=z):
+                arrived(grid.x, z, other_a)
+                copy(grid.x, z, other_a, across).start()
+
+        return carry
+
+    lax.fori_loop(1, line + 1, step, 0)
+
+    def last(z, carry):
+        arrived(1 - grid.x, z, carry_a)
+        arrived(1 - grid.x, z, other_a)
+        arrived(1 - grid.x, z, other_b)
+        pl.when(z != grid.z)(lambda: arrived(grid.x, z, other_b))
+        return carry
+
+    lax.fori_loop(0, line, last, 0)
+
+    def finish(z, carry):
+        away = z != grid.z
+        for x in (grid.x, 1 - grid.x):
+            for quarter in range(4):
+                share(x, z, quarter).wait()
+        for x, quarter in ((grid.x, carry_a), (grid.x, carry_b), (1 - grid.x, carry_b)):
+            to_mirror = jnp.logical_or(away, jnp.bool_(x is not grid.x))
+            pl.when(to_mirror)(
+                lambda x=x, quarter=quarter: copy(x, z, quarter, mirror).wait_send()
+            )
+            for link, go in (
+                (right, jnp.logical_and(z <= grid.z, grid.has_right)),
+                (left, jnp.logical_and(z >= grid.z, grid.has_left)),
+            ):
+                pl.when(go)(
+                    lambda x=x, quarter=quarter, link=link: copy(x, z, quarter, link).wait_send()
+                )
+        copy(grid.x, z, carry_a, across).wait_send()
+        copy(grid.x, z, other_a, across).wait_send()
+        return carry
+
+    lax.fori_loop(0, line, finish, 0)
+    copy(grid.x, grid.z, carry_b, across, True).wait_send()
+
+
+def weights_call(block, line):
+    rows, width = block.shape
+    units = 2 * line
+    return pl.pallas_call(
+        functools.partial(weights_kernel, line),
+        out_shape=jax.ShapeDtypeStruct((2 * units, rows, width), BF),
+        in_specs=[ANY],
+        out_specs=ANY,
+        scratch_shapes=[
+            pltpu.SemaphoreType.DMA((4, units, 4)), pltpu.SemaphoreType.DMA((4, units)),
+            pltpu.SemaphoreType.DMA((4, units)), pltpu.SemaphoreType.DMA((4, units)),
+            pltpu.VMEM((rows, width), BF), pltpu.SemaphoreType.DMA((1,)),
+        ],
+        compiler_params=pltpu.CompilerParams(
+            collective_id=4, has_side_effects=True, vmem_limit_bytes=32 * 2**20
+        ),
+        name="weights",
+    )(block)
+
+
+class Line:
+    def __init__(self, grid, block, everything, send, recv):
+        self.grid, self.block, self.everything = grid, block, everything
+        self.send, self.recv = send, recv
+
+    def copy(self, z, link, first=False):
+        grid = self.grid
+        there = self.everything.at[z]
+        here = self.block if first else there
+        device = (grid.right, grid.left)[link]
+        return remote(here, there, self.send.at[z, link], self.recv.at[z], device)
+
+    def send_own(self):
+        grid = self.grid
+        for link, go in ((0, grid.has_right), (1, grid.has_left)):
+            pl.when(go)(lambda link=link: self.copy(grid.z, link, True).start())
+
+    def forward(self, distance):
+        grid = self.grid
+        for z, there, link, go in (
+            (grid.z - distance, grid.z >= distance, 0, grid.has_right),
+            (grid.z + distance, grid.z + distance < grid.line, 1, grid.has_left),
+        ):
+
+            @pl.when(there)
+            def _(z=z, link=link, go=go):
+                self.copy(z, link).wait_recv()
+                pl.when(go)(lambda: self.copy(z, link).start())
+
+    def finish(self):
+        grid = self.grid
+
+        def step(z, carry):
+            for link, go in (
+                (0, jnp.logical_and(z <= grid.z, grid.has_right)),
+                (1, jnp.logical_and(z >= grid.z, grid.has_left)),
+            ):
+                pl.when(go)(lambda link=link: self.copy(z, link).wait_send())
+            return carry
+
+        lax.fori_loop(0, grid.line, step, 0)
+
+
+def halves(pair, half):
+    pair = pair.astype(F32)
+    turned = pltpu.roll(pair, HEAD_SIZE, 1)
+    lane = lax.broadcasted_iota(jnp.int32, pair.shape, 1) // HEAD_SIZE
+    first = jnp.where(half == 0, pair, turned)
+    second = jnp.where(half == 0, turned, pair)
+    both = jnp.concatenate([first, second], axis=0)
+    return jnp.where(jnp.concatenate([lane, lane], axis=0) == half, both, 0.0).astype(BF)
+
+
+def unhalves(both, half):
+    rows = both.shape[0] // 2
+    first, second = both[:rows], both[rows:]
+    lane = lax.broadcasted_iota(jnp.int32, first.shape, 1) // HEAD_SIZE
+    first = jnp.where(half == 0, first, pltpu.roll(first, HEAD_SIZE, 1))
+    second = jnp.where(half == 0, pltpu.roll(second, HEAD_SIZE, 1), second)
+    return jnp.where(lane == 0, first, second)
+
+
+def attend_kernel(
+    line, parts,
+    queries, keyed, tangent, bias, tokens, weights, gain,
+    attended, middle, normed, logs, keyed_out, tangent_all,
+    keyed_all, query_v, bias_v, token_v, weight_v, scores, probs, sums, stage, load_sem,
+    key_send, key_recv, send, recv, own_sem,
+):
+    grid = Grid(2, line)
+    rows, width = queries.shape
+    narrow = keyed.shape[1] // 2
+    total = bias.shape[1]
+    me = grid.slot(grid.x, grid.z)
+    grid.greet(False)
+    line_keys = Line(grid, keyed, keyed_all, key_send, key_recv)
+    gather = Gather(grid, tangent, tangent_all, send, recv, parts)
+    line_keys.send_own()
+    for part in range(parts):
+        gather.copy(grid.z, part, 2, True).start()
+    load_pairs(
+        [
+            (keyed, keyed_all.at[grid.z]),
+            (tangent, stage),
+            (queries, query_v),
+            (bias, bias_v),
+            (tokens, token_v),
+            (weights, weight_v),
+        ],
+        load_sem,
+    )
+    load_pairs([(stage, tangent_all.at[me])], own_sem)
+    for distance in range(line):
+        if distance:
+            line_keys.forward(distance)
+        for link, go in (
+            (0, jnp.logical_and(grid.z == distance, grid.has_right)),
+            (1, jnp.logical_and(line - 1 - grid.z == distance, grid.has_left)),
+        ):
+
+            @pl.when(go)
+            def _(link=link):
+                for part in range(parts):
+                    gather.copy(grid.z, part, link, True).start()
+
+
+    logs[...] = jnp.zeros_like(logs)
+    deep = 2 * rows
+    chunk = rows
+    pairs = width // (2 * HEAD_SIZE)
+    group = pairs // (narrow // (2 * HEAD_SIZE))
+
+    def advance(n):
+        gather.forward(n // parts + 1, n % parts)
+
+    def pair_step(i, carry):
+        c = pl.ds(pl.multiple_of(i * 128, 128), 128)
+        half = (i // (group // 2)) % 2
+        first_key = pl.multiple_of((i // group) * 128, 128)
+        keys = keyed_all[:, :, pl.ds(first_key, 128)].reshape(total, 128)
+        values = keyed_all[:, :, pl.ds(first_key + narrow, 128)].reshape(total, 128)
+        scores[...] = dot(halves(query_v[:, c], half), keys, NT)
+
+        def soft(j, inner):
+            here = pl.ds(pl.multiple_of(j * chunk, chunk), chunk)
+            there = pl.ds(pl.multiple_of((j * chunk) % rows, chunk), chunk)
+            value = scores[here, :] + bias_v[there, :]
+            top = jnp.max(value, axis=1, keepdims=True)
+            power = jnp.exp(value - top)
+            size = jnp.sum(power, axis=1, keepdims=True)
+            probs[here, :] = power.astype(BF)
+            sums[here, :] = jnp.broadcast_to(1.0 / size, (chunk, 128))
+            lane = lax.broadcasted_iota(jnp.int32, (chunk, 128), 1)
+            logs[here, :] = jnp.where(lane == i, top + jnp.log(size), logs[here, :])
+            return inner
+
+        lax.fori_loop(0, deep // chunk, soft, 0)
+        out = dot(probs[...], values, NN) * sums[...]
+        attended[:, c] = unhalves(out, half).astype(BF)
+
+        pl.when(i % 3 == 2)(lambda: advance(i // 3))
+        return carry
+
+    lax.fori_loop(0, pairs, pair_step, 0)
+    keyed_copy = pltpu.make_async_copy(keyed_all, keyed_out, load_sem.at[0])
+    keyed_copy.start()
+    advance(pairs // 3)
+    tile = 512
+
+    def out_step(j, carry):
+        c = pl.ds(pl.multiple_of(j * tile, tile), tile)
+        middle[:, c] = token_v[:, c].astype(F32) + dot(attended[...], weight_v[:, c], NN)
+        return carry
+
+    lax.fori_loop(0, width // tile, out_step, 0)
+
+    def norm_step(j, carry):
+        here = pl.ds(pl.multiple_of(j * chunk, chunk), chunk)
+        value = middle[here, :]
+        factor = lax.rsqrt(jnp.mean(value * value, axis=1, keepdims=True) + norm_eps)
+        normed[here, :] = (value * factor * gain[...]).astype(BF)
+        return carry
+
+    lax.fori_loop(0, rows // chunk, norm_step, 0)
+
+    def rest(n, carry):
+        advance(n)
+        return carry
+
+    lax.fori_loop(pairs // 3 + 1, (line - 1) * parts, rest, 0)
+    for z in range(line):
+        gather.wait_across(z)
+    keyed_copy.wait()
+    line_keys.finish()
+    gather.finish()
+
+
+def attend_call(queries, keyed, tangent, bias, tokens, weights, gain, line):
+    rows, width = queries.shape
+    both = keyed.shape[1]
+    total = bias.shape[1]
+    blocks, parts = 2 * line, 4
+    shapes = jax.ShapeDtypeStruct
+    vmem = pl.BlockSpec(memory_space=pltpu.VMEM)
+    return pl.pallas_call(
+        functools.partial(attend_kernel, line, parts),
+        out_shape=(
+            shapes((rows, width), BF), shapes((rows, width), F32), shapes((rows, width), BF),
+            shapes((2 * rows, 128), F32), shapes((line, rows, both), BF),
+            shapes((blocks, rows, width), BF),
+        ),
+        in_specs=[ANY] * 6 + [vmem],
+        out_specs=(vmem, vmem, vmem, vmem, ANY, ANY),
+        scratch_shapes=[
+            pltpu.VMEM((line, rows, both), BF),
+            pltpu.VMEM((rows, width), BF), pltpu.VMEM((rows, total), F32), pltpu.VMEM((rows, width), BF),
+            pltpu.VMEM(weights.shape, BF), pltpu.VMEM((2 * rows, total), F32), pltpu.VMEM((2 * rows, total), BF),
+            pltpu.VMEM((2 * rows, 128), F32), pltpu.VMEM((rows, width), BF), pltpu.SemaphoreType.DMA((6,)),
+            pltpu.SemaphoreType.DMA((line, 2)), pltpu.SemaphoreType.DMA((line,)),
+            pltpu.SemaphoreType.DMA((line, parts, 3)), pltpu.SemaphoreType.DMA((blocks, parts)),
+            pltpu.SemaphoreType.DMA((1,)),
+        ],
+        compiler_params=pltpu.CompilerParams(
+            collective_id=5, has_side_effects=True, vmem_limit_bytes=60 * 2**20
+        ),
+        name="attend",
+    )(queries, keyed, tangent, bias, tokens, weights, gain)
+
+
+def back_kernel(
+    line, parts, pass_at,
+    queries, keyed_all, grads, bias, logs, hidden_all, down_own, down_twin,
+    branch, grad_query, grad_keyed,
+    query_v, keyed_v, grad_v, bias_v, log_v, scores, gradients, probs, slopes, key_sum, value_sum,
+    down_w, hidden, load_sem,
+    partial, from_across, from_line, total, across_send, across_recv, line_send, line_recv,
+    key_partial, key_line, key_total, key_send, key_recv,
+):
+    grid = Grid(2, line)
+    cols, width = down_own.shape
+    rows = partial.shape[1]
+    narrow = keyed_all.shape[2] // 2
+    length = bias.shape[1]
+    grid.greet(False)
+    load_pairs(
+        [
+            (down_own, down_w.at[pl.ds(0, cols)]),
+            (down_twin, down_w.at[pl.ds(cols, cols)]),
+            (hidden_all, hidden),
+            (queries, query_v),
+            (keyed_all, keyed_v),
+            (grads, grad_v),
+            (bias, bias_v),
+            (logs, log_v),
+        ],
+        load_sem,
+    )
+    scatter = Scatter(
+        grid, partial, from_across, from_line, total,
+        (across_send, across_recv, line_send, line_recv), parts,
+    )
+    keyed_scatter = Scatter(
+        grid, key_partial, None, key_line, key_total, (None, None, key_send, key_recv), parts
+    )
+
+    def work(i, carry):
+        z = grid.order(line - 1 - i % line)
+        slot = grid.slot(jnp.where(i < line, 1 - grid.x, grid.x), z)
+        spot = pl.ds(pl.multiple_of(slot * rows, rows), rows)
+
+        def tile(j, inner):
+            c = pl.ds(pl.multiple_of(j * cols, cols), cols)
+            partial[slot, :, c] = dot(hidden[spot, :], down_w[:, c], NN).astype(BF)
+            return inner
+
+        lax.fori_loop(0, width // cols, tile, 0)
+        pl.when(i < line)(lambda: scatter.send_across(z))
+        return carry
+
+    lax.fori_loop(0, 2 * line, work, 0)
+    deep = 2 * rows
+    chunk = rows // 2
+    pairs = width // (2 * HEAD_SIZE)
+    group = pairs // (narrow // (2 * HEAD_SIZE))
+
+    def pair_step(i, carry):
+        c = pl.ds(pl.multiple_of(i * 128, 128), 128)
+        half = (i // (group // 2)) % 2
+        key_cols = pl.ds(pl.multiple_of((i // group) * 128, 128), 128)
+        value_cols = pl.ds(pl.multiple_of((i // group) * 128 + narrow, 128), 128)
+        keys = keyed_v[:, :, key_cols].reshape(length, 128)
+        values = keyed_v[:, :, value_cols].reshape(length, 128)
+        query = halves(query_v[:, c], half)
+        grad = halves(grad_v[:, c], half)
+        scores[...] = dot(query, keys, NT)
+        gradients[...] = dot(grad, values, NT)
+
+        def soft(j, inner):
+            here = pl.ds(pl.multiple_of(j * chunk, chunk), chunk)
+            there = pl.ds(pl.multiple_of((j * chunk) % rows, chunk), chunk)
+            lane = lax.broadcasted_iota(jnp.int32, (chunk, 128), 1)
+            log = jnp.sum(jnp.where(lane == i, log_v[here, :], 0.0), axis=1, keepdims=True)
+            prob = jnp.exp(scores[here, :] + bias_v[there, :] - log)
+            slope = gradients[here, :]
+            delta = jnp.sum(prob * slope, axis=1, keepdims=True)
+            probs[here, :] = prob.astype(BF)
+            slopes[here, :] = (prob * (slope - delta)).astype(BF)
+            return inner
+
+        lax.fori_loop(0, deep // chunk, soft, 0)
+        back = dot(slopes[...], keys, NN) * HEAD_SIZE ** (-0.5)
+        grad_query[:, c] = unhalves(back, half)
+        key_part = dot(slopes[...], query, TN)
+        value_part = dot(probs[...], grad, TN)
+
+        @pl.when(i % group == 0)
+        def _():
+            key_sum[...] = key_part
+            value_sum[...] = value_part
+
+        @pl.when(i % group != 0)
+        def _():
+            key_sum[...] += key_part
+            value_sum[...] += value_part
+
+        @pl.when(i % group == group - 1)
+        def _():
+            key_partial[:, :, key_cols] = key_sum[...].astype(BF).reshape(line, rows, 128)
+            key_partial[:, :, value_cols] = value_sum[...].astype(BF).reshape(line, rows, 128)
+
+        for k, when in zip(range(line - 1, 0, -1), pass_at):
+            pl.when(i == when)(lambda k=k: scatter.pass_on(grid.order(k)))
+        return carry
+
+    lax.fori_loop(0, pairs, pair_step, 0)
+
+    def along(i, carry):
+        keyed_scatter.pass_on(grid.order(line - 1 - i))
+        return carry
+
+    lax.fori_loop(0, line - 1, along, 0)
+    for k in range(line - 1 - len(pass_at), 0, -1):
+        scatter.pass_on(grid.order(k))
+    scatter.own(branch)
+    keyed_scatter.own(grad_keyed)
+    scatter.finish()
+    keyed_scatter.finish()
+
+
+def back_call(queries, keyed_all, grads, bias, logs, hidden_all, downs, line):
+    rows, width = queries.shape
+    both = keyed_all.shape[2]
+    cols, length = downs[0].shape[0], bias.shape[1]
+    parts = 2
+    shapes = jax.ShapeDtypeStruct
+    vmem = pl.BlockSpec(memory_space=pltpu.VMEM)
+    return pl.pallas_call(
+        functools.partial(back_kernel, line, parts, (4, 9, 15)),
+        out_shape=(
+            shapes((rows, width), F32), shapes((rows, width), F32), shapes((rows, both), F32),
+        ),
+        in_specs=[ANY] * 8,
+        out_specs=(vmem,) * 3,
+        scratch_shapes=[
+            pltpu.VMEM((rows, width), BF), pltpu.VMEM(keyed_all.shape, BF), pltpu.VMEM((rows, width), BF),
+            pltpu.VMEM((rows, length), F32), pltpu.VMEM(logs.shape, F32),
+            pltpu.VMEM((2 * rows, length), F32), pltpu.VMEM((2 * rows, length), F32),
+            pltpu.VMEM((2 * rows, length), BF), pltpu.VMEM((2 * rows, length), BF),
+            pltpu.VMEM((length, 128), F32), pltpu.VMEM((length, 128), F32),
+            pltpu.VMEM((2 * cols, width), BF), pltpu.VMEM(hidden_all.shape, BF),
+            pltpu.SemaphoreType.DMA((8,)),
+            *scatter_scratch(line, rows, width, parts),
+            pltpu.VMEM((line, rows, both), BF), pltpu.VMEM((2 * line - 2, rows, both), BF),
+            pltpu.VMEM((rows // parts, both), F32),
+            pltpu.SemaphoreType.DMA((line, parts)), pltpu.SemaphoreType.DMA((2 * line - 2, parts)),
+        ],
+        compiler_params=pltpu.CompilerParams(
+            collective_id=6, has_side_effects=True, vmem_limit_bytes=62 * 2**20
+        ),
+        name="back",
+    )(queries, keyed_all, grads, bias, logs, hidden_all, downs[0], downs[1])
+
+
 def body(
     tokens,
     places,
@@ -815,7 +1253,6 @@
     w_gate,
     w_up,
     w_down,
-    kernels,
 ):
     sequence_total, segment_length, width = tokens.shape
     total_length = places.shape[1]
@@ -878,39 +1315,19 @@
     normed_mlp = (unit_two * gain_second).astype(jnp.bfloat16)
     tangent = cotangent.reshape(total_rows, width)
     tangent_f = tangent.astype(jnp.float32)
-    if kernels:
-        line = lax.axis_size("context")
-        swap = [(i, i ^ 1) for i in range(lax.axis_size("fsdp"))]
-        gates, ups, downs = (
-            (w, lax.ppermute(w, "fsdp", swap)) for w in (w_gate, w_up, w_down)
-        )
-        grad_normed, _, _, hidden_all, *sums = feed_call(
-            normed_mlp, tangent, gates, ups, downs, line
-        )[:7]
-        branch = branch_call(hidden_all, downs, line, total_rows)
-        flip = [(i, 1 - i) for i in range(2)]
-        grad_w_gate, grad_w_up, grad_w_down = (
-            g.astype(jnp.float32) + lax.ppermute(g, "replica", flip).astype(jnp.float32)
-            for g in sums
-        )
-    else:
-        group = ("fsdp", "context")
-        normed_all = lax.all_gather(normed_mlp, group, axis=0, tiled=True)
-        tangent_all = lax.all_gather(tangent, group, axis=0, tiled=True)
-        branch_part, kept_values = feed_forward(normed_all, w_gate, w_up, w_down)
-        grad_part, grad_w_gate, grad_w_up, grad_w_down = feed_back(
-            normed_all, tangent_all, w_gate, w_up, w_down, kept_values
-        )
-        grad_normed = lax.psum_scatter(
-            grad_part.astype(jnp.bfloat16), group, scatter_dimension=0, tiled=True
-        ).astype(jnp.float32)
-        branch = lax.psum_scatter(
-            branch_part.astype(jnp.bfloat16), group, scatter_dimension=0, tiled=True
-        ).astype(jnp.float32)
-        grad_w_gate, grad_w_up, grad_w_down = (
-            lax.psum(g.astype(jnp.bfloat16), "replica").astype(jnp.float32)
-            for g in (grad_w_gate, grad_w_up, grad_w_down)
-        )
+    group = ("fsdp", "context")
+    normed_all = lax.all_gather(normed_mlp, group, axis=0, tiled=True)
+    tangent_all = lax.all_gather(tangent, group, axis=0, tiled=True)
+    branch_part, kept_values = feed_forward(normed_all, w_gate, w_up, w_down)
+    grad_part, grad_w_gate, grad_w_up, grad_w_down = feed_back(
+        normed_all, tangent_all, w_gate, w_up, w_down, kept_values
+    )
+    grad_normed = lax.psum_scatter(
+        grad_part.astype(jnp.bfloat16), group, scatter_dimension=0, tiled=True
+    ).astype(jnp.float32)
+    branch = lax.psum_scatter(
+        branch_part.astype(jnp.bfloat16), group, scatter_dimension=0, tiled=True
+    ).astype(jnp.float32)
     outcome = middle + branch
     scaled_two = grad_normed * gain_second
     term_gain_two = jnp.sum(grad_normed * unit_two, axis=0)
@@ -918,6 +1335,7 @@
         scaled_two - unit_two * jnp.mean(scaled_two * unit_two, axis=-1, keepdims=True)
     )
     grad_branch = grad_middle.astype(jnp.bfloat16)
+    term_out = times_t(attended, grad_branch)
     grad_attended = times_nt(grad_branch, out_w).astype(jnp.bfloat16)
     head_grad = query_head_rows(grad_attended, sequence_total, segment_length)
     grad_q, grad_k, grad_v = lax.map(
@@ -962,47 +1380,33 @@
         + times_nt(grad_key, key_weight_local)
         + times_nt(value_gradient, value_w)
     )
+    term_query = times_t(normed_tokens, grad_query)
+    term_key = times_t(normed_tokens, grad_key)
+    term_value = times_t(normed_tokens, value_gradient)
     scaled_one = grad_normed_one * gain_first
     term_gain_one = jnp.sum(grad_normed_one * unit_one, axis=0)
     grad_inputs = grad_middle + factor_one * (
         scaled_one - unit_one * jnp.mean(scaled_one * unit_one, axis=-1, keepdims=True)
     )
-    if kernels:
-        gains = jnp.stack([term_gain_one, term_gain_two], axis=1).astype(jnp.bfloat16)
-        gains = jnp.pad(gains, ((0, 0), (0, 126)))
-        grad_qkv = jnp.concatenate([grad_query, grad_key, value_gradient], axis=1)
-        packed = sums_call(
-            normed_tokens, attended, grad_qkv, grad_branch, gains, line, w_query.shape[0]
-        )
-        ends, start = [], 0
-        for size in (width, grad_key.shape[1], grad_key.shape[1], width, 1, 1):
-            ends.append(packed[:, start : start + size])
-            start += size
-        summed = (*ends[:4], grad_w_gate, grad_w_up, grad_w_down, ends[4][:, 0], ends[5][:, 0])
-    else:
-        term_out = times_t(attended, grad_branch)
-        term_query = times_t(normed_tokens, grad_query)
-        term_key = times_t(normed_tokens, grad_key)
-        term_value = times_t(normed_tokens, value_gradient)
-        share_query, share_key, share_value, share_out, share_gain_one, share_gain_two = (
-            lax.psum_scatter(term_query.astype(jnp.bfloat16), ("fsdp", "context"), scatter_dimension=0, tiled=True),
-            lax.psum_scatter(term_key.astype(jnp.bfloat16), ("fsdp", "context"), scatter_dimension=0, tiled=True),
-            lax.psum_scatter(term_value.astype(jnp.bfloat16), ("fsdp", "context"), scatter_dimension=0, tiled=True),
-            lax.psum_scatter(term_out.astype(jnp.bfloat16), ("fsdp", "context"), scatter_dimension=0, tiled=True),
-            lax.psum_scatter(term_gain_one, ("fsdp", "context"), scatter_dimension=0, tiled=True),
-            lax.psum_scatter(term_gain_two, ("fsdp", "context"), scatter_dimension=0, tiled=True),
-        )
-        summed = (
-            lax.psum(share_query.astype(jnp.bfloat16), "replica").astype(jnp.float32),
-            lax.psum(share_key.astype(jnp.bfloat16), "replica").astype(jnp.float32),
-            lax.psum(share_value.astype(jnp.bfloat16), "replica").astype(jnp.float32),
-            lax.psum(share_out.astype(jnp.bfloat16), "replica").astype(jnp.float32),
-            grad_w_gate,
-            grad_w_up,
-            grad_w_down,
-            lax.psum(share_gain_one.astype(jnp.bfloat16), "replica").astype(jnp.float32),
-            lax.psum(share_gain_two.astype(jnp.bfloat16), "replica").astype(jnp.float32),
-        )
+    share_query, share_key, share_value, share_out, share_gain_one, share_gain_two = (
+        lax.psum_scatter(term_query.astype(jnp.bfloat16), ("fsdp", "context"), scatter_dimension=0, tiled=True),
+        lax.psum_scatter(term_key.astype(jnp.bfloat16), ("fsdp", "context"), scatter_dimension=0, tiled=True),
+        lax.psum_scatter(term_value.astype(jnp.bfloat16), ("fsdp", "context"), scatter_dimension=0, tiled=True),
+        lax.psum_scatter(term_out.astype(jnp.bfloat16), ("fsdp", "context"), scatter_dimension=0, tiled=True),
+        lax.psum_scatter(term_gain_one, ("fsdp", "context"), scatter_dimension=0, tiled=True),
+        lax.psum_scatter(term_gain_two, ("fsdp", "context"), scatter_dimension=0, tiled=True),
+    )
+    summed = (
+        lax.psum(share_query.astype(jnp.bfloat16), "replica").astype(jnp.float32),
+        lax.psum(share_key.astype(jnp.bfloat16), "replica").astype(jnp.float32),
+        lax.psum(share_value.astype(jnp.bfloat16), "replica").astype(jnp.float32),
+        lax.psum(share_out.astype(jnp.bfloat16), "replica").astype(jnp.float32),
+        lax.psum(grad_w_gate.astype(jnp.bfloat16), "replica").astype(jnp.float32),
+        lax.psum(grad_w_up.astype(jnp.bfloat16), "replica").astype(jnp.float32),
+        lax.psum(grad_w_down.astype(jnp.bfloat16), "replica").astype(jnp.float32),
+        lax.psum(share_gain_one.astype(jnp.bfloat16), "replica").astype(jnp.float32),
+        lax.psum(share_gain_two.astype(jnp.bfloat16), "replica").astype(jnp.float32),
+    )
     out = outcome.astype(jnp.bfloat16).reshape(sequence_total, segment_length, width)
     grad_tokens = grad_inputs.astype(jnp.bfloat16).reshape(sequence_total, segment_length, width)
     return (
@@ -1020,6 +1424,113 @@
     )
 
 
+def kernel_body(
+    tokens,
+    places,
+    cotangent,
+    gain_attn,
+    gain_mlp,
+    w_query,
+    key_projection,
+    value_projection,
+    w_out,
+    w_gate,
+    w_up,
+    w_down,
+):
+    bf16, f32 = jnp.bfloat16, jnp.float32
+    sequence_total, segment_length, width = tokens.shape
+    total_length = places.shape[1]
+    line = lax.axis_size("context")
+    narrow = key_projection.shape[1]
+    run = w_query.shape[0]
+    flip = [(0, 1), (1, 0)]
+    swap = [(i, i ^ 1) for i in range(lax.axis_size("fsdp"))]
+    gates, ups, downs = ((w, lax.ppermute(w, "fsdp", swap)) for w in (w_gate, w_up, w_down))
+    position = lax.axis_index("context")
+    local_positions = lax.dynamic_slice_in_dim(places, position * segment_length, segment_length, 1)
+    rotary_angles = local_positions.reshape(segment_length).astype(f32)[:, None] * frequencies(
+        HEAD_SIZE // 2
+    )
+    gain_columns = jnp.pad(jnp.stack([gain_attn, gain_mlp], axis=1), ((0, 0), (0, 126)))
+    block = jnp.concatenate([w_query, key_projection, value_projection, gain_columns, w_out], axis=1)
+    weights = weights_call(block, line).reshape(width, block.shape[1])
+    mid = width + 2 * narrow
+    in_w, out_w = weights[:, : mid + 128], weights[:, mid + 128 :]
+    gain_first = weights[:, mid].astype(f32)
+    gain_second = weights[:, mid + 1].astype(f32)
+    inputs_f = tokens.astype(f32).reshape(segment_length, width)
+    factor_one = lax.rsqrt(jnp.mean(inputs_f * inputs_f, axis=-1, keepdims=True) + norm_eps)
+    unit_one = inputs_f * factor_one
+    normed_tokens = (unit_one * gain_first).astype(bf16)
+    projected = jnp.dot(normed_tokens, in_w, preferred_element_type=f32)
+
+    def heads(first, size):
+        return projected[:, first : first + size].reshape(segment_length, size // HEAD_SIZE, HEAD_SIZE)
+
+    query_rows = apply_rotary(heads(0, width), rotary_angles).astype(bf16)
+    scaled_query = (query_rows * HEAD_SIZE ** (-0.5)).astype(bf16).reshape(segment_length, width)
+    key_rows = apply_rotary(heads(width, narrow), rotary_angles).astype(bf16)
+    value_rows = projected[:, width + narrow : mid].astype(bf16)
+    keyed = jnp.concatenate([key_rows.reshape(segment_length, narrow), value_rows], axis=1)
+    allowed = places.reshape(1, total_length) <= local_positions.reshape(segment_length, 1)
+    bias = jnp.where(allowed, 0.0, -1e30).astype(f32)
+    tangent = cotangent.reshape(segment_length, width)
+    tangent_f = tangent.astype(f32)
+    attended, middle, normed_mlp, logs, keyed_all, tangent_all = attend_call(
+        scaled_query, keyed, tangent, bias, tokens.reshape(segment_length, width), out_w,
+        gain_second.reshape(1, width), line,
+    )
+    grad_normed, _, hidden_all, *sums = feed_call(normed_mlp, tangent_all, gates, ups, downs, line)[:6]
+    grad_w_gate, grad_w_up, grad_w_down = (
+        g.astype(f32) + lax.ppermute(g, "replica", flip).astype(f32) for g in sums
+    )
+    factor_two = lax.rsqrt(jnp.mean(middle * middle, axis=-1, keepdims=True) + norm_eps)
+    unit_two = middle * factor_two
+    scaled_two = grad_normed * gain_second
+    term_gain_two = jnp.sum(grad_normed * unit_two, axis=0)
+    grad_middle = tangent_f + factor_two * (
+        scaled_two - unit_two * jnp.mean(scaled_two * unit_two, axis=-1, keepdims=True)
+    )
+    grad_branch = grad_middle.astype(bf16)
+    grad_attended = times_nt(grad_branch, out_w).astype(bf16)
+    branch, grad_q, grad_keyed = back_call(
+        scaled_query, keyed_all, grad_attended, bias, logs, hidden_all, downs, line
+    )
+    outcome = middle + branch
+    grad_query = inverse_rotary(
+        grad_q.reshape(segment_length, QUERY_HEADS, HEAD_SIZE), rotary_angles
+    ).reshape(segment_length, width)
+    grad_key = inverse_rotary(
+        grad_keyed[:, :narrow].reshape(segment_length, KEY_VALUE_HEADS, HEAD_SIZE), rotary_angles
+    ).reshape(segment_length, narrow)
+    value_gradient = grad_keyed[:, narrow:]
+    grad_qkv = jnp.concatenate([grad_query, grad_key, value_gradient], axis=1).astype(bf16)
+    grad_normed_one = times_nt(grad_qkv, weights[:, :mid])
+    scaled_one = grad_normed_one * gain_first
+    term_gain_one = jnp.sum(grad_normed_one * unit_one, axis=0)
+    grad_inputs = grad_middle + factor_one * (
+        scaled_one - unit_one * jnp.mean(scaled_one * unit_one, axis=-1, keepdims=True)
+    )
+    gains = jnp.stack([term_gain_one, term_gain_two], axis=1).astype(bf16)
+    gains = jnp.pad(gains, ((0, 0), (0, 126)))
+    packed = sums_call(normed_tokens, attended, grad_qkv, grad_branch, gains, line, run)
+    ends, start = [], 0
+    for size in (width, narrow, narrow, width, 1, 1):
+        ends.append(packed[:, start : start + size])
+        start += size
+    return (
+        outcome.astype(bf16).reshape(tokens.shape),
+        grad_inputs.astype(bf16).reshape(tokens.shape),
+        *ends[:4],
+        grad_w_gate,
+        grad_w_up,
+        grad_w_down,
+        ends[4][:, 0],
+        ends[5][:, 0],
+    )
+
+
 def solution(mesh):
     placed = (
         P(("replica", "fsdp"), "context", None),
@@ -1037,7 +1548,7 @@
     )
     kernels = (mesh.shape["replica"], mesh.shape["fsdp"], mesh.shape["context"]) == (2, 4, 4)
     return jax.shard_map(
-        functools.partial(body, kernels=kernels),
+        kernel_body if kernels else body,
         mesh=mesh,
         in_specs=placed,
         out_specs=(

time: 1080 us -> 837 us (0.78)
  matrix products: 203 us -> 24.3 us
  Pallas kernels: 552 us -> 723 us
  waiting for transfers between devices: 143 us -> 0.02 us
  blocking collectives: 64.2 us -> 0 us
  between operations: 15 us -> 1.61 us
    pallas_call x1 -> x3, Pallas kernels: 102 us -> 367 us  [the longest x1 141 us: back_call(): pl.pallas_call(functools.partial(back_kernel, line, parts, (4, 9, 15)), o...]
    all_gather x6 -> x0, waiting for transfers between devices: 141 us -> none  [the longest x1 66.5 us: body(): lax.all_gather(w_query, ('fsdp', 'context'), axis=0, tiled=True)]
    dot_general x44 -> x1, matrix products: 110 us -> 7.58 us  [kernel_body(): projected = jnp.dot(normed_tokens, in_w, preferred_element_type=f32)]
    pallas_call x1, Pallas kernels: 306 us -> 213 us  [feed_call(): pl.pallas_call(functools.partial(feed_kernel, line, parts, tile), out_sha...]
    sub x16 -> x0, matrix products: 70.9 us -> none  [softmax_weights(): return jax.nn.softmax(scores, axis=-1)]
    all_gather x2 -> x0, blocking collectives: 64.2 us -> none  [the longest x1 33.9 us: body(): lax.all_gather(gain_attn, ('fsdp', 'context'), axis=0, tiled=True)]
    slice x3 -> x13, local copies, waits for them, and re-layouts: 6.7 us -> 23.4 us  [the longest x1 8.4 us: kernel_body(): in_w, out_w = (weights[:, :mid + 128], weights[:, mid + 128:])]
    dot_general x2 -> x0, local copies, waits for them, and re-layouts: 15.4 us -> none  [the longest x1 12.4 us: body(): jnp.dot(normed_tokens, query_w, preferred_element_type=jnp.float32)]
  transfers between devices with their start and end apart: 14 -> 6, of which waited for: 5 -> 0; matrix products, arithmetic and copies ran while one was open for 14% -> 9% of each run, Pallas kernels for 23% -> 45%
where the time goes in v4:
time: 837 us; the launch traced here: 829 us
  Pallas kernels  723 us (86%)
  local copies, waits for them, and re-layouts  41.7 us (5%)
  other arithmetic  33.1 us (4%)
  matrix products  24.3 us (3%)
    pallas_call x1, Pallas kernels, feed_call(): pl.pallas_call(functools.partial(feed_kernel, line, parts, tile), out_sha...  213 us
    pallas_call x1, Pallas kernels, sums_call(): pl.pallas_call(functools.partial(sums_kernel, line, parts), out_shape=jax...  143 us
    pallas_call x1, Pallas kernels, back_call(): pl.pallas_call(functools.partial(back_kernel, line, parts, (4, 9, 15)), o...  141 us
    pallas_call x1, Pallas kernels, attend_call(): pl.pallas_call(functools.partial(attend_kernel, line, parts), out_shape=(...  128 us
    pallas_call x1, Pallas kernels, weights_call(): pl.pallas_call(functools.partial(weights_kernel, line), out_shape=jax.Sha...  98.3 us
  transfers between devices with their start and end apart: 6, of which 0 were waited for; matrix products, arithmetic and copies ran while one was open for 9% of the time, Pallas kernels for 45%

profile of v4, /device:TPU:0, one launch (start us, length us, event | category | flops | bytes accessed | tf_op | source)
XLA Modules:
  0.0 828.6 jit_solution(7520505155511624854)
XLA Ops:
  0.6 0.5 collective-permute-start.2
  1.2 0.1 collective-permute-start
  1.2 0.4 collective-permute-start.1
  1.7 1.1 constant_dynamic-update-slice_fusion.3
  2.8 0.7 pad_maximum_fusion.6
  3.4 0.1 copy.38
  3.6 0.9 constant_dynamic-update-slice_fusion.2
  4.5 0.9 constant_dynamic-update-slice_fusion.1
  5.4 1.1 constant_dynamic-update-slice_fusion.block
  6.5 0.0 copy-start.5
  6.5 98.3 %weights.1 = bf16[16,128,5248]{2,1,0:T(8,128)(2,1)S(1)} custom-call(bf16[128,5248]{1,0:T(8,128)(2,1)S(1)} %constant_dynamic-update-slice_fusion.block), custom_call_target="tpu_custom_call" | custom-call | tf_op jit(solution)/shard_map/weights/pallas_call | solution.py:863
  104.8 7.1 copy-done
  112.0 1.0 convert_reduce_fusion
  113.0 0.3 fusion.15
  113.3 0.3 fusion.8.normed
  113.6 0.0 copy-start.9
  113.6 7.6 fusion
  121.2 0.9 slice.103
  122.2 0.9 copy-done.8
  123.1 8.4 %slice.107.weights = bf16[2048,2048]{1,0:T(8,128)(2,1)} slice(bf16[2048,5248]{1,0:T(8,128)(2,1)} %bitcast.34), slice={[0:2048], [3200:5248]} | slice | bytes 16777216 | tf_op jit(solution)/shard_map/slice | solution.py:1459
  131.5 1.4 copy.40
  132.9 0.2 multiply_cosine_fusion
  133.1 0.0 copy-start.14
  133.2 0.1 subtract_convert_fusion.3
  133.3 0.1 copy.41
  133.4 1.8 copy.39
  135.2 1.9 subtract_convert_fusion.1
  137.1 0.2 maximum_multiply_fusion
  137.4 1.4 copy.42.queries
  138.8 0.9 pad_maximum_fusion.2.keyed
  139.7 1.1 compare_select_fusion.bias
  140.8 127.6 %attend.1 = (bf16[256,2048]{1,0:T(8,128)(2,1)}, f32[256,2048]{1,0:T(8,128)}, bf16[256,2048]{1,0:T(8,128)(2,1)}, f32[512,128]{1,0:T(8,128)}, bf16[4,256,1024]{2,1...) custom-call(bf16[256,2048]{1,0:T(8,128)(2,1)} %copy.42.queries, bf16[256,1024]{1,0:T(8,128)(2,1)} %pad_maximum_fusion.2.keyed, ...), custom_call_target="tpu_custom_call" | custom-call | tf_op jit(solution)/shard_map/attend/pallas_call | solution.py:1064
  268.3 1.8 multiply_reduce_fusion.2
  270.2 212.9 %feed.1 = (f32[256,2048]{1,0:T(8,128)}, bf16[8,256,2048]{2,1,0:T(8,128)(2,1)}, bf16[2048,1024]{1,0:T(8,128)(2,1)}, bf16[2048,512]{1,0:T(8,128)(2,1)}, bf16[2048,...) custom-call(bf16[256,2048]{1,0:T(8,128)(2,1)} %get-tuple-element.27., ...), custom_call_target="tpu_custom_call" | custom-call | tf_op jit(solution)/shard_map/feed/pallas_call | solution.py:597
  483.1 2.9 multiply_reduce_fusion
  486.1 0.5 copy-done.3
  486.6 1.9 fusion.19.grad_out
  488.5 7.1 convolution_convert_fusion.grads
  495.6 141.4 %back.1 = (f32[256,2048]{1,0:T(8,128)}, f32[256,2048]{1,0:T(8,128)}, f32[256,1024]{1,0:T(8,128)}) custom-call(bf16[256,2048]{1,0:T(8,128)(2,1)} %copy.42.queries, bf16[4,256,1024]{2,1,0:T(8,128)(2,1)} %get-tuple-element.26.keyed_all, bf16[256,2048]{1,0:T(8,128)(2,1)} %convolution_convert_fusion.grads, f32[256,1024]{1,0:T(8,128)} %compare_select_fusion.bias, ...), custom_call_target="tpu_custom_call" | custom-call | tf_op jit(solution)/shard_map/back/pallas_call | solution.py:1216
  636.9 1.9 slice.87
  638.8 1.1 slice.143
  639.9 1.7 collective-permute-start.5
  641.6 0.4 collective-permute-start.4
  642.0 1.6 collective-permute-start.3
  643.6 1.9 copy.44
  645.6 0.3 add_convert_fusion.1
  645.9 0.1 pad_maximum_fusion.1
  646.0 0.0 copy-start.6
  646.0 0.6 copy.46
  646.7 1.2 copy.45
  647.9 0.1 add_convert_fusion.3
  648.0 0.1 copy.47
  648.2 9.6 %fusion.14 = (bf16[2048]{0:T(1024)(128)(2,1)S(1)}, f32[256]{0:T(256)S(1)}, f32[256,2048]{1,0:T(8,128)}) fusion(f32[256]{0:T(256)S(1)} %add_rsqrt_fusion.1, bf16[1,256,2048]{2,1,0:T(8,128)(2,1)S(1)} %copy-done.6, f32[2048]{0:T(1024)S(1)} %get-tuple-element.40, bf16[2048,5248]{1,0:T(8,128)(2,1)} %bitcast.36, bf16[256,512]{1,0:T(8,128)(2,1)S(1)} %slice.143, ...), kind=kOutput, calls=%fused_computation.20 | convolution fusion | flops 3229611776 | bytes 17315840 | tf_op jit(solution)/shard_map/dot_general | solution.py:54
  657.9 0.3 copy.48
  658.2 0.9 pad.9.gains
  659.1 1.3 pad_maximum_fusion.grad_qkv
  660.4 142.9 %sums.1 = f32[128,5248]{1,0:T(8,128)} custom-call(bf16[256,2048]{1,0:T(8,128)(2,1)} %copy-done.9, bf16[256,2048]{1,0:T(8,128)(2,1)} %get-tuple-element.35.attended, bf16[256,3072]{1,0:T(8,128)(2,1)} %pad_maximum_fusion.grad_qkv, bf16[256,2048]{1,0:T(8,128)(2,1)} %copy-done.10, bf16[2048,128]{1,0:T(8,128)(2,1)} %pad.9.gains), custom_call_target="tpu_custom_call" | custom-call | tf_op jit(solution)/shard_map/sums/pallas_call | solution.py:717
  803.3 1.9 fusion.21
  805.2 3.2 fusion.20
  808.4 1.6 slice_reduce_fusion
  810.0 4.9 fusion.17
  815.0 4.5 convert_add_fusion
  819.5 4.4 convert_add_fusion.1
  823.8 4.2 convert_add_fusion.2
  (55 shorter events, 0.3 us)
Async XLA Ops:
  0.6 269.5 %collective-permute-start.2 = (bf16[512,2048]{1,0:T(8,128)(2,1)}, bf16[512,2048]{1,0:T(8,128)(2,1)}, u32[]{:S(2)}, u32[]{:S(2)}) collective-permute-start(bf16[512,2048]{1,0:T(8,128)(2,1)} %down_own.3), channel_id=1, source_target_pairs={{0,4},{4,0},{8,12},{12,8},{1,5},{5,1},{9,13},{13,9},{2,6},{6,2},{1... | collective-permute-start | bytes 6291464 | tf_op jit(solution)/shard_map/ppermute | solution.py:1449
  1.2 269.0 %collective-permute-start = (bf16[2048,512]{1,0:T(8,128)(2,1)}, bf16[2048,512]{1,0:T(8,128)(2,1)}, u32[]{:S(2)}, u32[]{:S(2)}) collective-permute-start(bf16[2048,512]{1,0:T(8,128)(2,1)} %gate_own.1), channel_id=1, source_target_pairs={{0,4},{4,0},{8,12},{12,8},{1,5},{5,1},{9,13},{13,9},{2,6},{6,2},{1... | collective-permute-start | bytes 6291464 | tf_op jit(solution)/shard_map/ppermute | solution.py:1449
  1.2 268.9 %collective-permute-start.1 = (bf16[2048,512]{1,0:T(8,128)(2,1)}, bf16[2048,512]{1,0:T(8,128)(2,1)}, u32[]{:S(2)}, u32[]{:S(2)}) collective-permute-start(bf16[2048,512]{1,0:T(8,128)(2,1)} %up_own.1), channel_id=1, source_target_pairs={{0,4},{4,0},{8,12},{12,8},{1,5},{5,1},{9,13},{13,9},{2,6},{6,2},{1... | collective-permute-start | bytes 6291464 | tf_op jit(solution)/shard_map/ppermute | solution.py:1449
  6.5 106.4 %copy-start.5 = (bf16[1,256,2048]{2,1,0:T(8,128)(2,1)S(1)}, bf16[1,256,2048]{2,1,0:T(8,128)(2,1)}, u32[]{:S(2)}) copy-start(bf16[1,256,2048]{2,1,0:T(8,128)(2,1)} %param.12) | copy-start | bytes 3145732
  104.8 7.1 copy-start
  113.6 7.6 copy-start.9
  121.2 1.9 copy-start.8
  123.1 9.8 %copy-start.19 = (s32[1,1024]{1,0:T(1,128)S(1)}, s32[1,1024]{1,0:T(1,128)}, u32[]{:S(2)}) copy-start(s32[1,1024]{1,0:T(1,128)} %param.13) | copy-start | bytes 12292
  131.5 1.9 slice-start
  133.1 2.1 copy-start.14
  133.1 2.1 copy-start.16
  270.2 212.9 %copy-start.18 = (f32[2048]{0:T(1024)S(1)}, f32[2048]{0:T(1024)}, u32[]{:S(2)}) copy-start(f32[2048]{0:T(1024)} %get-tuple-element.39) | copy-start | bytes 24580
  483.1 3.0 copy-start.1
  483.1 3.5 copy-start.3
  488.5 7.1 copy-start.10
  639.9 175.1 %collective-permute-start.5 = (bf16[512,2048]{1,0:T(8,128)(2,1)}, bf16[512,2048]{1,0:T(8,128)(2,1)}, u32[]{:S(2)}, u32[]{:S(2)}) collective-permute-start(bf16[512,2048]{1,0:T(8,128)(2,1)} %get-tuple-element.38), channel_id=1, source_target_pairs={{0,16},{16,0},{1,17},{17,1},{2,18},{18,2},{3,19},{19,3},{4,20},{20... | collective-permute-start | bytes 6291464 | tf_op jit(solution)/shard_map/ppermute | solution.py:1486
  641.6 177.9 %collective-permute-start.4 = (bf16[2048,512]{1,0:T(8,128)(2,1)}, bf16[2048,512]{1,0:T(8,128)(2,1)}, u32[]{:S(2)}, u32[]{:S(2)}) collective-permute-start(bf16[2048,512]{1,0:T(8,128)(2,1)} %get-tuple-element.37), channel_id=1, source_target_pairs={{0,16},{16,0},{1,17},{17,1},{2,18},{18,2},{3,19},{19,3},{4,20},{20... | collective-permute-start | bytes 6291464 | tf_op jit(solution)/shard_map/ppermute | solution.py:1486
  642.0 181.9 %collective-permute-start.3 = (bf16[2048,512]{1,0:T(8,128)(2,1)}, bf16[2048,512]{1,0:T(8,128)(2,1)}, u32[]{:S(2)}, u32[]{:S(2)}) collective-permute-start(bf16[2048,512]{1,0:T(8,128)(2,1)} %get-tuple-element.36), channel_id=1, source_target_pairs={{0,16},{16,0},{1,17},{17,1},{2,18},{18,2},{3,19},{19,3},{4,20},{20... | collective-permute-start | bytes 6291464 | tf_op jit(solution)/shard_map/ppermute | solution.py:1486
  643.6 1.9 copy-start.15
  643.6 1.9 copy-start.17
  646.0 2.2 copy-start.6
  660.4 149.6 %copy-start.7 = (bf16[1,256,2048]{2,1,0:T(8,128)(2,1)S(1)}, bf16[1,256,2048]{2,1,0:T(8,128)(2,1)}, u32[]{:S(2)}) copy-start(bf16[1,256,2048]{2,1,0:T(8,128)(2,1)} %param.14) | copy-start | bytes 3145732
  805.2 4.9 copy-start.2
  805.2 4.9 copy-start.4
  810.0 4.9 copy-start.13
  815.0 4.5 copy-start.12
  819.5 4.4 copy-start.11

commit v5 on v4

--- a/solution.py
+++ b/solution.py
@@ -322,20 +322,18 @@
         pl.when(jnp.logical_and(z <= grid.z, grid.has_right))(lambda: self.add_line(z, part, True))
         pl.when(jnp.logical_and(z >= grid.z, grid.has_left))(lambda: self.add_line(z, part, False))
 
-    def pass_on(self, z):
+    def pass_on(self, z, parts=None):
         grid = self.grid
-        for part in range(self.parts):
+        for part in parts or range(self.parts):
             self.gather_sum(z, part)
             self.partial[self.place(z), self.run(part)] = self.total[...].astype(BF)
             pl.when(z < grid.z)(lambda part=part: self.along(z, part, True).start())
             pl.when(z > grid.z)(lambda part=part: self.along(z, part, False).start())
 
-    def own(self, result, after=None):
+    def own(self, result):
         for part in range(self.parts):
             self.gather_sum(self.grid.z, part)
-            result[self.run(part)] = self.total[...].astype(result.dtype)
-            if after is not None:
-                after(part)
+            result[self.run(part)] = self.total[...]
 
     def finish(self):
         grid = self.grid
@@ -624,30 +622,40 @@
     )(normed, tangent_all, gates[0], gates[1], ups[0], ups[1], downs[0], downs[1])
 
 
+class Thirds(Scatter):
+    def run(self, part):
+        quarter = self.rows
+        if part == 2:
+            return pl.ds(pl.multiple_of(self.grid.replica * quarter, quarter), quarter)
+        return pl.ds((2 + part) * quarter, quarter)
+
+
 def sums_kernel(
-    line, parts,
-    normed, attended, grad_qkv, grad_out, gains,
-    result,
-    both_normed, both_attended, both_qkv, both_out, both_gains, load_sem, twin_send, twin_recv,
+    line,
+    normed, attended, grad_qkv, grad_out, tokens, grad_middle, weights, gain, term_two,
+    result, grad_tokens,
+    both_normed, both_attended, both_qkv, both_out, load_sem, twin_send, twin_recv,
     partial, from_across, from_line, total, across_send, across_recv, line_send, line_recv,
-    mine, theirs, mirror_send, mirror_recv,
+    mine, theirs, mirror_send, mirror_recv, from_mirror, quarter_send, quarter_recv,
+    in_weights, weight_sem, token_v, middle_v, grad_normed, terms, own_terms, twin_terms,
 ):
     grid = Grid(2, line)
     rows, width = normed.shape
     run = partial.shape[1]
+    quarter = run // 4
     narrow = grad_qkv.shape[1]
     grid.greet(True, True)
-    scatter = Scatter(
+    scatter = Thirds(
         grid, partial, from_across, from_line, total,
-        (across_send, across_recv, line_send, line_recv), parts,
-    )
+        (across_send, across_recv, line_send, line_recv), 3,
+    )
+    scatter.rows = quarter
     own, twin = pl.ds(0, rows), pl.ds(rows, rows)
     pairs = [
+        (grad_qkv, both_qkv.at[own], both_qkv.at[twin]),
         (normed, both_normed.at[own], both_normed.at[twin]),
-        (grad_qkv, both_qkv.at[own], both_qkv.at[twin]),
+        (grad_out, both_out.at[own], both_out.at[twin]),
         (attended, both_attended.at[own], both_attended.at[twin]),
-        (grad_out, both_out.at[own], both_out.at[twin]),
-        (gains, both_gains.at[0], both_gains.at[1]),
     ]
     swaps = [
         remote(src, there, twin_send.at[i], twin_recv.at[i], grid.twin)
@@ -656,21 +664,43 @@
     for copy in swaps:
         copy.start()
     load_pairs([(src, here) for src, here, _ in pairs], load_sem)
+    later = [
+        pltpu.make_async_copy(src, dst, weight_sem.at[i])
+        for i, (src, dst) in enumerate(
+            (
+                (weights.at[:, :, pl.ds(0, narrow)], in_weights),
+                (tokens, token_v),
+                (grad_middle, middle_v),
+            )
+        )
+    ]
+    for copy in later:
+        copy.start()
     for copy in swaps:
         copy.wait()
     tall = line * run
     tile = 512
+    away = pl.ds(pl.multiple_of((1 - grid.replica) * quarter, quarter), quarter)
+    here = pl.ds(pl.multiple_of(grid.replica * quarter, quarter), quarter)
+
+    def to_mirror(slot):
+        return remote(
+            partial.at[slot, away], from_mirror.at[slot],
+            quarter_send.at[slot], quarter_recv.at[slot], grid.mirror,
+        )
+
+    def features(x):
+        return pl.ds(pl.multiple_of((x * 2 + grid.core) * tall, tall), tall)
 
     def column(j, carry):
         x = jnp.where(j == 0, 1 - grid.x, grid.x)
-        features = pl.ds(pl.multiple_of((x * 2 + grid.core) * tall, tall), tall)
         blocks = pl.ds(x * line, line)
 
         def wide(left, right, first):
             def step(i, inner):
                 c = pl.ds(pl.multiple_of(i * tile, tile), tile)
                 to = pl.ds(pl.multiple_of(first + i * tile, 128), tile)
-                value = dot(left[:, features], right[:, c], TN).astype(BF)
+                value = dot(left[:, features(x)], right[:, c], TN).astype(BF)
                 partial[blocks, :, to] = value.reshape(line, run, tile)
                 return inner
 
@@ -678,68 +708,149 @@
 
         wide(both_normed, both_qkv, 0)
         wide(both_attended, both_out, narrow)
-        pair = both_gains[0, features].astype(F32) + both_gains[1, features].astype(F32)
-        partial[blocks, :, narrow + width :] = pair.astype(BF).reshape(line, run, gains.shape[1])
-
-        @pl.when(j == 0)
-        def _():
-            for k in range(line - 1, -1, -1):
-                scatter.send_across(grid.order(k))
-
+        partial[blocks, :, narrow + width :] = jnp.zeros((line, run, 128), BF)
+        for k in range(line - 1, -1, -1):
+            z = grid.order(k)
+            to_mirror(grid.slot(x, z)).start()
+            pl.when(j == 0)(lambda z=z: scatter.across(z, 0).start())
         return carry
 
     lax.fori_loop(0, 2, column, 0)
-
-    def along(i, carry):
-        scatter.pass_on(grid.order(line - 1 - i))
+    for copy in later:
+        copy.wait()
+
+    def back_step(j, carry):
+        units = pl.ds(j * (tile // run), tile // run)
+        c = pl.ds(pl.multiple_of(j * tile, tile), tile)
+        right = in_weights[units].reshape(tile, narrow)
+        grad_normed[:, c] = dot(both_qkv[own, :], right, NT)
         return carry
 
-    lax.fori_loop(0, line - 1, along, 0)
-
-    def swap(part):
-        here = scatter.run(part)
+    lax.fori_loop(0, width // tile, back_step, 0)
+    terms[...] = jnp.zeros_like(terms)
+    chunk = 64
+
+    def norm_step(j, carry):
+        r = pl.ds(pl.multiple_of(j * chunk, chunk), chunk)
+        value = token_v[r, :].astype(F32)
+        factor = lax.rsqrt(jnp.mean(value * value, axis=1, keepdims=True) + norm_eps)
+        unit = value * factor
+        grad = grad_normed[r, :]
+        terms[0:1, :] += jnp.sum(grad * unit, axis=0, keepdims=True)
+        scaled = grad * gain[...]
+        mean = jnp.mean(scaled * unit, axis=1, keepdims=True)
+        grad_tokens[r, :] = (middle_v[r, :] + factor * (scaled - unit * mean)).astype(BF)
+        return carry
+
+    lax.fori_loop(0, rows // chunk, norm_step, 0)
+    terms[1:2, :] = term_two[...]
+    own_terms[...] = terms[...].astype(BF)
+    swap_terms = remote(own_terms, twin_terms, twin_send.at[4], twin_recv.at[4], grid.twin)
+    swap_terms.start()
+    swap_terms.wait()
+    for x in range(2):
+        for z in range(line):
+            first = pl.multiple_of((x * 2 + grid.core) * tall + z * run, run)
+            c = pl.ds(first, run)
+            value = own_terms[:, c].astype(F32) + twin_terms[:, c].astype(F32)
+            partial[x * line + z, 3 * quarter : 3 * quarter + 16, narrow + width :] = value.astype(BF)
+    for k in range(line - 1, -1, -1):
+        scatter.across(grid.order(k), 1).start()
+
+    def add_mirror(x):
+        def step(i, carry):
+            slot = grid.slot(x, grid.order(line - 1 - i))
+            to_mirror(slot).wait_recv()
+            value = partial[slot, here].astype(F32) + from_mirror[slot].astype(F32)
+            partial[slot, here] = value.astype(BF)
+            return carry
+
+        lax.fori_loop(0, line, step, 0)
+
+    add_mirror(1 - grid.x)
+    for k in range(line - 1, -1, -1):
+        scatter.across(grid.order(k), 2).start()
+
+    def swap(part, whole=True):
+        at = scatter.run(part)
         return remote(
-            mine.at[here], theirs.at[here], mirror_send.at[part], mirror_recv.at[part], grid.mirror
+            mine.at[at], theirs.at[at], mirror_send.at[part], mirror_recv.at[part], grid.mirror
         )
 
-    scatter.own(mine, lambda part: swap(part).start())
-    for part in range(parts):
+    def sweep(part):
+        def step(i, carry):
+            scatter.pass_on(grid.order(line - 1 - i), (part,))
+            return carry
+
+        lax.fori_loop(0, line - 1, step, 0)
+
+    def settle(part):
+        scatter.gather_sum(grid.z, part)
+        mine[scatter.run(part)] = total[...].astype(BF)
+        swap(part).start()
+
+    sweep(0)
+    sweep(1)
+    add_mirror(grid.x)
+    settle(0)
+    sweep(2)
+    settle(1)
+    settle(2)
+    result[here] = mine[here].astype(F32)
+    for part in range(2):
         swap(part).wait()
-        here = scatter.run(part)
-        result[here] = mine[here].astype(F32) + theirs[here].astype(F32)
+        at = scatter.run(part)
+        result[at] = mine[at].astype(F32) + theirs[at].astype(F32)
+    swap(2).wait_send()
+    remote(mine.at[away], theirs.at[away], mirror_send.at[2], mirror_recv.at[2], grid.mirror).wait_recv()
+    result[away] = theirs[away].astype(F32)
     scatter.finish()
 
-
-def sums_call(normed, attended, grad_qkv, grad_out, gains, line, run):
+    def sent(slot, carry):
+        to_mirror(slot).wait_send()
+        return carry
+
+    lax.fori_loop(0, 2 * line, sent, 0)
+
+
+def sums_call(normed, attended, grad_qkv, grad_out, tokens, grad_middle, weights, gain, term_two, line):
     rows, width = normed.shape
-    narrow, few = grad_qkv.shape[1], gains.shape[1]
-    whole, parts = narrow + width + few, 4
+    narrow = grad_qkv.shape[1]
+    run, whole = weights.shape[1:]
+    quarter = run // 4
+    vmem = pl.BlockSpec(memory_space=pltpu.VMEM)
+    dma = pltpu.SemaphoreType.DMA
+    like = lambda a: pltpu.VMEM(a.shape, a.dtype)
     return pl.pallas_call(
-        functools.partial(sums_kernel, line, parts),
-        out_shape=jax.ShapeDtypeStruct((run, whole), F32),
-        in_specs=[ANY] * 5,
-        out_specs=pl.BlockSpec(memory_space=pltpu.VMEM),
+        functools.partial(sums_kernel, line),
+        out_shape=(
+            jax.ShapeDtypeStruct((run, whole), F32), jax.ShapeDtypeStruct((rows, width), BF),
+        ),
+        in_specs=[ANY] * 7 + [vmem] * 2,
+        out_specs=(vmem, vmem),
         scratch_shapes=[
             pltpu.VMEM((2 * rows, width), BF), pltpu.VMEM((2 * rows, width), BF),
             pltpu.VMEM((2 * rows, narrow), BF), pltpu.VMEM((2 * rows, width), BF),
-            pltpu.VMEM((2, width, few), BF),
-            pltpu.SemaphoreType.DMA((5,)), pltpu.SemaphoreType.DMA((5,)), pltpu.SemaphoreType.DMA((5,)),
-            *scatter_scratch(line, run, whole, parts),
-            pltpu.VMEM((run, whole), BF), pltpu.VMEM((run, whole), BF),
-            pltpu.SemaphoreType.DMA((parts,)), pltpu.SemaphoreType.DMA((parts,)),
+            dma((4,)), dma((5,)), dma((5,)),
+            pltpu.VMEM((2 * line, run, whole), BF), pltpu.VMEM((line, run, whole), BF),
+            pltpu.VMEM((2 * line - 2, run, whole), BF), pltpu.VMEM((quarter, whole), F32),
+            dma((line, 3)), dma((line, 3)), dma((line, 3)), dma((2 * line - 2, 3)),
+            pltpu.VMEM((run, whole), BF), pltpu.VMEM((run, whole), BF), dma((3,)), dma((3,)),
+            pltpu.VMEM((2 * line, quarter, whole), BF), dma((2 * line,)), dma((2 * line,)),
+            pltpu.VMEM((weights.shape[0], run, narrow), BF), dma((3,)),
+            like(tokens), like(grad_middle), pltpu.VMEM((rows, width), F32),
+            pltpu.VMEM((16, width), F32), pltpu.VMEM((16, width), BF), pltpu.VMEM((16, width), BF),
         ],
         compiler_params=pltpu.CompilerParams(
-            collective_id=3, has_side_effects=True, vmem_limit_bytes=60 * 2**20
+            collective_id=3, has_side_effects=True, vmem_limit_bytes=63 * 2**20
         ),
         name="sums",
-    )(normed, attended, grad_qkv, grad_out, gains)
-
-
-def weights_kernel(line, block, everything, send, recv, twin_send, twin_recv, staged, load_sem):
-    grid = Grid(2, line)
+    )(normed, attended, grad_qkv, grad_out, tokens, grad_middle, weights, gain, term_two)
+
+
+def gather_weights(grid, block, everything, send, recv, twin_send, twin_recv, meanwhile):
+    line = grid.line
     rows = block.shape[0] // 4
-    grid.greet(True, True)
-    near = grid.x * line + grid.z
     carry_a, carry_b = grid.replica * 2, grid.replica * 2 + 1
     other_a, other_b = (1 - grid.replica) * 2, (1 - grid.replica) * 2 + 1
     right, left, across, mirror = range(4)
@@ -783,8 +894,7 @@
 
     for quarter in range(4):
         share(grid.x, grid.z, quarter, True).start()
-    load_pairs([(block, staged)], load_sem)
-    load_pairs([(staged, everything.at[(grid.x * 2 + grid.core) * line + grid.z])], load_sem)
+    meanwhile()
 
     arrived(1 - grid.x, grid.z, carry_b)
     copy(1 - grid.x, grid.z, carry_b, mirror).start()
@@ -857,26 +967,6 @@
     copy(grid.x, grid.z, carry_b, across, True).wait_send()
 
 
-def weights_call(block, line):
-    rows, width = block.shape
-    units = 2 * line
-    return pl.pallas_call(
-        functools.partial(weights_kernel, line),
-        out_shape=jax.ShapeDtypeStruct((2 * units, rows, width), BF),
-        in_specs=[ANY],
-        out_specs=ANY,
-        scratch_shapes=[
-            pltpu.SemaphoreType.DMA((4, units, 4)), pltpu.SemaphoreType.DMA((4, units)),
-            pltpu.SemaphoreType.DMA((4, units)), pltpu.SemaphoreType.DMA((4, units)),
-            pltpu.VMEM((rows, width), BF), pltpu.SemaphoreType.DMA((1,)),
-        ],
-        compiler_params=pltpu.CompilerParams(
-            collective_id=4, has_side_effects=True, vmem_limit_bytes=32 * 2**20
-        ),
-        name="weights",
-    )(block)
-
-
 class Line:
     def __init__(self, grid, block, everything, send, recv):
         self.grid, self.block, self.everything = grid, block, everything
@@ -918,6 +1008,20 @@
             return carry
 
         lax.fori_loop(0, grid.line, step, 0)
+
+
+def turn(value, cosine, sine, scale):
+    parts = []
+    lane = lax.broadcasted_iota(jnp.int32, (value.shape[0], 128), 1) % HEAD_SIZE
+    for first in range(0, value.shape[1], 128):
+        pair = value[:, first : first + 128]
+        swapped = jnp.where(
+            lane < HEAD_SIZE // 2,
+            pltpu.roll(pair, 128 - HEAD_SIZE // 2, 1),
+            pltpu.roll(pair, HEAD_SIZE // 2, 1),
+        )
+        parts.append(((pair * cosine[...] + swapped * sine[...]) * scale).astype(BF))
+    return parts[0] if len(parts) == 1 else jnp.concatenate(parts, axis=1)
 
 
 def halves(pair, half):
@@ -939,36 +1043,83 @@
     return jnp.where(lane == 0, first, second)
 
 
-def attend_kernel(
+def front_kernel(
     line, parts,
-    queries, keyed, tangent, bias, tokens, weights, gain,
-    attended, middle, normed, logs, keyed_out, tangent_all,
-    keyed_all, query_v, bias_v, token_v, weight_v, scores, probs, sums, stage, load_sem,
-    key_send, key_recv, send, recv, own_sem,
+    block, tokens, tangent, bias, cosine, sine,
+    attended, middle, normed, first_normed, queries, logs, keyed_out, tangent_all, weights_out,
+    everything, keyed, keyed_all, bias_v, token_v, cosine_v, sine_v, gain, scores, probs, sums, stage, load_sem,
+    key_send, key_recv, send, recv, own_sem, weight_send, weight_recv, twin_send, twin_recv,
 ):
     grid = Grid(2, line)
-    rows, width = queries.shape
+    rows, width = tokens.shape
     narrow = keyed.shape[1] // 2
     total = bias.shape[1]
+    extra = width + 2 * narrow
+    after = extra + 128
     me = grid.slot(grid.x, grid.z)
-    grid.greet(False)
+    chunk = rows // 2
+    tile = 512
+    grid.greet(True, True)
+
+    def meanwhile():
+        load_pairs(
+            [
+                (block, everything.at[(grid.x * 2 + grid.core) * line + grid.z]),
+                (tangent, stage),
+                (bias, bias_v),
+                (tokens, token_v),
+                (cosine, cosine_v),
+                (sine, sine_v),
+            ],
+            load_sem,
+        )
+        load_pairs([(stage, tangent_all.at[me])], own_sem)
+
+    gather_weights(
+        grid, block, everything, weight_send, weight_recv, twin_send, twin_recv, meanwhile
+    )
+    weights_copy = pltpu.make_async_copy(everything, weights_out, own_sem.at[1])
+    weights_copy.start()
+    units, run = everything.shape[0], everything.shape[1]
+    for unit in range(units):
+        for which in range(2):
+            gain[which : which + 1, unit * run : (unit + 1) * run] = everything[
+                unit, which : which + 1, extra:after
+            ].astype(F32)
+
+    def norm(source, target, which):
+        def step(j, carry):
+            here = pl.ds(pl.multiple_of(j * chunk, chunk), chunk)
+            value = source[here, :].astype(F32)
+            factor = lax.rsqrt(jnp.mean(value * value, axis=1, keepdims=True) + norm_eps)
+            target[here, :] = (value * factor * gain[which : which + 1, :]).astype(BF)
+            return carry
+
+        lax.fori_loop(0, rows // chunk, step, 0)
+
+    norm(token_v, first_normed, 0)
+
+    def project(c):
+        return dot(first_normed[...], everything[:, :, c].reshape(width, tile), NN)
+
+    for first in range(0, narrow, tile):
+        keyed[:, first : first + tile] = turn(project(slice(width + first, width + first + tile)), cosine_v, sine_v, 1.0)
+        keyed[:, narrow + first : narrow + first + tile] = project(
+            slice(width + narrow + first, width + narrow + first + tile)
+        ).astype(BF)
     line_keys = Line(grid, keyed, keyed_all, key_send, key_recv)
     gather = Gather(grid, tangent, tangent_all, send, recv, parts)
     line_keys.send_own()
     for part in range(parts):
         gather.copy(grid.z, part, 2, True).start()
-    load_pairs(
-        [
-            (keyed, keyed_all.at[grid.z]),
-            (tangent, stage),
-            (queries, query_v),
-            (bias, bias_v),
-            (tokens, token_v),
-            (weights, weight_v),
-        ],
-        load_sem,
-    )
-    load_pairs([(stage, tangent_all.at[me])], own_sem)
+    keyed_all[grid.z] = keyed[...]
+
+    def query_step(j, carry):
+        c = pl.ds(pl.multiple_of(j * tile, tile), tile)
+        queries[:, c] = turn(project(c), cosine_v, sine_v, HEAD_SIZE ** (-0.5))
+        return carry
+
+    lax.fori_loop(0, width // tile, query_step, 0)
     for distance in range(line):
         if distance:
             line_keys.forward(distance)
@@ -984,8 +1135,6 @@
 
 
     logs[...] = jnp.zeros_like(logs)
-    deep = 2 * rows
-    chunk = rows
     pairs = width // (2 * HEAD_SIZE)
     group = pairs // (narrow // (2 * HEAD_SIZE))
 
@@ -998,22 +1147,21 @@
         first_key = pl.multiple_of((i // group) * 128, 128)
         keys = keyed_all[:, :, pl.ds(first_key, 128)].reshape(total, 128)
         values = keyed_all[:, :, pl.ds(first_key + narrow, 128)].reshape(total, 128)
-        scores[...] = dot(halves(query_v[:, c], half), keys, NT)
+        scores[...] = dot(halves(queries[:, c], half), keys, NT)
 
         def soft(j, inner):
-            here = pl.ds(pl.multiple_of(j * chunk, chunk), chunk)
-            there = pl.ds(pl.multiple_of((j * chunk) % rows, chunk), chunk)
-            value = scores[here, :] + bias_v[there, :]
+            here = pl.ds(pl.multiple_of(j * rows, rows), rows)
+            value = scores[here, :] + bias_v[...]
             top = jnp.max(value, axis=1, keepdims=True)
             power = jnp.exp(value - top)
             size = jnp.sum(power, axis=1, keepdims=True)
             probs[here, :] = power.astype(BF)
-            sums[here, :] = jnp.broadcast_to(1.0 / size, (chunk, 128))
-            lane = lax.broadcasted_iota(jnp.int32, (chunk, 128), 1)
+            sums[here, :] = jnp.broadcast_to(1.0 / size, (rows, 128))
+            lane = lax.broadcasted_iota(jnp.int32, (rows, 128), 1)
             logs[here, :] = jnp.where(lane == i, top + jnp.log(size), logs[here, :])
             return inner
 
-        lax.fori_loop(0, deep // chunk, soft, 0)
+        lax.fori_loop(0, 2, soft, 0)
         out = dot(probs[...], values, NN) * sums[...]
         attended[:, c] = unhalves(out, half).astype(BF)
 
@@ -1024,23 +1172,16 @@
     keyed_copy = pltpu.make_async_copy(keyed_all, keyed_out, load_sem.at[0])
     keyed_copy.start()
     advance(pairs // 3)
-    tile = 512
 
     def out_step(j, carry):
         c = pl.ds(pl.multiple_of(j * tile, tile), tile)
-        middle[:, c] = token_v[:, c].astype(F32) + dot(attended[...], weight_v[:, c], NN)
+        w = pl.ds(pl.multiple_of(after + j * tile, 128), tile)
+        out = dot(attended[...], everything[:, :, w].reshape(width, tile), NN)
+        middle[:, c] = token_v[:, c].astype(F32) + out
         return carry
 
     lax.fori_loop(0, width // tile, out_step, 0)
-
-    def norm_step(j, carry):
-        here = pl.ds(pl.multiple_of(j * chunk, chunk), chunk)
-        value = middle[here, :]
-        factor = lax.rsqrt(jnp.mean(value * value, axis=1, keepdims=True) + norm_eps)
-        normed[here, :] = (value * factor * gain[...]).astype(BF)
-        return carry
-
-    lax.fori_loop(0, rows // chunk, norm_step, 0)
+    norm(middle, normed, 1)
 
     def rest(n, carry):
         advance(n)
@@ -1050,46 +1191,53 @@
     for z in range(line):
         gather.wait_across(z)
     keyed_copy.wait()
+    weights_copy.wait()
     line_keys.finish()
     gather.finish()
 
 
-def attend_call(queries, keyed, tangent, bias, tokens, weights, gain, line):
-    rows, width = queries.shape
-    both = keyed.shape[1]
+def front_call(block, tokens, tangent, bias, cosine, sine, line, narrow):
+    rows, width = tokens.shape
     total = bias.shape[1]
     blocks, parts = 2 * line, 4
     shapes = jax.ShapeDtypeStruct
     vmem = pl.BlockSpec(memory_space=pltpu.VMEM)
+    like = lambda a: pltpu.VMEM(a.shape, a.dtype)
     return pl.pallas_call(
-        functools.partial(attend_kernel, line, parts),
+        functools.partial(front_kernel, line, parts),
         out_shape=(
             shapes((rows, width), BF), shapes((rows, width), F32), shapes((rows, width), BF),
-            shapes((2 * rows, 128), F32), shapes((line, rows, both), BF),
-            shapes((blocks, rows, width), BF),
+            shapes((rows, width), BF), shapes((rows, width), BF),
+            shapes((2 * rows, 128), F32), shapes((line, rows, 2 * narrow), BF),
+            shapes((blocks, rows, width), BF), shapes((2 * blocks,) + block.shape, BF),
         ),
-        in_specs=[ANY] * 6 + [vmem],
-        out_specs=(vmem, vmem, vmem, vmem, ANY, ANY),
+        in_specs=[ANY] * 6,
+        out_specs=(vmem,) * 6 + (ANY,) * 3,
         scratch_shapes=[
-            pltpu.VMEM((line, rows, both), BF),
-            pltpu.VMEM((rows, width), BF), pltpu.VMEM((rows, total), F32), pltpu.VMEM((rows, width), BF),
-            pltpu.VMEM(weights.shape, BF), pltpu.VMEM((2 * rows, total), F32), pltpu.VMEM((2 * rows, total), BF),
+            pltpu.VMEM((2 * blocks,) + block.shape, BF),
+            pltpu.VMEM((rows, 2 * narrow), BF), pltpu.VMEM((line, rows, 2 * narrow), BF),
+            like(bias), like(tokens), like(cosine), like(sine), pltpu.VMEM((2, width), F32),
+            pltpu.VMEM((2 * rows, total), F32), pltpu.VMEM((2 * rows, total), BF),
             pltpu.VMEM((2 * rows, 128), F32), pltpu.VMEM((rows, width), BF), pltpu.SemaphoreType.DMA((6,)),
             pltpu.SemaphoreType.DMA((line, 2)), pltpu.SemaphoreType.DMA((line,)),
             pltpu.SemaphoreType.DMA((line, parts, 3)), pltpu.SemaphoreType.DMA((blocks, parts)),
-            pltpu.SemaphoreType.DMA((1,)),
+            pltpu.SemaphoreType.DMA((2,)),
+            pltpu.SemaphoreType.DMA((4, blocks, 4)), pltpu.SemaphoreType.DMA((4, blocks)),
+            pltpu.SemaphoreType.DMA((4, blocks)), pltpu.SemaphoreType.DMA((4, blocks)),
         ],
         compiler_params=pltpu.CompilerParams(
-            collective_id=5, has_side_effects=True, vmem_limit_bytes=60 * 2**20
+            collective_id=5, has_side_effects=True, vmem_limit_bytes=62 * 2**20
         ),
-        name="attend",
-    )(queries, keyed, tangent, bias, tokens, weights, gain)
+        name="front",
+    )(block, tokens, tangent, bias, cosine, sine)
 
 
 def back_kernel(
     line, parts, pass_at,
-    queries, keyed_all, grads, bias, logs, hidden_all, down_own, down_twin,
-    branch, grad_query, grad_keyed,
+    queries, keyed_all, grad_out, bias, logs, hidden_all, down_own, down_twin, weights, cosine, sine,
+    gate_sum, up_sum, down_sum,
+    branch, grad_qkv, gate_mirror, up_mirror, down_mirror,
+    out_v, out_w, cosine_v, sine_v, grad_keyed, mirror_send, mirror_recv,
     query_v, keyed_v, grad_v, bias_v, log_v, scores, gradients, probs, slopes, key_sum, value_sum,
     down_w, hidden, load_sem,
     partial, from_across, from_line, total, across_send, across_recv, line_send, line_recv,
@@ -1100,7 +1248,15 @@
     rows = partial.shape[1]
     narrow = keyed_all.shape[2] // 2
     length = bias.shape[1]
-    grid.greet(False)
+    grid.greet(False, True)
+    mirrored = [
+        remote(src, dst, mirror_send.at[i], mirror_recv.at[i], grid.mirror)
+        for i, (src, dst) in enumerate(
+            ((gate_sum, gate_mirror), (up_sum, up_mirror), (down_sum, down_mirror))
+        )
+    ]
+    for copy in mirrored:
+        copy.start()
     load_pairs(
         [
             (down_own, down_w.at[pl.ds(0, cols)]),
@@ -1108,9 +1264,11 @@
             (hidden_all, hidden),
             (queries, query_v),
             (keyed_all, keyed_v),
-            (grads, grad_v),
+            (grad_out, out_v),
             (bias, bias_v),
             (logs, log_v),
+            (cosine, cosine_v),
+            (sine, sine_v),
         ],
         load_sem,
     )
@@ -1136,7 +1294,19 @@
         pl.when(i < line)(lambda: scatter.send_across(z))
         return carry
 
-    lax.fori_loop(0, 2 * line, work, 0)
+    lax.fori_loop(0, line, work, 0)
+    tile = out_w.shape[0] * out_w.shape[1]
+    after = weights.shape[2] - width
+
+    def out_step(j, carry):
+        units = pl.ds(j * out_w.shape[0], out_w.shape[0])
+        load_pairs([(weights.at[units, :, pl.ds(after, width)], out_w)], load_sem)
+        c = pl.ds(pl.multiple_of(j * tile, tile), tile)
+        grad_v[:, c] = dot(out_v[...], out_w[...].reshape(tile, width), NT).astype(BF)
+        return carry
+
+    lax.fori_loop(0, width // tile, out_step, 0)
+    lax.fori_loop(line, 2 * line, work, 0)
     deep = 2 * rows
     chunk = rows // 2
     pairs = width // (2 * HEAD_SIZE)
@@ -1168,7 +1338,7 @@
 
         lax.fori_loop(0, deep // chunk, soft, 0)
         back = dot(slopes[...], keys, NN) * HEAD_SIZE ** (-0.5)
-        grad_query[:, c] = unhalves(back, half)
+        grad_qkv[:, c] = turn(unhalves(back, half), cosine_v, sine_v, 1.0)
         key_part = dot(slopes[...], query, TN)
         value_part = dot(probs[...], grad, TN)
 
@@ -1202,11 +1372,17 @@
         scatter.pass_on(grid.order(k))
     scatter.own(branch)
     keyed_scatter.own(grad_keyed)
+    grad_qkv[:, width : width + narrow] = turn(grad_keyed[:, :narrow], cosine_v, sine_v, 1.0)
+    grad_qkv[:, width + narrow :] = grad_keyed[:, narrow:].astype(BF)
+    for copy in mirrored:
+        copy.wait()
     scatter.finish()
     keyed_scatter.finish()
 
 
-def back_call(queries, keyed_all, grads, bias, logs, hidden_all, downs, line):
+def back_call(
+    queries, keyed_all, grad_out, bias, logs, hidden_all, downs, weights, cosine, sine, sums, line
+):
     rows, width = queries.shape
     both = keyed_all.shape[2]
     cols, length = downs[0].shape[0], bias.shape[1]
@@ -1216,18 +1392,22 @@
     return pl.pallas_call(
         functools.partial(back_kernel, line, parts, (4, 9, 15)),
         out_shape=(
-            shapes((rows, width), F32), shapes((rows, width), F32), shapes((rows, both), F32),
+            shapes((rows, width), F32), shapes((rows, width + both), BF),
+            *(shapes(s.shape, BF) for s in sums),
         ),
-        in_specs=[ANY] * 8,
-        out_specs=(vmem,) * 3,
+        in_specs=[ANY] * 14,
+        out_specs=(vmem,) * 2 + (ANY,) * 3,
         scratch_shapes=[
+            pltpu.VMEM((rows, width), BF), pltpu.VMEM((4, weights.shape[1], width), BF),
+            pltpu.VMEM(cosine.shape, F32), pltpu.VMEM(sine.shape, F32), pltpu.VMEM((rows, both), F32),
+            pltpu.SemaphoreType.DMA((3,)), pltpu.SemaphoreType.DMA((3,)),
             pltpu.VMEM((rows, width), BF), pltpu.VMEM(keyed_all.shape, BF), pltpu.VMEM((rows, width), BF),
             pltpu.VMEM((rows, length), F32), pltpu.VMEM(logs.shape, F32),
             pltpu.VMEM((2 * rows, length), F32), pltpu.VMEM((2 * rows, length), F32),
             pltpu.VMEM((2 * rows, length), BF), pltpu.VMEM((2 * rows, length), BF),
             pltpu.VMEM((length, 128), F32), pltpu.VMEM((length, 128), F32),
             pltpu.VMEM((2 * cols, width), BF), pltpu.VMEM(hidden_all.shape, BF),
-            pltpu.SemaphoreType.DMA((8,)),
+            pltpu.SemaphoreType.DMA((10,)),
             *scatter_scratch(line, rows, width, parts),
             pltpu.VMEM((line, rows, both), BF), pltpu.VMEM((2 * line - 2, rows, both), BF),
             pltpu.VMEM((rows // parts, both), F32),
@@ -1237,7 +1417,9 @@
             collective_id=6, has_side_effects=True, vmem_limit_bytes=62 * 2**20
         ),
         name="back",
-    )(queries, keyed_all, grads, bias, logs, hidden_all, downs[0], downs[1])
+    )(
+        queries, keyed_all, grad_out, bias, logs, hidden_all, *downs, weights, cosine, sine, *sums
+    )
 
 
 def body(
@@ -1444,7 +1626,6 @@
     line = lax.axis_size("context")
     narrow = key_projection.shape[1]
     run = w_query.shape[0]
-    flip = [(0, 1), (1, 0)]
     swap = [(i, i ^ 1) for i in range(lax.axis_size("fsdp"))]
     gates, ups, downs = ((w, lax.ppermute(w, "fsdp", swap)) for w in (w_gate, w_up, w_down))
     position = lax.axis_index("context")
@@ -1452,39 +1633,23 @@
     rotary_angles = local_positions.reshape(segment_length).astype(f32)[:, None] * frequencies(
         HEAD_SIZE // 2
     )
-    gain_columns = jnp.pad(jnp.stack([gain_attn, gain_mlp], axis=1), ((0, 0), (0, 126)))
-    block = jnp.concatenate([w_query, key_projection, value_projection, gain_columns, w_out], axis=1)
-    weights = weights_call(block, line).reshape(width, block.shape[1])
-    mid = width + 2 * narrow
-    in_w, out_w = weights[:, : mid + 128], weights[:, mid + 128 :]
-    gain_first = weights[:, mid].astype(f32)
-    gain_second = weights[:, mid + 1].astype(f32)
-    inputs_f = tokens.astype(f32).reshape(segment_length, width)
-    factor_one = lax.rsqrt(jnp.mean(inputs_f * inputs_f, axis=-1, keepdims=True) + norm_eps)
-    unit_one = inputs_f * factor_one
-    normed_tokens = (unit_one * gain_first).astype(bf16)
-    projected = jnp.dot(normed_tokens, in_w, preferred_element_type=f32)
-
-    def heads(first, size):
-        return projected[:, first : first + size].reshape(segment_length, size // HEAD_SIZE, HEAD_SIZE)
-
-    query_rows = apply_rotary(heads(0, width), rotary_angles).astype(bf16)
-    scaled_query = (query_rows * HEAD_SIZE ** (-0.5)).astype(bf16).reshape(segment_length, width)
-    key_rows = apply_rotary(heads(width, narrow), rotary_angles).astype(bf16)
-    value_rows = projected[:, width + narrow : mid].astype(bf16)
-    keyed = jnp.concatenate([key_rows.reshape(segment_length, narrow), value_rows], axis=1)
+    extra = jnp.pad(jnp.stack([gain_attn, gain_mlp]), ((0, run - 2), (0, 0)))
+    block = jnp.concatenate([w_query, key_projection, value_projection, extra, w_out], axis=1)
+    cosine, sine = jnp.cos(rotary_angles), jnp.sin(rotary_angles)
+    cosine = jnp.concatenate([cosine] * 4, axis=1)
+    sine = jnp.concatenate([-sine, sine] * 2, axis=1)
     allowed = places.reshape(1, total_length) <= local_positions.reshape(segment_length, 1)
     bias = jnp.where(allowed, 0.0, -1e30).astype(f32)
     tangent = cotangent.reshape(segment_length, width)
     tangent_f = tangent.astype(f32)
-    attended, middle, normed_mlp, logs, keyed_all, tangent_all = attend_call(
-        scaled_query, keyed, tangent, bias, tokens.reshape(segment_length, width), out_w,
-        gain_second.reshape(1, width), line,
-    )
+    rows = tokens.reshape(segment_length, width)
+    (
+        attended, middle, normed_mlp, normed_tokens, scaled_query, logs, keyed_all, tangent_all, weights,
+    ) = front_call(block, rows, tangent, bias, cosine, sine, line, narrow)
+    mid = width + 2 * narrow
+    gain_first = weights[:, 0, mid : mid + run].reshape(width).astype(f32)
+    gain_second = weights[:, 1, mid : mid + run].reshape(width).astype(f32)
     grad_normed, _, hidden_all, *sums = feed_call(normed_mlp, tangent_all, gates, ups, downs, line)[:6]
-    grad_w_gate, grad_w_up, grad_w_down = (
-        g.astype(f32) + lax.ppermute(g, "replica", flip).astype(f32) for g in sums
-    )
     factor_two = lax.rsqrt(jnp.mean(middle * middle, axis=-1, keepdims=True) + norm_eps)
     unit_two = middle * factor_two
     scaled_two = grad_normed * gain_second
@@ -1493,41 +1658,32 @@
         scaled_two - unit_two * jnp.mean(scaled_two * unit_two, axis=-1, keepdims=True)
     )
     grad_branch = grad_middle.astype(bf16)
-    grad_attended = times_nt(grad_branch, out_w).astype(bf16)
-    branch, grad_q, grad_keyed = back_call(
-        scaled_query, keyed_all, grad_attended, bias, logs, hidden_all, downs, line
+    branch, grad_qkv, *mirrored = back_call(
+        scaled_query, keyed_all, grad_branch, bias, logs, hidden_all, downs, weights, cosine, -sine,
+        sums, line,
     )
     outcome = middle + branch
-    grad_query = inverse_rotary(
-        grad_q.reshape(segment_length, QUERY_HEADS, HEAD_SIZE), rotary_angles
-    ).reshape(segment_length, width)
-    grad_key = inverse_rotary(
-        grad_keyed[:, :narrow].reshape(segment_length, KEY_VALUE_HEADS, HEAD_SIZE), rotary_angles
-    ).reshape(segment_length, narrow)
-    value_gradient = grad_keyed[:, narrow:]
-    grad_qkv = jnp.concatenate([grad_query, grad_key, value_gradient], axis=1).astype(bf16)
-    grad_normed_one = times_nt(grad_qkv, weights[:, :mid])
-    scaled_one = grad_normed_one * gain_first
-    term_gain_one = jnp.sum(grad_normed_one * unit_one, axis=0)
-    grad_inputs = grad_middle + factor_one * (
-        scaled_one - unit_one * jnp.mean(scaled_one * unit_one, axis=-1, keepdims=True)
-    )
-    gains = jnp.stack([term_gain_one, term_gain_two], axis=1).astype(bf16)
-    gains = jnp.pad(gains, ((0, 0), (0, 126)))
-    packed = sums_call(normed_tokens, attended, grad_qkv, grad_branch, gains, line, run)
+    grad_w_gate, grad_w_up, grad_w_down = (
+        a.astype(f32) + b.astype(f32) for a, b in zip(sums, mirrored)
+    )
+    packed, grad_tokens = sums_call(
+        normed_tokens, attended, grad_qkv, grad_branch, rows, grad_middle, weights,
+        gain_first.reshape(1, width), term_gain_two.reshape(1, width), line,
+    )
+    gains = packed[run * 3 // 4 : run * 3 // 4 + 2, mid + width :]
     ends, start = [], 0
-    for size in (width, narrow, narrow, width, 1, 1):
+    for size in (width, narrow, narrow, width):
         ends.append(packed[:, start : start + size])
         start += size
     return (
         outcome.astype(bf16).reshape(tokens.shape),
-        grad_inputs.astype(bf16).reshape(tokens.shape),
-        *ends[:4],
+        grad_tokens.reshape(tokens.shape),
+        *ends,
         grad_w_gate,
         grad_w_up,
         grad_w_down,
-        ends[4][:, 0],
-        ends[5][:, 0],
+        gains[0],
+        gains[1],
     )
 
 

time: 837 us -> 754 us (0.901)
  local copies, waits for them, and re-layouts: 41.7 us -> 13.6 us
  matrix products: 24.3 us -> 0 us
  other arithmetic: 33.1 us -> 23.3 us
  Pallas kernels: 723 us -> 714 us
    dot_general x3 -> x0, matrix products: 24.3 us -> none  [the longest x2 16.7 us: times_nt(): lax.dot_general(left, right, (((1,), (1,)), ((), ())), preferred_element_...]
    pallas_call x3 -> x2, Pallas kernels: 369 us -> 350 us  [the longest x1 228 us: front_call(): pl.pallas_call(functools.partial(front_kernel, line, parts), out_shape=(s...]
    slice x10 -> x0, local copies, waits for them, and re-layouts: 16.7 us -> none  [the longest x1 8.4 us: kernel_body(): in_w, out_w = (weights[:, :mid + 128], weights[:, mid + 128:])]
  transfers between devices with their start and end apart: 6 -> 3, of which waited for: 0 -> 0; matrix products, arithmetic and copies ran while one was open for 9% -> 1% of each run, Pallas kernels for 45% -> 30%
where the time goes in v5:
time: 754 us; the launch traced here: 753 us
  Pallas kernels  714 us (95%)
  other arithmetic  23.3 us (3%)
  local copies, waits for them, and re-layouts  13.6 us (2%)
    pallas_call x1, Pallas kernels, front_call(): pl.pallas_call(functools.partial(front_kernel, line, parts), out_shape=(s...  228 us
    pallas_call x1, Pallas kernels, feed_call(): pl.pallas_call(functools.partial(feed_kernel, line, parts, tile), out_sha...  215 us
    pallas_call x1, Pallas kernels, back_call(): pl.pallas_call(functools.partial(back_kernel, line, parts, (4, 9, 15)), o...  149 us
    pallas_call x1, Pallas kernels, sums_call(): pl.pallas_call(functools.partial(sums_kernel, line), out_shape=(jax.Shape...  122 us
  transfers between devices with their start and end apart: 3, of which 0 were waited for; matrix products, arithmetic and copies ran while one was open for 1% of the time, Pallas kernels for 30%

profile of v5, /device:TPU:0, one launch (start us, length us, event | category | flops | bytes accessed | tf_op | source)
XLA Modules:
  0.0 753.0 jit_solution(16315194496936543907)
XLA Ops:
  0.6 0.0 copy-start.13
  0.7 0.0 copy-start.12
  0.7 0.5 collective-permute-start.2
  1.2 0.1 collective-permute-start
  1.3 0.4 collective-permute-start.1
  1.7 1.1 constant_dynamic-update-slice_fusion.3
  2.8 0.7 constant_dynamic-slice_fusion
  3.5 0.9 constant_dynamic-update-slice_fusion.2
  4.4 0.9 constant_dynamic-update-slice_fusion.1
  5.3 0.7 fusion.5
  6.0 0.5 fusion.3
  6.5 1.0 fusion.6
  7.6 0.0 copy-done.12
  7.6 0.0 copy-start.6
  7.6 0.0 copy-done.13
  7.6 1.2 compare_select_fusion.bias
  8.8 0.2 copy-done.6
  9.0 227.5 %front.1 = (bf16[256,2048]{1,0:T(8,128)(2,1)}, f32[256,2048]{1,0:T(8,128)}, bf16[256,2048]{1,0:T(8,128)(2,1)}, bf16[256,2048]{1,0:T(8,128)(2,1)}, bf16[256,2048]...) custom-call(bf16[128,5248]{1,0:T(8,128)(2,1)} %copy-done.6, ...), custom_call_target="tpu_custom_call" | custom-call | tf_op jit(solution)/shard_map/front/pallas_call | solution.py:1206
  236.6 1.8 multiply_reduce_fusion.2
  238.4 1.4 bitcast_convert_fusion
  239.8 0.0 collective-permute-done.2.down_twin
  239.8 0.0 collective-permute-done.gate_twin
  239.8 0.0 collective-permute-done.1.up_twin
  239.8 215.2 %feed.1 = (f32[256,2048]{1,0:T(8,128)}, bf16[8,256,2048]{2,1,0:T(8,128)(2,1)}, bf16[2048,1024]{1,0:T(8,128)(2,1)}, bf16[2048,512]{1,0:T(8,128)(2,1)}, bf16[2048,...) custom-call(bf16[256,2048]{1,0:T(8,128)(2,1)} %get-tuple-element.35., ...), custom_call_target="tpu_custom_call" | custom-call | tf_op jit(solution)/shard_map/feed/pallas_call | solution.py:595
  455.0 0.0 copy-start
  455.0 0.0 copy-start.5
  455.0 3.5 multiply_reduce_fusion
  458.6 0.0 copy-done
  458.6 0.0 copy-done.5
  458.6 3.5 fusion.7
  462.1 149.4 %back.1 = (f32[256,2048]{1,0:T(8,128)}, bf16[256,3072]{1,0:T(8,128)(2,1)}, bf16[2048,512]{1,0:T(8,128)(2,1)}, bf16[2048,512]{1,0:T(8,128)(2,1)}, bf16[512,2048]{1,0:T(8,128)(2,1)}) custom-call(bf16[256,2048]{1,0:T(8,128)(2,1)} %get-tuple-element.33.queries, bf16[4,256,1024]{2,1,0:T(8,128)(2,1)} %get-tuple-element.34.keyed_all, ...), custom_call_target="tpu_custom_call" | custom-call | tf_op jit(solution)/shard_map/back/pallas_call | solution.py:1392
  611.5 122.1 %sums.1 = (f32[128,5248]{1,0:T(8,128)}, bf16[256,2048]{1,0:T(8,128)(2,1)}) custom-call(bf16[256,2048]{1,0:T(8,128)(2,1)} %get-tuple-element.45.normed, bf16[256,2048]{1,0:T(8,128)(2,1)} %get-tuple-element.46.attended, bf16[256,3072]{1,0:T(8,128)(2,1)} %get-tuple-element.47.grad_qkv, bf16[256,2048]{1,0:T(8,128)(2,1)} %get-tuple-element.57.grad_out, ...), custom_call_target="tpu_custom_call" | custom-call | tf_op jit(solution)/shard_map/sums/pallas_call | solution.py:824
  733.6 0.0 copy-start.4
  733.6 0.0 copy-start.10
  733.6 3.2 fusion.8
  736.8 1.9 fusion.9
  738.7 1.3 slice_bitcast_fusion
  740.0 0.0 copy-done.4
  740.0 0.0 copy-done.10
  740.0 0.0 copy-start.3
  740.0 0.0 copy-start.9
  740.0 2.8 convert_add_fusion
  742.8 0.0 copy-done.3
  742.8 0.4 copy-done.9
  743.2 0.0 copy-start.2
  743.2 0.0 copy-start.8
  743.2 2.8 convert_add_fusion.1
  746.0 0.0 copy-done.2
  746.0 1.0 copy-done.8
  747.0 0.0 copy-start.1
  747.0 0.0 copy-start.7
  747.0 2.8 convert_add_fusion.2
  749.7 0.0 copy-done.1
  749.7 1.0 copy-done.7
  750.7 0.0 copy-start.11
  750.7 1.2 fusion
  752.0 0.1 copy-done.11
  752.0 1.0 copy.29
  (5 shorter events, 0.1 us)
Async XLA Ops:
  0.6 7.0 copy-start.13
  0.7 6.9 copy-start.12
  0.7 239.2 %collective-permute-start.2 = (bf16[512,2048]{1,0:T(8,128)(2,1)}, bf16[512,2048]{1,0:T(8,128)(2,1)}, u32[]{:S(2)}, u32[]{:S(2)}) collective-permute-start(bf16[512,2048]{1,0:T(8,128)(2,1)} %down_own.3), channel_id=1, source_target_pairs={{0,4},{4,0},{8,12},{12,8},{1,5},{5,1},{9,13},{13,9},{2,6},{6,2},{1... | collective-permute-start | bytes 6291464 | tf_op jit(solution)/shard_map/ppermute | solution.py:1630
  1.2 238.7 %collective-permute-start = (bf16[2048,512]{1,0:T(8,128)(2,1)}, bf16[2048,512]{1,0:T(8,128)(2,1)}, u32[]{:S(2)}, u32[]{:S(2)}) collective-permute-start(bf16[2048,512]{1,0:T(8,128)(2,1)} %gate_own.1), channel_id=1, source_target_pairs={{0,4},{4,0},{8,12},{12,8},{1,5},{5,1},{9,13},{13,9},{2,6},{6,2},{1... | collective-permute-start | bytes 6291464 | tf_op jit(solution)/shard_map/ppermute | solution.py:1630
  1.3 238.6 %collective-permute-start.1 = (bf16[2048,512]{1,0:T(8,128)(2,1)}, bf16[2048,512]{1,0:T(8,128)(2,1)}, u32[]{:S(2)}, u32[]{:S(2)}) collective-permute-start(bf16[2048,512]{1,0:T(8,128)(2,1)} %up_own.1), channel_id=1, source_target_pairs={{0,4},{4,0},{8,12},{12,8},{1,5},{5,1},{9,13},{13,9},{2,6},{6,2},{1... | collective-permute-start | bytes 6291464 | tf_op jit(solution)/shard_map/ppermute | solution.py:1630
  7.6 1.4 copy-start.6
  455.0 3.6 copy-start
  455.0 3.6 copy-start.5
  733.6 6.4 copy-start.4
  733.6 6.4 copy-start.10
  740.0 2.8 copy-start.3
  740.0 3.3 copy-start.9
  743.2 2.8 copy-start.2
  743.2 3.7 copy-start.8
  747.0 2.8 copy-start.1
  747.0 3.7 copy-start.7
  750.7 1.3 copy-start.11

commit v6 on v5

--- a/solution.py
+++ b/solution.py
@@ -177,9 +177,12 @@
 
     def order(self, k):
         z, n = self.z, self.line
+        low = 2 * z < n
         near = 2 * jnp.minimum(z, n - 1 - z)
-        alternate = jnp.where(k % 2 == 1, z - (k + 1) // 2, z + k // 2)
-        return jnp.where(k <= near, alternate, jnp.where(2 * z < n, k, n - 1 - k))
+        away = jnp.where(k % 2 == 1, -((k + 1) // 2), k // 2)
+        return jnp.where(
+            k <= near, z + jnp.where(low, away, -away), jnp.where(low, k, n - 1 - k)
+        )
 
     def slot(self, x, z):
         return x * self.line + z
@@ -207,12 +210,21 @@
     )
 
 
+def each(count, action):
+    def step(i, carry):
+        action(i)
+        return carry
+
+    lax.fori_loop(0, count, step, 0)
+
+
 class Gather:
-    def __init__(self, grid, block, everything, send, recv, parts):
+    def __init__(self, grid, block, everything, send, recv, parts, cross=None):
         self.grid, self.everything, self.send, self.recv = grid, everything, send, recv
-        self.block = block
-        self.parts = parts
+        self.block, self.cross = block, cross
         self.rows = everything.shape[1] // parts
+        self.last = parts - 1
+        self.early = parts if cross is None else parts - 1
 
     def piece(self, x, z, part):
         start = pl.multiple_of(part * self.rows, self.rows)
@@ -222,62 +234,121 @@
         grid = self.grid
         device = (grid.right, grid.left, grid.across)[link]
         there = self.piece(grid.x, z, part)
-        here = self.block.at[pl.ds(part * self.rows, self.rows)] if first else there
+        start = pl.multiple_of(part * self.rows, self.rows)
+        here = self.block.at[pl.ds(start, self.rows)] if first else there
         return remote(
             here, there, self.send.at[z, part, link], self.recv.at[grid.slot(grid.x, z), part], device
         )
 
-    def links(self, z, action, first=False):
+    def other(self, z, link):
         grid = self.grid
-        for part in range(self.parts):
-            for link, go in (
-                (0, jnp.logical_and(z <= grid.z, grid.has_right)),
-                (1, jnp.logical_and(z >= grid.z, grid.has_left)),
-            ):
-                pl.when(go)(lambda part=part, link=link: action(self.copy(z, part, link, first)))
-            action(self.copy(z, part, 2, first))
-
-    def send_own(self):
-        self.links(self.grid.z, lambda c: c.start(), True)
-
-    def forward(self, distance, part):
+        here = self.piece(1 - grid.x, z, self.last)
+        sem = self.recv.at[grid.slot(1 - grid.x, z), self.last]
+        return remote(here, here, self.cross.at[z, link], sem, (grid.right, grid.left)[link])
+
+    def ways(self, z):
         grid = self.grid
-        for z, there, link, go in (
+        return (
+            (0, jnp.logical_and(z <= grid.z, grid.has_right)),
+            (1, jnp.logical_and(z >= grid.z, grid.has_left)),
+        )
+
+    def sides(self, distance):
+        grid = self.grid
+        return (
             (grid.z - distance, grid.z >= distance, 0, grid.has_right),
             (grid.z + distance, grid.z + distance < grid.line, 1, grid.has_left),
-        ):
+        )
+
+    def links(self, z, part, action, first=False, across=True):
+        for link, go in self.ways(z):
+            pl.when(go)(lambda link=link: action(self.copy(z, part, link, first)))
+        if across:
+            action(self.copy(z, part, 2, first))
+
+    def send_own(self):
+        grid = self.grid
+        start = lambda c: c.start()
+        if self.cross is not None:
+            self.copy(grid.z, self.last, 2, True).start()
+        each(self.early, lambda part: self.links(grid.z, part, start, True))
+        if self.cross is not None:
+            self.links(grid.z, self.last, start, True, False)
+
+    def turn_in(self):
+        grid = self.grid
+        self.other(grid.z, 0).wait_recv()
+        for link, go in self.ways(grid.z):
+            pl.when(go)(lambda link=link: self.other(grid.z, link).start())
+
+    def forward(self, distance, part, wait=True, along=True, across=True):
+        for z, there, link, go in self.sides(distance):
 
             @pl.when(there)
             def _(z=z, link=link, go=go):
-                self.copy(z, part, 2).wait_recv()
-                pl.when(go)(lambda: self.copy(z, part, link).start())
-                self.copy(z, part, 2).start()
+                if wait:
+                    self.copy(z, part, 2).wait_recv()
+                if along:
+                    pl.when(go)(lambda: self.copy(z, part, link).start())
+                if across:
+                    self.copy(z, part, 2).start()
+
+    def forward_last(self, distance):
+        for z, there, link, go in self.sides(distance):
+
+            @pl.when(there)
+            def _(z=z, link=link, go=go):
+                self.copy(z, self.last, 2).wait_recv()
+                pl.when(go)(lambda: self.copy(z, self.last, link).start())
+                self.other(z, link).wait_recv()
+                pl.when(go)(lambda: self.other(z, link).start())
 
     def wait_across(self, z):
         grid = self.grid
-        for part in range(self.parts):
+
+        def wait(part):
             here = self.piece(1 - grid.x, z, part)
             sem = self.recv.at[grid.slot(1 - grid.x, z), part]
             remote(here, here, self.send.at[z, part, 2], sem, grid.across).wait_recv()
 
+        each(self.early, wait)
+
     def finish(self):
-        def step(z, carry):
-            self.links(z, lambda c: c.wait_send())
-            return carry
-
-        lax.fori_loop(0, self.grid.line, step, 0)
+        done = lambda c: c.wait_send()
+
+        def place(z):
+            each(self.early, lambda part: self.links(z, part, done))
+            if self.cross is not None:
+                self.links(z, self.last, done, across=False)
+                for link, go in self.ways(z):
+                    pl.when(go)(lambda link=link: self.other(z, link).wait_send())
+
+        each(self.grid.line, place)
+        if self.cross is not None:
+            self.copy(self.grid.z, self.last, 2).wait_send()
 
 
 class Scatter:
-    def __init__(self, grid, partial, from_across, from_line, total, sems, parts):
+    def __init__(self, grid, partial, from_across, from_line, total, sems, parts, cross=None):
         self.grid, self.partial, self.from_across = grid, partial, from_across
         self.from_line, self.total = from_line, total
         self.across_send, self.across_recv, self.line_send, self.line_recv = sems
-        self.parts = parts
+        self.parts, self.cross = parts, cross
         self.rows = partial.shape[1] // parts
+        self.early = parts if cross is None else parts - 1
+        self.last = parts - 1
 
     def run(self, part):
-        return pl.ds(part * self.rows, self.rows)
+        return pl.ds(pl.multiple_of(part * self.rows, self.rows), self.rows)
+
+    def steps(self):
+        return (self.grid.line - 1) * self.early
+
+    def rank(self, j):
+        return self.grid.order(self.grid.line - 1 - j)
+
+    def step(self, n):
+        self.pass_on(self.rank(n // self.early), n % self.early)
 
     def place(self, z):
         return z if self.from_across is None else self.grid.slot(self.grid.x, z)
@@ -292,61 +363,120 @@
             grid.across,
         )
 
+    def arrival(self, z, leftward):
+        return z if leftward else z - 1 + self.grid.line - 1
+
     def along(self, z, part, leftward):
         grid = self.grid
-        place = z if leftward else z - 1 + grid.line - 1
+        arrival = self.arrival(z, leftward)
         return remote(
             self.partial.at[self.place(z), self.run(part)],
-            self.from_line.at[place, self.run(part)],
+            self.from_line.at[arrival, self.run(part)],
             self.line_send.at[z, part],
-            self.line_recv.at[place, part],
+            self.line_recv.at[arrival, part],
             grid.left if leftward else grid.right,
         )
 
+    def other(self, z, leftward):
+        grid = self.grid
+        buffer, send, recv = self.cross
+        arrival = self.arrival(z, leftward)
+        return remote(
+            self.partial.at[grid.slot(1 - grid.x, z), self.run(self.last)],
+            buffer.at[arrival],
+            send.at[z],
+            recv.at[arrival],
+            grid.left if leftward else grid.right,
+        )
+
     def send_across(self, z):
-        for part in range(self.parts):
-            self.across(z, part).start()
-
-    def add_line(self, z, part, leftward):
-        self.along(z, part, leftward).wait_recv()
-        place = z if leftward else z - 1 + self.grid.line - 1
-        self.total[...] += self.from_line[place, self.run(part)].astype(F32)
+        each(self.early, lambda part: self.across(z, part).start())
+
+    def both_ways(self, z, action):
+        grid = self.grid
+        pl.when(jnp.logical_and(z <= grid.z, grid.has_right))(lambda: action(True))
+        pl.when(jnp.logical_and(z >= grid.z, grid.has_left))(lambda: action(False))
+
+    def add_line(self, z, part):
+        def add(leftward):
+            self.along(z, part, leftward).wait_recv()
+            arrival = self.arrival(z, leftward)
+            self.total[...] += self.from_line[arrival, self.run(part)].astype(F32)
+
+        self.both_ways(z, add)
 
     def gather_sum(self, z, part):
-        grid = self.grid
         value = self.partial[self.place(z), self.run(part)].astype(F32)
         if self.from_across is not None:
             self.across(z, part).wait_recv()
             value = value + self.from_across[z, self.run(part)].astype(F32)
         self.total[...] = value
-        pl.when(jnp.logical_and(z <= grid.z, grid.has_right))(lambda: self.add_line(z, part, True))
-        pl.when(jnp.logical_and(z >= grid.z, grid.has_left))(lambda: self.add_line(z, part, False))
-
-    def pass_on(self, z, parts=None):
+        self.add_line(z, part)
+
+    def send_along(self, z, part):
         grid = self.grid
-        for part in parts or range(self.parts):
-            self.gather_sum(z, part)
-            self.partial[self.place(z), self.run(part)] = self.total[...].astype(BF)
-            pl.when(z < grid.z)(lambda part=part: self.along(z, part, True).start())
-            pl.when(z > grid.z)(lambda part=part: self.along(z, part, False).start())
+        self.partial[self.place(z), self.run(part)] = self.total[...].astype(BF)
+        pl.when(z < grid.z)(lambda: self.along(z, part, True).start())
+        pl.when(z > grid.z)(lambda: self.along(z, part, False).start())
+
+    def pass_on(self, z, part):
+        self.gather_sum(z, part)
+        self.send_along(z, part)
+
+    def add_other(self, z):
+        grid, run = self.grid, self.run(self.last)
+        slot = grid.slot(1 - grid.x, z)
+        self.total[...] = self.partial[slot, run].astype(F32)
+
+        def add(leftward):
+            self.other(z, leftward).wait_recv()
+            self.total[...] += self.cross[0][self.arrival(z, leftward)].astype(F32)
+
+        self.both_ways(z, add)
+        self.partial[slot, run] = self.total[...].astype(BF)
+
+    def last_step(self, m):
+        grid = self.grid
+        z = grid.order(grid.line - 1 - m)
+        self.add_other(z)
+
+        @pl.when(z == grid.z)
+        def _():
+            self.across(z, self.last).start()
+
+        @pl.when(z != grid.z)
+        def _():
+            pl.when(z < grid.z)(lambda: self.other(z, True).start())
+            pl.when(z > grid.z)(lambda: self.other(z, False).start())
+            self.total[...] = self.partial[self.place(z), self.run(self.last)].astype(F32)
+            self.add_line(z, self.last)
+            self.send_along(z, self.last)
 
     def own(self, result):
-        for part in range(self.parts):
+        def part_sum(part):
             self.gather_sum(self.grid.z, part)
             result[self.run(part)] = self.total[...]
 
+        each(self.parts, part_sum)
+
     def finish(self):
         grid = self.grid
 
-        def step(z, carry):
-            for part in range(self.parts):
-                if self.from_across is not None:
-                    self.across(z, part).wait_send()
-                pl.when(z < grid.z)(lambda part=part: self.along(z, part, True).wait_send())
-                pl.when(z > grid.z)(lambda part=part: self.along(z, part, False).wait_send())
-            return carry
-
-        lax.fori_loop(0, grid.line, step, 0)
+        def place(z):
+            def part_done(part):
+                pl.when(z < grid.z)(lambda: self.along(z, part, True).wait_send())
+                pl.when(z > grid.z)(lambda: self.along(z, part, False).wait_send())
+
+            each(self.parts, part_done)
+            if self.from_across is not None:
+                each(self.early, lambda part: self.across(z, part).wait_send())
+            if self.cross is not None:
+                pl.when(z < grid.z)(lambda: self.other(z, True).wait_send())
+                pl.when(z > grid.z)(lambda: self.other(z, False).wait_send())
+
+        each(grid.line, place)
+        if self.cross is not None:
+            self.across(grid.z, self.last).wait_send()
 
 
 def scatter_scratch(line, rows, width, parts):
@@ -377,6 +507,7 @@
     part_gate, part_up, part_down,
     gate_w, up_w, down_w, hidden, dgate, dup, rows_n, rows_t,
     partial, from_across, from_line, total, across_send, across_recv, line_send, line_recv,
+    other_line, other_send, other_recv, gather_cross,
     gather_send, gather_recv, load_sem, wide, tile_sem, stage_a, stage_b, stage_sem, stage_recv, piece_a, piece_b, piece_sem, hidden_sem,
 ):
     grid = Grid(2, line)
@@ -385,15 +516,13 @@
     blocks = 2 * line
     me = grid.slot(grid.x, grid.z)
     grid.greet(True)
-    gathers = [
-        Gather(grid, normed, normed_all, gather_send.at[0], gather_recv.at[0], parts),
-    ]
+    gather = Gather(grid, normed, normed_all, gather_send, gather_recv, parts, gather_cross)
     scatter = Scatter(
         grid, partial, from_across, from_line, total,
         (across_send, across_recv, line_send, line_recv), parts,
-    )
-    for gather in gathers:
-        gather.send_own()
+        (other_line, other_send, other_recv),
+    )
+    gather.send_own()
     load_pairs(
         [
             (gate_own, gate_w.at[:, pl.ds(0, cols)]),
@@ -407,24 +536,40 @@
         load_sem,
     )
     load_pairs([(rows_n, normed_all.at[me])], load_sem)
-
-    def work(slot):
-        load_pairs([(normed_all.at[slot], rows_n), (tangent_all.at[slot], rows_t)], load_sem)
+    gather.turn_in()
+
+    forwards = (line - 1) * parts
+
+    def advance(n):
+        distance, part = n // parts + 1, n % parts
+
+        @pl.when(n < forwards)
+        def _():
+            pl.when(part < gather.early)(lambda: gather.forward(distance, part))
+            pl.when(part == gather.last)(lambda: gather.forward_last(distance))
+
+        return n + 1
+
+    def work(slot, n):
+        tangent_load = pltpu.make_async_copy(tangent_all.at[slot], rows_t, load_sem.at[1])
+        tangent_load.start()
+        load_pairs([(normed_all.at[slot], rows_n)], load_sem)
         spot = pl.ds(pl.multiple_of(slot * rows, rows), rows)
 
-        def hidden_tile(j, carry):
+        def hidden_tile(j, n):
             c = pl.ds(pl.multiple_of(j * cols, cols), cols)
             gate = dot(rows_n[...], gate_w[:, c], NN)
             up = dot(rows_n[...], up_w[:, c], NN)
+            pl.when(j == 0)(tangent_load.wait)
             grad = dot(rows_t[...], down_w[c, :], NT)
             sig = jax.nn.sigmoid(gate)
             silu = gate * sig
             hidden[spot, c] = (silu * up).astype(BF)
             dgate[spot, c] = (grad * up * (sig * (1.0 + gate * (1.0 - sig)))).astype(BF)
             dup[spot, c] = (grad * silu).astype(BF)
-            return carry
-
-        lax.fori_loop(0, 2, hidden_tile, 0)
+            return advance(n)
+
+        n = lax.fori_loop(0, 2, hidden_tile, n)
 
         def back_tile(j, carry):
             c = pl.ds(pl.multiple_of(j * cols, cols), cols)
@@ -433,37 +578,29 @@
             return carry
 
         lax.fori_loop(0, width // cols, back_tile, 0)
-
-    def stage(distance, carry):
-        @pl.when(distance + 1 < line)
-        def _():
-            for gather in gathers:
-                for part in range(parts):
-                    gather.forward(distance + 1, part)
-
-        def visit(i, inner):
+        return advance(n)
+
+    def stage(distance, n):
+        def visit(i, n):
             z = grid.z + jnp.where(i % 2 == 0, -distance, distance)
             inside = jnp.logical_and(z >= 0, z < line)
 
-            @pl.when(jnp.logical_and(inside, jnp.logical_or(distance > 0, i % 2 == 0)))
-            def _():
-                @pl.when(i >= 2)
-                def _():
-                    for gather in gathers:
-                        gather.wait_across(z)
-
-                work(grid.slot(jnp.where(i < 2, grid.x, 1 - grid.x), z))
-
-            return inner
-
-        lax.fori_loop(0, 4, visit, 0)
-        return carry
-
-    lax.fori_loop(0, line, stage, 0)
+            def block(n):
+                n = lax.fori_loop(n, jnp.maximum(n, distance * parts), lambda m, c: advance(m), n)
+                pl.when(i >= 2)(lambda: gather.wait_across(z))
+                return work(grid.slot(jnp.where(i < 2, grid.x, 1 - grid.x), z), n)
+
+            go = jnp.logical_and(inside, jnp.logical_or(distance > 0, i % 2 == 0))
+            return lax.cond(go, block, lambda n: n, n)
+
+        return lax.fori_loop(0, 4, visit, n)
+
+    count = lax.fori_loop(0, line, stage, 0)
+    lax.fori_loop(count, jnp.maximum(count, forwards), lambda m, c: advance(m), 0)
     hidden_copy = pltpu.make_async_copy(hidden, hidden_all, hidden_sem)
     hidden_copy.start()
-    for k in range(line - 1, -1, -1):
-        scatter.send_across(grid.order(k))
+    for j in range(line):
+        scatter.send_across(scatter.rank(j))
 
     tiles = width // tile
 
@@ -568,18 +705,26 @@
             for copy in results(t):
                 copy.start()
 
-        for k in range(line - 1, 0, -1):
-            when = 2 * tiles - 1 - (k - 1) * (tiles // (line - 1))
-            pl.when(t == when)(lambda k=k: scatter.pass_on(grid.order(k)))
+        n = t - 2 * lag
+        pl.when(n >= 0)(lambda: scatter.step(n))
+        m = t // 3 - lag
+        ready = jnp.logical_and(t % 3 == 2, jnp.logical_and(m >= 0, m < line))
+        pl.when(ready)(lambda: scatter.last_step(m))
         return carry
 
+    lag = jnp.where(jnp.logical_and(grid.has_left, grid.has_right), 1, 0)
     lax.fori_loop(0, 2 * tiles, weights, 0)
+
+    def rest(n, carry):
+        scatter.step(n)
+        return carry
+
+    lax.fori_loop(2 * tiles - 2 * lag, scatter.steps(), rest, 0)
     scatter.own(grad_sum)
     for t in (2 * tiles - 2, 2 * tiles - 1):
         for copy in results(t):
             copy.wait()
-    for gather in gathers:
-        gather.finish()
+    gather.finish()
     scatter.finish()
     hidden_copy.wait()
 
@@ -587,7 +732,7 @@
 def feed_call(normed, tangent_all, gates, ups, downs, line):
     rows, width = normed.shape
     cols = gates[0].shape[1]
-    blocks, parts, tile = 2 * line, 2, 256
+    blocks, parts, tile = 2 * line, 8, 256
     tiles = width // tile
     tall = blocks * rows
     shapes = jax.ShapeDtypeStruct
@@ -607,7 +752,10 @@
             pltpu.VMEM((tall, 2 * cols), BF), pltpu.VMEM((tall, 2 * cols), BF), pltpu.VMEM((tall, 2 * cols), BF),
             pltpu.VMEM((rows, width), BF), pltpu.VMEM((rows, width), BF),
             *scatter_scratch(line, rows, width, parts),
-            pltpu.SemaphoreType.DMA((1, line, parts, 3)), pltpu.SemaphoreType.DMA((1, blocks, parts)),
+            pltpu.VMEM((2 * line - 2, rows // parts, width), BF),
+            pltpu.SemaphoreType.DMA((line,)), pltpu.SemaphoreType.DMA((2 * line - 2,)),
+            pltpu.SemaphoreType.DMA((line, 2)),
+            pltpu.SemaphoreType.DMA((line, parts, 3)), pltpu.SemaphoreType.DMA((blocks, parts)),
             pltpu.SemaphoreType.DMA((8,)),
             pltpu.VMEM((2, 2, blocks, rows, tile), BF), pltpu.SemaphoreType.DMA((2, 2)),
             pltpu.VMEM((2, 2, tile, cols), BF), pltpu.VMEM((2, cols, tile), BF),
@@ -625,14 +773,14 @@
 class Thirds(Scatter):
     def run(self, part):
         quarter = self.rows
-        if part == 2:
-            return pl.ds(pl.multiple_of(self.grid.replica * quarter, quarter), quarter)
-        return pl.ds((2 + part) * quarter, quarter)
+        start = jnp.where(part == 2, self.grid.replica, 2 + part) * quarter
+        return pl.ds(pl.multiple_of(start, quarter), quarter)
 
 
 def sums_kernel(
     line,
-    normed, attended, grad_qkv, grad_out, tokens, grad_middle, weights, gain, term_two,
+    normed, attended, grad_qkv, grad_out, twin_normed, twin_attended, twin_out,
+    tokens, grad_middle, weights, gain, term_two,
     result, grad_tokens,
     both_normed, both_attended, both_qkv, both_out, load_sem, twin_send, twin_recv,
     partial, from_across, from_line, total, across_send, across_recv, line_send, line_recv,
@@ -651,19 +799,20 @@
     )
     scatter.rows = quarter
     own, twin = pl.ds(0, rows), pl.ds(rows, rows)
-    pairs = [
-        (grad_qkv, both_qkv.at[own], both_qkv.at[twin]),
-        (normed, both_normed.at[own], both_normed.at[twin]),
-        (grad_out, both_out.at[own], both_out.at[twin]),
-        (attended, both_attended.at[own], both_attended.at[twin]),
-    ]
-    swaps = [
-        remote(src, there, twin_send.at[i], twin_recv.at[i], grid.twin)
-        for i, (src, _, there) in enumerate(pairs)
-    ]
-    for copy in swaps:
-        copy.start()
-    load_pairs([(src, here) for src, here, _ in pairs], load_sem)
+    swap_qkv = remote(grad_qkv, both_qkv.at[twin], twin_send.at[0], twin_recv.at[0], grid.twin)
+    swap_qkv.start()
+    load_pairs(
+        [
+            (attended, both_attended.at[own]),
+            (twin_attended, both_attended.at[twin]),
+            (grad_out, both_out.at[own]),
+            (twin_out, both_out.at[twin]),
+            (normed, both_normed.at[own]),
+            (twin_normed, both_normed.at[twin]),
+            (grad_qkv, both_qkv.at[own]),
+        ],
+        load_sem,
+    )
     later = [
         pltpu.make_async_copy(src, dst, weight_sem.at[i])
         for i, (src, dst) in enumerate(
@@ -676,8 +825,6 @@
     ]
     for copy in later:
         copy.start()
-    for copy in swaps:
-        copy.wait()
     tall = line * run
     tile = 512
     away = pl.ds(pl.multiple_of((1 - grid.replica) * quarter, quarter), quarter)
@@ -706,8 +853,9 @@
 
             lax.fori_loop(0, right.shape[1] // tile, step, 0)
 
+        wide(both_attended, both_out, narrow)
+        pl.when(j == 0)(swap_qkv.wait)
         wide(both_normed, both_qkv, 0)
-        wide(both_attended, both_out, narrow)
         partial[blocks, :, narrow + width :] = jnp.zeros((line, run, 128), BF)
         for k in range(line - 1, -1, -1):
             z = grid.order(k)
@@ -745,7 +893,7 @@
     lax.fori_loop(0, rows // chunk, norm_step, 0)
     terms[1:2, :] = term_two[...]
     own_terms[...] = terms[...].astype(BF)
-    swap_terms = remote(own_terms, twin_terms, twin_send.at[4], twin_recv.at[4], grid.twin)
+    swap_terms = remote(own_terms, twin_terms, twin_send.at[1], twin_recv.at[1], grid.twin)
     swap_terms.start()
     swap_terms.wait()
     for x in range(2):
@@ -779,7 +927,7 @@
 
     def sweep(part):
         def step(i, carry):
-            scatter.pass_on(grid.order(line - 1 - i), (part,))
+            scatter.pass_on(grid.order(line - 1 - i), part)
             return carry
 
         lax.fori_loop(0, line - 1, step, 0)
@@ -813,7 +961,9 @@
     lax.fori_loop(0, 2 * line, sent, 0)
 
 
-def sums_call(normed, attended, grad_qkv, grad_out, tokens, grad_middle, weights, gain, term_two, line):
+def sums_call(
+    normed, attended, grad_qkv, grad_out, twins, tokens, grad_middle, weights, gain, term_two, line
+):
     rows, width = normed.shape
     narrow = grad_qkv.shape[1]
     run, whole = weights.shape[1:]
@@ -826,12 +976,12 @@
         out_shape=(
             jax.ShapeDtypeStruct((run, whole), F32), jax.ShapeDtypeStruct((rows, width), BF),
         ),
-        in_specs=[ANY] * 7 + [vmem] * 2,
+        in_specs=[ANY] * 10 + [vmem] * 2,
         out_specs=(vmem, vmem),
         scratch_shapes=[
             pltpu.VMEM((2 * rows, width), BF), pltpu.VMEM((2 * rows, width), BF),
             pltpu.VMEM((2 * rows, narrow), BF), pltpu.VMEM((2 * rows, width), BF),
-            dma((4,)), dma((5,)), dma((5,)),
+            dma((7,)), dma((2,)), dma((2,)),
             pltpu.VMEM((2 * line, run, whole), BF), pltpu.VMEM((line, run, whole), BF),
             pltpu.VMEM((2 * line - 2, run, whole), BF), pltpu.VMEM((quarter, whole), F32),
             dma((line, 3)), dma((line, 3)), dma((line, 3)), dma((2 * line - 2, 3)),
@@ -845,10 +995,14 @@
             collective_id=3, has_side_effects=True, vmem_limit_bytes=63 * 2**20
         ),
         name="sums",
-    )(normed, attended, grad_qkv, grad_out, tokens, grad_middle, weights, gain, term_two)
-
-
-def gather_weights(grid, block, everything, send, recv, twin_send, twin_recv, meanwhile):
+    )(
+        normed, attended, grad_qkv, grad_out, *twins, tokens, grad_middle, weights, gain, term_two
+    )
+
+
+def gather_weights(
+    grid, block, everything, send, recv, twin_send, twin_recv, meanwhile, afterwards
+):
     line = grid.line
     rows = block.shape[0] // 4
     carry_a, carry_b = grid.replica * 2, grid.replica * 2 + 1
@@ -908,19 +1062,21 @@
         )
 
     def step(distance, carry):
-        for z, there, link, go in sides(distance):
-
-            @pl.when(there)
-            def _(z=z, link=link, go=go):
-                for x, quarter in (
-                    (grid.x, carry_a),
-                    (grid.x, carry_b),
-                    (1 - grid.x, carry_b),
-                ):
-                    arrived(x, z, quarter)
+        for x, quarter in (
+            (grid.x, carry_a),
+            (grid.x, carry_b),
+            (1 - grid.x, carry_b),
+        ):
+            for z, there, link, go in sides(distance):
+
+                @pl.when(there)
+                def _(x=x, quarter=quarter, z=z, link=link, go=go):
+                    copy(x, z, quarter, across).wait_recv()
+                    pl.when(go)(lambda: copy(x, z, quarter, link).start())
                     copy(x, z, quarter, mirror).start()
-                    pl.when(go)(lambda x=x, quarter=quarter: copy(x, z, quarter, link).start())
-                copy(grid.x, z, carry_a, across).start()
+                    if quarter is carry_a:
+                        copy(x, z, quarter, across).start()
+                    share(x, z, quarter).start()
 
         for z, there, _, _ in sides(distance - 1):
 
@@ -932,6 +1088,7 @@
         return carry
 
     lax.fori_loop(1, line + 1, step, 0)
+    afterwards()
 
     def last(z, carry):
         arrived(1 - grid.x, z, carry_a)
@@ -1045,7 +1202,7 @@
 
 def front_kernel(
     line, parts,
-    block, tokens, tangent, bias, cosine, sine,
+    query_w, key_w, value_w, extra_w, out_w, tokens, tangent, bias, cosine, sine,
     attended, middle, normed, first_normed, queries, logs, keyed_out, tangent_all, weights_out,
     everything, keyed, keyed_all, bias_v, token_v, cosine_v, sine_v, gain, scores, probs, sums, stage, load_sem,
     key_send, key_recv, send, recv, own_sem, weight_send, weight_recv, twin_send, twin_recv,
@@ -1059,12 +1216,17 @@
     me = grid.slot(grid.x, grid.z)
     chunk = rows // 2
     tile = 512
+    block = everything.at[(grid.x * 2 + grid.core) * line + grid.z]
+    first, packs = 0, []
+    for part in (query_w, key_w, value_w, extra_w, out_w):
+        packs.append((part, block.at[:, pl.ds(first, part.shape[1])]))
+        first += part.shape[1]
+    load_pairs(packs, load_sem)
     grid.greet(True, True)
 
     def meanwhile():
         load_pairs(
             [
-                (block, everything.at[(grid.x * 2 + grid.core) * line + grid.z]),
                 (tangent, stage),
                 (bias, bias_v),
                 (tokens, token_v),
@@ -1075,8 +1237,10 @@
         )
         load_pairs([(stage, tangent_all.at[me])], own_sem)
 
+    gather = Gather(grid, tangent, tangent_all, send, recv, parts)
     gather_weights(
-        grid, block, everything, weight_send, weight_recv, twin_send, twin_recv, meanwhile
+        grid, block, everything, weight_send, weight_recv, twin_send, twin_recv, meanwhile,
+        gather.send_own,
     )
     weights_copy = pltpu.make_async_copy(everything, weights_out, own_sem.at[1])
     weights_copy.start()
@@ -1108,10 +1272,9 @@
             slice(width + narrow + first, width + narrow + first + tile)
         ).astype(BF)
     line_keys = Line(grid, keyed, keyed_all, key_send, key_recv)
-    gather = Gather(grid, tangent, tangent_all, send, recv, parts)
     line_keys.send_own()
     for part in range(parts):
-        gather.copy(grid.z, part, 2, True).start()
+        gather.forward(1, part, along=False)
     keyed_all[grid.z] = keyed[...]
 
     def query_step(j, carry):
@@ -1120,26 +1283,17 @@
         return carry
 
     lax.fori_loop(0, width // tile, query_step, 0)
-    for distance in range(line):
-        if distance:
-            line_keys.forward(distance)
-        for link, go in (
-            (0, jnp.logical_and(grid.z == distance, grid.has_right)),
-            (1, jnp.logical_and(line - 1 - grid.z == distance, grid.has_left)),
-        ):
-
-            @pl.when(go)
-            def _(link=link):
-                for part in range(parts):
-                    gather.copy(grid.z, part, link, True).start()
-
+    for distance in range(1, line):
+        line_keys.forward(distance)
+    for part in range(parts):
+        gather.forward(1, part, wait=False, across=False)
 
     logs[...] = jnp.zeros_like(logs)
     pairs = width // (2 * HEAD_SIZE)
     group = pairs // (narrow // (2 * HEAD_SIZE))
 
     def advance(n):
-        gather.forward(n // parts + 1, n % parts)
+        gather.forward(n // parts + 2, n % parts)
 
     def pair_step(i, carry):
         c = pl.ds(pl.multiple_of(i * 128, 128), 128)
@@ -1165,13 +1319,12 @@
         out = dot(probs[...], values, NN) * sums[...]
         attended[:, c] = unhalves(out, half).astype(BF)
 
-        pl.when(i % 3 == 2)(lambda: advance(i // 3))
+        pl.when(i % 2 == 1)(lambda: advance(i // 2))
         return carry
 
     lax.fori_loop(0, pairs, pair_step, 0)
     keyed_copy = pltpu.make_async_copy(keyed_all, keyed_out, load_sem.at[0])
     keyed_copy.start()
-    advance(pairs // 3)
 
     def out_step(j, carry):
         c = pl.ds(pl.multiple_of(j * tile, tile), tile)
@@ -1187,7 +1340,7 @@
         advance(n)
         return carry
 
-    lax.fori_loop(pairs // 3 + 1, (line - 1) * parts, rest, 0)
+    lax.fori_loop(pairs // 2, (line - 2) * parts, rest, 0)
     for z in range(line):
         gather.wait_across(z)
     keyed_copy.wait()
@@ -1196,8 +1349,10 @@
     gather.finish()
 
 
-def front_call(block, tokens, tangent, bias, cosine, sine, line, narrow):
+def front_call(pieces, tokens, tangent, bias, cosine, sine, line):
     rows, width = tokens.shape
+    narrow = pieces[1].shape[1]
+    unit = (pieces[0].shape[0], sum(p.shape[1] for p in pieces))
     total = bias.shape[1]
     blocks, parts = 2 * line, 4
     shapes = jax.ShapeDtypeStruct
@@ -1209,12 +1364,12 @@
             shapes((rows, width), BF), shapes((rows, width), F32), shapes((rows, width), BF),
             shapes((rows, width), BF), shapes((rows, width), BF),
             shapes((2 * rows, 128), F32), shapes((line, rows, 2 * narrow), BF),
-            shapes((blocks, rows, width), BF), shapes((2 * blocks,) + block.shape, BF),
+            shapes((blocks, rows, width), BF), shapes((2 * blocks,) + unit, BF),
         ),
-        in_specs=[ANY] * 6,
+        in_specs=[ANY] * 10,
         out_specs=(vmem,) * 6 + (ANY,) * 3,
         scratch_shapes=[
-            pltpu.VMEM((2 * blocks,) + block.shape, BF),
+            pltpu.VMEM((2 * blocks,) + unit, BF),
             pltpu.VMEM((rows, 2 * narrow), BF), pltpu.VMEM((line, rows, 2 * narrow), BF),
             like(bias), like(tokens), like(cosine), like(sine), pltpu.VMEM((2, width), F32),
             pltpu.VMEM((2 * rows, total), F32), pltpu.VMEM((2 * rows, total), BF),
@@ -1229,14 +1384,14 @@
             collective_id=5, has_side_effects=True, vmem_limit_bytes=62 * 2**20
         ),
         name="front",
-    )(block, tokens, tangent, bias, cosine, sine)
+    )(*pieces, tokens, tangent, bias, cosine, sine)
 
 
 def back_kernel(
-    line, parts, pass_at,
+    line, parts,
     queries, keyed_all, grad_out, bias, logs, hidden_all, down_own, down_twin, weights, cosine, sine,
-    gate_sum, up_sum, down_sum,
-    branch, grad_qkv, gate_mirror, up_mirror, down_mirror,
+    gate_sum, up_sum, down_sum, normed, attended,
+    branch, grad_qkv, gate_mirror, up_mirror, down_mirror, twin_normed, twin_attended, twin_out,
     out_v, out_w, cosine_v, sine_v, grad_keyed, mirror_send, mirror_recv,
     query_v, keyed_v, grad_v, bias_v, log_v, scores, gradients, probs, slopes, key_sum, value_sum,
     down_w, hidden, load_sem,
@@ -1248,7 +1403,15 @@
     rows = partial.shape[1]
     narrow = keyed_all.shape[2] // 2
     length = bias.shape[1]
-    grid.greet(False, True)
+    grid.greet(True, True)
+    swapped = [
+        remote(src, dst, mirror_send.at[3 + i], mirror_recv.at[3 + i], grid.twin)
+        for i, (src, dst) in enumerate(
+            ((normed, twin_normed), (attended, twin_attended), (grad_out, twin_out))
+        )
+    ]
+    for copy in swapped:
+        copy.start()
     mirrored = [
         remote(src, dst, mirror_send.at[i], mirror_recv.at[i], grid.mirror)
         for i, (src, dst) in enumerate(
@@ -1357,31 +1520,38 @@
             key_partial[:, :, key_cols] = key_sum[...].astype(BF).reshape(line, rows, 128)
             key_partial[:, :, value_cols] = value_sum[...].astype(BF).reshape(line, rows, 128)
 
-        for k, when in zip(range(line - 1, 0, -1), pass_at):
-            pl.when(i == when)(lambda k=k: scatter.pass_on(grid.order(k)))
+        pl.when(i % pace == 0)(lambda: scatter.step(i // pace + early))
         return carry
 
+    pace = 4
+    early = jnp.where(jnp.logical_and(grid.has_left, grid.has_right), 0, 1)
+    pl.when(early == 1)(lambda: scatter.step(0))
     lax.fori_loop(0, pairs, pair_step, 0)
 
+    def rest(n, carry):
+        scatter.step(n)
+        return carry
+
+    lax.fori_loop(pairs // pace + early, scatter.steps(), rest, 0)
+
     def along(i, carry):
-        keyed_scatter.pass_on(grid.order(line - 1 - i))
+        keyed_scatter.step(i)
         return carry
 
-    lax.fori_loop(0, line - 1, along, 0)
-    for k in range(line - 1 - len(pass_at), 0, -1):
-        scatter.pass_on(grid.order(k))
+    lax.fori_loop(0, keyed_scatter.steps(), along, 0)
     scatter.own(branch)
     keyed_scatter.own(grad_keyed)
     grad_qkv[:, width : width + narrow] = turn(grad_keyed[:, :narrow], cosine_v, sine_v, 1.0)
     grad_qkv[:, width + narrow :] = grad_keyed[:, narrow:].astype(BF)
-    for copy in mirrored:
+    for copy in mirrored + swapped:
         copy.wait()
     scatter.finish()
     keyed_scatter.finish()
 
 
 def back_call(
-    queries, keyed_all, grad_out, bias, logs, hidden_all, downs, weights, cosine, sine, sums, line
+    queries, keyed_all, grad_out, bias, logs, hidden_all, downs, weights, cosine, sine, sums,
+    normed, attended, line,
 ):
     rows, width = queries.shape
     both = keyed_all.shape[2]
@@ -1390,17 +1560,17 @@
     shapes = jax.ShapeDtypeStruct
     vmem = pl.BlockSpec(memory_space=pltpu.VMEM)
     return pl.pallas_call(
-        functools.partial(back_kernel, line, parts, (4, 9, 15)),
+        functools.partial(back_kernel, line, parts),
         out_shape=(
             shapes((rows, width), F32), shapes((rows, width + both), BF),
-            *(shapes(s.shape, BF) for s in sums),
+            *(shapes(s.shape, BF) for s in sums), *(shapes((rows, width), BF),) * 3,
         ),
-        in_specs=[ANY] * 14,
-        out_specs=(vmem,) * 2 + (ANY,) * 3,
+        in_specs=[ANY] * 16,
+        out_specs=(vmem,) * 2 + (ANY,) * 6,
         scratch_shapes=[
             pltpu.VMEM((rows, width), BF), pltpu.VMEM((4, weights.shape[1], width), BF),
             pltpu.VMEM(cosine.shape, F32), pltpu.VMEM(sine.shape, F32), pltpu.VMEM((rows, both), F32),
-            pltpu.SemaphoreType.DMA((3,)), pltpu.SemaphoreType.DMA((3,)),
+            pltpu.SemaphoreType.DMA((6,)), pltpu.SemaphoreType.DMA((6,)),
             pltpu.VMEM((rows, width), BF), pltpu.VMEM(keyed_all.shape, BF), pltpu.VMEM((rows, width), BF),
             pltpu.VMEM((rows, length), F32), pltpu.VMEM(logs.shape, F32),
             pltpu.VMEM((2 * rows, length), F32), pltpu.VMEM((2 * rows, length), F32),
@@ -1418,7 +1588,8 @@
         ),
         name="back",
     )(
-        queries, keyed_all, grad_out, bias, logs, hidden_all, *downs, weights, cosine, sine, *sums
+        queries, keyed_all, grad_out, bias, logs, hidden_all, *downs, weights, cosine, sine, *sums,
+        normed, attended,
     )
 
 
@@ -1634,7 +1805,7 @@
         HEAD_SIZE // 2
     )
     extra = jnp.pad(jnp.stack([gain_attn, gain_mlp]), ((0, run - 2), (0, 0)))
-    block = jnp.concatenate([w_query, key_projection, value_projection, extra, w_out], axis=1)
+    pieces = (w_query, key_projection, value_projection, extra, w_out)
     cosine, sine = jnp.cos(rotary_angles), jnp.sin(rotary_angles)
     cosine = jnp.concatenate([cosine] * 4, axis=1)
     sine = jnp.concatenate([-sine, sine] * 2, axis=1)
@@ -1645,7 +1816,7 @@
     rows = tokens.reshape(segment_length, width)
     (
         attended, middle, normed_mlp, normed_tokens, scaled_query, logs, keyed_all, tangent_all, weights,
-    ) = front_call(block, rows, tangent, bias, cosine, sine, line, narrow)
+    ) = front_call(pieces, rows, tangent, bias, cosine, sine, line)
     mid = width + 2 * narrow
     gain_first = weights[:, 0, mid : mid + run].reshape(width).astype(f32)
     gain_second = weights[:, 1, mid : mid + run].reshape(width).astype(f32)
@@ -1658,16 +1829,16 @@
         scaled_two - unit_two * jnp.mean(scaled_two * unit_two, axis=-1, keepdims=True)
     )
     grad_branch = grad_middle.astype(bf16)
-    branch, grad_qkv, *mirrored = back_call(
+    branch, grad_qkv, *others = back_call(
         scaled_query, keyed_all, grad_branch, bias, logs, hidden_all, downs, weights, cosine, -sine,
-        sums, line,
+        sums, normed_tokens, attended, line,
     )
     outcome = middle + branch
     grad_w_gate, grad_w_up, grad_w_down = (
-        a.astype(f32) + b.astype(f32) for a, b in zip(sums, mirrored)
+        a.astype(f32) + b.astype(f32) for a, b in zip(sums, others[:3])
     )
     packed, grad_tokens = sums_call(
-        normed_tokens, attended, grad_qkv, grad_branch, rows, grad_middle, weights,
+        normed_tokens, attended, grad_qkv, grad_branch, others[3:], rows, grad_middle, weights,
         gain_first.reshape(1, width), term_gain_two.reshape(1, width), line,
     )
     gains = packed[run * 3 // 4 : run * 3 // 4 + 2, mid + width :]

time: 754 us -> 680 us (0.902)
  Pallas kernels: 714 us -> 642 us
    pallas_call x1, Pallas kernels: 228 us -> 196 us  [front_call(): pl.pallas_call(functools.partial(front_kernel, line, parts), out_shape=(s...]
    pallas_call x1, Pallas kernels: 215 us -> 186 us  [feed_call(): pl.pallas_call(functools.partial(feed_kernel, line, parts, tile), out_sha...]
    pallas_call x1, Pallas kernels: 149 us -> 141 us  [back_call(): pl.pallas_call(functools.partial(back_kernel, line, parts), out_shape=(sh...]
  transfers between devices with their start and end apart: 3 -> 3, of which waited for: 0 -> 0; matrix products, arithmetic and copies ran while one was open for 1% -> 1% of each run, Pallas kernels for 30% -> 29%
where the time goes in v6:
time: 680 us; the launch traced here: 679 us
  Pallas kernels  642 us (94%)
  other arithmetic  24.5 us (4%)
  local copies, waits for them, and re-layouts  10.5 us (2%)
    pallas_call x1, Pallas kernels, front_call(): pl.pallas_call(functools.partial(front_kernel, line, parts), out_shape=(s...  196 us
    pallas_call x1, Pallas kernels, feed_call(): pl.pallas_call(functools.partial(feed_kernel, line, parts, tile), out_sha...  186 us
    pallas_call x1, Pallas kernels, back_call(): pl.pallas_call(functools.partial(back_kernel, line, parts), out_shape=(sh...  141 us
    pallas_call x1, Pallas kernels, sums_call(): pl.pallas_call(functools.partial(sums_kernel, line), out_shape=(jax.Shape...  120 us
  transfers between devices with their start and end apart: 3, of which 0 were waited for; matrix products, arithmetic and copies ran while one was open for 1% of the time, Pallas kernels for 29%

profile of v6, /device:TPU:0, one launch (start us, length us, event | category | flops | bytes accessed | tf_op | source)
XLA Modules:
  0.0 678.6 jit_solution(11778113451559917448)
XLA Ops:
  0.6 0.5 collective-permute-start.2
  1.2 0.1 collective-permute-start
  1.2 0.4 collective-permute-start.1
  1.7 0.7 constant_dynamic-slice_fusion
  2.4 1.3 fusion.4.extra_w
  3.7 0.5 fusion.3
  4.2 1.0 fusion.5
  5.2 1.8 compare_select_fusion.bias
  7.0 195.6 %front.1 = (bf16[256,2048]{1,0:T(8,128)(2,1)}, f32[256,2048]{1,0:T(8,128)}, bf16[256,2048]{1,0:T(8,128)(2,1)}, bf16[256,2048]{1,0:T(8,128)(2,1)}, bf16[256,2048]...) custom-call(bf16[128,2048]{1,0:T(8,128)(2,1)} %query_w.1, ...), custom_call_target="tpu_custom_call" | custom-call | tf_op jit(solution)/shard_map/front/pallas_call | solution.py:1361
  202.7 1.8 multiply_reduce_fusion.2
  204.5 1.4 bitcast_convert_fusion
  205.9 0.0 collective-permute-done.2.down_twin
  205.9 0.0 collective-permute-done.gate_twin
  205.9 0.0 collective-permute-done.1.up_twin
  205.9 185.7 %feed.1 = (f32[256,2048]{1,0:T(8,128)}, bf16[8,256,2048]{2,1,0:T(8,128)(2,1)}, bf16[2048,1024]{1,0:T(8,128)(2,1)}, bf16[2048,512]{1,0:T(8,128)(2,1)}, bf16[2048,...) custom-call(bf16[256,2048]{1,0:T(8,128)(2,1)} %get-tuple-element.38., ...), custom_call_target="tpu_custom_call" | custom-call | tf_op jit(solution)/shard_map/feed/pallas_call | solution.py:740
  391.7 0.0 copy-start
  391.7 0.0 copy-start.2
  391.7 3.5 multiply_reduce_fusion
  395.2 0.0 copy-done
  395.2 0.0 copy-done.2
  395.2 3.5 fusion.6
  398.7 140.8 %back.1 = (f32[256,2048]{1,0:T(8,128)}, bf16[256,3072]{1,0:T(8,128)(2,1)}, bf16[2048,512]{1,0:T(8,128)(2,1)}, bf16[2048,512]{1,0:T(8,128)(2,1)}, bf16[512,2048]{...) custom-call(bf16[256,2048]{1,0:T(8,128)(2,1)} %get-tuple-element.36.queries, ...), custom_call_target="tpu_custom_call" | custom-call | tf_op jit(solution)/shard_map/back/pallas_call | solution.py:1562
  539.5 119.7 %sums.1 = (f32[128,5248]{1,0:T(8,128)}, bf16[256,2048]{1,0:T(8,128)(2,1)}) custom-call(bf16[256,2048]{1,0:T(8,128)(2,1)} %get-tuple-element.47.normed, bf16[256,2048]{1,0:T(8,128)(2,1)} %get-tuple-element.48.attended, bf16[256,3072]{1,0:T(8,128)(2,1)} %get-tuple-element.50.grad_qkv, bf16[256,2048]{1,0:T(8,128)(2,1)} %get-tuple-element.63.grad_out, ...), custom_call_target="tpu_custom_call" | custom-call | tf_op jit(solution)/shard_map/sums/pallas_call | solution.py:974
  659.2 0.0 copy-start.5
  659.2 0.0 copy-start.9
  659.2 3.2 fusion.7
  662.5 1.9 fusion.8
  664.3 1.3 slice_bitcast_fusion
  665.6 0.0 copy-done.5
  665.6 0.0 copy-done.9
  665.6 0.0 copy-start.4
  665.6 0.0 copy-start.8
  665.6 2.8 convert_add_fusion
  668.4 0.0 copy-done.4
  668.4 0.4 copy-done.8
  668.9 0.0 copy-start.3
  668.9 0.0 copy-start.7
  668.9 2.8 convert_add_fusion.1
  671.6 0.0 copy-done.3
  671.6 1.0 copy-done.7
  672.6 0.0 copy-start.1
  672.6 0.0 copy-start.6
  672.6 2.8 convert_add_fusion.2
  675.4 0.0 copy-done.1
  675.4 1.0 copy-done.6
  676.3 0.0 copy-start.10
  676.3 1.2 fusion
  677.6 0.1 copy-done.10
  677.6 1.0 copy.25
  (4 shorter events, 0.0 us)
Async XLA Ops:
  0.6 205.3 %collective-permute-start.2 = (bf16[512,2048]{1,0:T(8,128)(2,1)}, bf16[512,2048]{1,0:T(8,128)(2,1)}, u32[]{:S(2)}, u32[]{:S(2)}) collective-permute-start(bf16[512,2048]{1,0:T(8,128)(2,1)} %down_own.3), channel_id=1, source_target_pairs={{0,4},{4,0},{8,12},{12,8},{1,5},{5,1},{9,13},{13,9},{2,6},{6,2},{1... | collective-permute-start | bytes 6291464 | tf_op jit(solution)/shard_map/ppermute | solution.py:1801
  1.2 204.8 %collective-permute-start = (bf16[2048,512]{1,0:T(8,128)(2,1)}, bf16[2048,512]{1,0:T(8,128)(2,1)}, u32[]{:S(2)}, u32[]{:S(2)}) collective-permute-start(bf16[2048,512]{1,0:T(8,128)(2,1)} %gate_own.1), channel_id=1, source_target_pairs={{0,4},{4,0},{8,12},{12,8},{1,5},{5,1},{9,13},{13,9},{2,6},{6,2},{1... | collective-permute-start | bytes 6291464 | tf_op jit(solution)/shard_map/ppermute | solution.py:1801
  1.2 204.7 %collective-permute-start.1 = (bf16[2048,512]{1,0:T(8,128)(2,1)}, bf16[2048,512]{1,0:T(8,128)(2,1)}, u32[]{:S(2)}, u32[]{:S(2)}) collective-permute-start(bf16[2048,512]{1,0:T(8,128)(2,1)} %up_own.1), channel_id=1, source_target_pairs={{0,4},{4,0},{8,12},{12,8},{1,5},{5,1},{9,13},{13,9},{2,6},{6,2},{1... | collective-permute-start | bytes 6291464 | tf_op jit(solution)/shard_map/ppermute | solution.py:1801
  391.7 3.6 copy-start
  391.7 3.6 copy-start.2
  659.2 6.4 copy-start.5
  659.2 6.4 copy-start.9
  665.6 2.8 copy-start.4
  665.6 3.3 copy-start.8
  668.9 2.8 copy-start.3
  668.9 3.7 copy-start.7
  672.6 2.8 copy-start.1
  672.6 3.7 copy-start.6
  676.3 1.3 copy-start.10

commit v7 on v6

--- a/solution.py
+++ b/solution.py
@@ -155,6 +155,9 @@
 NN = (((1,), (0,)), ((), ()))
 NT = (((1,), (1,)), ((), ()))
 TN = (((0,), (0,)), ((), ()))
+
+
+EARLY = 3
 
 
 def dot(left, right, dims):
@@ -504,7 +507,8 @@
     line, parts, tile,
     normed, tangent_all, gate_own, gate_twin, up_own, up_twin, down_own, down_twin,
     grad_sum, normed_all, hidden_all, grad_gate, grad_up, grad_down,
-    part_gate, part_up, part_down,
+    mirror_gate, mirror_up, mirror_down, part_gate, part_up, part_down,
+    mirror_send, mirror_recv,
     gate_w, up_w, down_w, hidden, dgate, dup, rows_n, rows_t,
     partial, from_across, from_line, total, across_send, across_recv, line_send, line_recv,
     other_line, other_send, other_recv, gather_cross,
@@ -515,7 +519,7 @@
     cols = gate_own.shape[1]
     blocks = 2 * line
     me = grid.slot(grid.x, grid.z)
-    grid.greet(True)
+    grid.greet(True, True)
     gather = Gather(grid, normed, normed_all, gather_send, gather_recv, parts, gather_cross)
     scatter = Scatter(
         grid, partial, from_across, from_line, total,
@@ -603,6 +607,8 @@
         scatter.send_across(scatter.rank(j))
 
     tiles = width // tile
+
+    early_tiles = mirror_send.shape[0]
 
     def wide_loads(t, start):
         j, buf = t % tiles, t % 2
@@ -639,6 +645,20 @@
             )
         ]
 
+    def mirrored(t):
+        j = t % tiles
+        c = pl.ds(pl.multiple_of(j * tile, tile), tile)
+        return [
+            remote(src, dst, mirror_send.at[j, i], mirror_recv.at[j, i], grid.mirror)
+            for i, (src, dst) in enumerate(
+                (
+                    (grad_gate.at[c, :], mirror_gate.at[c, :]),
+                    (grad_up.at[c, :], mirror_up.at[c, :]),
+                    (grad_down.at[:, c], mirror_down.at[:, c]),
+                )
+            )
+        ]
+
     def pieces(t):
         c = pl.ds(pl.multiple_of((t % tiles) * tile, tile), tile)
         return [
@@ -692,6 +712,11 @@
             def _():
                 for copy in results(t - 2):
                     copy.wait()
+
+                @pl.when(t < tiles + 2 + early_tiles)
+                def _():
+                    for copy in mirrored(t - 2):
+                        copy.start()
 
             mine = slice(0, cols)
             own_gate = dot(tokens, dgate[:, mine], TN)
@@ -727,6 +752,9 @@
     gather.finish()
     scatter.finish()
     hidden_copy.wait()
+    for t in range(early_tiles):
+        for copy in mirrored(t):
+            copy.wait()
 
 
 def feed_call(normed, tangent_all, gates, ups, downs, line):
@@ -744,10 +772,12 @@
             hbm(blocks, rows, width), hbm(tall, 2 * cols),
             hbm(width, cols), hbm(width, cols), hbm(cols, width),
             hbm(width, cols), hbm(width, cols), hbm(cols, width),
+            hbm(width, cols), hbm(width, cols), hbm(cols, width),
         ),
         in_specs=[ANY] * 8,
-        out_specs=(pl.BlockSpec(memory_space=pltpu.VMEM),) + (ANY,) * 8,
+        out_specs=(pl.BlockSpec(memory_space=pltpu.VMEM),) + (ANY,) * 11,
         scratch_shapes=[
+            pltpu.SemaphoreType.DMA((EARLY, 3)), pltpu.SemaphoreType.DMA((EARLY, 3)),
             pltpu.VMEM((width, 2 * cols), BF), pltpu.VMEM((width, 2 * cols), BF), pltpu.VMEM((2 * cols, width), BF),
             pltpu.VMEM((tall, 2 * cols), BF), pltpu.VMEM((tall, 2 * cols), BF), pltpu.VMEM((tall, 2 * cols), BF),
             pltpu.VMEM((rows, width), BF), pltpu.VMEM((rows, width), BF),
@@ -779,9 +809,11 @@
 
 def sums_kernel(
     line,
-    normed, attended, grad_qkv, grad_out, twin_normed, twin_attended, twin_out,
+    normed, attended, grad_qkv, grad_out, twin_normed, twin_attended, twin_out, out_across,
     tokens, grad_middle, weights, gain, term_two,
-    result, grad_tokens,
+    result, result_out, grad_tokens,
+    across_v, out_partial, out_line, out_total, out_send, out_recv, out_mine, out_theirs, out_sem,
+    near_send, near_recv,
     both_normed, both_attended, both_qkv, both_out, load_sem, twin_send, twin_recv,
     partial, from_across, from_line, total, across_send, across_recv, line_send, line_recv,
     mine, theirs, mirror_send, mirror_recv, from_mirror, quarter_send, quarter_recv,
@@ -807,6 +839,7 @@
             (twin_attended, both_attended.at[twin]),
             (grad_out, both_out.at[own]),
             (twin_out, both_out.at[twin]),
+            (out_across, across_v),
             (normed, both_normed.at[own]),
             (twin_normed, both_normed.at[twin]),
             (grad_qkv, both_qkv.at[own]),
@@ -830,6 +863,24 @@
     away = pl.ds(pl.multiple_of((1 - grid.replica) * quarter, quarter), quarter)
     here = pl.ds(pl.multiple_of(grid.replica * quarter, quarter), quarter)
 
+    outs = Scatter(
+        grid, out_partial, None, out_line, out_total, (None, None, out_send, out_recv), 4
+    )
+
+    near = remote(near_send, near_recv, out_sem.at[2], out_sem.at[3], grid.across)
+
+    def near_step(i):
+        c = pl.ds(pl.multiple_of(i * tile, tile), tile)
+        first = ((1 - grid.x) * 2 + grid.core) * tall + grid.z * run
+        mine = pl.ds(pl.multiple_of(first, run), run)
+        near_send[:, c] = dot(both_attended[:, mine], both_out[:, c], TN).astype(BF)
+
+    def out_step(i):
+        c = pl.ds(pl.multiple_of(i * tile, tile), tile)
+        value = dot(both_attended[:, features(grid.x)], both_out[:, c], TN)
+        value = value.reshape(line, run, tile) + across_v[:, :, c].astype(F32)
+        out_partial[:, :, c] = value.astype(BF)
+
     def to_mirror(slot):
         return remote(
             partial.at[slot, away], from_mirror.at[slot],
@@ -853,17 +904,21 @@
 
             lax.fori_loop(0, right.shape[1] // tile, step, 0)
 
-        wide(both_attended, both_out, narrow)
-        pl.when(j == 0)(swap_qkv.wait)
         wide(both_normed, both_qkv, 0)
-        partial[blocks, :, narrow + width :] = jnp.zeros((line, run, 128), BF)
+        partial[blocks, :, narrow:] = jnp.zeros((line, run, 128), BF)
         for k in range(line - 1, -1, -1):
             z = grid.order(k)
             to_mirror(grid.slot(x, z)).start()
             pl.when(j == 0)(lambda z=z: scatter.across(z, 0).start())
         return carry
 
+    across_v[grid.z] = jnp.zeros((run, width), BF)
+    each(width // tile, out_step)
+    each(width // tile, near_step)
+    swap_qkv.wait()
     lax.fori_loop(0, 2, column, 0)
+    near.start()
+    each(outs.steps(), outs.step)
     for copy in later:
         copy.wait()
 
@@ -901,7 +956,7 @@
             first = pl.multiple_of((x * 2 + grid.core) * tall + z * run, run)
             c = pl.ds(first, run)
             value = own_terms[:, c].astype(F32) + twin_terms[:, c].astype(F32)
-            partial[x * line + z, 3 * quarter : 3 * quarter + 16, narrow + width :] = value.astype(BF)
+            partial[x * line + z, 3 * quarter : 3 * quarter + 16, narrow:] = value.astype(BF)
     for k in range(line - 1, -1, -1):
         scatter.across(grid.order(k), 1).start()
 
@@ -937,6 +992,12 @@
         mine[scatter.run(part)] = total[...].astype(BF)
         swap(part).start()
 
+    outs.own(result_out)
+    near.wait()
+    result_out[...] += near_recv[...].astype(F32)
+    out_mine[...] = result_out[...].astype(BF)
+    out_swap = remote(out_mine, out_theirs, out_sem.at[0], out_sem.at[1], grid.mirror)
+    out_swap.start()
     sweep(0)
     sweep(1)
     add_mirror(grid.x)
@@ -952,6 +1013,9 @@
     swap(2).wait_send()
     remote(mine.at[away], theirs.at[away], mirror_send.at[2], mirror_recv.at[2], grid.mirror).wait_recv()
     result[away] = theirs[away].astype(F32)
+    out_swap.wait()
+    result_out[...] = out_mine[...].astype(F32) + out_theirs[...].astype(F32)
+    outs.finish()
     scatter.finish()
 
     def sent(slot, carry):
@@ -962,11 +1026,11 @@
 
 
 def sums_call(
-    normed, attended, grad_qkv, grad_out, twins, tokens, grad_middle, weights, gain, term_two, line
+    normed, attended, grad_qkv, grad_out, others, tokens, grad_middle, weights, gain, term_two, line
 ):
     rows, width = normed.shape
     narrow = grad_qkv.shape[1]
-    run, whole = weights.shape[1:]
+    run, whole = weights.shape[1], narrow + 128
     quarter = run // 4
     vmem = pl.BlockSpec(memory_space=pltpu.VMEM)
     dma = pltpu.SemaphoreType.DMA
@@ -974,14 +1038,20 @@
     return pl.pallas_call(
         functools.partial(sums_kernel, line),
         out_shape=(
-            jax.ShapeDtypeStruct((run, whole), F32), jax.ShapeDtypeStruct((rows, width), BF),
+            jax.ShapeDtypeStruct((run, whole), F32), jax.ShapeDtypeStruct((run, width), F32),
+            jax.ShapeDtypeStruct((rows, width), BF),
         ),
-        in_specs=[ANY] * 10 + [vmem] * 2,
-        out_specs=(vmem, vmem),
+        in_specs=[ANY] * 11 + [vmem] * 2,
+        out_specs=(vmem,) * 3,
         scratch_shapes=[
+            pltpu.VMEM((line, run, width), BF), pltpu.VMEM((line, run, width), BF),
+            pltpu.VMEM((2 * line - 2, run, width), BF), pltpu.VMEM((quarter, width), F32),
+            dma((line, 4)), dma((2 * line - 2, 4)),
+            pltpu.VMEM((run, width), BF), pltpu.VMEM((run, width), BF), dma((4,)),
+            pltpu.VMEM((run, width), BF), pltpu.VMEM((run, width), BF),
             pltpu.VMEM((2 * rows, width), BF), pltpu.VMEM((2 * rows, width), BF),
             pltpu.VMEM((2 * rows, narrow), BF), pltpu.VMEM((2 * rows, width), BF),
-            dma((7,)), dma((2,)), dma((2,)),
+            dma((8,)), dma((2,)), dma((2,)),
             pltpu.VMEM((2 * line, run, whole), BF), pltpu.VMEM((line, run, whole), BF),
             pltpu.VMEM((2 * line - 2, run, whole), BF), pltpu.VMEM((quarter, whole), F32),
             dma((line, 3)), dma((line, 3)), dma((line, 3)), dma((2 * line - 2, 3)),
@@ -996,7 +1066,7 @@
         ),
         name="sums",
     )(
-        normed, attended, grad_qkv, grad_out, *twins, tokens, grad_middle, weights, gain, term_two
+        normed, attended, grad_qkv, grad_out, *others, tokens, grad_middle, weights, gain, term_two
     )
 
 
@@ -1238,9 +1308,16 @@
         load_pairs([(stage, tangent_all.at[me])], own_sem)
 
     gather = Gather(grid, tangent, tangent_all, send, recv, parts)
+    soon = parts // 2
+
+    def tangent_first():
+        gather.send_own()
+        for part in range(soon):
+            gather.forward(1, part)
+
     gather_weights(
         grid, block, everything, weight_send, weight_recv, twin_send, twin_recv, meanwhile,
-        gather.send_own,
+        tangent_first,
     )
     weights_copy = pltpu.make_async_copy(everything, weights_out, own_sem.at[1])
     weights_copy.start()
@@ -1273,7 +1350,7 @@
         ).astype(BF)
     line_keys = Line(grid, keyed, keyed_all, key_send, key_recv)
     line_keys.send_own()
-    for part in range(parts):
+    for part in range(soon, parts):
         gather.forward(1, part, along=False)
     keyed_all[grid.z] = keyed[...]
 
@@ -1285,7 +1362,7 @@
     lax.fori_loop(0, width // tile, query_step, 0)
     for distance in range(1, line):
         line_keys.forward(distance)
-    for part in range(parts):
+    for part in range(soon, parts):
         gather.forward(1, part, wait=False, across=False)
 
     logs[...] = jnp.zeros_like(logs)
@@ -1390,8 +1467,9 @@
 def back_kernel(
     line, parts,
     queries, keyed_all, grad_out, bias, logs, hidden_all, down_own, down_twin, weights, cosine, sine,
-    gate_sum, up_sum, down_sum, normed, attended,
+    gate_sum, up_sum, down_sum, _gate, _up, _down, normed, attended,
     branch, grad_qkv, gate_mirror, up_mirror, down_mirror, twin_normed, twin_attended, twin_out,
+    out_across, both_attended, both_out, out_partial, out_send, out_recv,
     out_v, out_w, cosine_v, sine_v, grad_keyed, mirror_send, mirror_recv,
     query_v, keyed_v, grad_v, bias_v, log_v, scores, gradients, probs, slopes, key_sum, value_sum,
     down_w, hidden, load_sem,
@@ -1412,10 +1490,15 @@
     ]
     for copy in swapped:
         copy.start()
+    left = pl.ds(EARLY * 256, width - EARLY * 256)
     mirrored = [
         remote(src, dst, mirror_send.at[i], mirror_recv.at[i], grid.mirror)
         for i, (src, dst) in enumerate(
-            ((gate_sum, gate_mirror), (up_sum, up_mirror), (down_sum, down_mirror))
+            (
+                (gate_sum.at[left, :], gate_mirror.at[left, :]),
+                (up_sum.at[left, :], up_mirror.at[left, :]),
+                (down_sum.at[:, left], down_mirror.at[:, left]),
+            )
         )
     ]
     for copy in mirrored:
@@ -1440,7 +1523,8 @@
         (across_send, across_recv, line_send, line_recv), parts,
     )
     keyed_scatter = Scatter(
-        grid, key_partial, None, key_line, key_total, (None, None, key_send, key_recv), parts
+        grid, key_partial, None, key_line, key_total, (None, None, key_send, key_recv),
+        key_partial.shape[1] // rows,
     )
 
     def work(i, carry):
@@ -1469,7 +1553,7 @@
         return carry
 
     lax.fori_loop(0, width // tile, out_step, 0)
-    lax.fori_loop(line, 2 * line, work, 0)
+    work(line, 0)
     deep = 2 * rows
     chunk = rows // 2
     pairs = width // (2 * HEAD_SIZE)
@@ -1517,11 +1601,56 @@
 
         @pl.when(i % group == group - 1)
         def _():
-            key_partial[:, :, key_cols] = key_sum[...].astype(BF).reshape(line, rows, 128)
-            key_partial[:, :, value_cols] = value_sum[...].astype(BF).reshape(line, rows, 128)
+            spot = pl.ds(pl.multiple_of((i // group) * rows, rows), rows)
+            key_partial[:, spot, 0:128] = key_sum[...].astype(BF).reshape(line, rows, 128)
+            key_partial[:, spot, 128:256] = value_sum[...].astype(BF).reshape(line, rows, 128)
+            pl.when(i // group + early > 0)(lambda: keyed_steps(i // group + early - 1))
+
+        @pl.when(i % 6 == 2)
+        def _():
+            work(line + 1 + i // 6, 0)
+
+        pl.when(i == pairs // 2 - 2)(out_gradients)
 
         pl.when(i % pace == 0)(lambda: scatter.step(i // pace + early))
         return carry
+
+    run = out_partial.shape[1]
+
+    def outward(z):
+        return remote(
+            out_partial.at[z], out_across.at[z], out_send.at[z], out_recv.at[z], grid.across
+        )
+
+    def away(action):
+        each(line, lambda z: pl.when(z != grid.z)(lambda: action(outward(z))))
+
+    def out_gradients():
+        for copy in swapped[1:]:
+            copy.wait()
+        own, twin = pl.ds(0, rows), pl.ds(rows, rows)
+        load_pairs(
+            [
+                (attended, both_attended.at[own]),
+                (twin_attended, both_attended.at[twin]),
+                (grad_out, both_out.at[own]),
+                (twin_out, both_out.at[twin]),
+            ],
+            load_sem,
+        )
+        tall = line * run
+        first = pl.multiple_of(((1 - grid.x) * 2 + grid.core) * tall, tall)
+
+        def tile_step(j):
+            c = pl.ds(pl.multiple_of(j * 512, 512), 512)
+            value = dot(both_attended[:, pl.ds(first, tall)], both_out[:, c], TN).astype(BF)
+            out_partial[:, :, c] = value.reshape(line, run, 512)
+
+        each(width // 512, tile_step)
+        away(lambda c: c.start())
+
+    def keyed_steps(g):
+        each(line - 1, lambda j: keyed_scatter.pass_on(keyed_scatter.rank(j), g))
 
     pace = 4
     early = jnp.where(jnp.logical_and(grid.has_left, grid.has_right), 0, 1)
@@ -1534,27 +1663,28 @@
 
     lax.fori_loop(pairs // pace + early, scatter.steps(), rest, 0)
 
-    def along(i, carry):
-        keyed_scatter.step(i)
-        return carry
-
-    lax.fori_loop(0, keyed_scatter.steps(), along, 0)
+    pl.when(early == 0)(lambda: keyed_steps(pairs // group - 1))
     scatter.own(branch)
     keyed_scatter.own(grad_keyed)
-    grad_qkv[:, width : width + narrow] = turn(grad_keyed[:, :narrow], cosine_v, sine_v, 1.0)
-    grad_qkv[:, width + narrow :] = grad_keyed[:, narrow:].astype(BF)
-    for copy in mirrored + swapped:
+    for g in range(pairs // group):
+        both = grad_keyed[g * rows : (g + 1) * rows, :]
+        first = width + g * 128
+        grad_qkv[:, first : first + 128] = turn(both[:, :128], cosine_v, sine_v, 1.0)
+        grad_qkv[:, first + narrow : first + narrow + 128] = both[:, 128:].astype(BF)
+    for copy in mirrored + swapped[:1]:
         copy.wait()
+    away(lambda c: c.wait())
     scatter.finish()
     keyed_scatter.finish()
 
 
 def back_call(
     queries, keyed_all, grad_out, bias, logs, hidden_all, downs, weights, cosine, sine, sums,
-    normed, attended, line,
+    mirrors, normed, attended, line,
 ):
     rows, width = queries.shape
     both = keyed_all.shape[2]
+    groups, run = both // 256, weights.shape[1]
     cols, length = downs[0].shape[0], bias.shape[1]
     parts = 2
     shapes = jax.ShapeDtypeStruct
@@ -1564,12 +1694,18 @@
         out_shape=(
             shapes((rows, width), F32), shapes((rows, width + both), BF),
             *(shapes(s.shape, BF) for s in sums), *(shapes((rows, width), BF),) * 3,
+            shapes((line, run, width), BF),
         ),
-        in_specs=[ANY] * 16,
-        out_specs=(vmem,) * 2 + (ANY,) * 6,
+        in_specs=[ANY] * 19,
+        out_specs=(vmem,) * 2 + (ANY,) * 7,
+        input_output_aliases={14: 2, 15: 3, 16: 4},
         scratch_shapes=[
-            pltpu.VMEM((rows, width), BF), pltpu.VMEM((4, weights.shape[1], width), BF),
-            pltpu.VMEM(cosine.shape, F32), pltpu.VMEM(sine.shape, F32), pltpu.VMEM((rows, both), F32),
+            pltpu.VMEM((2 * rows, width), BF), pltpu.VMEM((2 * rows, width), BF),
+            pltpu.VMEM((line, run, width), BF),
+            pltpu.SemaphoreType.DMA((line,)), pltpu.SemaphoreType.DMA((line,)),
+            pltpu.VMEM((rows, width), BF), pltpu.VMEM((4, run, width), BF),
+            pltpu.VMEM(cosine.shape, F32), pltpu.VMEM(sine.shape, F32),
+            pltpu.VMEM((groups * rows, 256), F32),
             pltpu.SemaphoreType.DMA((6,)), pltpu.SemaphoreType.DMA((6,)),
             pltpu.VMEM((rows, width), BF), pltpu.VMEM(keyed_all.shape, BF), pltpu.VMEM((rows, width), BF),
             pltpu.VMEM((rows, length), F32), pltpu.VMEM(logs.shape, F32),
@@ -1579,9 +1715,9 @@
             pltpu.VMEM((2 * cols, width), BF), pltpu.VMEM(hidden_all.shape, BF),
             pltpu.SemaphoreType.DMA((10,)),
             *scatter_scratch(line, rows, width, parts),
-            pltpu.VMEM((line, rows, both), BF), pltpu.VMEM((2 * line - 2, rows, both), BF),
-            pltpu.VMEM((rows // parts, both), F32),
-            pltpu.SemaphoreType.DMA((line, parts)), pltpu.SemaphoreType.DMA((2 * line - 2, parts)),
+            pltpu.VMEM((line, groups * rows, 256), BF), pltpu.VMEM((2 * line - 2, groups * rows, 256), BF),
+            pltpu.VMEM((rows, 256), F32),
+            pltpu.SemaphoreType.DMA((line, groups)), pltpu.SemaphoreType.DMA((2 * line - 2, groups)),
         ],
         compiler_params=pltpu.CompilerParams(
             collective_id=6, has_side_effects=True, vmem_limit_bytes=62 * 2**20
@@ -1589,7 +1725,7 @@
         name="back",
     )(
         queries, keyed_all, grad_out, bias, logs, hidden_all, *downs, weights, cosine, sine, *sums,
-        normed, attended,
+        *mirrors, normed, attended,
     )
 
 
@@ -1820,7 +1956,7 @@
     mid = width + 2 * narrow
     gain_first = weights[:, 0, mid : mid + run].reshape(width).astype(f32)
     gain_second = weights[:, 1, mid : mid + run].reshape(width).astype(f32)
-    grad_normed, _, hidden_all, *sums = feed_call(normed_mlp, tangent_all, gates, ups, downs, line)[:6]
+    grad_normed, _, hidden_all, *sums = feed_call(normed_mlp, tangent_all, gates, ups, downs, line)[:9]
     factor_two = lax.rsqrt(jnp.mean(middle * middle, axis=-1, keepdims=True) + norm_eps)
     unit_two = middle * factor_two
     scaled_two = grad_normed * gain_second
@@ -1831,25 +1967,26 @@
     grad_branch = grad_middle.astype(bf16)
     branch, grad_qkv, *others = back_call(
         scaled_query, keyed_all, grad_branch, bias, logs, hidden_all, downs, weights, cosine, -sine,
-        sums, normed_tokens, attended, line,
+        sums[:3], sums[3:], normed_tokens, attended, line,
     )
     outcome = middle + branch
     grad_w_gate, grad_w_up, grad_w_down = (
-        a.astype(f32) + b.astype(f32) for a, b in zip(sums, others[:3])
-    )
-    packed, grad_tokens = sums_call(
+        a.astype(f32) + b.astype(f32) for a, b in zip(sums[:3], others[:3])
+    )
+    packed, grad_w_out, grad_tokens = sums_call(
         normed_tokens, attended, grad_qkv, grad_branch, others[3:], rows, grad_middle, weights,
         gain_first.reshape(1, width), term_gain_two.reshape(1, width), line,
     )
-    gains = packed[run * 3 // 4 : run * 3 // 4 + 2, mid + width :]
+    gains = packed[run * 3 // 4 : run * 3 // 4 + 2, mid:]
     ends, start = [], 0
-    for size in (width, narrow, narrow, width):
+    for size in (width, narrow, narrow):
         ends.append(packed[:, start : start + size])
         start += size
     return (
         outcome.astype(bf16).reshape(tokens.shape),
         grad_tokens.reshape(tokens.shape),
         *ends,
+        grad_w_out,
         grad_w_gate,
         grad_w_up,
         grad_w_down,

time: 680 us -> 667 us (0.981)
  Pallas kernels: 642 us -> 627 us
    pallas_call x1, Pallas kernels: 120 us -> 104 us  [sums_call(): pl.pallas_call(functools.partial(sums_kernel, line), out_shape=(jax.Shape...]
  transfers between devices with their start and end apart: 3 -> 3, of which waited for: 0 -> 0; matrix products, arithmetic and copies ran while one was open for 1% -> 1% of each run, Pallas kernels for 29% -> 30%
where the time goes in v7:
time: 667 us; the launch traced here: 666 us
  Pallas kernels  627 us (94%)
  other arithmetic  26.2 us (4%)
  local copies, waits for them, and re-layouts  10.8 us (2%)
    pallas_call x1, Pallas kernels, front_call(): pl.pallas_call(functools.partial(front_kernel, line, parts), out_shape=(s...  197 us
    pallas_call x1, Pallas kernels, feed_call(): pl.pallas_call(functools.partial(feed_kernel, line, parts, tile), out_sha...  187 us
    pallas_call x1, Pallas kernels, back_call(): pl.pallas_call(functools.partial(back_kernel, line, parts), out_shape=(sh...  139 us
    pallas_call x1, Pallas kernels, sums_call(): pl.pallas_call(functools.partial(sums_kernel, line), out_shape=(jax.Shape...  104 us
  transfers between devices with their start and end apart: 3, of which 0 were waited for; matrix products, arithmetic and copies ran while one was open for 1% of the time, Pallas kernels for 30%

profile of v7, /device:TPU:0, one launch (start us, length us, event | category | flops | bytes accessed | tf_op | source)
XLA Modules:
  0.0 666.1 jit_solution(2697273402551624489)
XLA Ops:
  0.6 0.5 collective-permute-start.2
  1.2 0.1 collective-permute-start
  1.2 0.4 collective-permute-start.1
  1.7 0.7 constant_dynamic-slice_fusion
  2.4 1.3 fusion.4.extra_w
  3.7 0.5 fusion.3
  4.2 1.0 fusion.5
  5.2 1.8 compare_select_fusion.bias
  7.0 196.8 %front.1 = (bf16[256,2048]{1,0:T(8,128)(2,1)}, f32[256,2048]{1,0:T(8,128)}, bf16[256,2048]{1,0:T(8,128)(2,1)}, bf16[256,2048]{1,0:T(8,128)(2,1)}, bf16[256,2048]...) custom-call(bf16[128,2048]{1,0:T(8,128)(2,1)} %query_w.1, ...), custom_call_target="tpu_custom_call" | custom-call | tf_op jit(solution)/shard_map/front/pallas_call | solution.py:1438
  203.8 1.8 multiply_reduce_fusion.2
  205.6 1.4 bitcast_convert_fusion
  207.0 0.0 collective-permute-done.2.down_twin
  207.0 0.0 collective-permute-done.gate_twin
  207.0 0.0 collective-permute-done.1.up_twin
  207.1 187.3 %feed.1 = (f32[256,2048]{1,0:T(8,128)}, bf16[8,256,2048]{2,1,0:T(8,128)(2,1)}, bf16[2048,1024]{1,0:T(8,128)(2,1)}, bf16[2048,512]{1,0:T(8,128)(2,1)}, bf16[2048,...) custom-call(bf16[256,2048]{1,0:T(8,128)(2,1)} %get-tuple-element.43., ...), custom_call_target="tpu_custom_call" | custom-call | tf_op jit(solution)/shard_map/feed/pallas_call | solution.py:768
  394.4 0.0 copy-start
  394.4 0.0 copy-start.7
  394.4 3.5 multiply_reduce_fusion
  397.9 0.0 copy-done
  397.9 0.0 copy-done.7
  397.9 3.5 fusion.6
  401.4 138.9 %back.1 = (f32[256,2048]{1,0:T(8,128)}, bf16[256,3072]{1,0:T(8,128)(2,1)}, bf16[2048,512]{1,0:T(8,128)(2,1)}, bf16[2048,512]{1,0:T(8,128)(2,1)}, bf16[512,2048]{...) custom-call(bf16[256,2048]{1,0:T(8,128)(2,1)} %get-tuple-element.41., ...), custom_call_target="tpu_custom_call", output_to_operand_aliasing={{2}: (14, {}), {3}: (15, {}), {4}: (16, {})} | custom-call | tf_op jit(solution)/shard_map/back/pallas_call | solution.py:1692
  540.3 104.4 %sums.1 = (f32[128,3200]{1,0:T(8,128)}, f32[128,2048]{1,0:T(8,128)}, bf16[256,2048]{1,0:T(8,128)(2,1)}) custom-call(bf16[256,2048]{1,0:T(8,128)(2,1)} %get-tuple-element.55.normed, bf16[256,2048]{1,0:T(8,128)(2,1)} %get-tuple-element.56.attended, bf16[256,3072]{1,0:T(8,128)(2,1)} %get-tuple-element.58.grad_qkv, ...), custom_call_target="tpu_custom_call" | custom-call | tf_op jit(solution)/shard_map/sums/pallas_call | solution.py:1038
  644.7 0.0 copy-start.4
  644.7 2.4 slice.26
  647.1 1.9 fusion.7
  649.0 1.3 slice_bitcast_fusion
  650.2 0.0 copy-done.4
  650.2 0.0 copy-start.3
  650.2 0.0 copy-start.6
  650.3 4.5 convert_add_fusion
  654.8 0.0 copy-done.3
  654.8 0.0 copy-done.6
  654.8 0.0 copy-start.2
  654.8 0.0 copy-start.5
  654.8 2.8 convert_add_fusion.1
  657.5 0.0 copy-done.2
  657.5 1.0 copy-done.5
  658.5 0.0 copy-start.1
  658.5 0.0 copy-start.8
  658.5 2.8 convert_add_fusion.2
  661.3 0.0 copy-done.1
  661.3 1.0 copy-done.8
  662.2 0.0 copy-start.10
  662.3 1.2 fusion
  663.5 0.0 copy-start.9
  663.5 0.1 copy-done.10
  663.5 1.0 copy.32
  664.5 0.6 copy-done.9
  665.1 1.0 copy.33
  (4 shorter events, 0.0 us)
Async XLA Ops:
  0.6 206.4 %collective-permute-start.2 = (bf16[512,2048]{1,0:T(8,128)(2,1)}, bf16[512,2048]{1,0:T(8,128)(2,1)}, u32[]{:S(2)}, u32[]{:S(2)}) collective-permute-start(bf16[512,2048]{1,0:T(8,128)(2,1)} %down_own.3), channel_id=1, source_target_pairs={{0,4},{4,0},{8,12},{12,8},{1,5},{5,1},{9,13},{13,9},{2,6},{6,2},{1... | collective-permute-start | bytes 6291464 | tf_op jit(solution)/shard_map/ppermute | solution.py:1937
  1.2 205.9 %collective-permute-start = (bf16[2048,512]{1,0:T(8,128)(2,1)}, bf16[2048,512]{1,0:T(8,128)(2,1)}, u32[]{:S(2)}, u32[]{:S(2)}) collective-permute-start(bf16[2048,512]{1,0:T(8,128)(2,1)} %gate_own.1), channel_id=1, source_target_pairs={{0,4},{4,0},{8,12},{12,8},{1,5},{5,1},{9,13},{13,9},{2,6},{6,2},{1... | collective-permute-start | bytes 6291464 | tf_op jit(solution)/shard_map/ppermute | solution.py:1937
  1.2 205.8 %collective-permute-start.1 = (bf16[2048,512]{1,0:T(8,128)(2,1)}, bf16[2048,512]{1,0:T(8,128)(2,1)}, u32[]{:S(2)}, u32[]{:S(2)}) collective-permute-start(bf16[2048,512]{1,0:T(8,128)(2,1)} %up_own.1), channel_id=1, source_target_pairs={{0,4},{4,0},{8,12},{12,8},{1,5},{5,1},{9,13},{13,9},{2,6},{6,2},{1... | collective-permute-start | bytes 6291464 | tf_op jit(solution)/shard_map/ppermute | solution.py:1937
  394.4 3.6 copy-start
  394.4 3.6 copy-start.7
  644.7 5.6 copy-start.4
  650.2 4.5 copy-start.3
  650.2 4.5 copy-start.6
  654.8 2.8 copy-start.2
  654.8 3.7 copy-start.5
  658.5 2.8 copy-start.1
  658.5 3.7 copy-start.8
  662.2 1.3 copy-start.10
  663.5 1.6 copy-start.9

commit v8 on v7

--- a/solution.py
+++ b/solution.py
@@ -813,7 +813,7 @@
     tokens, grad_middle, weights, gain, term_two,
     result, result_out, grad_tokens,
     across_v, out_partial, out_line, out_total, out_send, out_recv, out_mine, out_theirs, out_sem,
-    near_send, near_recv,
+    near_send, near_recv, near_sem,
     both_normed, both_attended, both_qkv, both_out, load_sem, twin_send, twin_recv,
     partial, from_across, from_line, total, across_send, across_recv, line_send, line_recv,
     mine, theirs, mirror_send, mirror_recv, from_mirror, quarter_send, quarter_recv,
@@ -867,13 +867,20 @@
         grid, out_partial, None, out_line, out_total, (None, None, out_send, out_recv), 4
     )
 
-    near = remote(near_send, near_recv, out_sem.at[2], out_sem.at[3], grid.across)
+    nears = [
+        remote(near_send.at[j], near_recv.at[j], near_sem.at[0, j], near_sem.at[1, j], grid.across)
+        for j in range(2)
+    ]
 
     def near_step(i):
         c = pl.ds(pl.multiple_of(i * tile, tile), tile)
-        first = ((1 - grid.x) * 2 + grid.core) * tall + grid.z * run
-        mine = pl.ds(pl.multiple_of(first, run), run)
-        near_send[:, c] = dot(both_attended[:, mine], both_out[:, c], TN).astype(BF)
+        for j in range(2):
+            first = ((1 - grid.x) * 2 + grid.core) * tall + grid.order(j) * run
+            theirs = pl.ds(pl.multiple_of(first, run), run)
+            near_send[j, :, c] = dot(both_attended[:, theirs], both_out[:, c], TN).astype(BF)
+
+    def sweep(part):
+        each(line - 1, lambda i: scatter.pass_on(scatter.rank(i), part))
 
     def out_step(i):
         c = pl.ds(pl.multiple_of(i * tile, tile), tile)
@@ -912,13 +919,22 @@
             pl.when(j == 0)(lambda z=z: scatter.across(z, 0).start())
         return carry
 
-    across_v[grid.z] = jnp.zeros((run, width), BF)
+    for j in range(2):
+        across_v[grid.order(j)] = jnp.zeros((run, width), BF)
+    each(width // tile, near_step)
+    nears[1].start()
     each(width // tile, out_step)
-    each(width // tile, near_step)
+    early_outs = (line - 2) * outs.early
+    middling = jnp.logical_and(grid.has_left, grid.has_right)
+
+    def when_end(action):
+        pl.when(jnp.logical_not(middling))(action)
+
+    when_end(lambda: each(early_outs, outs.step))
     swap_qkv.wait()
     lax.fori_loop(0, 2, column, 0)
-    near.start()
-    each(outs.steps(), outs.step)
+    nears[0].start()
+    when_end(lambda: sweep(0))
     for copy in later:
         copy.wait()
 
@@ -940,7 +956,7 @@
         unit = value * factor
         grad = grad_normed[r, :]
         terms[0:1, :] += jnp.sum(grad * unit, axis=0, keepdims=True)
-        scaled = grad * gain[...]
+        scaled = grad * gain[0:1, :]
         mean = jnp.mean(scaled * unit, axis=1, keepdims=True)
         grad_tokens[r, :] = (middle_v[r, :] + factor * (scaled - unit * mean)).astype(BF)
         return carry
@@ -973,6 +989,20 @@
     add_mirror(1 - grid.x)
     for k in range(line - 1, -1, -1):
         scatter.across(grid.order(k), 2).start()
+    pl.when(middling)(lambda: each(early_outs, outs.step))
+    nears[1].wait()
+    next_place = grid.order(1)
+    out_partial[next_place] = (
+        out_partial[next_place].astype(F32) + near_recv[1].astype(F32)
+    ).astype(BF)
+    pl.when(middling)(lambda: sweep(0))
+
+    def out_rest(n, carry):
+        outs.step(n)
+        return carry
+
+    lax.fori_loop(early_outs, outs.steps(), out_rest, 0)
+    sweep(1)
 
     def swap(part, whole=True):
         at = scatter.run(part)
@@ -980,26 +1010,17 @@
             mine.at[at], theirs.at[at], mirror_send.at[part], mirror_recv.at[part], grid.mirror
         )
 
-    def sweep(part):
-        def step(i, carry):
-            scatter.pass_on(grid.order(line - 1 - i), part)
-            return carry
-
-        lax.fori_loop(0, line - 1, step, 0)
-
     def settle(part):
         scatter.gather_sum(grid.z, part)
         mine[scatter.run(part)] = total[...].astype(BF)
         swap(part).start()
 
     outs.own(result_out)
-    near.wait()
-    result_out[...] += near_recv[...].astype(F32)
+    nears[0].wait()
+    result_out[...] += near_recv[0].astype(F32)
     out_mine[...] = result_out[...].astype(BF)
     out_swap = remote(out_mine, out_theirs, out_sem.at[0], out_sem.at[1], grid.mirror)
     out_swap.start()
-    sweep(0)
-    sweep(1)
     add_mirror(grid.x)
     settle(0)
     sweep(2)
@@ -1047,8 +1068,8 @@
             pltpu.VMEM((line, run, width), BF), pltpu.VMEM((line, run, width), BF),
             pltpu.VMEM((2 * line - 2, run, width), BF), pltpu.VMEM((quarter, width), F32),
             dma((line, 4)), dma((2 * line - 2, 4)),
-            pltpu.VMEM((run, width), BF), pltpu.VMEM((run, width), BF), dma((4,)),
-            pltpu.VMEM((run, width), BF), pltpu.VMEM((run, width), BF),
+            pltpu.VMEM((run, width), BF), pltpu.VMEM((run, width), BF), dma((2,)),
+            pltpu.VMEM((2, run, width), BF), pltpu.VMEM((2, run, width), BF), dma((2, 2)),
             pltpu.VMEM((2 * rows, width), BF), pltpu.VMEM((2 * rows, width), BF),
             pltpu.VMEM((2 * rows, narrow), BF), pltpu.VMEM((2 * rows, width), BF),
             dma((8,)), dma((2,)), dma((2,)),
@@ -1194,6 +1215,10 @@
     copy(grid.x, grid.z, carry_b, across, True).wait_send()
 
 
+def mask(places, own_places):
+    return jnp.where(places[...] <= own_places[...], 0.0, -1e30).astype(F32)
+
+
 class Line:
     def __init__(self, grid, block, everything, send, recv):
         self.grid, self.block, self.everything = grid, block, everything
@@ -1272,33 +1297,38 @@
 
 def front_kernel(
     line, parts,
-    query_w, key_w, value_w, extra_w, out_w, tokens, tangent, bias, cosine, sine,
-    attended, middle, normed, first_normed, queries, logs, keyed_out, tangent_all, weights_out,
-    everything, keyed, keyed_all, bias_v, token_v, cosine_v, sine_v, gain, scores, probs, sums, stage, load_sem,
+    query_w, key_w, value_w, out_w, tokens, tangent, cosine, sine, gain_one, gain_two, places, own_places,
+    attended, middle, normed, first_normed, queries, logs, gain, keyed_out, tangent_all, weights_out,
+    everything, keyed, keyed_all, bias_v, token_v, cosine_v, sine_v, scores, probs, sums, stage, load_sem,
     key_send, key_recv, send, recv, own_sem, weight_send, weight_recv, twin_send, twin_recv,
 ):
     grid = Grid(2, line)
     rows, width = tokens.shape
     narrow = keyed.shape[1] // 2
-    total = bias.shape[1]
+    total = places.shape[1]
     extra = width + 2 * narrow
     after = extra + 128
     me = grid.slot(grid.x, grid.z)
     chunk = rows // 2
     tile = 512
     block = everything.at[(grid.x * 2 + grid.core) * line + grid.z]
-    first, packs = 0, []
-    for part in (query_w, key_w, value_w, extra_w, out_w):
-        packs.append((part, block.at[:, pl.ds(first, part.shape[1])]))
-        first += part.shape[1]
-    load_pairs(packs, load_sem)
+    starts = (0, width, width + narrow, after)
+    load_pairs(
+        [
+            (part, block.at[:, pl.ds(first, part.shape[1])])
+            for first, part in zip(starts, (query_w, key_w, value_w, out_w))
+        ],
+        load_sem,
+    )
+    row = lax.broadcasted_iota(jnp.int32, (16, 128), 0)
+    both_gains = jnp.where(row == 0, gain_one[...].astype(F32), gain_two[...].astype(F32))
+    everything[(grid.x * 2 + grid.core) * line + grid.z, 0:16, extra:after] = both_gains.astype(BF)
     grid.greet(True, True)
 
     def meanwhile():
         load_pairs(
             [
                 (tangent, stage),
-                (bias, bias_v),
                 (tokens, token_v),
                 (cosine, cosine_v),
                 (sine, sine_v),
@@ -1306,9 +1336,10 @@
             load_sem,
         )
         load_pairs([(stage, tangent_all.at[me])], own_sem)
+        bias_v[...] = mask(places, own_places)
 
     gather = Gather(grid, tangent, tangent_all, send, recv, parts)
-    soon = parts // 2
+    soon = 1
 
     def tangent_first():
         gather.send_own()
@@ -1360,17 +1391,20 @@
         return carry
 
     lax.fori_loop(0, width // tile, query_step, 0)
-    for distance in range(1, line):
+    def advance(n):
+        gather.forward(n // parts + 2, n % parts)
+
+    for distance in range(1, line - 1):
         line_keys.forward(distance)
     for part in range(soon, parts):
         gather.forward(1, part, wait=False, across=False)
+    for n in range(soon):
+        advance(n)
+    line_keys.forward(line - 1)
 
     logs[...] = jnp.zeros_like(logs)
     pairs = width // (2 * HEAD_SIZE)
     group = pairs // (narrow // (2 * HEAD_SIZE))
-
-    def advance(n):
-        gather.forward(n // parts + 2, n % parts)
 
     def pair_step(i, carry):
         c = pl.ds(pl.multiple_of(i * 128, 128), 128)
@@ -1396,7 +1430,8 @@
         out = dot(probs[...], values, NN) * sums[...]
         attended[:, c] = unhalves(out, half).astype(BF)
 
-        pl.when(i % 2 == 1)(lambda: advance(i // 2))
+        n = soon + i // 2
+        pl.when(jnp.logical_and(i % 2 == 1, n < (line - 2) * parts))(lambda: advance(n))
         return carry
 
     lax.fori_loop(0, pairs, pair_step, 0)
@@ -1417,7 +1452,7 @@
         advance(n)
         return carry
 
-    lax.fori_loop(pairs // 2, (line - 2) * parts, rest, 0)
+    lax.fori_loop(soon + pairs // 2, (line - 2) * parts, rest, 0)
     for z in range(line):
         gather.wait_across(z)
     keyed_copy.wait()
@@ -1426,11 +1461,11 @@
     gather.finish()
 
 
-def front_call(pieces, tokens, tangent, bias, cosine, sine, line):
+def front_call(pieces, tokens, tangent, cosine, sine, gains, places, own_places, line):
     rows, width = tokens.shape
     narrow = pieces[1].shape[1]
-    unit = (pieces[0].shape[0], sum(p.shape[1] for p in pieces))
-    total = bias.shape[1]
+    unit = (pieces[0].shape[0], sum(p.shape[1] for p in pieces) + 128)
+    total = places.shape[1]
     blocks, parts = 2 * line, 4
     shapes = jax.ShapeDtypeStruct
     vmem = pl.BlockSpec(memory_space=pltpu.VMEM)
@@ -1440,15 +1475,16 @@
         out_shape=(
             shapes((rows, width), BF), shapes((rows, width), F32), shapes((rows, width), BF),
             shapes((rows, width), BF), shapes((rows, width), BF),
-            shapes((2 * rows, 128), F32), shapes((line, rows, 2 * narrow), BF),
+            shapes((2 * rows, 128), F32), shapes((2, width), F32),
+            shapes((line, rows, 2 * narrow), BF),
             shapes((blocks, rows, width), BF), shapes((2 * blocks,) + unit, BF),
         ),
-        in_specs=[ANY] * 10,
-        out_specs=(vmem,) * 6 + (ANY,) * 3,
+        in_specs=[ANY] * 8 + [vmem] * 4,
+        out_specs=(vmem,) * 7 + (ANY,) * 3,
         scratch_shapes=[
             pltpu.VMEM((2 * blocks,) + unit, BF),
             pltpu.VMEM((rows, 2 * narrow), BF), pltpu.VMEM((line, rows, 2 * narrow), BF),
-            like(bias), like(tokens), like(cosine), like(sine), pltpu.VMEM((2, width), F32),
+            pltpu.VMEM((rows, total), F32), like(tokens), like(cosine), like(sine),
             pltpu.VMEM((2 * rows, total), F32), pltpu.VMEM((2 * rows, total), BF),
             pltpu.VMEM((2 * rows, 128), F32), pltpu.VMEM((rows, width), BF), pltpu.SemaphoreType.DMA((6,)),
             pltpu.SemaphoreType.DMA((line, 2)), pltpu.SemaphoreType.DMA((line,)),
@@ -1461,16 +1497,18 @@
             collective_id=5, has_side_effects=True, vmem_limit_bytes=62 * 2**20
         ),
         name="front",
-    )(*pieces, tokens, tangent, bias, cosine, sine)
+    )(*pieces, tokens, tangent, cosine, sine, *gains, places, own_places)
 
 
 def back_kernel(
     line, parts,
-    queries, keyed_all, grad_out, bias, logs, hidden_all, down_own, down_twin, weights, cosine, sine,
+    places, own_places, queries, keyed_all, middle, grad_normed, tangent, gain, logs, hidden_all,
+    down_own, down_twin, weights, cosine, sine,
     gate_sum, up_sum, down_sum, _gate, _up, _down, normed, attended,
-    branch, grad_qkv, gate_mirror, up_mirror, down_mirror, twin_normed, twin_attended, twin_out,
+    branch, grad_qkv, term_two, gate_mirror, up_mirror, down_mirror,
+    twin_normed, twin_attended, twin_out, grad_out, grad_middle,
     out_across, both_attended, both_out, out_partial, out_send, out_recv,
-    out_v, out_w, cosine_v, sine_v, grad_keyed, mirror_send, mirror_recv,
+    norm_sem, gain_v, out_v, out_w, cosine_v, sine_v, grad_keyed, mirror_send, mirror_recv,
     query_v, keyed_v, grad_v, bias_v, log_v, scores, gradients, probs, slopes, key_sum, value_sum,
     down_w, hidden, load_sem,
     partial, from_across, from_line, total, across_send, across_recv, line_send, line_recv,
@@ -1480,15 +1518,15 @@
     cols, width = down_own.shape
     rows = partial.shape[1]
     narrow = keyed_all.shape[2] // 2
-    length = bias.shape[1]
+    length = places.shape[1]
     grid.greet(True, True)
     swapped = [
         remote(src, dst, mirror_send.at[3 + i], mirror_recv.at[3 + i], grid.twin)
         for i, (src, dst) in enumerate(
-            ((normed, twin_normed), (attended, twin_attended), (grad_out, twin_out))
+            ((normed, twin_normed), (attended, twin_attended), (out_v, twin_out))
         )
     ]
-    for copy in swapped:
+    for copy in swapped[:2]:
         copy.start()
     left = pl.ds(EARLY * 256, width - EARLY * 256)
     mirrored = [
@@ -1510,14 +1548,14 @@
             (hidden_all, hidden),
             (queries, query_v),
             (keyed_all, keyed_v),
-            (grad_out, out_v),
-            (bias, bias_v),
+            (gain, gain_v),
             (logs, log_v),
             (cosine, cosine_v),
             (sine, sine_v),
         ],
         load_sem,
     )
+    bias_v[...] = mask(places, own_places)
     scatter = Scatter(
         grid, partial, from_across, from_line, total,
         (across_send, across_recv, line_send, line_recv), parts,
@@ -1541,7 +1579,58 @@
         pl.when(i < line)(lambda: scatter.send_across(z))
         return carry
 
+    deep = 2 * rows
+    middle_v, normed_v, tangent_v = scores, gradients, probs
+    half_width = width // 2
+    norm_loads = [
+        pltpu.make_async_copy(
+            src.at[:, pl.ds(h * half_width, half_width)], dst.at[pl.ds(h * rows, rows), :], norm_sem.at[i, h]
+        )
+        for i, (src, dst) in enumerate(
+            ((middle, middle_v), (grad_normed, normed_v), (tangent, tangent_v))
+        )
+        for h in range(2)
+    ]
+    for copy in norm_loads:
+        copy.start()
     lax.fori_loop(0, line, work, 0)
+    for copy in norm_loads:
+        copy.wait()
+    term_two[...] = jnp.zeros_like(term_two)
+    few = rows // 4
+
+    def norm_step(j):
+        spots = [pl.ds(pl.multiple_of(h * rows + j * few, few), few) for h in range(2)]
+        here = pl.ds(pl.multiple_of(j * few, few), few)
+        sides = [pl.ds(h * half_width, half_width) for h in range(2)]
+        values = [middle_v[s, :] for s in spots]
+        square = sum(jnp.sum(v * v, axis=1, keepdims=True) for v in values)
+        factor = lax.rsqrt(square / width + norm_eps)
+        units = [v * factor for v in values]
+        grads = [normed_v[s, :] for s in spots]
+        scaled = [g * gain_v[1:2, c] for g, c in zip(grads, sides)]
+        dots = sum(jnp.sum(s * u, axis=1, keepdims=True) for s, u in zip(scaled, units))
+        mean = dots / width
+        for spot, c, grad, unit, scale in zip(spots, sides, grads, units, scaled):
+            term_two[:, c] += jnp.sum(grad * unit, axis=0, keepdims=True)
+            value = tangent_v[spot, :].astype(F32) + factor * (scale - unit * mean)
+            branch[here, c] = value
+            out_v[here, c] = value.astype(BF)
+
+    each(rows // few, norm_step)
+    norm_copies = [
+        pltpu.make_async_copy(branch, grad_middle, norm_sem.at[0, 0]),
+        pltpu.make_async_copy(out_v, grad_out, norm_sem.at[0, 1]),
+    ]
+    for copy in norm_copies + swapped[2:]:
+        copy.start()
+    work(line, 0)
+    lag = jnp.where(jnp.logical_and(grid.has_left, grid.has_right), 2, 0)
+
+    def paced(position):
+        pl.when(position >= lag)(lambda: scatter.step(position - lag))
+
+    paced(0)
     tile = out_w.shape[0] * out_w.shape[1]
     after = weights.shape[2] - width
 
@@ -1550,11 +1639,10 @@
         load_pairs([(weights.at[units, :, pl.ds(after, width)], out_w)], load_sem)
         c = pl.ds(pl.multiple_of(j * tile, tile), tile)
         grad_v[:, c] = dot(out_v[...], out_w[...].reshape(tile, width), NT).astype(BF)
+        pl.when(j % 2 == 1)(lambda: paced(1 + j // 2))
         return carry
 
     lax.fori_loop(0, width // tile, out_step, 0)
-    work(line, 0)
-    deep = 2 * rows
     chunk = rows // 2
     pairs = width // (2 * HEAD_SIZE)
     group = pairs // (narrow // (2 * HEAD_SIZE))
@@ -1612,7 +1700,8 @@
 
         pl.when(i == pairs // 2 - 2)(out_gradients)
 
-        pl.when(i % pace == 0)(lambda: scatter.step(i // pace + early))
+        done = (3 * i + 1) // 5
+        pl.when((3 * i + 4) // 5 > done)(lambda: paced(3 + done))
         return carry
 
     run = out_partial.shape[1]
@@ -1623,7 +1712,8 @@
         )
 
     def away(action):
-        each(line, lambda z: pl.when(z != grid.z)(lambda: action(outward(z))))
+        for j in range(line - 2):
+            action(outward(scatter.rank(j)))
 
     def out_gradients():
         for copy in swapped[1:]:
@@ -1633,7 +1723,7 @@
             [
                 (attended, both_attended.at[own]),
                 (twin_attended, both_attended.at[twin]),
-                (grad_out, both_out.at[own]),
+                (out_v, both_out.at[own]),
                 (twin_out, both_out.at[twin]),
             ],
             load_sem,
@@ -1652,18 +1742,18 @@
     def keyed_steps(g):
         each(line - 1, lambda j: keyed_scatter.pass_on(keyed_scatter.rank(j), g))
 
-    pace = 4
     early = jnp.where(jnp.logical_and(grid.has_left, grid.has_right), 0, 1)
-    pl.when(early == 1)(lambda: scatter.step(0))
     lax.fori_loop(0, pairs, pair_step, 0)
 
     def rest(n, carry):
         scatter.step(n)
         return carry
 
-    lax.fori_loop(pairs // pace + early, scatter.steps(), rest, 0)
+    lax.fori_loop(3 + (3 * pairs + 1) // 5 - lag, scatter.steps(), rest, 0)
 
     pl.when(early == 0)(lambda: keyed_steps(pairs // group - 1))
+    for copy in norm_copies:
+        copy.wait()
     scatter.own(branch)
     keyed_scatter.own(grad_keyed)
     for g in range(pairs // group):
@@ -1679,30 +1769,32 @@
 
 
 def back_call(
-    queries, keyed_all, grad_out, bias, logs, hidden_all, downs, weights, cosine, sine, sums,
+    places, own_places, queries, keyed_all, middle, grad_normed, tangent, gain, logs, hidden_all, downs,
+    weights, cosine, sine, sums,
     mirrors, normed, attended, line,
 ):
     rows, width = queries.shape
     both = keyed_all.shape[2]
     groups, run = both // 256, weights.shape[1]
-    cols, length = downs[0].shape[0], bias.shape[1]
-    parts = 2
+    cols, length = downs[0].shape[0], places.shape[1]
+    parts = 4
     shapes = jax.ShapeDtypeStruct
     vmem = pl.BlockSpec(memory_space=pltpu.VMEM)
     return pl.pallas_call(
         functools.partial(back_kernel, line, parts),
         out_shape=(
-            shapes((rows, width), F32), shapes((rows, width + both), BF),
-            *(shapes(s.shape, BF) for s in sums), *(shapes((rows, width), BF),) * 3,
-            shapes((line, run, width), BF),
+            shapes((rows, width), F32), shapes((rows, width + both), BF), shapes((1, width), F32),
+            *(shapes(s.shape, BF) for s in sums), *(shapes((rows, width), BF),) * 4,
+            shapes((rows, width), F32), shapes((line, run, width), BF),
         ),
-        in_specs=[ANY] * 19,
-        out_specs=(vmem,) * 2 + (ANY,) * 7,
-        input_output_aliases={14: 2, 15: 3, 16: 4},
+        in_specs=[vmem] * 2 + [ANY] * 21,
+        out_specs=(vmem,) * 3 + (ANY,) * 9,
+        input_output_aliases={18: 3, 19: 4, 20: 5},
         scratch_shapes=[
             pltpu.VMEM((2 * rows, width), BF), pltpu.VMEM((2 * rows, width), BF),
             pltpu.VMEM((line, run, width), BF),
             pltpu.SemaphoreType.DMA((line,)), pltpu.SemaphoreType.DMA((line,)),
+            pltpu.SemaphoreType.DMA((3, 2)), pltpu.VMEM(gain.shape, F32),
             pltpu.VMEM((rows, width), BF), pltpu.VMEM((4, run, width), BF),
             pltpu.VMEM(cosine.shape, F32), pltpu.VMEM(sine.shape, F32),
             pltpu.VMEM((groups * rows, 256), F32),
@@ -1724,7 +1816,8 @@
         ),
         name="back",
     )(
-        queries, keyed_all, grad_out, bias, logs, hidden_all, *downs, weights, cosine, sine, *sums,
+        places, own_places, queries, keyed_all, middle, grad_normed, tangent, gain, logs, hidden_all,
+        *downs, weights, cosine, sine, *sums,
         *mirrors, normed, attended,
     )
 
@@ -1940,42 +2033,33 @@
     rotary_angles = local_positions.reshape(segment_length).astype(f32)[:, None] * frequencies(
         HEAD_SIZE // 2
     )
-    extra = jnp.pad(jnp.stack([gain_attn, gain_mlp]), ((0, run - 2), (0, 0)))
-    pieces = (w_query, key_projection, value_projection, extra, w_out)
+    pieces = (w_query, key_projection, value_projection, w_out)
     cosine, sine = jnp.cos(rotary_angles), jnp.sin(rotary_angles)
     cosine = jnp.concatenate([cosine] * 4, axis=1)
     sine = jnp.concatenate([-sine, sine] * 2, axis=1)
-    allowed = places.reshape(1, total_length) <= local_positions.reshape(segment_length, 1)
-    bias = jnp.where(allowed, 0.0, -1e30).astype(f32)
+    own_places = local_positions.reshape(segment_length, 1)
+    places = places.reshape(1, total_length)
+    gains = (gain_attn.reshape(1, run), gain_mlp.reshape(1, run))
     tangent = cotangent.reshape(segment_length, width)
-    tangent_f = tangent.astype(f32)
     rows = tokens.reshape(segment_length, width)
     (
-        attended, middle, normed_mlp, normed_tokens, scaled_query, logs, keyed_all, tangent_all, weights,
-    ) = front_call(pieces, rows, tangent, bias, cosine, sine, line)
+        attended, middle, normed_mlp, normed_tokens, scaled_query, logs, gain, keyed_all, tangent_all,
+        weights,
+    ) = front_call(pieces, rows, tangent, cosine, sine, gains, places, own_places, line)
     mid = width + 2 * narrow
-    gain_first = weights[:, 0, mid : mid + run].reshape(width).astype(f32)
-    gain_second = weights[:, 1, mid : mid + run].reshape(width).astype(f32)
     grad_normed, _, hidden_all, *sums = feed_call(normed_mlp, tangent_all, gates, ups, downs, line)[:9]
-    factor_two = lax.rsqrt(jnp.mean(middle * middle, axis=-1, keepdims=True) + norm_eps)
-    unit_two = middle * factor_two
-    scaled_two = grad_normed * gain_second
-    term_gain_two = jnp.sum(grad_normed * unit_two, axis=0)
-    grad_middle = tangent_f + factor_two * (
-        scaled_two - unit_two * jnp.mean(scaled_two * unit_two, axis=-1, keepdims=True)
-    )
-    grad_branch = grad_middle.astype(bf16)
-    branch, grad_qkv, *others = back_call(
-        scaled_query, keyed_all, grad_branch, bias, logs, hidden_all, downs, weights, cosine, -sine,
-        sums[:3], sums[3:], normed_tokens, attended, line,
-    )
+    branch, grad_qkv, term_two, *others = back_call(
+        places, own_places, scaled_query, keyed_all, middle, grad_normed, tangent, gain, logs,
+        hidden_all, downs, weights, cosine, -sine, sums[:3], sums[3:], normed_tokens, attended, line,
+    )
+    twins, (grad_branch, grad_middle, out_across) = others[3:6], others[6:]
     outcome = middle + branch
     grad_w_gate, grad_w_up, grad_w_down = (
         a.astype(f32) + b.astype(f32) for a, b in zip(sums[:3], others[:3])
     )
     packed, grad_w_out, grad_tokens = sums_call(
-        normed_tokens, attended, grad_qkv, grad_branch, others[3:], rows, grad_middle, weights,
-        gain_first.reshape(1, width), term_gain_two.reshape(1, width), line,
+        normed_tokens, attended, grad_qkv, grad_branch, (*twins, out_across), rows, grad_middle,
+        weights, gain, term_two, line,
     )
     gains = packed[run * 3 // 4 : run * 3 // 4 + 2, mid:]
     ends, start = [], 0

time: 667 us -> 638 us (0.957)
  Pallas kernels: 627 us -> 611 us
  other arithmetic: 26.2 us -> 13.6 us
    pallas_call x1, Pallas kernels: 139 us -> 132 us  [back_call(): pl.pallas_call(functools.partial(back_kernel, line, parts), out_shape=(sh...]
  transfers between devices with their start and end apart: 3 -> 3, of which waited for: 0 -> 0; matrix products, arithmetic and copies ran while one was open for 1% -> 0% of each run, Pallas kernels for 30% -> 30%
where the time goes in v8:
time: 638 us; the launch traced here: 637 us
  Pallas kernels  611 us (96%)
  other arithmetic  13.6 us (2%)
  local copies, waits for them, and re-layouts  10.8 us (2%)
    pallas_call x1, Pallas kernels, front_call(): pl.pallas_call(functools.partial(front_kernel, line, parts), out_shape=(s...  193 us
    pallas_call x1, Pallas kernels, feed_call(): pl.pallas_call(functools.partial(feed_kernel, line, parts, tile), out_sha...  184 us
    pallas_call x1, Pallas kernels, back_call(): pl.pallas_call(functools.partial(back_kernel, line, parts), out_shape=(sh...  132 us
    pallas_call x1, Pallas kernels, sums_call(): pl.pallas_call(functools.partial(sums_kernel, line), out_shape=(jax.Shape...  101 us
  transfers between devices with their start and end apart: 3, of which 0 were waited for; matrix products, arithmetic and copies ran while one was open for 0% of the time, Pallas kernels for 30%

profile of v8, /device:TPU:0, one launch (start us, length us, event | category | flops | bytes accessed | tf_op | source)
XLA Modules:
  0.0 637.0 jit_solution(6990927044994021618)
XLA Ops:
  0.6 0.5 collective-permute-start
  1.2 0.1 collective-permute-start.1
  1.2 0.4 collective-permute-start.2
  1.7 0.7 dynamic-slice_bitcast_fusion
  2.4 0.8 copy.29.own_places
  3.2 0.5 fusion.1
  3.7 1.0 fusion.2
  4.7 193.4 %front.1 = (bf16[256,2048]{1,0:T(8,128)(2,1)}, f32[256,2048]{1,0:T(8,128)}, bf16[256,2048]{1,0:T(8,128)(2,1)}, bf16[256,2048]{1,0:T(8,128)(2,1)}, bf16[256,2048]...) custom-call(bf16[128,2048]{1,0:T(8,128)(2,1)} %query_w.1, ...), custom_call_target="tpu_custom_call" | custom-call | tf_op jit(solution)/shard_map/front/pallas_call | solution.py:1473
  198.1 0.0 collective-permute-done.gate_twin
  198.1 0.0 collective-permute-done.1.up_twin
  198.1 0.0 collective-permute-done.2.down_twin
  198.1 184.2 %feed.1 = (f32[256,2048]{1,0:T(8,128)}, bf16[8,256,2048]{2,1,0:T(8,128)(2,1)}, bf16[2048,1024]{1,0:T(8,128)(2,1)}, bf16[2048,512]{1,0:T(8,128)(2,1)}, bf16[2048,...) custom-call(bf16[256,2048]{1,0:T(8,128)(2,1)} %get-tuple-element.47., ...), custom_call_target="tpu_custom_call" | custom-call | tf_op jit(solution)/shard_map/feed/pallas_call | solution.py:768
  382.4 132.0 %back.1 = (f32[256,2048]{1,0:T(8,128)}, bf16[256,3072]{1,0:T(8,128)(2,1)}, f32[1,2048]{1,0:T(1,128)}, bf16[2048,512]{1,0:T(8,128)(2,1)}, bf16[2048,512]{1,0:T(8,...) custom-call(s32[1,1024]{1,0:T(1,128)} %places.3, ...), custom_call_target="tpu_custom_call", output_to_operand_aliasing={{3}: (18, {}), {4}: (19, {}), {5}: (20, {})} | custom-call | tf_op jit(solution)/shard_map/back/pallas_call | solution.py:1783
  514.4 101.2 %sums.1 = (f32[128,3200]{1,0:T(8,128)}, f32[128,2048]{1,0:T(8,128)}, bf16[256,2048]{1,0:T(8,128)(2,1)}) custom-call(bf16[256,2048]{1,0:T(8,128)(2,1)} %get-tuple-element.60.normed, bf16[256,2048]{1,0:T(8,128)(2,1)} %get-tuple-element.61.attended, bf16[256,3072]{1,0:T(8,128)(2,1)} %get-tuple-element.63.grad_qkv, ...), custom_call_target="tpu_custom_call" | custom-call | tf_op jit(solution)/shard_map/sums/pallas_call | solution.py:1059
  615.7 0.0 copy-start
  615.7 1.3 slice_bitcast_fusion
  617.0 1.9 fusion.3
  618.9 2.3 slice.18
  621.2 0.0 copy-done
  621.2 0.0 copy-start.3
  621.2 0.0 copy-start.4
  621.2 3.0 fusion
  624.2 0.0 copy-done.3
  624.2 0.0 copy-done.4
  624.2 0.0 copy-start.2
  624.2 0.0 copy-start.5
  624.2 2.8 convert_add_fusion.2
  626.9 0.0 copy-done.2
  626.9 1.0 copy-done.5
  627.9 0.0 copy-start.1
  627.9 0.0 copy-start.6
  627.9 2.8 convert_add_fusion.1
  630.7 0.0 copy-done.1
  630.7 1.0 copy-done.6
  631.7 0.0 copy-start.8
  631.7 2.8 convert_add_fusion
  634.5 0.0 copy-start.7
  634.5 0.0 copy-done.8
  634.5 1.0 copy.36
  635.4 0.6 copy-done.7
  636.1 1.0 copy.37
  (1 shorter events, 0.0 us)
Async XLA Ops:
  0.6 197.5 %collective-permute-start = (bf16[2048,512]{1,0:T(8,128)(2,1)}, bf16[2048,512]{1,0:T(8,128)(2,1)}, u32[]{:S(2)}, u32[]{:S(2)}) collective-permute-start(bf16[2048,512]{1,0:T(8,128)(2,1)} %gate_own.1), channel_id=1, source_target_pairs={{0,4},{4,0},{8,12},{12,8},{1,5},{5,1},{9,13},{13,9},{2,6},{6,2},{1... | collective-permute-start | bytes 6291464 | tf_op jit(solution)/shard_map/ppermute | solution.py:2030
  1.2 197.0 %collective-permute-start.1 = (bf16[2048,512]{1,0:T(8,128)(2,1)}, bf16[2048,512]{1,0:T(8,128)(2,1)}, u32[]{:S(2)}, u32[]{:S(2)}) collective-permute-start(bf16[2048,512]{1,0:T(8,128)(2,1)} %up_own.1), channel_id=1, source_target_pairs={{0,4},{4,0},{8,12},{12,8},{1,5},{5,1},{9,13},{13,9},{2,6},{6,2},{1... | collective-permute-start | bytes 6291464 | tf_op jit(solution)/shard_map/ppermute | solution.py:2030
  1.2 196.9 %collective-permute-start.2 = (bf16[512,2048]{1,0:T(8,128)(2,1)}, bf16[512,2048]{1,0:T(8,128)(2,1)}, u32[]{:S(2)}, u32[]{:S(2)}) collective-permute-start(bf16[512,2048]{1,0:T(8,128)(2,1)} %down_own.3), channel_id=1, source_target_pairs={{0,4},{4,0},{8,12},{12,8},{1,5},{5,1},{9,13},{13,9},{2,6},{6,2},{1... | collective-permute-start | bytes 6291464 | tf_op jit(solution)/shard_map/ppermute | solution.py:2030
  615.7 5.5 copy-start
  621.2 3.0 copy-start.3
  621.2 3.0 copy-start.4
  624.2 2.8 copy-start.2
  624.2 3.7 copy-start.5
  627.9 2.8 copy-start.1
  627.9 3.7 copy-start.6
  631.7 2.8 copy-start.8
  634.5 1.6 copy-start.7

commit v9 on v8

--- a/solution.py
+++ b/solution.py
@@ -157,7 +157,7 @@
 TN = (((0,), (0,)), ((), ()))
 
 
-EARLY = 3
+EARLY = 2
 
 
 def dot(left, right, dims):
@@ -730,7 +730,7 @@
             for copy in results(t):
                 copy.start()
 
-        n = t - 2 * lag
+        n = t - 3 * lag
         pl.when(n >= 0)(lambda: scatter.step(n))
         m = t // 3 - lag
         ready = jnp.logical_and(t % 3 == 2, jnp.logical_and(m >= 0, m < line))
@@ -744,7 +744,7 @@
         scatter.step(n)
         return carry
 
-    lax.fori_loop(2 * tiles - 2 * lag, scatter.steps(), rest, 0)
+    lax.fori_loop(2 * tiles - 3 * lag, scatter.steps(), rest, 0)
     scatter.own(grad_sum)
     for t in (2 * tiles - 2, 2 * tiles - 1):
         for copy in results(t):

time: 638 us -> 630 us (0.987)
  Pallas kernels: 611 us -> 603 us
  transfers between devices with their start and end apart: 3 -> 3, of which waited for: 0 -> 0; matrix products, arithmetic and copies ran while one was open for 0% -> 0% of each run, Pallas kernels for 30% -> 31%
where the time goes in v9:
time: 630 us; the launch traced here: 629 us
  Pallas kernels  603 us (96%)
  other arithmetic  13.6 us (2%)
  local copies, waits for them, and re-layouts  10.8 us (2%)
    pallas_call x1, Pallas kernels, front_call(): pl.pallas_call(functools.partial(front_kernel, line, parts), out_shape=(s...  193 us
    pallas_call x1, Pallas kernels, feed_call(): pl.pallas_call(functools.partial(feed_kernel, line, parts, tile), out_sha...  181 us
    pallas_call x1, Pallas kernels, back_call(): pl.pallas_call(functools.partial(back_kernel, line, parts), out_shape=(sh...  129 us
    pallas_call x1, Pallas kernels, sums_call(): pl.pallas_call(functools.partial(sums_kernel, line), out_shape=(jax.Shape...  99.2 us
  transfers between devices with their start and end apart: 3, of which 0 were waited for; matrix products, arithmetic and copies ran while one was open for 0% of the time, Pallas kernels for 31%

profile of v9, /device:TPU:0, one launch (start us, length us, event | category | flops | bytes accessed | tf_op | source)
XLA Modules:
  0.0 628.7 jit_solution(8919430751896752251)
XLA Ops:
  0.6 0.5 collective-permute-start
  1.2 0.1 collective-permute-start.1
  1.2 0.4 collective-permute-start.2
  1.7 0.7 dynamic-slice_bitcast_fusion
  2.4 0.8 copy.29.own_places
  3.2 0.5 fusion.1
  3.7 1.0 fusion.2
  4.7 193.4 %front.1 = (bf16[256,2048]{1,0:T(8,128)(2,1)}, f32[256,2048]{1,0:T(8,128)}, bf16[256,2048]{1,0:T(8,128)(2,1)}, bf16[256,2048]{1,0:T(8,128)(2,1)}, bf16[256,2048]...) custom-call(bf16[128,2048]{1,0:T(8,128)(2,1)} %query_w.1, ...), custom_call_target="tpu_custom_call" | custom-call | tf_op jit(solution)/shard_map/front/pallas_call | solution.py:1473
  198.1 0.0 collective-permute-done.gate_twin
  198.1 0.0 collective-permute-done.1.up_twin
  198.1 0.0 collective-permute-done.2.down_twin
  198.1 181.5 %feed.1 = (f32[256,2048]{1,0:T(8,128)}, bf16[8,256,2048]{2,1,0:T(8,128)(2,1)}, bf16[2048,1024]{1,0:T(8,128)(2,1)}, bf16[2048,512]{1,0:T(8,128)(2,1)}, bf16[2048,...) custom-call(bf16[256,2048]{1,0:T(8,128)(2,1)} %get-tuple-element.47., ...), custom_call_target="tpu_custom_call" | custom-call | tf_op jit(solution)/shard_map/feed/pallas_call | solution.py:768
  379.6 128.5 %back.1 = (f32[256,2048]{1,0:T(8,128)}, bf16[256,3072]{1,0:T(8,128)(2,1)}, f32[1,2048]{1,0:T(1,128)}, bf16[2048,512]{1,0:T(8,128)(2,1)}, bf16[2048,512]{1,0:T(8,...) custom-call(s32[1,1024]{1,0:T(1,128)} %places.3, ...), custom_call_target="tpu_custom_call", output_to_operand_aliasing={{3}: (18, {}), {4}: (19, {}), {5}: (20, {})} | custom-call | tf_op jit(solution)/shard_map/back/pallas_call | solution.py:1783
  508.2 99.2 %sums.1 = (f32[128,3200]{1,0:T(8,128)}, f32[128,2048]{1,0:T(8,128)}, bf16[256,2048]{1,0:T(8,128)(2,1)}) custom-call(bf16[256,2048]{1,0:T(8,128)(2,1)} %get-tuple-element.60.normed, bf16[256,2048]{1,0:T(8,128)(2,1)} %get-tuple-element.61.attended, bf16[256,3072]{1,0:T(8,128)(2,1)} %get-tuple-element.63.grad_qkv, ...), custom_call_target="tpu_custom_call" | custom-call | tf_op jit(solution)/shard_map/sums/pallas_call | solution.py:1059
  607.4 0.0 copy-start
  607.4 1.3 slice_bitcast_fusion
  608.7 1.9 fusion.3
  610.6 2.3 slice.18
  612.9 0.0 copy-done
  612.9 0.0 copy-start.3
  612.9 0.0 copy-start.4
  612.9 3.0 fusion
  615.9 0.0 copy-done.3
  615.9 0.0 copy-done.4
  615.9 0.0 copy-start.2
  615.9 0.0 copy-start.5
  615.9 2.8 convert_add_fusion.2
  618.6 0.0 copy-done.2
  618.6 1.0 copy-done.5
  619.6 0.0 copy-start.1
  619.6 0.0 copy-start.6
  619.6 2.8 convert_add_fusion.1
  622.4 0.0 copy-done.1
  622.4 1.0 copy-done.6
  623.3 0.0 copy-start.8
  623.3 2.8 convert_add_fusion
  626.2 0.0 copy-start.7
  626.2 0.0 copy-done.8
  626.2 1.0 copy.36
  627.1 0.6 copy-done.7
  627.8 1.0 copy.37
  (1 shorter events, 0.0 us)
Async XLA Ops:
  0.6 197.5 %collective-permute-start = (bf16[2048,512]{1,0:T(8,128)(2,1)}, bf16[2048,512]{1,0:T(8,128)(2,1)}, u32[]{:S(2)}, u32[]{:S(2)}) collective-permute-start(bf16[2048,512]{1,0:T(8,128)(2,1)} %gate_own.1), channel_id=1, source_target_pairs={{0,4},{4,0},{8,12},{12,8},{1,5},{5,1},{9,13},{13,9},{2,6},{6,2},{1... | collective-permute-start | bytes 6291464 | tf_op jit(solution)/shard_map/ppermute | solution.py:2030
  1.2 197.0 %collective-permute-start.1 = (bf16[2048,512]{1,0:T(8,128)(2,1)}, bf16[2048,512]{1,0:T(8,128)(2,1)}, u32[]{:S(2)}, u32[]{:S(2)}) collective-permute-start(bf16[2048,512]{1,0:T(8,128)(2,1)} %up_own.1), channel_id=1, source_target_pairs={{0,4},{4,0},{8,12},{12,8},{1,5},{5,1},{9,13},{13,9},{2,6},{6,2},{1... | collective-permute-start | bytes 6291464 | tf_op jit(solution)/shard_map/ppermute | solution.py:2030
  1.2 196.9 %collective-permute-start.2 = (bf16[512,2048]{1,0:T(8,128)(2,1)}, bf16[512,2048]{1,0:T(8,128)(2,1)}, u32[]{:S(2)}, u32[]{:S(2)}) collective-permute-start(bf16[512,2048]{1,0:T(8,128)(2,1)} %down_own.3), channel_id=1, source_target_pairs={{0,4},{4,0},{8,12},{12,8},{1,5},{5,1},{9,13},{13,9},{2,6},{6,2},{1... | collective-permute-start | bytes 6291464 | tf_op jit(solution)/shard_map/ppermute | solution.py:2030
  607.4 5.5 copy-start
  612.9 3.0 copy-start.3
  612.9 3.0 copy-start.4
  615.9 2.8 copy-start.2
  615.9 3.7 copy-start.5
  619.6 2.8 copy-start.1
  619.6 3.7 copy-start.6
  623.3 2.8 copy-start.8
  626.2 1.6 copy-start.7

commit v10 on v9

--- a/solution.py
+++ b/solution.py
@@ -1505,10 +1505,10 @@
     places, own_places, queries, keyed_all, middle, grad_normed, tangent, gain, logs, hidden_all,
     down_own, down_twin, weights, cosine, sine,
     gate_sum, up_sum, down_sum, _gate, _up, _down, normed, attended,
-    branch, grad_qkv, term_two, gate_mirror, up_mirror, down_mirror,
+    out_v, grad_qkv, term_two, gate_mirror, up_mirror, down_mirror,
     twin_normed, twin_attended, twin_out, grad_out, grad_middle,
     out_across, both_attended, both_out, out_partial, out_send, out_recv,
-    norm_sem, gain_v, out_v, out_w, cosine_v, sine_v, grad_keyed, mirror_send, mirror_recv,
+    norm_sem, gain_v, branch, out_w, cosine_v, sine_v, grad_keyed, mirror_send, mirror_recv,
     query_v, keyed_v, grad_v, bias_v, log_v, scores, gradients, probs, slopes, key_sum, value_sum,
     down_w, hidden, load_sem,
     partial, from_across, from_line, total, across_send, across_recv, line_send, line_recv,
@@ -1754,7 +1754,14 @@
     pl.when(early == 0)(lambda: keyed_steps(pairs // group - 1))
     for copy in norm_copies:
         copy.wait()
+    for copy in norm_loads[:2]:
+        copy.start()
     scatter.own(branch)
+    for copy in norm_loads[:2]:
+        copy.wait()
+    for h in range(2):
+        c = slice(h * half_width, (h + 1) * half_width)
+        out_v[:, c] = (middle_v[h * rows : (h + 1) * rows, :] + branch[:, c]).astype(BF)
     keyed_scatter.own(grad_keyed)
     for g in range(pairs // group):
         both = grad_keyed[g * rows : (g + 1) * rows, :]
@@ -1783,7 +1790,7 @@
     return pl.pallas_call(
         functools.partial(back_kernel, line, parts),
         out_shape=(
-            shapes((rows, width), F32), shapes((rows, width + both), BF), shapes((1, width), F32),
+            shapes((rows, width), BF), shapes((rows, width + both), BF), shapes((1, width), F32),
             *(shapes(s.shape, BF) for s in sums), *(shapes((rows, width), BF),) * 4,
             shapes((rows, width), F32), shapes((line, run, width), BF),
         ),
@@ -1795,7 +1802,7 @@
             pltpu.VMEM((line, run, width), BF),
             pltpu.SemaphoreType.DMA((line,)), pltpu.SemaphoreType.DMA((line,)),
             pltpu.SemaphoreType.DMA((3, 2)), pltpu.VMEM(gain.shape, F32),
-            pltpu.VMEM((rows, width), BF), pltpu.VMEM((4, run, width), BF),
+            pltpu.VMEM((rows, width), F32), pltpu.VMEM((4, run, width), BF),
             pltpu.VMEM(cosine.shape, F32), pltpu.VMEM(sine.shape, F32),
             pltpu.VMEM((groups * rows, 256), F32),
             pltpu.SemaphoreType.DMA((6,)), pltpu.SemaphoreType.DMA((6,)),
@@ -2048,12 +2055,11 @@
     ) = front_call(pieces, rows, tangent, cosine, sine, gains, places, own_places, line)
     mid = width + 2 * narrow
     grad_normed, _, hidden_all, *sums = feed_call(normed_mlp, tangent_all, gates, ups, downs, line)[:9]
-    branch, grad_qkv, term_two, *others = back_call(
+    out, grad_qkv, term_two, *others = back_call(
         places, own_places, scaled_query, keyed_all, middle, grad_normed, tangent, gain, logs,
         hidden_all, downs, weights, cosine, -sine, sums[:3], sums[3:], normed_tokens, attended, line,
     )
     twins, (grad_branch, grad_middle, out_across) = others[3:6], others[6:]
-    outcome = middle + branch
     grad_w_gate, grad_w_up, grad_w_down = (
         a.astype(f32) + b.astype(f32) for a, b in zip(sums[:3], others[:3])
     )
@@ -2067,7 +2073,7 @@
         ends.append(packed[:, start : start + size])
         start += size
     return (
-        outcome.astype(bf16).reshape(tokens.shape),
+        out.reshape(tokens.shape),
         grad_tokens.reshape(tokens.shape),
         *ends,
         grad_w_out,

time: 630 us -> 628 us (level)
  no operation moved by 1% of the time
where the time goes in v10:
time: 628 us; the launch traced here: 627 us
  Pallas kernels  602 us (96%)
  other arithmetic  12.2 us (2%)
  local copies, waits for them, and re-layouts  10.8 us (2%)
    pallas_call x1, Pallas kernels, front_call(): pl.pallas_call(functools.partial(front_kernel, line, parts), out_shape=(s...  193 us
    pallas_call x1, Pallas kernels, feed_call(): pl.pallas_call(functools.partial(feed_kernel, line, parts, tile), out_sha...  182 us
    pallas_call x1, Pallas kernels, back_call(): pl.pallas_call(functools.partial(back_kernel, line, parts), out_shape=(sh...  128 us
    pallas_call x1, Pallas kernels, sums_call(): pl.pallas_call(functools.partial(sums_kernel, line), out_shape=(jax.Shape...  99.2 us
  transfers between devices with their start and end apart: 3, of which 0 were waited for; matrix products, arithmetic and copies ran while one was open for 0% of the time, Pallas kernels for 31%

profile of v10, /device:TPU:0, one launch (start us, length us, event | category | flops | bytes accessed | tf_op | source)
XLA Modules:
  0.0 627.0 jit_solution(10686425155857825765)
XLA Ops:
  0.6 0.5 collective-permute-start
  1.2 0.1 collective-permute-start.1
  1.2 0.4 collective-permute-start.2
  1.7 0.7 dynamic-slice_convert_fusion
  2.4 0.8 copy.30.own_places
  3.2 0.5 fusion
  3.7 1.0 fusion.1
  4.7 193.4 %front.1 = (bf16[256,2048]{1,0:T(8,128)(2,1)}, f32[256,2048]{1,0:T(8,128)}, bf16[256,2048]{1,0:T(8,128)(2,1)}, bf16[256,2048]{1,0:T(8,128)(2,1)}, bf16[256,2048]...) custom-call(bf16[128,2048]{1,0:T(8,128)(2,1)} %query_w.1, ...), custom_call_target="tpu_custom_call" | custom-call | tf_op jit(solution)/shard_map/front/pallas_call | solution.py:1473
  198.1 0.0 collective-permute-done.gate_twin
  198.1 0.0 collective-permute-done.1.up_twin
  198.1 0.0 collective-permute-done.2.down_twin
  198.1 181.5 %feed.1 = (f32[256,2048]{1,0:T(8,128)}, bf16[8,256,2048]{2,1,0:T(8,128)(2,1)}, bf16[2048,1024]{1,0:T(8,128)(2,1)}, bf16[2048,512]{1,0:T(8,128)(2,1)}, bf16[2048,...) custom-call(bf16[256,2048]{1,0:T(8,128)(2,1)} %get-tuple-element.47., ...), custom_call_target="tpu_custom_call" | custom-call | tf_op jit(solution)/shard_map/feed/pallas_call | solution.py:768
  379.7 128.2 %back.1 = (bf16[256,2048]{1,0:T(8,128)(2,1)}, bf16[256,3072]{1,0:T(8,128)(2,1)}, f32[1,2048]{1,0:T(1,128)}, bf16[2048,512]{1,0:T(8,128)(2,1)}, bf16[2048,512]{1,...) custom-call(s32[1,1024]{1,0:T(1,128)} %places.3, ...), custom_call_target="tpu_custom_call", output_to_operand_aliasing={{3}: (18, {}), {4}: (19, {}), {5}: (20, {})} | custom-call | tf_op jit(solution)/shard_map/back/pallas_call | solution.py:1790
  507.9 99.2 %sums.1 = (f32[128,3200]{1,0:T(8,128)}, f32[128,2048]{1,0:T(8,128)}, bf16[256,2048]{1,0:T(8,128)(2,1)}) custom-call(bf16[256,2048]{1,0:T(8,128)(2,1)} %get-tuple-element.60.normed, bf16[256,2048]{1,0:T(8,128)(2,1)} %get-tuple-element.61.attended, bf16[256,3072]{1,0:T(8,128)(2,1)} %get-tuple-element.63.grad_qkv, ...), custom_call_target="tpu_custom_call" | custom-call | tf_op jit(solution)/shard_map/sums/pallas_call | solution.py:1059
  607.0 0.0 copy-start.2
  607.0 1.4 slice_bitcast_fusion
  608.4 1.9 fusion.2
  610.3 2.3 slice.18
  612.6 0.0 copy-done.2
  612.6 0.0 copy-start.1
  612.6 0.0 copy-start.3
  612.6 4.4 convert_add_fusion.2
  616.9 0.0 copy-done.1
  616.9 0.0 copy-done.3
  616.9 0.0 copy-start
  616.9 0.0 copy-start.4
  616.9 2.8 convert_add_fusion.1
  619.7 0.0 copy-done
  619.7 1.0 copy-done.4
  620.7 0.0 copy-start.5
  620.7 2.8 convert_add_fusion
  623.5 0.0 copy-start.7
  623.5 0.0 copy-done.5
  623.5 0.0 copy-start.6
  623.5 1.0 copy.37
  624.5 0.6 copy-done.7
  625.1 1.0 copy.38
  626.1 0.0 copy-done.6
  626.1 1.0 copy.39
  (1 shorter events, 0.0 us)
Async XLA Ops:
  0.6 197.5 %collective-permute-start = (bf16[2048,512]{1,0:T(8,128)(2,1)}, bf16[2048,512]{1,0:T(8,128)(2,1)}, u32[]{:S(2)}, u32[]{:S(2)}) collective-permute-start(bf16[2048,512]{1,0:T(8,128)(2,1)} %gate_own.1), channel_id=1, source_target_pairs={{0,4},{4,0},{8,12},{12,8},{1,5},{5,1},{9,13},{13,9},{2,6},{6,2},{1... | collective-permute-start | bytes 6291464 | tf_op jit(solution)/shard_map/ppermute | solution.py:2037
  1.2 197.0 %collective-permute-start.1 = (bf16[2048,512]{1,0:T(8,128)(2,1)}, bf16[2048,512]{1,0:T(8,128)(2,1)}, u32[]{:S(2)}, u32[]{:S(2)}) collective-permute-start(bf16[2048,512]{1,0:T(8,128)(2,1)} %up_own.1), channel_id=1, source_target_pairs={{0,4},{4,0},{8,12},{12,8},{1,5},{5,1},{9,13},{13,9},{2,6},{6,2},{1... | collective-permute-start | bytes 6291464 | tf_op jit(solution)/shard_map/ppermute | solution.py:2037
  1.2 196.9 %collective-permute-start.2 = (bf16[512,2048]{1,0:T(8,128)(2,1)}, bf16[512,2048]{1,0:T(8,128)(2,1)}, u32[]{:S(2)}, u32[]{:S(2)}) collective-permute-start(bf16[512,2048]{1,0:T(8,128)(2,1)} %down_own.3), channel_id=1, source_target_pairs={{0,4},{4,0},{8,12},{12,8},{1,5},{5,1},{9,13},{13,9},{2,6},{6,2},{1... | collective-permute-start | bytes 6291464 | tf_op jit(solution)/shard_map/ppermute | solution.py:2037
  607.0 5.5 copy-start.2
  612.6 4.4 copy-start.1
  612.6 4.4 copy-start.3
  616.9 2.8 copy-start
  616.9 3.7 copy-start.4
  620.7 2.8 copy-start.5
  623.5 1.6 copy-start.7
  623.5 2.6 copy-start.6
